TPU v7x, 32 devices: a whole 2x2x4 slice. The times are simulated.
32 devices in a mesh: tok: 8 (over z, y), tp: 4 (over x, core).
Axes of the slice: x: 2, y: 2, z: 4, core: 2. Of those that a mesh axis runs over, the one named last changes fastest.
Arguments:
- block_input: bfloat16 [24, 1152, 1024], P('tok', 'tp'), may hold values from -6 to 6
- condition: bfloat16 [24, 1152], P('tok'), may hold values from -6 to 6
- timesteps: int32 [24], P('tok'), may hold values from 0 to 999
- head_mask: int32 [24, 16], P('tok', 'tp'), may hold values from 0 to 1, as said below
- group_mask: int32 [24, 16], P('tok', 'tp'), may hold values from 0 to 1, as said below
- w_ada: bfloat16 [1152, 6, 1152], P('tok', None, 'tp'), may hold values from -0.176776695 to 0.176776695
- b_ada: bfloat16 [6, 1152], P(None, 'tp'), may hold values from -2 to 2
- w_qkv: bfloat16 [1152, 3, 1152], P('tok', None, 'tp'), may hold values from -0.176776695 to 0.176776695
- b_qv: bfloat16 [2, 1152], P(None, 'tp'), may hold values from -2 to 2
- w_out: bfloat16 [1152, 1152], P('tp', 'tok'), may hold values from -0.70710678 to 0.70710678
- b_out: bfloat16 [1152], P('tp'), may hold values from -2 to 2
- w_up: bfloat16 [1152, 4608], P('tok', 'tp'), may hold values from -0.176776695 to 0.176776695
- b_up: bfloat16 [4608], P('tp'), may hold values from -2 to 2
- w_down: bfloat16 [4608, 1152], P('tp', 'tok'), may hold values from -0.176776695 to 0.176776695
- b_down: bfloat16 [1152], P('tp'), may hold values from -2 to 2
- w_head: bfloat16 [256, 16], P('tok', 'tp'), may hold values from -0.375 to 0.375
- b_head: bfloat16 [16], P('tp'), may hold values from -2.5 to 2.5
- w_group: bfloat16 [256, 16], P('tok', 'tp'), may hold values from -0.375 to 0.375
- b_group: bfloat16 [16], P('tp'), may hold values from -2.5 to 2.5
- cotangent: bfloat16 [24, 1152, 1024], P('tok', 'tp'), may hold values from -6 to 6
Outputs:
- block_output: bfloat16 [24, 1152, 1024], P('tok', 'tp')
- grad_input: float32 [24, 1152, 1024], P('tok', 'tp')
- grad_condition: float32 [24, 1152], P('tok')
- grad_w_ada: float32 [1152, 6, 1152], P('tok', None, 'tp')
- grad_b_ada: float32 [6, 1152], P(None, 'tp')
- grad_w_qkv: float32 [1152, 3, 1152], P('tok', None, 'tp')
- grad_b_qv: float32 [2, 1152], P(None, 'tp')
- grad_w_out: float32 [1152, 1152], P('tp', 'tok')
- grad_b_out: float32 [1152], P('tp')
- grad_w_up: float32 [1152, 4608], P('tok', 'tp')
- grad_b_up: float32 [4608], P('tp')
- grad_w_down: float32 [4608, 1152], P('tp', 'tok')
- grad_b_down: float32 [1152], P('tp')
- grad_w_head: float32 [256, 16], P('tok', 'tp')
- grad_b_head: float32 [16], P('tp')
- grad_w_group: float32 [256, 16], P('tok', 'tp')
- grad_b_group: float32 [16], P('tp')
Inputs may be any that keep to these rules, and one draw needn't show every extreme that they name: `head_mask`: an image with timestep t keeps exactly 16 - (3 * 16 * t) // 4000 heads; which ones varies from image to image. `group_mask`: an image with timestep t keeps exactly 16 - (3 * 16 * t) // 4000 channel groups; which ones varies from image to image.
All inputs are finite; a program needn't handle non-finite values.
Results may differ from a plain program's by a relative error of at most 0.009.
Values may be sent and summed in bfloat16 or wider, within the bound.
A program may use at most 192 MiB of HBM per device.

v0:
```python
import math

import jax
import jax.numpy as jnp
from jax import lax
from jax.sharding import PartitionSpec as P

D = 1152
HD = 72
FF = 4608
FREQ = 256
GROUPS = 16
LEN = 1024


wide_type = jnp.float32
narrow_type = jnp.bfloat16
eps_norm = 1e-06
exact_mode = lax.Precision.HIGHEST


def embed_time(timesteps):
    half_width = FREQ // 2
    indices = jnp.arange(half_width, dtype=wide_type)
    freq_rates = jnp.exp(-math.log(10000.0) * indices / half_width)
    angles = timesteps.astype(wide_type)[:, None] * freq_rates[None, :]
    return jnp.concatenate([jnp.cos(angles), jnp.sin(angles)], axis=1)


def pick_mod(modulation, index):
    return modulation[:, index][:, None, :]


def smooth_gate(values):
    return jax.nn.gelu(values, approximate=True)


def row_stats(values):
    totals = lax.psum((jnp.sum(values, axis=-1), jnp.sum(values * values, axis=-1)), "tp")
    centre = totals[0] / D
    spread = totals[1] / D - centre * centre
    inverse = lax.rsqrt(spread + eps_norm)
    return ((values - centre[..., None]) * inverse[..., None], inverse)


def attend_item(inputs):
    queries, keys_in, values_in = inputs
    scores = jnp.dot(queries, keys_in.T, preferred_element_type=wide_type) * HD ** (-0.5)
    highest = jnp.max(scores, axis=-1, keepdims=True)
    totals = jnp.sum(jnp.exp(scores - highest), axis=-1, keepdims=True)
    logsum = highest + jnp.log(totals)
    weights = jnp.exp(scores - logsum).astype(narrow_type)
    return (jnp.dot(weights, values_in, preferred_element_type=wide_type), logsum[:, 0])


def attend_back(inputs):
    queries, keys_in, values_in, grad_items, logsum = inputs
    factor = HD ** (-0.5)
    scores = jnp.dot(queries, keys_in.T, preferred_element_type=wide_type) * factor
    weights = jnp.exp(scores - logsum[:, None])
    grad_weights = jnp.dot(grad_items, values_in.T, preferred_element_type=wide_type)
    grad_values = jnp.dot(
        weights.astype(narrow_type).T, grad_items, preferred_element_type=wide_type
    )
    inner_sum = jnp.sum(weights * grad_weights, axis=-1, keepdims=True)
    grad_scores = (weights * (grad_weights - inner_sum)).astype(narrow_type)
    grad_queries = jnp.dot(grad_scores, keys_in, preferred_element_type=wide_type) * factor
    grad_keys = jnp.dot(grad_scores.T, queries, preferred_element_type=wide_type) * factor
    return (
        grad_queries.astype(narrow_type),
        grad_keys.astype(narrow_type),
        grad_values.astype(narrow_type),
    )


def body(
    block_input,
    condition,
    timesteps,
    head_mask,
    group_mask,
    w_ada,
    b_ada,
    w_qkv,
    b_qv,
    w_out,
    b_out,
    w_up,
    b_up,
    w_down,
    b_down,
    w_head,
    b_head,
    w_group,
    b_group,
    cotangent,
):
    images = condition.shape[0]
    local_width = block_input.shape[1]
    local_heads = head_mask.shape[1]
    local_groups = group_mask.shape[1]
    group_width = FF // GROUPS

    def fetch_weights():
        return (
            lax.all_gather(w_ada, "tok", axis=0, tiled=True),
            lax.all_gather(w_qkv, "tok", axis=0, tiled=True),
            lax.all_gather(w_up, "tok", axis=0, tiled=True),
            lax.all_gather(w_head, "tok", axis=0, tiled=True),
            lax.all_gather(w_group, "tok", axis=0, tiled=True),
            lax.all_gather(w_out, "tok", axis=1, tiled=True),
            lax.all_gather(w_down, "tok", axis=1, tiled=True),
        )

    def to_items(tensor):
        shaped = tensor.reshape(images, LEN, local_heads, HD).transpose(0, 2, 1, 3)
        return shaped.reshape(images * local_heads, LEN, HD)

    def from_items(tensor):
        shaped = tensor.reshape(images, local_heads, LEN, HD).transpose(0, 2, 1, 3)
        return shaped.reshape(images, LEN, local_width)

    ada_full, qkv_full, up_full, head_full, group_full, out_full, down_full = fetch_weights()
    time_feat = embed_time(timesteps).astype(narrow_type)
    cond_wide = condition.astype(wide_type)
    cond_act = jax.nn.silu(cond_wide).astype(narrow_type)
    modulation = jnp.einsum(
        "bd,dke->bke", cond_act, ada_full, preferred_element_type=wide_type
    ) + b_ada.astype(wide_type)
    head_sig = jax.nn.sigmoid(
        jnp.dot(time_feat, head_full, preferred_element_type=wide_type) + b_head.astype(wide_type)
    )
    head_gate = head_mask.astype(wide_type) * head_sig
    group_sig = jax.nn.sigmoid(
        jnp.dot(time_feat, group_full, preferred_element_type=wide_type) + b_group.astype(wide_type)
    )
    group_gate = group_mask.astype(wide_type) * group_sig
    row_data = jnp.transpose(block_input.astype(wide_type), (0, 2, 1))
    normed_one, inverse_one = row_stats(row_data)
    scale_one = pick_mod(modulation, 1)
    attn_in = (normed_one * (1.0 + scale_one) + pick_mod(modulation, 0)).astype(narrow_type)
    attn_full = lax.all_gather(attn_in, "tp", axis=2, tiled=True)
    projected = jnp.einsum("bld,dke->blke", attn_full, qkv_full, preferred_element_type=wide_type)
    queries = (projected[:, :, 0] + b_qv[0].astype(wide_type)).astype(narrow_type)
    keys_in = projected[:, :, 1].astype(narrow_type)
    values_in = (projected[:, :, 2] + b_qv[1].astype(wide_type)).astype(narrow_type)
    item_inputs = (to_items(queries), to_items(keys_in), to_items(values_in))
    attn_raw, logsum = lax.map(attend_item, item_inputs)
    attn_out = from_items(attn_raw)
    gate_cols = jnp.repeat(head_gate, HD, axis=1)
    concat = (attn_out * gate_cols[:, None, :]).astype(narrow_type)
    attn_part = jnp.einsum("blh,he->ble", concat, out_full, preferred_element_type=wide_type)
    branch_one = lax.psum_scatter(attn_part, "tp", scatter_dimension=2, tiled=True) + b_out.astype(
        wide_type
    )
    gate_one = pick_mod(modulation, 2)
    mid_rows = row_data + gate_one * branch_one
    normed_two, inverse_two = row_stats(mid_rows)
    scale_two = pick_mod(modulation, 4)
    mlp_in = (normed_two * (1.0 + scale_two) + pick_mod(modulation, 3)).astype(narrow_type)
    mlp_full = lax.all_gather(mlp_in, "tp", axis=2, tiled=True)
    hidden_pre = jnp.einsum(
        "bld,df->blf", mlp_full, up_full, preferred_element_type=wide_type
    ) + b_up.astype(wide_type)
    activated = smooth_gate(hidden_pre)
    group_cols = jnp.repeat(group_gate, group_width, axis=1)
    hidden = (activated * group_cols[:, None, :]).astype(narrow_type)
    mlp_part = jnp.einsum("blf,fe->ble", hidden, down_full, preferred_element_type=wide_type)
    branch_two = lax.psum_scatter(
        mlp_part.astype(jnp.bfloat16), "tp", scatter_dimension=2, tiled=True
    ).astype(jnp.float32) + b_down.astype(wide_type)
    gate_two = pick_mod(modulation, 5)
    block_output = jnp.transpose((mid_rows + gate_two * branch_two).astype(narrow_type), (0, 2, 1))
    ada_back, qkv_back, up_back, head_back, group_back, out_back, down_back = fetch_weights()
    grad_out = jnp.transpose(cotangent.astype(wide_type), (0, 2, 1))
    grad_gate_two = jnp.sum(grad_out * branch_two, axis=1)
    grad_two = (gate_two * grad_out).astype(narrow_type)
    grad_b_down = jnp.sum(grad_two.astype(wide_type), axis=(0, 1))
    grad_two_full = lax.all_gather(grad_two, "tp", axis=2, tiled=True)
    grad_w_down = jnp.einsum("blf,ble->fe", hidden, grad_two_full, preferred_element_type=wide_type)
    grad_hid = jnp.einsum("ble,fe->blf", grad_two_full, down_back, preferred_element_type=wide_type)
    grad_group_gate = jnp.sum(
        (grad_hid * activated).reshape(images, LEN, local_groups, group_width), axis=(1, 3)
    )
    gelu_back = jax.vjp(smooth_gate, hidden_pre)[1]
    grad_pre = gelu_back(grad_hid * group_cols[:, None, :])[0].astype(narrow_type)
    grad_b_up = jnp.sum(grad_pre.astype(wide_type), axis=(0, 1))
    grad_w_up = jnp.einsum("bld,blf->df", mlp_full, grad_pre, preferred_element_type=wide_type)
    grad_mlp_part = jnp.einsum("blf,df->bld", grad_pre, up_back, preferred_element_type=wide_type)
    grad_norm_two = lax.psum_scatter(grad_mlp_part, "tp", scatter_dimension=2, tiled=True)
    grad_shift_two = jnp.sum(grad_norm_two, axis=1)
    grad_scale_two = jnp.sum(grad_norm_two * normed_two, axis=1)
    grad_n_two = grad_norm_two * (1.0 + scale_two)
    sums_two = lax.psum(
        (jnp.sum(grad_n_two, axis=-1), jnp.sum(grad_n_two * normed_two, axis=-1)), "tp"
    )
    grad_mid = grad_out + inverse_two[..., None] * (
        grad_n_two - sums_two[0][..., None] / D - normed_two * sums_two[1][..., None] / D
    )
    grad_gate_one = jnp.sum(grad_mid * branch_one, axis=1)
    grad_one = (gate_one * grad_mid).astype(narrow_type)
    grad_b_out = jnp.sum(grad_one.astype(wide_type), axis=(0, 1))
    grad_one_full = lax.all_gather(grad_one, "tp", axis=2, tiled=True)
    grad_w_out = jnp.einsum("blh,ble->he", concat, grad_one_full, preferred_element_type=wide_type)
    grad_concat = jnp.einsum(
        "ble,he->blh", grad_one_full, out_back, preferred_element_type=wide_type
    )
    grad_head_gate = jnp.sum(
        (attn_out * grad_concat).reshape(images, LEN, local_heads, HD), axis=(1, 3)
    )
    grad_mixed = (grad_concat * gate_cols[:, None, :]).astype(narrow_type)
    back_inputs = item_inputs + (to_items(grad_mixed), logsum)
    grad_q_items, grad_k_items, grad_v_items = lax.map(attend_back, back_inputs)
    grad_queries = from_items(grad_q_items)
    grad_values = from_items(grad_v_items)
    grad_qkv = jnp.stack([grad_queries, from_items(grad_k_items), grad_values], axis=2)
    grad_b_qv = jnp.stack(
        [
            jnp.sum(grad_queries.astype(wide_type), axis=(0, 1)),
            jnp.sum(grad_values.astype(wide_type), axis=(0, 1)),
        ]
    )
    grad_w_qkv = jnp.einsum("bld,blke->dke", attn_full, grad_qkv, preferred_element_type=wide_type)
    grad_attn_part = jnp.einsum(
        "blke,dke->bld", grad_qkv, qkv_back, preferred_element_type=wide_type
    )
    grad_norm_one = lax.psum_scatter(
        grad_attn_part.astype(jnp.bfloat16), "tp", scatter_dimension=2, tiled=True
    ).astype(jnp.float32)
    grad_shift_one = jnp.sum(grad_norm_one, axis=1)
    grad_scale_one = jnp.sum(grad_norm_one * normed_one, axis=1)
    grad_n_one = grad_norm_one * (1.0 + scale_one)
    grad_modulation = jnp.stack(
        [
            grad_shift_one,
            grad_scale_one,
            grad_gate_one,
            grad_shift_two,
            grad_scale_two,
            grad_gate_two,
        ],
        axis=1,
    )
    cond_part = jnp.einsum(
        "bke,dke->bd", grad_modulation, ada_back.astype(wide_type), precision=exact_mode
    )
    sums_one = lax.psum(
        (jnp.sum(grad_n_one, axis=-1), jnp.sum(grad_n_one * normed_one, axis=-1), cond_part), "tp"
    )
    grad_input = grad_mid + inverse_one[..., None] * (
        grad_n_one - sums_one[0][..., None] / D - normed_one * sums_one[1][..., None] / D
    )
    grad_condition = jax.vjp(jax.nn.silu, cond_wide)[1](sums_one[2])[0]
    grad_w_ada = jnp.einsum(
        "bd,bke->dke", cond_act.astype(wide_type), grad_modulation, precision=exact_mode
    )
    grad_b_ada = jnp.sum(grad_modulation, axis=0)
    time_wide = time_feat.astype(wide_type)
    head_logit = grad_head_gate * head_mask.astype(wide_type) * head_sig * (1.0 - head_sig)
    grad_w_head = jnp.dot(time_wide.T, head_logit, precision=exact_mode)
    grad_b_head = jnp.sum(head_logit, axis=0)
    group_logit = grad_group_gate * group_mask.astype(wide_type) * group_sig * (1.0 - group_sig)
    grad_w_group = jnp.dot(time_wide.T, group_logit, precision=exact_mode)
    grad_b_group = jnp.sum(group_logit, axis=0)
    reduced = (
        lax.psum_scatter(grad_w_ada, "tok", scatter_dimension=0, tiled=True),
        lax.psum_scatter(grad_w_qkv, "tok", scatter_dimension=0, tiled=True),
        lax.psum_scatter(grad_w_up, "tok", scatter_dimension=0, tiled=True),
        lax.psum_scatter(grad_w_head, "tok", scatter_dimension=0, tiled=True),
        lax.psum_scatter(grad_w_group, "tok", scatter_dimension=0, tiled=True),
        lax.psum_scatter(grad_w_out, "tok", scatter_dimension=1, tiled=True),
        lax.psum_scatter(grad_w_down, "tok", scatter_dimension=1, tiled=True),
    )
    biases = lax.psum(
        (grad_b_ada, grad_b_qv, grad_b_out, grad_b_up, grad_b_down, grad_b_head, grad_b_group),
        "tok",
    )
    return (
        block_output,
        jnp.transpose(grad_input, (0, 2, 1)),
        grad_condition,
        reduced[0],
        biases[0],
        reduced[1],
        biases[1],
        reduced[5],
        biases[2],
        reduced[2],
        biases[3],
        reduced[6],
        biases[4],
        reduced[3],
        biases[5],
        reduced[4],
        biases[6],
    )


def solution(mesh):
    return jax.shard_map(
        body,
        mesh=mesh,
        in_specs=(
            P("tok", "tp", None),
            P("tok", None),
            P("tok"),
            P("tok", "tp"),
            P("tok", "tp"),
            P("tok", None, "tp"),
            P(None, "tp"),
            P("tok", None, "tp"),
            P(None, "tp"),
            P("tp", "tok"),
            P("tp"),
            P("tok", "tp"),
            P("tp"),
            P("tp", "tok"),
            P("tp"),
            P("tok", "tp"),
            P("tp"),
            P("tok", "tp"),
            P("tp"),
            P("tok", "tp", None),
        ),
        out_specs=(
            P("tok", "tp", None),
            P("tok", "tp", None),
            P("tok", None),
            P("tok", None, "tp"),
            P(None, "tp"),
            P("tok", None, "tp"),
            P(None, "tp"),
            P("tp", "tok"),
            P("tp"),
            P("tok", "tp"),
            P("tp"),
            P("tp", "tok"),
            P("tp"),
            P("tok", "tp"),
            P("tp"),
            P("tok", "tp"),
            P("tp"),
        ),
        check_vma=False,
    )
```

profile of v0, /device:TPU:0, one launch (start us, length us, event | category | flops | bytes accessed | tf_op | source)
XLA Modules:
  0.0 1885.9 jit_solution(13868853548286337409)
XLA Ops:
  11.5 12.9 all-reduce.4
  24.5 75.6 %all-gather.11.cloned.1.call-done = bf16[1152,6,288]{2,0,1:T(8,128)(2,1)} async-done(((bf16[144,6,288]{2,0,1:T(8,128)(2,1)}), bf16[1152,6,288]{2,0,1:T(8,128)(2,1)}) %all-gather.11.cloned.1.call-update) | async-done | bytes 3981328 | tf_op jit(solution)/shard_map/all_gather | solution.py:106
  100.1 3.3 convolution_add_fusion
  106.7 17.8 all-gather
  125.7 36.9 %all_gather.42 = bf16[288,1152]{0,1:T(8,128)(2,1)} all-gather(bf16[288,144]{0,1:T(8,128)(2,1)S(1)} %copy-done.15), channel_id=1, replica_groups=mesh['tok'=8,'tp'=4] {'tok'}, dimensions={1}, use_global_device_ids=true | all-gather | bytes 746496 | tf_op jit(solution)/shard_map/all_gather | solution.py:111
  162.6 5.1 all-gather.15.cloned.1.call-done
  167.7 52.9 %all-gather.13.cloned.1.call-done = bf16[3,1024,1152]{1,2,0:T(8,128)(2,1)} async-done(((bf16[3,1024,288]{1,2,0:T(8,128)(2,1)}), bf16[3,1024,1152]{1,2,0:T(8,128)(2,1)}) %all-gather.13.cloned.1.call-update) | async-done | bytes 7077904 | tf_op jit(solution)/shard_map/all_gather | solution.py:142
  220.6 11.7 fusion.62
  235.6 2.8 copy.90
  239.7 3.2 copy.88
  245.8 4.4 copy.89
  250.2 76.2 %while.26 = (s32[]{:T(128)}, f32[12,1024,72]{1,2,0:T(8,128)}, f32[12,1024]{1,0:T(8,128)}, bf16[12,1024,72]{2,1,0:T(8,128)(2,1)S(1)}, bf16[12,1024,72]{2,1,0:T(8,...) while((s32[]{:T(128)}, f32[12,1024,72]{1,2,0:T(8,128)}, f32[12,1024]{1,0:T(8,128)}, ...), condition=%wide.region_7.8_spmd, body=%wide.region_4.7_spmd.sunk | while | flops 310377472 | bytes 13703257 | solution.py:148
  252.6 2.5 fusion.176
  259.0 2.5 fusion.176
  265.3 2.5 fusion.176
  278.0 2.5 fusion.176
  284.4 2.5 fusion.176
  297.1 2.5 fusion.176
  303.4 2.5 fusion.176
  316.1 2.5 fusion.176
  322.5 2.5 fusion.176
  326.4 3.4 fusion.80
  331.2 7.0 fusion.112
  343.5 104.3 %reduce-scatter.16.cloned.1.call-done = f32[3,1024,288]{1,2,0:T(8,128)} async-done(((f32[3,1024,1152]{1,2,0:T(8,128)}), f32[3,1024,288]{1,2,0:T(8,128)}) %reduce-scatter.16.cloned.1.call-update) | async-done | bytes 3538960 | tf_op jit(solution)/shard_map/reduce_scatter | solution.py:153
  447.9 4.2 fusion.136
  452.0 11.3 all-reduce.3
  467.3 20.9 %all-gather.1 = bf16[8,32,4]{1,2,0:T(4,128)(2,1)S(1)} all-gather(bf16[1,32,4]{1,2,0:T(4,128)(2,1)} %bitcast.292), channel_id=1, replica_groups=mesh['tok'=8,'tp'=4] {'tok'}, dimensions={0}, use_global_device_ids=true | all-gather | bytes 2304 | tf_op jit(solution)/shard_map/all_gather | solution.py:110
  495.6 9.4 all-gather.21.cloned.1.call-done
  504.9 51.5 %all-gather.23.cloned.1.call-done = bf16[3,1024,1152]{1,2,0:T(8,128)(2,1)} async-done(((bf16[3,1024,288]{1,2,0:T(8,128)(2,1)}), bf16[3,1024,1152]{1,2,0:T(8,128)(2,1)}) %all-gather.23.cloned.1.call-update) | async-done | bytes 7077904 | tf_op jit(solution)/shard_map/all_gather | solution.py:179
  556.4 16.2 fusion.91
  572.6 41.0 %all-gather.19.cloned.1.call-done = bf16[1152,1152]{1,0:T(8,128)(2,1)} async-done(((bf16[144,1152]{1,0:T(8,128)(2,1)}), bf16[1152,1152]{1,0:T(8,128)(2,1)}) %all-gather.19.cloned.1.call-update) | async-done | bytes 2654224 | tf_op jit(solution)/shard_map/all_gather | solution.py:108
  613.6 51.0 %all-gather.17.cloned.1.call-done = bf16[3,1024,1152]{1,2,0:T(8,128)(2,1)} async-done(((bf16[3,1024,288]{1,2,0:T(8,128)(2,1)}), bf16[3,1024,1152]{1,2,0:T(8,128)(2,1)}) %all-gather.17.cloned.1.call-update) | async-done | bytes 7077904 | tf_op jit(solution)/shard_map/all_gather | solution.py:161
  664.7 30.7 %convert_reduce_fusion = (f32[1152]{0:T(1024)}, bf16[3,1024,1152]{2,1,0:T(8,128)(2,1)S(1)}, f32[3,1152]{1,0:T(4,128)}, f32[3,1024,1152]{2,1,0:T(8,128)}) fusion(f32[1152]{0:T(1024)} %convert_element_type.162, f32[3,1024,1152]{2,1,0:T(8,128)} %fusion.91, f32[3,1152]{1,0:T(4,128)} %mul.333, bf16[3,1024,1152]{1,2,0:T(8,128)(2,1)} %all-gather.17.cloned.1.call-done, ...), kind=kOutput, calls=%fused_computation.67 | convolution fusion | flops 8249273856 | bytes 45158400 | tf_op jit(solution)/shard_map/bld,df->blf/dot_general | solution.py:162
  695.3 2.8 copy-done.45
  698.1 11.9 fusion.94
  710.1 16.3 convolution_convert_fusion
  727.7 92.0 %reduce-scatter.20.cloned.1.call-done = f32[3,1024,288]{1,2,0:T(8,128)} async-done(((f32[3,1024,1152]{1,2,0:T(8,128)}), f32[3,1024,288]{1,2,0:T(8,128)}) %reduce-scatter.20.cloned.1.call-update) | async-done | bytes 3538960 | tf_op jit(solution)/shard_map/reduce_scatter | solution.py:190
  819.7 4.0 multiply_reduce_fusion.3
  823.7 11.5 all-reduce.2
  836.5 49.4 %reduce-scatter.18.cloned.1.call-done = bf16[3,1024,288]{1,2,0:T(8,128)(2,1)} async-done(((bf16[3,1024,1152]{1,2,0:T(8,128)(2,1)}), bf16[3,1024,288]{1,2,0:T(8,128)(2,1)}) %reduce-scatter.18.cloned.1.call-update) | async-done | bytes 1769488 | tf_op jit(solution)/shard_map/reduce_scatter | solution.py:169
  885.9 8.6 convert_reduce_fusion.3
  894.6 50.9 %all-gather.25.cloned.1.call-done = bf16[3,1024,1152]{1,2,0:T(8,128)(2,1)} async-done(((bf16[3,1024,288]{1,2,0:T(8,128)(2,1)}), bf16[3,1024,1152]{1,2,0:T(8,128)(2,1)}) %all-gather.25.cloned.1.call-update) | async-done | bytes 7077904 | tf_op jit(solution)/shard_map/all_gather | solution.py:203
  945.5 6.2 fusion.110
  953.9 3.4 copy.83
  957.3 140.2 %while.27 = (s32[]{:T(128)}, bf16[12,1024,72]{1,2,0:T(8,128)(2,1)}, bf16[12,1024,72]{1,2,0:T(8,128)(2,1)}, bf16[12,1024,72]{1,2,0:T(8,128)(2,1)}, bf16[12,1024,7...) while((s32[]{:T(128)}, bf16[12,1024,72]{1,2,0:T(8,128)(2,1)}, ...), condition=%wide.region_21.22_spmd, body=%wide.region_19.21_spmd.sunk | while | flops 767925248 | bytes 33768552 | solution.py:213
  1097.5 12.1 bitcast_convert_fusion
  1112.8 16.2 convolution_bitcast_fusion.1
  1129.8 19.1 %convolution_bitcast_fusion = f32[1152,1152]{0,1:T(8,128)} fusion(bf16[3,1024,1152]{1,2,0:T(8,128)(2,1)} %all-gather.23.cloned.1.call-done, f32[3,1152]{1,0:T(4,128)S(1)} %copy-done.27, f32[3,1024,1152]{2,1,0:T(8,128)} %get-tuple-element.260, f32[1152]{0:T(1024)S(1)} %copy-done.38), kind=kOutput, calls=%fused_computation.70 | convolution fusion | flops 8192655360 | bytes 26560512 | tf_op jit(solution)/shard_map/blf,ble->fe/dot_general | solution.py:180
  1150.4 7.3 convolution_bitcast_fusion.2
  1157.8 13.8 fusion.67
  1171.6 4.5 multiply_reduce_fusion.4
  1176.2 3.7 fusion.75
  1180.6 7.2 fusion.123
  1189.1 48.7 %reduce-scatter.36.cloned.1.call-done = f32[32,4]{1,0:T(8,128)} async-done(((f32[256,4]{1,0:T(8,128)}), f32[32,4]{1,0:T(8,128)}) %reduce-scatter.36.cloned.1.call-update) | async-done | bytes 528
  1247.7 53.7 %reduce-scatter.34.cloned.1.call-done = f32[32,4]{1,0:T(8,128)} async-done(((f32[256,4]{1,0:T(8,128)}), f32[32,4]{1,0:T(8,128)}) %reduce-scatter.34.cloned.1.call-update) | async-done | bytes 528
  1304.2 38.1 %all-reduce = (f32[6,288]{1,0:T(8,128)}, f32[2,288]{1,0:T(2,128)}, f32[288]{0:T(512)}, f32[1152]{0:T(1024)}, f32[288]{0:T(512)}, /*index=5*/f32[4]{0:T(128)}, f32[4]{0:T(128)}) all-reduce(f32[6,288]{1,0:T(8,128)} %reduce_sum.262, f32[2,288]{1,0:T(2,128)} %pad_maximum_fusion.7, ...), channel_id=1, replica_groups=mesh['tok'=8,'tp'=4] {'tok'}, use_global_device_ids=true, to_apply=%region_36.37 | all-reduce | flops 4040 | bytes 32320 | tf_op jit(solution)/shard_map/psum | solution.py:274
  1342.3 7.4 convolution_bitcast_fusion.3
  1349.7 12.5 all-reduce.1
  1364.3 5.2 fusion.73
  1369.5 39.6 %reduce-scatter.30.cloned.1.call-done = f32[144,1152]{1,0:T(8,128)} async-done(((f32[1152,1152]{1,0:T(8,128)}), f32[144,1152]{1,0:T(8,128)}) %reduce-scatter.30.cloned.1.call-update) | async-done | bytes 663568 | tf_op jit(solution)/shard_map/reduce_scatter | solution.py:268
  1409.2 108.4 %reduce-scatter.32.cloned.1.call-done = f32[1152,144]{0,1:T(8,128)} async-done(((f32[1152,1152]{0,1:T(8,128)}), f32[1152,144]{0,1:T(8,128)}) %reduce-scatter.32.cloned.1.call-update) | async-done | bytes 663568 | tf_op jit(solution)/shard_map/reduce_scatter | solution.py:272
  1517.5 69.7 %reduce-scatter.28.cloned.1.call-done = f32[288,144]{0,1:T(8,128)} async-done(((f32[288,1152]{0,1:T(8,128)}), f32[288,144]{0,1:T(8,128)}) %reduce-scatter.28.cloned.1.call-update) | async-done | bytes 165904 | tf_op jit(solution)/shard_map/reduce_scatter | solution.py:271
  1587.2 107.5 %reduce-scatter.26.cloned.1.call-done = f32[144,3,288]{2,0,1:T(8,128)} async-done(((f32[1152,3,288]{2,0,1:T(8,128)}), f32[144,3,288]{2,0,1:T(8,128)}) %reduce-scatter.26.cloned.1.call-update) | async-done | bytes 497680 | tf_op jit(solution)/shard_map/reduce_scatter | solution.py:267
  1694.8 184.3 %reduce-scatter.24.cloned.1.call-done = f32[144,6,288]{2,0,1:T(8,128)} async-done(((f32[1152,6,288]{2,0,1:T(8,128)}), f32[144,6,288]{2,0,1:T(8,128)}) %reduce-scatter.24.cloned.1.call-update) | async-done | bytes 995344 | tf_op jit(solution)/shard_map/reduce_scatter | solution.py:266
  (332 shorter events, 254.2 us)
Async XLA Ops:
  7.2 92.9 %all-gather.11.cloned.1.call-start = ((), (), s32[]{:S(2)}) async-start(), calls=%async_computation.11 | async-start | bytes 5971968 | tf_op jit(solution)/shard_map/all_gather | solution.py:106
  7.9 159.8 %all-gather.15.cloned.1.call-start = ((), (), s32[]{:S(2)}) async-start(), calls=%async_computation.13 | async-start | bytes 2985984 | tf_op jit(solution)/shard_map/all_gather | solution.py:107
  8.7 211.9 %all-gather.13.cloned.1.call-start = ((), (), s32[]{:S(2)}) async-start(), calls=%async_computation.12 | async-start | bytes 8847360 | tf_op jit(solution)/shard_map/all_gather | solution.py:142
  9.4 95.2 %copy-start = (bf16[3,288,1024]{2,1,0:T(8,128)(2,1)S(1)}, bf16[3,288,1024]{2,1,0:T(8,128)(2,1)}, u32[]{:S(2)}) copy-start(bf16[3,288,1024]{2,1,0:T(8,128)(2,1)} %param.24) | copy-start | bytes 5308420
  24.4 82.1 %copy-start.11 = (f32[3,1024]{1,0:T(4,128)}, f32[3,1024]{1,0:T(4,128)S(1)}, u32[]{:S(2)}) copy-start(f32[3,1024]{1,0:T(4,128)S(1)} %get-tuple-element.252) | copy-start | bytes 36868
  24.5 82.1 %copy-start.13 = (f32[3,1024]{1,0:T(4,128)}, f32[3,1024]{1,0:T(4,128)S(1)}, u32[]{:S(2)}) copy-start(f32[3,1024]{1,0:T(4,128)S(1)} %get-tuple-element.253) | copy-start | bytes 36868
  103.4 3.3 copy-start.43
  103.4 3.3 copy-start.40
  103.4 21.2 %copy-start.44 = (bf16[4]{0:T(256)(128)(2,1)S(1)}, bf16[4]{0:T(256)(128)(2,1)}, u32[]{:S(2)}) copy-start(bf16[4]{0:T(256)(128)(2,1)} %param.40) | copy-start | bytes 28
  103.4 21.3 %copy-start.34 = (s32[3,4]{1,0:T(4,128)S(1)}, s32[3,4]{1,0:T(4,128)}, u32[]{:S(2)}) copy-start(s32[3,4]{1,0:T(4,128)} %param.27) | copy-start | bytes 148
  103.4 22.2 %copy-start.39 = (bf16[2,288]{1,0:T(2,128)(2,1)S(1)}, bf16[2,288]{1,0:T(2,128)(2,1)}, u32[]{:S(2)}) copy-start(bf16[2,288]{1,0:T(2,128)(2,1)} %param.32) | copy-start | bytes 3460
  103.4 22.2 %copy-start.15 = (bf16[288,144]{0,1:T(8,128)(2,1)S(1)}, bf16[288,144]{0,1:T(8,128)(2,1)}, u32[]{:S(2)}) copy-start(bf16[288,144]{0,1:T(8,128)(2,1)} %param.33) | copy-start | bytes 248836
  104.1 234.8 %copy-start.18 = (f32[3,288]{1,0:T(4,128)}, f32[3,288]{1,0:T(4,128)S(1)}, u32[]{:S(2)}) copy-start(f32[3,288]{1,0:T(4,128)S(1)} %get-tuple-element.244) | copy-start | bytes 10372
  106.6 341.3 %reduce-scatter.16.cloned.1.call-start = ((), (), s32[]{:S(2)}) async-start(), calls=%async_computation.14 | async-start | bytes 17694720 | tf_op jit(solution)/shard_map/reduce_scatter | solution.py:153
  124.7 0.7 copy-start.29
  124.7 0.7 copy-start.31
  125.6 200.8 %copy-start.19 = (f32[3,288]{1,0:T(4,128)}, f32[3,288]{1,0:T(4,128)S(1)}, u32[]{:S(2)}) copy-start(f32[3,288]{1,0:T(4,128)S(1)} %mul.315) | copy-start | bytes 10372
  326.4 11.8 copy-start.2
  326.4 4.7 copy-start.8
  329.9 1.3 copy-start.5
  338.2 1.5 copy-start.4
  338.2 4.7 copy-start.41
  338.2 166.7 %all-gather.21.cloned.1.call-start = ((), (), s32[]{:S(2)}) async-start(), calls=%async_computation.17 | async-start | bytes 2985984 | tf_op jit(solution)/shard_map/all_gather | solution.py:112
  338.8 217.6 %all-gather.23.cloned.1.call-start = ((), (), s32[]{:S(2)}) async-start(), calls=%async_computation.19 | async-start | bytes 8847360 | tf_op jit(solution)/shard_map/all_gather | solution.py:179
  342.0 271.7 %all-gather.19.cloned.1.call-start = ((), (), s32[]{:S(2)}) async-start(), calls=%async_computation.16 | async-start | bytes 2985984 | tf_op jit(solution)/shard_map/all_gather | solution.py:108
  342.7 321.9 %all-gather.17.cloned.1.call-start = ((), (), s32[]{:S(2)}) async-start(), calls=%async_computation.15 | async-start | bytes 8847360 | tf_op jit(solution)/shard_map/all_gather | solution.py:161
  464.1 0.6 copy-start.14
  467.2 352.5 %reduce-scatter.20.cloned.1.call-start = ((), (), s32[]{:S(2)}) async-start(), calls=%async_computation.20 | async-start | bytes 17694720 | tf_op jit(solution)/shard_map/reduce_scatter | solution.py:190
  664.7 33.5 %copy-start.42 = (bf16[1152,1152]{1,0:T(8,128)(2,1)S(1)}, bf16[1152,1152]{1,0:T(8,128)(2,1)}, u32[]{:S(2)}) copy-start(bf16[1152,1152]{1,0:T(8,128)(2,1)} %all-gather.19.cloned.1.call-done) | copy-start | bytes 7962628
  695.3 2.8 copy-start.45
  710.0 175.8 %reduce-scatter.18.cloned.1.call-start = ((), (), s32[]{:S(2)}) async-start(), calls=%async_computation.18 | async-start | bytes 8847360 | tf_op jit(solution)/shard_map/reduce_scatter | solution.py:169
  726.4 219.1 %all-gather.25.cloned.1.call-start = ((), (), s32[]{:S(2)}) async-start(), calls=%async_computation.21 | async-start | bytes 8847360 | tf_op jit(solution)/shard_map/all_gather | solution.py:203
  894.5 281.6 %reduce-scatter.22.cloned.1.call-start = ((), (), s32[]{:S(2)}) async-start(), calls=%async_computation.22 | async-start | bytes 8847360 | tf_op jit(solution)/shard_map/reduce_scatter | solution.py:227
  894.6 57.1 %copy-start.3 = (f32[12,1024,72]{1,2,0:T(8,128)S(1)}, f32[12,1024,72]{1,2,0:T(8,128)}, u32[]{:S(2)}) copy-start(f32[12,1024,72]{1,2,0:T(8,128)} %get-tuple-element.99) | copy-start | bytes 10616836
  894.6 57.1 %copy-start.20 = (f32[3,288]{1,0:T(4,128)S(1)}, f32[3,288]{1,0:T(4,128)}, u32[]{:S(2)}) copy-start(f32[3,288]{1,0:T(4,128)} %copy-done.19) | copy-start | bytes 10372
  1109.7 0.7 copy-start.28
  1109.7 0.9 copy-start.30
  1109.7 0.9 copy-start.32
  1109.7 0.9 copy-start.33
  1109.7 0.9 copy-start.37
  1109.7 2.1 copy-start.35
  1109.7 2.1 copy-start.36
  1109.7 128.0 %reduce-scatter.36.cloned.1.call-start = ((), (), s32[]{:S(2)}) async-start(), calls=%async_computation.29 | async-start | bytes 147456
  1110.6 18.5 copy-start.26
  1111.5 189.9 %reduce-scatter.34.cloned.1.call-start = ((), (), s32[]{:S(2)}) async-start(), calls=%async_computation.28 | async-start | bytes 147456
  1111.8 17.3 copy-start.25
  1112.7 296.4 %reduce-scatter.30.cloned.1.call-start = ((), (), s32[]{:S(2)}) async-start(), calls=%async_computation.26 | async-start | bytes 5971968 | tf_op jit(solution)/shard_map/reduce_scatter | solution.py:268
  1129.0 0.7 copy-start.27
  1129.0 0.7 copy-start.38
  1129.1 388.5 %reduce-scatter.32.cloned.1.call-start = ((), (), s32[]{:S(2)}) async-start(), calls=%async_computation.27 | async-start | bytes 5971968 | tf_op jit(solution)/shard_map/reduce_scatter | solution.py:272
  1148.9 1.5 copy-start.6
  1148.9 8.9 copy-start.9
  1148.9 438.3 %reduce-scatter.28.cloned.1.call-start = ((), (), s32[]{:S(2)}) async-start(), calls=%async_computation.25 | async-start | bytes 1990656 | tf_op jit(solution)/shard_map/reduce_scatter | solution.py:271
  1157.7 537.0 %reduce-scatter.26.cloned.1.call-start = ((), (), s32[]{:S(2)}) async-start(), calls=%async_computation.24 | async-start | bytes 5971968 | tf_op jit(solution)/shard_map/reduce_scatter | solution.py:267
  1171.6 707.5 %reduce-scatter.24.cloned.1.call-start = ((), (), s32[]{:S(2)}) async-start(), calls=%async_computation.23 | async-start | bytes 11943936 | tf_op jit(solution)/shard_map/reduce_scatter | solution.py:266
  1171.6 4.5 copy-start.1
  1171.6 4.5 copy-start.12
  1176.1 3.8 copy-start.24
  1176.1 3.8 copy-start.22
  1176.1 3.8 copy-start.21
  1176.2 3.8 copy-start.23
  1176.2 4.4 copy-start.17
  1180.0 0.6 copy-start.10
  1241.4 122.9 %copy-start.7 = (bf16[3,1024,288]{1,2,0:T(8,128)(2,1)S(1)}, bf16[3,1024,288]{1,2,0:T(8,128)(2,1)}, u32[]{:S(2)}) copy-start(bf16[3,1024,288]{1,2,0:T(8,128)(2,1)} %reduce-scatter.22.cloned.1.call-done) | copy-start | bytes 5308420
  (1 other events, 0.6 us)
Sparse Core Ops, SparseCore 0:
  10.3 89.7 all-gather.10
  102.3 65.3 all-gather.14
  169.8 50.7 all-gather.12
  338.3 109.4 reduce-scatter.15
  449.9 55.0 all-gather.20
  506.9 49.4 all-gather.22
  558.6 55.0 all-gather.18
  615.2 49.4 all-gather.16
  710.2 109.4 reduce-scatter.19
  822.1 63.7 reduce-scatter.17
  894.6 50.8 all-gather.24
  1109.9 63.6 reduce-scatter.21
  1176.9 60.8 reduce-scatter.35
  1241.5 59.8 reduce-scatter.33
  1305.4 103.6 reduce-scatter.29
  1413.6 103.8 reduce-scatter.31
  1521.4 65.7 reduce-scatter.27
  1591.7 103.0 reduce-scatter.25
  1698.9 180.0 reduce-scatter.23
where the time goes:
time: 1890 us
  waiting for transfers between devices  1200 us (63%)
  matrix products  358 us (19%)
  blocking collectives  162 us (9%)
  other arithmetic  89.6 us (5%)
  local copies, waits for them, and re-layouts  62.7 us (3%)
    reduce_scatter x1, waiting for transfers between devices, body(): lax.psum_scatter(grad_w_ada, 'tok', scatter_dimension=0, tiled=True)  184 us
    reduce_scatter x1, waiting for transfers between devices, body(): lax.psum_scatter(grad_w_down, 'tok', scatter_dimension=1, tiled=True)  108 us
    reduce_scatter x1, waiting for transfers between devices, body(): lax.psum_scatter(grad_w_qkv, 'tok', scatter_dimension=0, tiled=True)  108 us
    unnamed x21, waiting for transfers between devices  105 us
    reduce_scatter x1, waiting for transfers between devices, body(): lax.psum_scatter(attn_part, 'tp', scatter_dimension=2, tiled=True)  104 us
    reduce_scatter x1, waiting for transfers between devices, body(): lax.psum_scatter(grad_mlp_part, 'tp', scatter_dimension=2, tiled=True)  92 us
    all_gather x1, waiting for transfers between devices, fetch_weights(): lax.all_gather(w_ada, 'tok', axis=0, tiled=True)  75.6 us
    reduce_scatter x1, waiting for transfers between devices, body(): lax.psum_scatter(grad_w_out, 'tok', scatter_dimension=1, tiled=True)  69.7 us
  transfers between devices with their start and end apart: 19, of which 18 were waited for; matrix products, arithmetic and copies ran while one was open for 9% of the time, Pallas kernels for 0%

commit v1 on v0

v1 whole, which is shorter than its diff:
```python
import functools
import math

import jax
import jax.numpy as jnp
from jax import lax
from jax.experimental import pallas as pl
from jax.experimental.pallas import tpu as pltpu
from jax.sharding import PartitionSpec as P

D = 1152
HD = 72
HP = 80
FF = 4608
FREQ = 256
GROUPS = 16
GW = FF // GROUPS
LEN = 1024
EPS = 1e-06
SCALE = HD**-0.5
SCALE2 = SCALE / math.log(2.0)

f32 = jnp.float32
bf16 = jnp.bfloat16
exact_mode = lax.Precision.HIGHEST


def dot(a, b, ca, cb):
    return lax.dot_general(a, b, (((ca,), (cb,)), ((), ())), preferred_element_type=f32)


def embed_time(timesteps):
    half_width = FREQ // 2
    indices = jnp.arange(half_width, dtype=f32)
    freq_rates = jnp.exp(-math.log(10000.0) * indices / half_width)
    angles = timesteps.astype(f32)[:, None] * freq_rates[None, :]
    return jnp.concatenate([jnp.cos(angles), jnp.sin(angles)], axis=1)


def attn_fwd_kernel(gate_ref, q_ref, k_ref, v_ref, mixed_ref, concat_ref, lse_ref):
    gate = gate_ref[pl.program_id(0)]
    keys = k_ref[0].T
    s = jnp.dot(keys, q_ref[0], preferred_element_type=f32)
    top = jnp.max(s, axis=0, keepdims=True)
    p = jnp.exp2((s - top) * SCALE2).astype(bf16)
    out = jnp.dot(v_ref[0], p, preferred_element_type=f32)
    total = out[HD : HD + 1]
    mixed = out * (1.0 / total)
    mixed_ref[0] = mixed
    concat_ref[0] = (mixed * gate).astype(bf16)
    lse_ref[0] = top * SCALE2 + jnp.log2(total)


def attn_fwd(gate, qkv):
    heads = gate.shape[0]
    spec = pl.BlockSpec((1, HP, LEN), lambda i: (i, 0, 0))
    row = pl.BlockSpec((1, 1, LEN), lambda i: (i, 0, 0))
    return pl.pallas_call(
        attn_fwd_kernel,
        grid=(heads,),
        in_specs=[pl.BlockSpec(memory_space=pltpu.SMEM)]
        + [pl.BlockSpec((1, HP, LEN), lambda i, k=k: (i + k * heads, 0, 0)) for k in range(3)],
        out_specs=[spec, spec, row],
        out_shape=[
            jax.ShapeDtypeStruct((heads, HP, LEN), f32),
            jax.ShapeDtypeStruct((heads, HP, LEN), bf16),
            jax.ShapeDtypeStruct((heads, 1, LEN), f32),
        ],
        compiler_params=pltpu.CompilerParams(vmem_limit_bytes=48 * 2**20),
        cost_estimate=pl.CostEstimate(
            flops=heads * 4 * LEN * LEN * 256,
            bytes_accessed=heads * HP * LEN * 14,
            transcendentals=heads * LEN * LEN,
        ),
        name="attn_fwd",
    )(gate, qkv, qkv, qkv)


def attn_bwd_kernel(
    chunk, gate_ref, q_ref, k_ref, v_ref, gc_ref, mixed_ref, lse_ref, dq_ref, dk_ref, dv_ref, hg_ref
):
    gate = gate_ref[pl.program_id(0)]
    keys_t = k_ref[0]
    keys = keys_t.T
    values = v_ref[0].T
    gc = gc_ref[0]
    inner = jnp.sum(mixed_ref[0] * gc, axis=0, keepdims=True)
    hg_ref[0] = inner
    delta = gate * inner
    grad = (gate * gc).astype(bf16)
    dv = jnp.zeros((LEN, HP), f32)
    dk = jnp.zeros((LEN, HP), f32)
    for j in range(LEN // chunk):
        part = slice(j * chunk, (j + 1) * chunk)
        q = q_ref[0, :, part]
        do = grad[:, part]
        s = jnp.dot(keys, q, preferred_element_type=f32)
        p = jnp.exp2(s * SCALE2 - lse_ref[0, :, part])
        dp = jnp.dot(values, do, preferred_element_type=f32)
        ds = (p * (dp - delta[:, part])).astype(bf16)
        dv = dv + jnp.dot(p.astype(bf16), do.T, preferred_element_type=f32)
        dk = dk + jnp.dot(ds, q.T, preferred_element_type=f32)
        dq = jnp.dot(keys_t, ds, preferred_element_type=f32)
        dq_ref[0, :, part] = (dq * SCALE).astype(bf16)
    dk_ref[0] = (dk * SCALE).T.astype(bf16)
    dv_ref[0] = dv.T.astype(bf16)


def attn_bwd(gate, qkv, gc, mixed, lse):
    heads = gate.shape[0]
    spec = pl.BlockSpec((1, HP, LEN), lambda i: (i, 0, 0))
    row = pl.BlockSpec((1, 1, LEN), lambda i: (i, 0, 0))
    grads = jax.ShapeDtypeStruct((heads, HP, LEN), bf16)
    return pl.pallas_call(
        functools.partial(attn_bwd_kernel, 256),
        grid=(heads,),
        in_specs=[pl.BlockSpec(memory_space=pltpu.SMEM)]
        + [pl.BlockSpec((1, HP, LEN), lambda i, k=k: (i + k * heads, 0, 0)) for k in range(3)]
        + [spec, spec, row],
        out_specs=[spec, spec, spec, row],
        out_shape=[grads, grads, grads, jax.ShapeDtypeStruct((heads, 1, LEN), f32)],
        compiler_params=pltpu.CompilerParams(vmem_limit_bytes=48 * 2**20),
        cost_estimate=pl.CostEstimate(
            flops=heads * 10 * LEN * LEN * 256,
            bytes_accessed=heads * HP * LEN * 20,
            transcendentals=heads * LEN * LEN,
        ),
        name="attn_bwd",
    )(gate, qkv, qkv, qkv, gc, mixed, lse)


def make_body(NT, NP):
    NX = NP // 2
    SUB = NT // NP
    RB = D // NT
    CB = D // NP
    T = LEN // NX
    wide = 4 if NT >= 16 else 2
    tall = NT // wide
    cycle = [r * wide for r in reversed(range(tall))]
    for r in range(tall):
        cols = list(range(1, wide))
        cycle += [r * wide + c for c in (cols if r % 2 == 0 else cols[::-1])]
    place = [cycle.index(t) for t in range(NT)]
    right_pairs = [(cycle[i], cycle[(i + 1) % NT]) for i in range(NT)]
    left_pairs = [(b, a) for a, b in right_pairs]
    n_right = NT // 2
    n_left = NT - 1 - n_right

    def hop(v, right):
        return lax.ppermute(v, "tok", right_pairs if right else left_pairs)

    def tp_xor(v, r):
        return lax.ppermute(v, "tp", [(p, p ^ r) for p in range(NP)])

    def tok_shift(v, k):
        return lax.ppermute(v, "tok", [(t, (t + k) % NT) for t in range(NT)])

    def swap_tokens(v, k, axis):
        if k == 0:
            return v
        parts = [lax.slice_in_dim(v, (j ^ k) * T, (j ^ k) * T + T, axis=axis) for j in range(NX)]
        return jnp.concatenate(parts, axis=axis)

    def body(
        block_input,
        condition,
        timesteps,
        head_mask,
        group_mask,
        w_ada,
        b_ada,
        w_qkv,
        b_qv,
        w_out,
        b_out,
        w_up,
        b_up,
        w_down,
        b_down,
        w_head,
        b_head,
        w_group,
        b_group,
        cotangent,
    ):
        I = condition.shape[0]
        HL = head_mask.shape[1]
        GL = group_mask.shape[1]
        FL = w_up.shape[1]
        FR = FREQ // NT
        t = lax.axis_index("tok")
        p = lax.axis_index("tp")
        xi = p // 2
        my_place = jnp.array(place, jnp.int32)[t]
        ring = jnp.array(cycle, jnp.int32)

        def block_of(d):
            tt = ring[(my_place + d + NT) % NT]
            return jnp.bitwise_xor(tt // SUB, p) * SUB + tt % SUB

        def gather_rows(shard):
            pieces = [(0, shard)]
            v = shard
            for d in range(1, n_right + 1):
                v = hop(v, True)
                pieces.append((-d, v))
            v = shard
            for d in range(1, n_left + 1):
                v = hop(v, False)
                pieces.append((d, v))
            full = jnp.zeros((NT,) + shard.shape, shard.dtype)
            for d, v in pieces:
                full = lax.dynamic_update_slice(full, v[None], (block_of(d), 0, 0))
            return full.reshape(D, -1)

        def scatter_rows(full):
            blocks = full.reshape(NT, RB, -1)

            def own(d):
                return lax.dynamic_index_in_dim(blocks, block_of(d), 0, keepdims=False)

            total = own(0)
            for count, right in ((n_right, True), (n_left, False)):
                v = None
                for d in range(count, 0, -1):
                    term = own(d if right else -d)
                    v = hop((term if v is None else term + v.astype(f32)).astype(bf16), right)
                total = total + v.astype(f32)
            return total

        def own_order(v, axis):
            parts = [
                lax.dynamic_slice_in_dim(v, jnp.bitwise_xor(j, xi) * T, T, axis=axis)
                for j in range(NX)
            ]
            return jnp.concatenate(parts, axis=axis)

        xin = own_order(block_input, 2)
        cot_in = own_order(cotangent, 2)

        def gather_features(own):
            blocks = [None] * NP
            for k in range(NX):
                v = own if k == 0 else swap_tokens(tp_xor(own, 2 * k), k, 1)
                blocks[2 * k] = v
                blocks[2 * k + 1] = tp_xor(v, 1)
            return blocks

        rows_blocks = [gather_features(xin[i]) for i in range(I)]
        rows_full = [jnp.concatenate(b, axis=0) for b in rows_blocks]

        time_feat = embed_time(timesteps).astype(bf16)
        cond_wide = condition.astype(f32)
        cond_act = jax.nn.silu(cond_wide).astype(bf16)
        message = jnp.concatenate(
            [cond_act.reshape(I, NT, RB), time_feat.reshape(I, NT, FR)], axis=2
        ).transpose(1, 0, 2)
        rolled = lax.dynamic_slice_in_dim(
            jnp.concatenate([message, message], axis=0), t, NT, axis=0
        )
        feats = jnp.stack([rolled[0]] + [tok_shift(rolled[k], k) for k in range(1, NT)])
        feats = feats.reshape(NT * I, RB + FR)
        cond_rows, time_rows = feats[:, :RB], feats[:, RB:]
        w_gates = jnp.concatenate([w_head, w_group], axis=1)
        part = jnp.concatenate(
            [dot(cond_rows, w_ada.reshape(RB, 6 * CB), 1, 0), dot(time_rows, w_gates, 1, 0)],
            axis=1,
        ).reshape(NT, I, -1)
        summed = part[0]
        for k in range(1, NT):
            summed = summed + tok_shift(part[k], NT - k)
        modulation = summed[:, : 6 * CB].reshape(I, 6, CB) + b_ada.astype(f32)
        head_sig = jax.nn.sigmoid(summed[:, 6 * CB : 6 * CB + HL] + b_head.astype(f32))
        group_sig = jax.nn.sigmoid(summed[:, 6 * CB + HL :] + b_group.astype(f32))
        head_gate = head_mask.astype(f32) * head_sig
        group_gate = group_mask.astype(f32) * group_sig
        tp_message = jnp.concatenate(
            [
                modulation.reshape(-1),
                b_out.astype(f32),
                b_down.astype(f32),
                group_gate.reshape(-1),
                b_up.astype(f32),
            ]
        )
        others = [tp_message] + [tp_xor(tp_message, r) for r in range(1, NP)]
        n_mod = I * 6 * CB
        vectors = jnp.stack(
            [m[: n_mod + 2 * CB].reshape(I * 6 + 2, CB) for m in others], axis=1
        ).reshape(I * 6 + 2, D)
        columns = vectors.T

        def mod(i, k):
            return lax.slice_in_dim(columns, i * 6 + k, i * 6 + k + 1, axis=1)

        out_bias = columns[:, I * 6 : I * 6 + 1]
        down_bias = columns[:, I * 6 + 1 : I * 6 + 2]
        base = n_mod + 2 * CB
        gates_x = jnp.concatenate(
            [others[2 * k][base : base + I * GL].reshape(I, GL) for k in range(NX)], axis=1
        )
        gate_cols = jnp.repeat(gates_x, GW, axis=1).T
        up_bias = jnp.concatenate([others[2 * k][base + I * GL :] for k in range(NX)])[:, None]

        qkv_shard = jnp.pad(
            w_qkv.reshape(RB, 3, HL, HD), ((0, 0), (0, 0), (0, 0), (0, HP - HD))
        ).reshape(RB, 3 * HL * HP)
        out_shard = jnp.pad(w_out.T.reshape(RB, HL, HD), ((0, 0), (0, 0), (0, HP - HD))).reshape(
            RB, HL * HP
        )
        up_shard = jnp.concatenate(
            [w_up] + [tp_xor(w_up, 2 * k) for k in range(1, NX)], axis=1
        )
        down_shard = w_down.T
        down_shard = jnp.concatenate(
            [down_shard] + [tp_xor(down_shard, 2 * k) for k in range(1, NX)], axis=1
        )
        qkv_full = gather_rows(qkv_shard)
        out_full = gather_rows(out_shard)
        up_full = gather_rows(up_shard)
        down_full = gather_rows(down_shard)
        qv = b_qv.astype(f32).reshape(2, HL, HD)
        qv_bias = jnp.stack(
            [
                jnp.pad(qv[0], ((0, 0), (0, HP - HD))),
                jnp.zeros((HL, HP), f32),
                jnp.concatenate(
                    [qv[1], jnp.ones((HL, 1), f32), jnp.zeros((HL, HP - HD - 1), f32)], axis=1
                ),
            ]
        ).reshape(3 * HL * HP, 1)

        def stats(v):
            centre = jnp.sum(v, axis=0, keepdims=True) * (1.0 / D)
            square = jnp.sum(v * v, axis=0, keepdims=True) * (1.0 / D)
            return centre, lax.rsqrt(square - centre * centre + EPS)

        fwd = []
        for i in range(I):
            wide_rows = rows_full[i].astype(f32)
            centre, inverse = stats(wide_rows)
            attn_in = ((wide_rows - centre) * inverse * (1.0 + mod(i, 1)) + mod(i, 0)).astype(bf16)
            qkv = (dot(qkv_full, attn_in, 0, 0) + qv_bias).astype(bf16).reshape(3 * HL, HP, LEN)
            mixed, concat, lse = attn_fwd(head_gate[i], qkv)
            concat = concat.reshape(HL * HP, LEN)
            part = dot(out_full, concat, 1, 0).reshape(NX, 2, CB, LEN)
            got = tp_xor(part[:, 1].astype(bf16), 1)
            both = part[:, 0] + got.astype(f32)
            total = both[:, :, :T]
            for k in range(1, NX):
                got = tp_xor(both[:, :, k * T : (k + 1) * T].astype(bf16), 2 * k).astype(f32)
                total = total + jnp.stack([got[j ^ k] for j in range(NX)])
            total_other = tp_xor(total, 1)
            branch_one = jnp.stack([total, total_other], axis=1).reshape(D, T) + out_bias
            fwd.append((centre, inverse, attn_in, qkv, mixed, concat, lse, branch_one))

        mids = []
        for i in range(I):
            branch_one = fwd[i][-1]
            cot_blocks = []
            for k in range(NX):
                v = (
                    cot_in[i, :, :T]
                    if k == 0
                    else tp_xor(cot_in[i, :, k * T : (k + 1) * T], 2 * k)
                )
                cot_blocks += [v, tp_xor(v, 1)]
            cot = jnp.concatenate(cot_blocks, axis=0).astype(f32)
            mid_rows = rows_full[i][:, :T].astype(f32) + mod(i, 2) * branch_one
            centre, inverse = stats(mid_rows)
            normed = (mid_rows - centre) * inverse
            mlp_in = (normed * (1.0 + mod(i, 4)) + mod(i, 3)).astype(bf16)
            grad_two = (mod(i, 5) * cot).astype(bf16)
            pre = dot(up_full, mlp_in, 0, 0) + up_bias
            grad_hid = dot(down_full, grad_two, 0, 0)
            gate = gate_cols[:, i : i + 1]
            inner = jnp.tanh(math.sqrt(2.0 / math.pi) * (pre + 0.044715 * pre * pre * pre))
            act = 0.5 * pre * (1.0 + inner)
            slope = 0.5 * (1.0 + inner) + 0.5 * pre * (1.0 - inner * inner) * math.sqrt(
                2.0 / math.pi
            ) * (1.0 + 3.0 * 0.044715 * pre * pre)
            hidden = (act * gate).astype(bf16)
            grad_pre = (slope * gate * grad_hid).astype(bf16)
            gate_sums = jnp.sum(jnp.sum(grad_hid * act, axis=1).reshape(NX * GL, GW), axis=1)
            up_sums = jnp.sum(grad_pre.astype(f32), axis=1)
            gpart = dot(up_full, grad_pre, 1, 0)
            got = tp_xor(gpart.astype(bf16), 1).reshape(NX, 2, CB, T)
            got = jnp.stack([got[:, 1], got[:, 0]], axis=1).reshape(D, T)
            gnorm = gpart + got.astype(f32)
            shift_sums = jnp.sum(gnorm, axis=1)
            scale_sums = jnp.sum(gnorm * normed, axis=1)
            g = gnorm * (1.0 + mod(i, 4))
            mean_g = jnp.sum(g, axis=0, keepdims=True) * (1.0 / D)
            mean_gn = jnp.sum(g * normed, axis=0, keepdims=True) * (1.0 / D)
            grad_mid = cot + inverse * (g - mean_g - normed * mean_gn)
            gate_one_sums = jnp.sum(grad_mid * branch_one, axis=1)
            grad_one = (mod(i, 2) * grad_mid).astype(bf16)
            out_sums = jnp.sum(grad_one.astype(f32), axis=1)
            own_half = grad_one.reshape(NX, 2, CB, T)[:, 0]
            tok_blocks = [grad_one]
            for k in range(1, NX):
                got = tp_xor(own_half, 2 * k)
                got = jnp.stack([got[j ^ k] for j in range(NX)])
                tok_blocks.append(jnp.stack([got, tp_xor(got, 1)], axis=1).reshape(D, T))
            grad_one_full = jnp.concatenate(tok_blocks, axis=1)
            mid_blocks = [grad_mid[:CB]]
            for k in range(1, NX):
                mid_blocks.append(
                    tp_xor(grad_mid[2 * k * CB : (2 * k + 1) * CB].astype(bf16), 2 * k).astype(f32)
                )
            grad_mid_own = jnp.concatenate(mid_blocks, axis=1)
            bpart = dot(down_full, hidden, 1, 0).reshape(NX, 2, CB, T)
            branch_two = (
                bpart[:, 0]
                + tp_xor(bpart[:, 1].astype(bf16), 1).astype(f32)
                + down_bias.reshape(NX, 2, CB, 1)[:, 0]
            )
            half = lambda v: v.reshape(NX, 2, CB, -1)[:, 0]
            gate_two_sums = jnp.sum(half(cot) * branch_two, axis=2)
            out_half = (half(mid_rows) + half(mod(i, 5)) * branch_two).astype(bf16)
            out_blocks = [out_half[0]] + [tp_xor(out_half[k], 2 * k) for k in range(1, NX)]
            out_own = jnp.concatenate(out_blocks, axis=1)
            down_sums = jnp.sum(grad_two.astype(f32), axis=1)
            mids.append(
                dict(
                    grad_two=grad_two,
                    hidden=hidden,
                    grad_pre=grad_pre,
                    mlp_in=mlp_in,
                    grad_one_full=grad_one_full,
                    grad_mid_own=grad_mid_own,
                    out_own=out_own,
                    sums=(gate_one_sums, shift_sums, scale_sums),
                    gate_two_sums=gate_two_sums,
                    gate_sums=gate_sums,
                    up_sums=up_sums,
                    out_sums=out_sums,
                    down_sums=down_sums,
                )
            )

        block_output = own_order(jnp.stack([m["out_own"] for m in mids]), 2)

        grad_down = sum(dot(m["grad_two"], m["hidden"], 1, 1) for m in mids)
        grad_up = sum(dot(m["mlp_in"], m["grad_pre"], 1, 1) for m in mids)
        grad_down = scatter_rows(grad_down)
        grad_up = scatter_rows(grad_up)

        def x_sum(v):
            total = v[:, :FL]
            for k in range(1, NX):
                got = tp_xor(v[:, k * FL : (k + 1) * FL].astype(bf16), 2 * k)
                total = total + got.astype(f32)
            return total

        grad_down = x_sum(grad_down)
        grad_up = x_sum(grad_up)

        def x_message(k):
            parts = []
            for m in mids:
                for v in m["sums"]:
                    parts.append(v[2 * k * CB : (2 * k + 1) * CB])
                parts.append(m["gate_two_sums"][k])
                parts.append(m["gate_sums"][k * GL : (k + 1) * GL])
            for name, size in (("out_sums", 2 * k * CB), ("down_sums", 2 * k * CB)):
                parts.append(sum(m[name] for m in mids)[size : size + CB])
            parts.append(sum(m["up_sums"] for m in mids)[k * FL : (k + 1) * FL])
            return jnp.concatenate(parts)

        x_total = x_message(0)
        for k in range(1, NX):
            x_total = x_total + tp_xor(x_message(k), 2 * k)
        per = 4 * CB + GL
        per_image = x_total[: I * per].reshape(I, per)
        late_mods = per_image[:, : 4 * CB].reshape(I, 4, CB)
        grad_group_gate = per_image[:, 4 * CB :]
        bias_sums = x_total[I * per :]

        backs = []
        for i in range(I):
            centre, inverse, attn_in, qkv, mixed, concat, lse, _ = fwd[i]
            m = mids[i]
            gc = dot(out_full, m["grad_one_full"], 0, 0).reshape(HL, HP, LEN)
            dq, dk, dv, inner = attn_bwd(head_gate[i], qkv, gc, mixed, lse)
            dqkv = jnp.concatenate([dq, dk, dv], axis=0).reshape(3 * HL * HP, LEN)
            part = dot(qkv_full, dqkv, 1, 0).reshape(NX, 2, CB, LEN)
            got = tp_xor(part[:, 1].astype(bf16), 1)
            both = part[:, 0] + got.astype(f32)
            gnorm = both[0]
            for k in range(1, NX):
                got = tp_xor(both[k].astype(bf16), 2 * k).astype(f32)
                gnorm = gnorm + swap_tokens(got, k, 1)
            normed = (xin[i].astype(f32) - centre) * inverse
            own_cols = columns[:CB]
            g = gnorm * (1.0 + own_cols[:, i * 6 + 1 : i * 6 + 2])
            sums = jnp.stack([jnp.sum(g, axis=0), jnp.sum(g * normed, axis=0)])
            total = sums
            for r in range(1, NP):
                total = total + swap_tokens(tp_xor(sums, r), r // 2, 1)
            grad_in = m["grad_mid_own"] + inverse * (
                g - total[0:1] * (1.0 / D) - normed * (total[1:2] * (1.0 / D))
            )
            backs.append(
                dict(
                    dqkv=dqkv,
                    grad_in=grad_in,
                    shift=jnp.sum(gnorm, axis=1),
                    scale=jnp.sum(gnorm * normed, axis=1),
                    heads=jnp.sum(inner, axis=(1, 2)),
                    q_sums=jnp.sum(dq.astype(f32), axis=2)[:, :HD].reshape(-1),
                    v_sums=jnp.sum(dv.astype(f32), axis=2)[:, :HD].reshape(-1),
                )
            )
        grad_input = own_order(jnp.stack([b["grad_in"] for b in backs]), 2)

        grad_out = sum(
            dot(m["grad_one_full"], f[5], 1, 1) for m, f in zip(mids, fwd)
        )
        grad_out = scatter_rows(grad_out)
        grad_qkv = sum(dot(f[2], b["dqkv"], 1, 1) for f, b in zip(fwd, backs))
        grad_qkv = scatter_rows(grad_qkv)

        grad_mod = jnp.stack(
            [
                jnp.stack([b["shift"] for b in backs]),
                jnp.stack([b["scale"] for b in backs]),
                late_mods[:, 0],
                late_mods[:, 1],
                late_mods[:, 2],
                late_mods[:, 3],
            ],
            axis=1,
        )
        grad_head_gate = jnp.stack([b["heads"] for b in backs])
        head_logit = grad_head_gate * head_mask.astype(f32) * head_sig * (1.0 - head_sig)
        group_logit = grad_group_gate * group_mask.astype(f32) * group_sig * (1.0 - group_sig)
        last = jnp.concatenate(
            [
                jnp.concatenate([grad_mod.reshape(I, -1), head_logit, group_logit], axis=1).reshape(
                    -1
                ),
                sum(b["q_sums"] for b in backs),
                sum(b["v_sums"] for b in backs),
                bias_sums,
            ]
        )
        lasts = jnp.stack([last] + [tok_shift(last, k) for k in range(1, NT)])
        n_head = I * (6 * CB + HL + GL)
        per_all = lasts[:, :n_head].reshape(NT * I, -1)
        mods_all = per_all[:, : 6 * CB]
        logits_all = per_all[:, 6 * CB :]
        biases = jnp.sum(lasts[:, n_head:], axis=0)
        cond_f = cond_rows.astype(f32)
        grad_w_ada = lax.dot_general(
            cond_f, mods_all, (((0,), (0,)), ((), ())), precision=exact_mode
        ).reshape(RB, 6, CB)
        grad_b_ada = jnp.sum(mods_all, axis=0).reshape(6, CB)
        grad_w_gates = lax.dot_general(
            time_rows.astype(f32), logits_all, (((0,), (0,)), ((), ())), precision=exact_mode
        )
        grad_b_gates = jnp.sum(logits_all, axis=0)
        cond_part = lax.dot_general(
            mods_all,
            w_ada.reshape(RB, 6 * CB).astype(f32),
            (((1,), (1,)), ((), ())),
            precision=exact_mode,
        ).reshape(NT, I, RB)
        cond_parts = jnp.stack(
            [cond_part[0]] + [tok_shift(cond_part[k], NT - k) for k in range(1, NT)]
        )
        cond_parts = lax.dynamic_slice_in_dim(
            jnp.concatenate([cond_parts, cond_parts], axis=0), (NT - t) % NT, NT, axis=0
        )
        cond_sum = cond_parts.transpose(1, 0, 2).reshape(I, D)
        cond_total = cond_sum
        for r in range(1, NP):
            cond_total = cond_total + tp_xor(cond_sum, r)
        grad_condition = jax.vjp(jax.nn.silu, cond_wide)[1](cond_total)[0]

        n_qv = 2 * HL * HD
        return (
            block_output,
            grad_input,
            grad_condition,
            grad_w_ada,
            grad_b_ada,
            grad_qkv.reshape(RB, 3, HL, HP)[..., :HD].reshape(RB, 3, HL * HD),
            biases[:n_qv].reshape(2, HL * HD),
            grad_out.reshape(RB, HL, HP)[..., :HD].reshape(RB, HL * HD).T,
            biases[n_qv : n_qv + CB],
            grad_up,
            biases[n_qv + 2 * CB :],
            grad_down.T,
            biases[n_qv + CB : n_qv + 2 * CB],
            grad_w_gates[:, :HL],
            grad_b_gates[:HL],
            grad_w_gates[:, HL:],
            grad_b_gates[HL:],
        )

    return body


def solution(mesh):
    return jax.shard_map(
        make_body(mesh.shape["tok"], mesh.shape["tp"]),
        mesh=mesh,
        in_specs=(
            P("tok", "tp", None),
            P("tok", None),
            P("tok"),
            P("tok", "tp"),
            P("tok", "tp"),
            P("tok", None, "tp"),
            P(None, "tp"),
            P("tok", None, "tp"),
            P(None, "tp"),
            P("tp", "tok"),
            P("tp"),
            P("tok", "tp"),
            P("tp"),
            P("tp", "tok"),
            P("tp"),
            P("tok", "tp"),
            P("tp"),
            P("tok", "tp"),
            P("tp"),
            P("tok", "tp", None),
        ),
        out_specs=(
            P("tok", "tp", None),
            P("tok", "tp", None),
            P("tok", None),
            P("tok", None, "tp"),
            P(None, "tp"),
            P("tok", None, "tp"),
            P(None, "tp"),
            P("tp", "tok"),
            P("tp"),
            P("tok", "tp"),
            P("tp"),
            P("tp", "tok"),
            P("tp"),
            P("tok", "tp"),
            P("tp"),
            P("tok", "tp"),
            P("tp"),
        ),
        check_vma=False,
    )
```

time: 1890 us -> 988 us (0.52)
  waiting for transfers between devices: 1200 us -> 282 us
  matrix products: 358 us -> 180 us
  blocking collectives: 162 us -> 0 us
  starting transfers between devices: 0.95 us -> 145 us
  local copies, waits for them, and re-layouts: 62.7 us -> 168 us
  Pallas kernels: 0 us -> 60 us
  between operations: 14.9 us -> 34.6 us
    reduce_scatter x9 -> x0, waiting for transfers between devices: 755 us -> none  [the longest x1 184 us: body(): lax.psum_scatter(grad_w_ada, 'tok', scatter_dimension=0, tiled=True)]
    all_gather x8 -> x0, waiting for transfers between devices: 337 us -> none  [the longest x1 75.6 us: fetch_weights(): lax.all_gather(w_ada, 'tok', axis=0, tiled=True)]
    ppermute x0 -> x155, waiting for transfers between devices: none -> 282 us  [the longest x71 169 us: tp_xor(): return lax.ppermute(v, 'tp', [(p, p ^ r) for p in range(NP)])]
    dot_general x101 -> x41, matrix products: 356 us -> 180 us  [the longest x38 179 us: dot(): lax.dot_general(a, b, (((ca,), (cb,)), ((), ())), preferred_element_type=...]
    ppermute x0 -> x155, starting transfers between devices: none -> 145 us  [the longest x56 59.5 us: hop(): return lax.ppermute(v, 'tok', right_pairs if right else left_pairs)]
    unnamed x21 -> x0, waiting for transfers between devices: 105 us -> none
    psum x5 -> x0, blocking collectives: 86.2 us -> none  [the longest x1 38.1 us: body(): lax.psum((grad_b_ada, grad_b_qv, grad_b_out, grad_b_up, grad_b_down, grad...]
    all_gather x3 -> x0, blocking collectives: 75.6 us -> none  [the longest x1 36.9 us: fetch_weights(): lax.all_gather(w_out, 'tok', axis=1, tiled=True)]
  transfers between devices with their start and end apart: 19 -> 155, of which waited for: 18 -> 49; matrix products, arithmetic and copies ran while one was open for 9% -> 31% of each run, Pallas kernels for 0% -> 6%
where the time goes in v1:
time: 988 us; the launch traced here: 976 us
  waiting for transfers between devices  282 us (29%)
  matrix products  180 us (18%)
  local copies, waits for them, and re-layouts  168 us (17%)
  starting transfers between devices  145 us (15%)
  other arithmetic  105 us (11%)
  Pallas kernels  60 us (6%)
  between operations  34.6 us (4%)
    dot_general x38, matrix products, dot(): lax.dot_general(a, b, (((ca,), (cb,)), ((), ())), preferred_element_type=...  179 us
    ppermute x71, waiting for transfers between devices, tp_xor(): return lax.ppermute(v, 'tp', [(p, p ^ r) for p in range(NP)])  169 us
    ppermute x56, waiting for transfers between devices, hop(): return lax.ppermute(v, 'tok', right_pairs if right else left_pairs)  109 us
    ppermute x56, starting transfers between devices, hop(): return lax.ppermute(v, 'tok', right_pairs if right else left_pairs)  59.5 us
    ppermute x28, starting transfers between devices, tok_shift(): return lax.ppermute(v, 'tok', [(t, (t + k) % NT) for t in range(NT)])  44.6 us
    unnamed x459, local copies, waits for them, and re-layouts  43.7 us
    ppermute x71, starting transfers between devices, tp_xor(): return lax.ppermute(v, 'tp', [(p, p ^ r) for p in range(NP)])  41.2 us
    pallas_call x3, Pallas kernels, attn_bwd(): pl.pallas_call(functools.partial(attn_bwd_kernel, 256), grid=(heads,), in...  37.9 us
  transfers between devices with their start and end apart: 155, of which 49 were waited for; matrix products, arithmetic and copies ran while one was open for 31% of the time, Pallas kernels for 6%

profile of v1, /device:TPU:0, one launch (start us, length us, event | category | flops | bytes accessed | tf_op | source)
XLA Modules:
  0.0 975.7 jit_solution(4587168679199920983)
XLA Ops:
  110.3 4.9 collective-permute-done.25
  119.9 5.0 collective-permute-done.37
  149.9 8.4 collective-permute-done.64
  158.4 12.6 %collective-permute-done.56 = bf16[288,1024]{1,0:T(8,128)(2,1)S(1)} collective-permute-done((bf16[288,1024]{1,0:T(8,128)(2,1)S(1)}, bf16[288,1024]{1,0:T(8,128)(2,1)S(1)}, u32[]{:S(2)}, u32[]{:S(2)}) %collective-permute-start.56) | collective-permute-done | bytes 589856 | tf_op jit(solution)/shard_map/ppermute | solution.py:154
  172.9 10.3 %collective-permute-done.1 = bf16[288,1024]{1,0:T(8,128)(2,1)S(1)} collective-permute-done((bf16[288,1024]{1,0:T(8,128)(2,1)S(1)}, bf16[288,1024]{1,0:T(8,128)(2,1)S(1)}, u32[]{:S(2)}, u32[]{:S(2)}) %collective-permute-start.1) | collective-permute-done | bytes 589856 | tf_op jit(solution)/shard_map/ppermute | solution.py:154
  186.5 7.0 collective-permute-done.29
  198.3 13.4 %collective-permute-done.38 = bf16[144,2304]{1,0:T(8,128)(2,1)S(1)} collective-permute-done((bf16[144,2304]{1,0:T(8,128)(2,1)}, bf16[144,2304]{1,0:T(8,128)(2,1)S(1)}, u32[]{:S(2)}, u32[]{:S(2)}) %collective-permute-start.38) | collective-permute-done | bytes 663584 | tf_op jit(solution)/shard_map/ppermute | solution.py:151
  214.0 6.4 collective-permute-done.30
  225.8 5.5 add_convert_fusion
  231.4 7.4 attn_fwd.5
  246.1 5.6 add_convert_fusion.1
  251.7 7.4 attn_fwd.4
  268.7 5.6 add_convert_fusion.2
  274.3 7.4 attn_fwd.3
  288.5 14.5 %collective-permute-done.48 = bf16[144,2304]{1,0:T(8,128)(2,1)S(1)} collective-permute-done((bf16[144,2304]{1,0:T(8,128)(2,1)}, bf16[144,2304]{1,0:T(8,128)(2,1)S(1)}, u32[]{:S(2)}, u32[]{:S(2)}) %collective-permute-start.48) | collective-permute-done | bytes 663584 | tf_op jit(solution)/shard_map/ppermute | solution.py:151
  306.0 12.7 %collective-permute-done.40 = bf16[144,2304]{1,0:T(8,128)(2,1)S(1)} collective-permute-done((bf16[144,2304]{1,0:T(8,128)(2,1)S(1)}, bf16[144,2304]{1,0:T(8,128)(2,1)S(1)}, u32[]{:S(2)}, u32[]{:S(2)}) %collective-permute-start.40) | collective-permute-done | bytes 663584 | tf_op jit(solution)/shard_map/ppermute | solution.py:151
  328.0 9.0 collective-permute-done.67
  339.4 11.2 %collective-permute-done.59 = bf16[2,288,512]{2,1,0:T(8,128)(2,1)S(1)} collective-permute-done((bf16[2,288,512]{2,1,0:T(8,128)(2,1)S(1)}, bf16[2,288,512]{2,1,0:T(8,128)(2,1)S(1)}, u32[]{:S(2)}, u32[]{:S(2)}) %collective-permute-start.59) | collective-permute-done | bytes 589856 | tf_op jit(solution)/shard_map/ppermute | solution.py:154
  352.9 8.6 collective-permute-done.35
  379.4 8.4 convolution_add_fusion.6
  387.8 6.7 fusion.221
  394.6 6.9 convert_reduce_fusion.5
  401.4 6.0 fusion.236
  407.5 4.8 fusion.286
  412.3 4.5 fusion.60
  416.8 3.7 convolution_add_fusion.5
  420.4 4.5 fusion.41
  424.9 7.1 convert_reduce_fusion.4
  432.1 13.5 %convolution_add_fusion.1 = f32[1152,2304]{1,0:T(8,128)} fusion(f32[1152,2304]{1,0:T(8,128)} %fusion.221, bf16[1152,512]{1,0:T(8,128)(2,1)S(1)} %get-tuple-element.345, f32[1152]{0:T(1024)S(1)} %get-tuple-element.311, f32[2304]{0:T(1024)S(1)} %get-tuple-element.323, f32[2304,512]{0,1:T(8,128)} %copy-done.69), kind=kOutput, calls=%fused_computation.1 | convolution fusion | flops 2734129152 | bytes 27145728 | tf_op jit(solution)/shard_map/dot_general | solution.py:29
  445.7 4.1 convolution_add_fusion.4
  449.8 4.6 fusion.39
  454.4 6.9 convert_reduce_fusion.3
  461.3 13.7 %convolution_add_fusion = f32[1152,2304]{1,0:T(8,128)} fusion(f32[1152,2304]{1,0:T(8,128)} %convolution_add_fusion.1, bf16[1152,512]{1,0:T(8,128)(2,1)S(1)} %copy-done.32, f32[1152]{0:T(1024)S(1)} %copy-done.94, f32[2304]{0:T(1024)S(1)} %copy-done.130, f32[2304,512]{0,1:T(8,128)} %copy-done.68), kind=kOutput, calls=%fused_computation | convolution fusion | flops 2734129152 | bytes 27145728 | tf_op jit(solution)/shard_map/dot_general | solution.py:29
  479.5 4.7 fusion.287
  484.2 6.7 convolution_add_fusion.3
  491.0 5.9 convolution_add_fusion.2
  509.4 5.8 fusion.285
  531.5 5.9 collective-permute-done.62
  537.5 5.9 collective-permute-done.70
  587.1 15.5 %collective-permute-done.75 = bf16[288,512]{1,0:T(8,128)(2,1)S(1)} collective-permute-done((bf16[288,512]{1,0:T(8,128)(2,1)}, bf16[288,512]{1,0:T(8,128)(2,1)S(1)}, u32[]{:S(2)}, u32[]{:S(2)}) %collective-permute-start.75) | collective-permute-done | bytes 294944 | tf_op jit(solution)/shard_map/ppermute | solution.py:154
  603.9 5.0 collective-permute-done.87
  610.2 5.0 collective-permute-done.99
  618.6 9.2 collective-permute-done.88
  628.7 9.4 collective-permute-done.100
  649.6 12.7 %attn_bwd.3 = (bf16[4,80,1024]{2,1,0:T(8,128)(2,1)S(1)}, bf16[4,80,1024]{2,1,0:T(8,128)(2,1)S(1)}, bf16[4,80,1024]{2,1,0:T(8,128)(2,1)S(1)}, f32[4,1,1024]{2,1,0:T(1,128)S(1)}) custom-call(f32[4]{0:T(128)S(1)} %get-tuple-element.538.gate_ref, bf16[12,80,1024]{2,1,0:T(8,128)(2,1)} %bitcast.740, bf16[12,80,1024]{2,1,0:T(8,128)(2,1)} %bitcast.741, ...), custom_call_target="tpu_custom_call" | custom-call | flops 10737418240 | bytes 6553600 | tf_op jit(solution)/shard_map/attn_bwd/pallas_call | solution.py:114
  681.5 12.5 %attn_bwd.4 = (bf16[4,80,1024]{2,1,0:T(8,128)(2,1)S(1)}, bf16[4,80,1024]{2,1,0:T(8,128)(2,1)S(1)}, bf16[4,80,1024]{2,1,0:T(8,128)(2,1)S(1)}, f32[4,1,1024]{2,1,0:T(1,128)S(1)}) custom-call(f32[4]{0:T(128)S(1)} %copy-done.9, bf16[12,80,1024]{2,1,0:T(8,128)(2,1)} %bitcast.734, bf16[12,80,1024]{2,1,0:T(8,128)(2,1)} %bitcast.735, ...), custom_call_target="tpu_custom_call" | custom-call | flops 10737418240 | bytes 6553600 | tf_op jit(solution)/shard_map/attn_bwd/pallas_call | solution.py:114
  696.4 5.0 fusion.230
  703.9 4.9 fusion.233
  708.8 12.7 %attn_bwd.5 = (bf16[4,80,1024]{2,1,0:T(8,128)(2,1)S(1)}, bf16[4,80,1024]{2,1,0:T(8,128)(2,1)S(1)}, bf16[4,80,1024]{2,1,0:T(8,128)(2,1)S(1)}, f32[4,1,1024]{2,1,0:T(1,128)S(1)}) custom-call(f32[4]{0:T(128)S(1)} %copy-done.7, bf16[12,80,1024]{2,1,0:T(8,128)(2,1)} %bitcast.728, bf16[12,80,1024]{2,1,0:T(8,128)(2,1)} %bitcast.729, ...), custom_call_target="tpu_custom_call" | custom-call | flops 10737418240 | bytes 6553600 | tf_op jit(solution)/shard_map/attn_bwd/pallas_call | solution.py:114
  723.9 7.6 add_add_fusion
  731.5 5.9 copy.572
  741.4 4.9 fusion.66
  749.3 4.3 fusion.64
  756.6 4.3 fusion.62
  766.6 3.6 collective-permute-done.133
  783.4 12.6 %collective-permute-done.137 = bf16[144,320]{1,0:T(8,128)(2,1)S(1)} collective-permute-done((bf16[144,320]{1,0:T(8,128)(2,1)S(1)}, bf16[144,320]{1,0:T(8,128)(2,1)S(1)}, u32[]{:S(2)}, u32[]{:S(2)}) %collective-permute-start.137) | collective-permute-done | bytes 92192 | tf_op jit(solution)/shard_map/ppermute | solution.py:151
  804.9 8.0 collective-permute-done.138
  820.3 5.3 collective-permute-done.142
  826.8 7.9 collective-permute-done.145
  853.0 5.3 collective-permute-done.146
  867.4 3.5 collective-permute-done.79
  873.0 10.7 %collective-permute-done.91 = bf16[288,1024]{1,0:T(8,128)(2,1)} collective-permute-done((bf16[288,1024]{1,0:T(8,128)(2,1)}, bf16[288,1024]{1,0:T(8,128)(2,1)}, u32[]{:S(2)}, u32[]{:S(2)}) %collective-permute-start.91) | collective-permute-done | bytes 589856 | tf_op jit(solution)/shard_map/ppermute | solution.py:154
  886.1 8.9 collective-permute-done.103
  951.2 4.3 collective-permute-start.115
  (1149 shorter events, 459.2 us)
Async XLA Ops:
  2.4 31.1 %collective-permute-start.3 = (bf16[3,176]{1,0:T(4,128)(2,1)S(1)}, bf16[3,176]{1,0:T(4,128)(2,1)S(1)}, u32[]{:S(2)}, u32[]{:S(2)}) collective-permute-start(bf16[3,176]{1,0:T(4,128)(2,1)S(1)} %bitcast.879), channel_id=1, source_target_pairs={{0,4},{4,8},{8,12},{12,16},{16,20},{20,24},{24,28},{28,0},{1,5},{5... | collective-permute-start | bytes 3176 | tf_op jit(solution)/shard_map/ppermute | solution.py:157
  5.5 29.5 %collective-permute-start.4 = (bf16[3,176]{1,0:T(4,128)(2,1)S(1)}, bf16[3,176]{1,0:T(4,128)(2,1)S(1)}, u32[]{:S(2)}, u32[]{:S(2)}) collective-permute-start(bf16[3,176]{1,0:T(4,128)(2,1)S(1)} %bitcast.878), channel_id=1, source_target_pairs={{0,8},{4,12},{8,16},{12,20},{16,24},{20,28},{24,0},{28,4},{1,9},{5... | collective-permute-start | bytes 3176 | tf_op jit(solution)/shard_map/ppermute | solution.py:157
  7.1 33.6 %collective-permute-start.5 = (bf16[3,176]{1,0:T(4,128)(2,1)S(1)}, bf16[3,176]{1,0:T(4,128)(2,1)S(1)}, u32[]{:S(2)}, u32[]{:S(2)}) collective-permute-start(bf16[3,176]{1,0:T(4,128)(2,1)S(1)} %bitcast.872), channel_id=1, source_target_pairs={{0,12},{4,16},{8,20},{12,24},{16,28},{20,0},{24,4},{28,8},{1,13},{... | collective-permute-start | bytes 3176 | tf_op jit(solution)/shard_map/ppermute | solution.py:157
  9.6 31.1 %collective-permute-start.6 = (bf16[3,176]{1,0:T(4,128)(2,1)S(1)}, bf16[3,176]{1,0:T(4,128)(2,1)S(1)}, u32[]{:S(2)}, u32[]{:S(2)}) collective-permute-start(bf16[3,176]{1,0:T(4,128)(2,1)S(1)} %bitcast.874), channel_id=1, source_target_pairs={{0,16},{4,20},{8,24},{12,28},{16,0},{20,4},{24,8},{28,12},{1,17},{... | collective-permute-start | bytes 3176 | tf_op jit(solution)/shard_map/ppermute | solution.py:157
  10.8 29.9 %collective-permute-start.7 = (bf16[3,176]{1,0:T(4,128)(2,1)S(1)}, bf16[3,176]{1,0:T(4,128)(2,1)S(1)}, u32[]{:S(2)}, u32[]{:S(2)}) collective-permute-start(bf16[3,176]{1,0:T(4,128)(2,1)S(1)} %bitcast.876), channel_id=1, source_target_pairs={{0,20},{4,24},{8,28},{12,0},{16,4},{20,8},{24,12},{28,16},{1,21},{... | collective-permute-start | bytes 3176 | tf_op jit(solution)/shard_map/ppermute | solution.py:157
  46.7 33.5 %collective-permute-start.12 = (f32[3,1736]{1,0:T(4,128)}, f32[3,1736]{1,0:T(4,128)}, u32[]{:S(2)}, u32[]{:S(2)}) collective-permute-start(f32[3,1736]{1,0:T(4,128)} %get-tuple-element.452), channel_id=1, source_target_pairs={{0,20},{4,24},{8,28},{12,0},{16,4},{20,8},{24,12},{28,16},{1,21},{... | collective-permute-start | bytes 62504 | tf_op jit(solution)/shard_map/ppermute | solution.py:157
  48.5 33.2 %collective-permute-start.13 = (f32[3,1736]{1,0:T(4,128)}, f32[3,1736]{1,0:T(4,128)}, u32[]{:S(2)}, u32[]{:S(2)}) collective-permute-start(f32[3,1736]{1,0:T(4,128)} %get-tuple-element.453), channel_id=1, source_target_pairs={{0,16},{4,20},{8,24},{12,28},{16,0},{20,4},{24,8},{28,12},{1,17},{... | collective-permute-start | bytes 62504 | tf_op jit(solution)/shard_map/ppermute | solution.py:157
  49.8 32.6 %collective-permute-start.14 = (f32[3,1736]{1,0:T(4,128)}, f32[3,1736]{1,0:T(4,128)}, u32[]{:S(2)}, u32[]{:S(2)}) collective-permute-start(f32[3,1736]{1,0:T(4,128)} %get-tuple-element.454), channel_id=1, source_target_pairs={{0,12},{4,16},{8,20},{12,24},{16,28},{20,0},{24,4},{28,8},{1,13},{... | collective-permute-start | bytes 62504 | tf_op jit(solution)/shard_map/ppermute | solution.py:157
  51.4 31.0 %collective-permute-start.15 = (f32[3,1736]{1,0:T(4,128)}, f32[3,1736]{1,0:T(4,128)}, u32[]{:S(2)}, u32[]{:S(2)}) collective-permute-start(f32[3,1736]{1,0:T(4,128)} %get-tuple-element.456), channel_id=1, source_target_pairs={{0,8},{4,12},{8,16},{12,20},{16,24},{20,28},{24,0},{28,4},{1,9},{5... | collective-permute-start | bytes 62504 | tf_op jit(solution)/shard_map/ppermute | solution.py:157
  53.6 28.8 %collective-permute-start.16 = (f32[3,1736]{1,0:T(4,128)}, f32[3,1736]{1,0:T(4,128)}, u32[]{:S(2)}, u32[]{:S(2)}) collective-permute-start(f32[3,1736]{1,0:T(4,128)} %get-tuple-element.455), channel_id=1, source_target_pairs={{0,4},{4,8},{8,12},{12,16},{16,20},{20,24},{24,28},{28,0},{1,5},{5... | collective-permute-start | bytes 62504 | tf_op jit(solution)/shard_map/ppermute | solution.py:157
  81.7 26.7 %collective-permute-start.24 = (bf16[144,320]{1,0:T(8,128)(2,1)}, bf16[144,320]{1,0:T(8,128)(2,1)S(1)}, u32[]{:S(2)}, u32[]{:S(2)}) collective-permute-start(bf16[144,320]{1,0:T(8,128)(2,1)} %reshape.690), channel_id=1, source_target_pairs={{16,24},{8,16},{0,8},{4,0},{12,4},{20,12},{28,20},{24,28},{17,25},... | collective-permute-start | bytes 276488 | tf_op jit(solution)/shard_map/ppermute | solution.py:151
  89.3 27.4 %collective-permute-start.45 = (bf16[144,1152]{1,0:T(8,128)(2,1)}, bf16[144,1152]{1,0:T(8,128)(2,1)}, u32[]{:S(2)}, u32[]{:S(2)}) collective-permute-start(bf16[144,1152]{1,0:T(8,128)(2,1)} %param.33), channel_id=1, source_target_pairs={{0,2},{1,3},{2,0},{3,1},{4,6},{5,7},{6,4},{7,5},{8,10},{9,11},{10,... | collective-permute-start | bytes 995336 | tf_op jit(solution)/shard_map/ppermute | solution.py:154
  93.4 38.7 %collective-permute-start.72 = (bf16[288,512]{1,0:T(8,128)(2,1)}, bf16[288,512]{1,0:T(8,128)(2,1)}, u32[]{:S(2)}, u32[]{:S(2)}) collective-permute-start(bf16[288,512]{1,0:T(8,128)(2,1)} %get-tuple-element.392), channel_id=1, source_target_pairs={{0,2},{1,3},{2,0},{3,1},{4,6},{5,7},{6,4},{7,5},{8,10},{9,11},{10,... | collective-permute-start | bytes 884744 | tf_op jit(solution)/shard_map/ppermute | solution.py:154
  104.7 33.9 %collective-permute-start.71 = (bf16[288,512]{1,0:T(8,128)(2,1)}, bf16[288,512]{1,0:T(8,128)(2,1)}, u32[]{:S(2)}, u32[]{:S(2)}) collective-permute-start(bf16[288,512]{1,0:T(8,128)(2,1)} %get-tuple-element.389), channel_id=1, source_target_pairs={{0,1},{1,0},{2,3},{3,2},{4,5},{5,4},{6,7},{7,6},{8,9},{9,8},{10,11... | collective-permute-start | bytes 884744 | tf_op jit(solution)/shard_map/ppermute | solution.py:154
  108.5 25.1 %collective-permute-start.84 = (bf16[288,512]{1,0:T(8,128)(2,1)}, bf16[288,512]{1,0:T(8,128)(2,1)}, u32[]{:S(2)}, u32[]{:S(2)}) collective-permute-start(bf16[288,512]{1,0:T(8,128)(2,1)} %get-tuple-element.390), channel_id=1, source_target_pairs={{0,2},{1,3},{2,0},{3,1},{4,6},{5,7},{6,4},{7,5},{8,10},{9,11},{10,... | collective-permute-start | bytes 884744 | tf_op jit(solution)/shard_map/ppermute | solution.py:154
  143.7 79.7 %collective-permute-start.63 = (bf16[288,1024]{1,0:T(8,128)(2,1)S(1)}, bf16[288,1024]{1,0:T(8,128)(2,1)S(1)}, u32[]{:S(2)}, u32[]{:S(2)}) collective-permute-start(bf16[288,1024]{1,0:T(8,128)(2,1)S(1)} %bitcast.767), channel_id=1, source_target_pairs={{0,1},{1,0},{2,3},{3,2},{4,5},{5,4},{6,7},{7,6},{8,9},{9,8},{10,11... | collective-permute-start | bytes 1769480 | tf_op jit(solution)/shard_map/ppermute | solution.py:154
  145.4 25.6 %collective-permute-start.56 = (bf16[288,1024]{1,0:T(8,128)(2,1)S(1)}, bf16[288,1024]{1,0:T(8,128)(2,1)S(1)}, u32[]{:S(2)}, u32[]{:S(2)}) collective-permute-start(bf16[288,1024]{1,0:T(8,128)(2,1)S(1)} %bitcast.769), channel_id=1, source_target_pairs={{0,2},{1,3},{2,0},{3,1},{4,6},{5,7},{6,4},{7,5},{8,10},{9,11},{10,... | collective-permute-start | bytes 1769480 | tf_op jit(solution)/shard_map/ppermute | solution.py:154
  146.0 37.2 %collective-permute-start.1 = (bf16[288,1024]{1,0:T(8,128)(2,1)S(1)}, bf16[288,1024]{1,0:T(8,128)(2,1)S(1)}, u32[]{:S(2)}, u32[]{:S(2)}) collective-permute-start(bf16[288,1024]{1,0:T(8,128)(2,1)S(1)} %bitcast.772), channel_id=1, source_target_pairs={{0,2},{1,3},{2,0},{3,1},{4,6},{5,7},{6,4},{7,5},{8,10},{9,11},{10,... | collective-permute-start | bytes 1769480 | tf_op jit(solution)/shard_map/ppermute | solution.py:154
  149.9 90.3 %collective-permute-start.55 = (bf16[288,1024]{1,0:T(8,128)(2,1)S(1)}, bf16[288,1024]{1,0:T(8,128)(2,1)S(1)}, u32[]{:S(2)}, u32[]{:S(2)}) collective-permute-start(bf16[288,1024]{1,0:T(8,128)(2,1)S(1)} %bitcast.770), channel_id=1, source_target_pairs={{0,1},{1,0},{2,3},{3,2},{4,5},{5,4},{6,7},{7,6},{8,9},{9,8},{10,11... | collective-permute-start | bytes 1769480 | tf_op jit(solution)/shard_map/ppermute | solution.py:154
  158.3 35.9 %collective-permute-start.32 = (bf16[144,960]{1,0:T(8,128)(2,1)S(1)}, bf16[144,960]{1,0:T(8,128)(2,1)S(1)}, u32[]{:S(2)}, u32[]{:S(2)}) collective-permute-start(bf16[144,960]{1,0:T(8,128)(2,1)S(1)} %collective-permute-done.31), channel_id=1, source_target_pairs={{16,24},{8,16},{0,8},{4,0},{12,4},{20,12},{28,20},{24,28},{17,25},... | collective-permute-start | bytes 829448 | tf_op jit(solution)/shard_map/ppermute | solution.py:151
  171.0 24.7 %collective-permute-start.46 = (bf16[144,2304]{1,0:T(8,128)(2,1)}, bf16[144,2304]{1,0:T(8,128)(2,1)}, u32[]{:S(2)}, u32[]{:S(2)}) collective-permute-start(bf16[144,2304]{1,0:T(8,128)(2,1)} %constant_dynamic-update-slice_fusion), channel_id=1, source_target_pairs={{24,16},{16,8},{8,0},{0,4},{4,12},{12,20},{20,28},{28,24},{25,17},... | collective-permute-start | bytes 1990664 | tf_op jit(solution)/shard_map/ppermute | solution.py:151
  193.5 69.7 %collective-permute-start = (bf16[288,1024]{1,0:T(8,128)(2,1)S(1)}, bf16[288,1024]{1,0:T(8,128)(2,1)}, u32[]{:S(2)}, u32[]{:S(2)}) collective-permute-start(bf16[288,1024]{1,0:T(8,128)(2,1)S(1)} %bitcast.773), channel_id=1, source_target_pairs={{0,1},{1,0},{2,3},{3,2},{4,5},{5,4},{6,7},{7,6},{8,9},{9,8},{10,11... | collective-permute-start | bytes 1769480 | tf_op jit(solution)/shard_map/ppermute | solution.py:154
  195.6 27.0 %collective-permute-start.33 = (bf16[144,960]{1,0:T(8,128)(2,1)S(1)}, bf16[144,960]{1,0:T(8,128)(2,1)S(1)}, u32[]{:S(2)}, u32[]{:S(2)}) collective-permute-start(bf16[144,960]{1,0:T(8,128)(2,1)S(1)} %collective-permute-done.32), channel_id=1, source_target_pairs={{16,24},{8,16},{0,8},{4,0},{12,4},{20,12},{28,20},{24,28},{17,25},... | collective-permute-start | bytes 829448 | tf_op jit(solution)/shard_map/ppermute | solution.py:151
  222.6 42.4 %collective-permute-start.50 = (bf16[144,2304]{1,0:T(8,128)(2,1)}, bf16[144,2304]{1,0:T(8,128)(2,1)}, u32[]{:S(2)}, u32[]{:S(2)}) collective-permute-start(bf16[144,2304]{1,0:T(8,128)(2,1)} %constant_dynamic-update-slice_fusion), channel_id=1, source_target_pairs={{16,24},{8,16},{0,8},{4,0},{12,4},{20,12},{28,20},{24,28},{17,25},... | collective-permute-start | bytes 1990664 | tf_op jit(solution)/shard_map/ppermute | solution.py:151
  223.4 42.0 %collective-permute-start.42 = (bf16[144,2304]{1,0:T(8,128)(2,1)}, bf16[144,2304]{1,0:T(8,128)(2,1)}, u32[]{:S(2)}, u32[]{:S(2)}) collective-permute-start(bf16[144,2304]{1,0:T(8,128)(2,1)} %pad_maximum_fusion.28), channel_id=1, source_target_pairs={{16,24},{8,16},{0,8},{4,0},{12,4},{20,12},{28,20},{24,28},{17,25},... | collective-permute-start | bytes 1990664 | tf_op jit(solution)/shard_map/ppermute | solution.py:151
  240.2 26.0 %collective-permute-start.2 = (bf16[288,1024]{1,0:T(8,128)(2,1)}, bf16[288,1024]{1,0:T(8,128)(2,1)}, u32[]{:S(2)}, u32[]{:S(2)}) collective-permute-start(bf16[288,1024]{1,0:T(8,128)(2,1)} %pad_maximum_fusion.30), channel_id=1, source_target_pairs={{0,1},{1,0},{2,3},{3,2},{4,5},{5,4},{6,7},{7,6},{8,9},{9,8},{10,11... | collective-permute-start | bytes 1769480 | tf_op jit(solution)/shard_map/ppermute | solution.py:154
  241.9 41.4 %collective-permute-start.47 = (bf16[144,2304]{1,0:T(8,128)(2,1)}, bf16[144,2304]{1,0:T(8,128)(2,1)}, u32[]{:S(2)}, u32[]{:S(2)}) collective-permute-start(bf16[144,2304]{1,0:T(8,128)(2,1)} %collective-permute-done.46), channel_id=1, source_target_pairs={{24,16},{16,8},{8,0},{0,4},{4,12},{12,20},{20,28},{28,24},{25,17},... | collective-permute-start | bytes 1990664 | tf_op jit(solution)/shard_map/ppermute | solution.py:151
  265.0 40.1 %collective-permute-start.51 = (bf16[144,2304]{1,0:T(8,128)(2,1)}, bf16[144,2304]{1,0:T(8,128)(2,1)}, u32[]{:S(2)}, u32[]{:S(2)}) collective-permute-start(bf16[144,2304]{1,0:T(8,128)(2,1)} %collective-permute-done.50), channel_id=1, source_target_pairs={{16,24},{8,16},{0,8},{4,0},{12,4},{20,12},{28,20},{24,28},{17,25},... | collective-permute-start | bytes 1990664 | tf_op jit(solution)/shard_map/ppermute | solution.py:151
  265.3 39.9 %collective-permute-start.43 = (bf16[144,2304]{1,0:T(8,128)(2,1)}, bf16[144,2304]{1,0:T(8,128)(2,1)}, u32[]{:S(2)}, u32[]{:S(2)}) collective-permute-start(bf16[144,2304]{1,0:T(8,128)(2,1)} %collective-permute-done.42), channel_id=1, source_target_pairs={{16,24},{8,16},{0,8},{4,0},{12,4},{20,12},{28,20},{24,28},{17,25},... | collective-permute-start | bytes 1990664 | tf_op jit(solution)/shard_map/ppermute | solution.py:151
  266.2 54.9 %collective-permute-start.66 = (bf16[2,288,1024]{2,1,0:T(8,128)(2,1)}, bf16[2,288,1024]{2,1,0:T(8,128)(2,1)}, u32[]{:S(2)}, u32[]{:S(2)}) collective-permute-start(bf16[2,288,1024]{2,1,0:T(8,128)(2,1)} %fusion.83), channel_id=1, source_target_pairs={{0,1},{1,0},{2,3},{3,2},{4,5},{5,4},{6,7},{7,6},{8,9},{9,8},{10,11... | collective-permute-start | bytes 3538952 | tf_op jit(solution)/shard_map/ppermute | solution.py:154
  283.3 40.2 %collective-permute-start.58 = (bf16[2,288,1024]{2,1,0:T(8,128)(2,1)S(1)}, bf16[2,288,1024]{2,1,0:T(8,128)(2,1)S(1)}, u32[]{:S(2)}, u32[]{:S(2)}) collective-permute-start(bf16[2,288,1024]{2,1,0:T(8,128)(2,1)S(1)} %fusion.82), channel_id=1, source_target_pairs={{0,1},{1,0},{2,3},{3,2},{4,5},{5,4},{6,7},{7,6},{8,9},{9,8},{10,11... | collective-permute-start | bytes 3538952 | tf_op jit(solution)/shard_map/ppermute | solution.py:154
  305.2 65.0 %collective-permute-start.52 = (bf16[144,2304]{1,0:T(8,128)(2,1)}, bf16[144,2304]{1,0:T(8,128)(2,1)S(1)}, u32[]{:S(2)}, u32[]{:S(2)}) collective-permute-start(bf16[144,2304]{1,0:T(8,128)(2,1)} %collective-permute-done.51), channel_id=1, source_target_pairs={{16,24},{8,16},{0,8},{4,0},{12,4},{20,12},{28,20},{24,28},{17,25},... | collective-permute-start | bytes 1990664 | tf_op jit(solution)/shard_map/ppermute | solution.py:151
  318.7 52.4 %collective-permute-start.44 = (bf16[144,2304]{1,0:T(8,128)(2,1)}, bf16[144,2304]{1,0:T(8,128)(2,1)S(1)}, u32[]{:S(2)}, u32[]{:S(2)}) collective-permute-start(bf16[144,2304]{1,0:T(8,128)(2,1)} %collective-permute-done.43), channel_id=1, source_target_pairs={{16,24},{8,16},{0,8},{4,0},{12,4},{20,12},{28,20},{24,28},{17,25},... | collective-permute-start | bytes 1990664 | tf_op jit(solution)/shard_map/ppermute | solution.py:151
  321.1 41.1 %collective-permute-start.49 = (bf16[144,2304]{1,0:T(8,128)(2,1)S(1)}, bf16[144,2304]{1,0:T(8,128)(2,1)S(1)}, u32[]{:S(2)}, u32[]{:S(2)}) collective-permute-start(bf16[144,2304]{1,0:T(8,128)(2,1)S(1)} %collective-permute-done.48), channel_id=1, source_target_pairs={{24,16},{16,8},{8,0},{0,4},{4,12},{12,20},{20,28},{28,24},{25,17},... | collective-permute-start | bytes 1990664 | tf_op jit(solution)/shard_map/ppermute | solution.py:151
  326.0 41.8 %collective-permute-start.41 = (bf16[144,2304]{1,0:T(8,128)(2,1)S(1)}, bf16[144,2304]{1,0:T(8,128)(2,1)S(1)}, u32[]{:S(2)}, u32[]{:S(2)}) collective-permute-start(bf16[144,2304]{1,0:T(8,128)(2,1)S(1)} %collective-permute-done.40), channel_id=1, source_target_pairs={{24,16},{16,8},{8,0},{0,4},{4,12},{12,20},{20,28},{28,24},{25,17},... | collective-permute-start | bytes 1990664 | tf_op jit(solution)/shard_map/ppermute | solution.py:151
  477.9 44.9 %collective-permute-start.147 = (bf16[144,2304]{1,0:T(8,128)(2,1)}, bf16[144,2304]{1,0:T(8,128)(2,1)}, u32[]{:S(2)}, u32[]{:S(2)}) collective-permute-start(bf16[144,2304]{1,0:T(8,128)(2,1)} %get-tuple-element.367), channel_id=1, source_target_pairs={{24,16},{16,8},{8,0},{0,4},{4,12},{12,20},{20,28},{28,24},{25,17},... | collective-permute-start | bytes 1990664 | tf_op jit(solution)/shard_map/ppermute | solution.py:151
  499.8 26.2 %collective-permute-start.139 = (bf16[144,2304]{1,0:T(8,128)(2,1)}, bf16[144,2304]{1,0:T(8,128)(2,1)}, u32[]{:S(2)}, u32[]{:S(2)}) collective-permute-start(bf16[144,2304]{1,0:T(8,128)(2,1)} %get-tuple-element.371), channel_id=1, source_target_pairs={{24,16},{16,8},{8,0},{0,4},{4,12},{12,20},{20,28},{28,24},{25,17},... | collective-permute-start | bytes 1990664 | tf_op jit(solution)/shard_map/ppermute | solution.py:151
  515.2 30.5 %collective-permute-start.74 = (bf16[1152,512]{1,0:T(8,128)(2,1)S(1)}, bf16[1152,512]{1,0:T(8,128)(2,1)S(1)}, u32[]{:S(2)}, u32[]{:S(2)}) collective-permute-start(bf16[1152,512]{1,0:T(8,128)(2,1)S(1)} %copy-done.194), channel_id=1, source_target_pairs={{0,1},{1,0},{2,3},{3,2},{4,5},{5,4},{6,7},{7,6},{8,9},{9,8},{10,11... | collective-permute-start | bytes 3538952 | tf_op jit(solution)/shard_map/ppermute | solution.py:154
  515.8 31.7 %collective-permute-start.86 = (bf16[1152,512]{1,0:T(8,128)(2,1)S(1)}, bf16[1152,512]{1,0:T(8,128)(2,1)S(1)}, u32[]{:S(2)}, u32[]{:S(2)}) collective-permute-start(bf16[1152,512]{1,0:T(8,128)(2,1)S(1)} %copy-done.195), channel_id=1, source_target_pairs={{0,1},{1,0},{2,3},{3,2},{4,5},{5,4},{6,7},{7,6},{8,9},{9,8},{10,11... | collective-permute-start | bytes 3538952 | tf_op jit(solution)/shard_map/ppermute | solution.py:154
  531.1 107.1 %collective-permute-start.151 = (bf16[144,2304]{1,0:T(8,128)(2,1)}, bf16[144,2304]{1,0:T(8,128)(2,1)}, u32[]{:S(2)}, u32[]{:S(2)}) collective-permute-start(bf16[144,2304]{1,0:T(8,128)(2,1)} %get-tuple-element.368), channel_id=1, source_target_pairs={{16,24},{8,16},{0,8},{4,0},{12,4},{20,12},{28,20},{24,28},{17,25},... | collective-permute-start | bytes 1990664 | tf_op jit(solution)/shard_map/ppermute | solution.py:151
  543.4 98.8 %collective-permute-start.143 = (bf16[144,2304]{1,0:T(8,128)(2,1)}, bf16[144,2304]{1,0:T(8,128)(2,1)}, u32[]{:S(2)}, u32[]{:S(2)}) collective-permute-start(bf16[144,2304]{1,0:T(8,128)(2,1)} %get-tuple-element.372), channel_id=1, source_target_pairs={{16,24},{8,16},{0,8},{4,0},{12,4},{20,12},{28,20},{24,28},{17,25},... | collective-permute-start | bytes 1990664 | tf_op jit(solution)/shard_map/ppermute | solution.py:151
  545.7 36.0 %collective-permute-start.148 = (bf16[144,2304]{1,0:T(8,128)(2,1)}, bf16[144,2304]{1,0:T(8,128)(2,1)}, u32[]{:S(2)}, u32[]{:S(2)}) collective-permute-start(bf16[144,2304]{1,0:T(8,128)(2,1)} %fusion.71), channel_id=1, source_target_pairs={{24,16},{16,8},{8,0},{0,4},{4,12},{12,20},{20,28},{28,24},{25,17},... | collective-permute-start | bytes 1990664 | tf_op jit(solution)/shard_map/ppermute | solution.py:151
  547.4 37.5 %collective-permute-start.140 = (bf16[144,2304]{1,0:T(8,128)(2,1)}, bf16[144,2304]{1,0:T(8,128)(2,1)}, u32[]{:S(2)}, u32[]{:S(2)}) collective-permute-start(bf16[144,2304]{1,0:T(8,128)(2,1)} %fusion.77), channel_id=1, source_target_pairs={{24,16},{16,8},{8,0},{0,4},{4,12},{12,20},{20,28},{28,24},{25,17},... | collective-permute-start | bytes 1990664 | tf_op jit(solution)/shard_map/ppermute | solution.py:151
  579.7 36.9 %collective-permute-start.76 = (bf16[2,288,512]{2,1,0:T(8,128)(2,1)}, bf16[2,288,512]{2,1,0:T(8,128)(2,1)}, u32[]{:S(2)}, u32[]{:S(2)}) collective-permute-start(bf16[2,288,512]{2,1,0:T(8,128)(2,1)} %slice_bitcast_fusion.19), channel_id=1, source_target_pairs={{0,2},{1,3},{2,0},{3,1},{4,6},{5,7},{6,4},{7,5},{8,10},{9,11},{10,... | collective-permute-start | bytes 1769480 | tf_op jit(solution)/shard_map/ppermute | solution.py:154
  584.9 23.9 %collective-permute-start.87 = (bf16[288,512]{1,0:T(8,128)(2,1)S(1)}, bf16[288,512]{1,0:T(8,128)(2,1)S(1)}, u32[]{:S(2)}, u32[]{:S(2)}) collective-permute-start(bf16[288,512]{1,0:T(8,128)(2,1)S(1)} %copy-done.106), channel_id=1, source_target_pairs={{0,2},{1,3},{2,0},{3,1},{4,6},{5,7},{6,4},{7,5},{8,10},{9,11},{10,... | collective-permute-start | bytes 884744 | tf_op jit(solution)/shard_map/ppermute | solution.py:154
  638.3 24.3 %collective-permute-start.89 = (bf16[2,288,512]{2,1,0:T(8,128)(2,1)S(1)}, bf16[2,288,512]{2,1,0:T(8,128)(2,1)S(1)}, u32[]{:S(2)}, u32[]{:S(2)}) collective-permute-start(bf16[2,288,512]{2,1,0:T(8,128)(2,1)S(1)} %get-tuple-element.423), channel_id=1, source_target_pairs={{0,1},{1,0},{2,3},{3,2},{4,5},{5,4},{6,7},{7,6},{8,9},{9,8},{10,11... | collective-permute-start | bytes 1769480 | tf_op jit(solution)/shard_map/ppermute | solution.py:154
  638.8 28.0 %collective-permute-start.101 = (bf16[2,288,512]{2,1,0:T(8,128)(2,1)S(1)}, bf16[2,288,512]{2,1,0:T(8,128)(2,1)S(1)}, u32[]{:S(2)}, u32[]{:S(2)}) collective-permute-start(bf16[2,288,512]{2,1,0:T(8,128)(2,1)S(1)} %get-tuple-element.429), channel_id=1, source_target_pairs={{0,1},{1,0},{2,3},{3,2},{4,5},{5,4},{6,7},{7,6},{8,9},{9,8},{10,11... | collective-permute-start | bytes 1769480 | tf_op jit(solution)/shard_map/ppermute | solution.py:154
  642.2 137.2 %collective-permute-start.152 = (bf16[144,2304]{1,0:T(8,128)(2,1)}, bf16[144,2304]{1,0:T(8,128)(2,1)}, u32[]{:S(2)}, u32[]{:S(2)}) collective-permute-start(bf16[144,2304]{1,0:T(8,128)(2,1)} %get-tuple-element.366), channel_id=1, source_target_pairs={{16,24},{8,16},{0,8},{4,0},{12,4},{20,12},{28,20},{24,28},{17,25},... | collective-permute-start | bytes 1990664 | tf_op jit(solution)/shard_map/ppermute | solution.py:151
  642.9 173.9 %collective-permute-start.150 = (bf16[144,2304]{1,0:T(8,128)(2,1)}, bf16[144,2304]{1,0:T(8,128)(2,1)}, u32[]{:S(2)}, u32[]{:S(2)}) collective-permute-start(bf16[144,2304]{1,0:T(8,128)(2,1)} %get-tuple-element.365), channel_id=1, source_target_pairs={{24,16},{16,8},{8,0},{0,4},{4,12},{12,20},{20,28},{28,24},{25,17},... | collective-permute-start | bytes 1990664 | tf_op jit(solution)/shard_map/ppermute | solution.py:151
  676.9 87.6 %collective-permute-start.132 = (bf16[144,320]{1,0:T(8,128)(2,1)}, bf16[144,320]{1,0:T(8,128)(2,1)}, u32[]{:S(2)}, u32[]{:S(2)}) collective-permute-start(bf16[144,320]{1,0:T(8,128)(2,1)} %get-tuple-element.387), channel_id=1, source_target_pairs={{24,16},{16,8},{8,0},{0,4},{4,12},{12,20},{20,28},{28,24},{25,17},... | collective-permute-start | bytes 276488 | tf_op jit(solution)/shard_map/ppermute | solution.py:151
  677.4 95.1 %collective-permute-start.136 = (bf16[144,320]{1,0:T(8,128)(2,1)S(1)}, bf16[144,320]{1,0:T(8,128)(2,1)}, u32[]{:S(2)}, u32[]{:S(2)}) collective-permute-start(bf16[144,320]{1,0:T(8,128)(2,1)S(1)} %get-tuple-element.388), channel_id=1, source_target_pairs={{16,24},{8,16},{0,8},{4,0},{12,4},{20,12},{28,20},{24,28},{17,25},... | collective-permute-start | bytes 276488 | tf_op jit(solution)/shard_map/ppermute | solution.py:151
  739.5 38.0 %collective-permute-start.125 = (bf16[144,960]{1,0:T(8,128)(2,1)}, bf16[144,960]{1,0:T(8,128)(2,1)}, u32[]{:S(2)}, u32[]{:S(2)}) collective-permute-start(bf16[144,960]{1,0:T(8,128)(2,1)} %get-tuple-element.378), channel_id=1, source_target_pairs={{24,16},{16,8},{8,0},{0,4},{4,12},{12,20},{20,28},{28,24},{25,17},... | collective-permute-start | bytes 829448 | tf_op jit(solution)/shard_map/ppermute | solution.py:151
  772.6 27.3 %collective-permute-start.144 = (bf16[144,2304]{1,0:T(8,128)(2,1)}, bf16[144,2304]{1,0:T(8,128)(2,1)S(1)}, u32[]{:S(2)}, u32[]{:S(2)}) collective-permute-start(bf16[144,2304]{1,0:T(8,128)(2,1)} %get-tuple-element.370), channel_id=1, source_target_pairs={{16,24},{8,16},{0,8},{4,0},{12,4},{20,12},{28,20},{24,28},{17,25},... | collective-permute-start | bytes 1990664 | tf_op jit(solution)/shard_map/ppermute | solution.py:151
  775.1 39.6 %collective-permute-start.129 = (bf16[144,960]{1,0:T(8,128)(2,1)S(1)}, bf16[144,960]{1,0:T(8,128)(2,1)}, u32[]{:S(2)}, u32[]{:S(2)}) collective-permute-start(bf16[144,960]{1,0:T(8,128)(2,1)S(1)} %get-tuple-element.379), channel_id=1, source_target_pairs={{16,24},{8,16},{0,8},{4,0},{12,4},{20,12},{28,20},{24,28},{17,25},... | collective-permute-start | bytes 829448 | tf_op jit(solution)/shard_map/ppermute | solution.py:151
  814.7 27.7 %collective-permute-start.78 = (bf16[2,288,1024]{2,1,0:T(8,128)(2,1)}, bf16[2,288,1024]{2,1,0:T(8,128)(2,1)S(1)}, u32[]{:S(2)}, u32[]{:S(2)}) collective-permute-start(bf16[2,288,1024]{2,1,0:T(8,128)(2,1)} %fusion.84), channel_id=1, source_target_pairs={{0,1},{1,0},{2,3},{3,2},{4,5},{5,4},{6,7},{7,6},{8,9},{9,8},{10,11... | collective-permute-start | bytes 3538952 | tf_op jit(solution)/shard_map/ppermute | solution.py:154
  814.7 30.7 %collective-permute-start.90 = (bf16[2,288,1024]{2,1,0:T(8,128)(2,1)}, bf16[2,288,1024]{2,1,0:T(8,128)(2,1)S(1)}, u32[]{:S(2)}, u32[]{:S(2)}) collective-permute-start(bf16[2,288,1024]{2,1,0:T(8,128)(2,1)} %fusion.85), channel_id=1, source_target_pairs={{0,1},{1,0},{2,3},{3,2},{4,5},{5,4},{6,7},{7,6},{8,9},{9,8},{10,11... | collective-permute-start | bytes 3538952 | tf_op jit(solution)/shard_map/ppermute | solution.py:154
  816.8 31.0 %collective-permute-start.102 = (bf16[2,288,1024]{2,1,0:T(8,128)(2,1)}, bf16[2,288,1024]{2,1,0:T(8,128)(2,1)S(1)}, u32[]{:S(2)}, u32[]{:S(2)}) collective-permute-start(bf16[2,288,1024]{2,1,0:T(8,128)(2,1)} %fusion.86), channel_id=1, source_target_pairs={{0,1},{1,0},{2,3},{3,2},{4,5},{5,4},{6,7},{7,6},{8,9},{9,8},{10,11... | collective-permute-start | bytes 3538952 | tf_op jit(solution)/shard_map/ppermute | solution.py:154
  834.6 25.1 %collective-permute-start.128 = (bf16[144,960]{1,0:T(8,128)(2,1)S(1)}, bf16[144,960]{1,0:T(8,128)(2,1)S(1)}, u32[]{:S(2)}, u32[]{:S(2)}) collective-permute-start(bf16[144,960]{1,0:T(8,128)(2,1)S(1)} %get-tuple-element.376), channel_id=1, source_target_pairs={{24,16},{16,8},{8,0},{0,4},{4,12},{12,20},{20,28},{28,24},{25,17},... | collective-permute-start | bytes 829448 | tf_op jit(solution)/shard_map/ppermute | solution.py:151
  851.2 32.5 %collective-permute-start.91 = (bf16[288,1024]{1,0:T(8,128)(2,1)}, bf16[288,1024]{1,0:T(8,128)(2,1)}, u32[]{:S(2)}, u32[]{:S(2)}) collective-permute-start(bf16[288,1024]{1,0:T(8,128)(2,1)} %fusion.123), channel_id=1, source_target_pairs={{0,2},{1,3},{2,0},{3,1},{4,6},{5,7},{6,4},{7,5},{8,10},{9,11},{10,... | collective-permute-start | bytes 1769480 | tf_op jit(solution)/shard_map/ppermute | solution.py:154
  858.3 36.7 %collective-permute-start.103 = (bf16[288,1024]{1,0:T(8,128)(2,1)}, bf16[288,1024]{1,0:T(8,128)(2,1)}, u32[]{:S(2)}, u32[]{:S(2)}) collective-permute-start(bf16[288,1024]{1,0:T(8,128)(2,1)} %fusion.124), channel_id=1, source_target_pairs={{0,2},{1,3},{2,0},{3,1},{4,6},{5,7},{6,4},{7,5},{8,10},{9,11},{10,... | collective-permute-start | bytes 1769480 | tf_op jit(solution)/shard_map/ppermute | solution.py:154
  903.8 39.2 %collective-permute-start.108 = (f32[7512]{0:T(1024)}, f32[7512]{0:T(1024)S(1)}, u32[]{:S(2)}, u32[]{:S(2)}) collective-permute-start(f32[7512]{0:T(1024)} %concatenate.261), channel_id=1, source_target_pairs={{0,4},{4,8},{8,12},{12,16},{16,20},{20,24},{24,28},{28,0},{1,5},{5... | collective-permute-start | bytes 90152 | tf_op jit(solution)/shard_map/ppermute | solution.py:157
  904.6 40.2 %collective-permute-start.109 = (f32[7512]{0:T(1024)}, f32[7512]{0:T(1024)S(1)}, u32[]{:S(2)}, u32[]{:S(2)}) collective-permute-start(f32[7512]{0:T(1024)} %concatenate.261), channel_id=1, source_target_pairs={{0,8},{4,12},{8,16},{12,20},{16,24},{20,28},{24,0},{28,4},{1,9},{5... | collective-permute-start | bytes 90152 | tf_op jit(solution)/shard_map/ppermute | solution.py:157
  905.7 43.1 %collective-permute-start.110 = (f32[7512]{0:T(1024)}, f32[7512]{0:T(1024)S(1)}, u32[]{:S(2)}, u32[]{:S(2)}) collective-permute-start(f32[7512]{0:T(1024)} %concatenate.261), channel_id=1, source_target_pairs={{0,12},{4,16},{8,20},{12,24},{16,28},{20,0},{24,4},{28,8},{1,13},{... | collective-permute-start | bytes 90152 | tf_op jit(solution)/shard_map/ppermute | solution.py:157
  908.3 40.6 %collective-permute-start.111 = (f32[7512]{0:T(1024)}, f32[7512]{0:T(1024)S(1)}, u32[]{:S(2)}, u32[]{:S(2)}) collective-permute-start(f32[7512]{0:T(1024)} %concatenate.261), channel_id=1, source_target_pairs={{0,16},{4,20},{8,24},{12,28},{16,0},{20,4},{24,8},{28,12},{1,17},{... | collective-permute-start | bytes 90152 | tf_op jit(solution)/shard_map/ppermute | solution.py:157
  (303 other events, 5113.3 us)

commit v2 on v1

--- a/solution.py
+++ b/solution.py
@@ -129,19 +129,376 @@
     )(gate, qkv, qkv, qkv, gc, mixed, lse)
 
 
+MESH = pl.DeviceIdType.MESH
+ML = 384
+
+
+def xor(v, k):
+    out, bit = 0, 1
+    while bit <= k or bit <= 8:
+        b = (v // bit) % 2
+        out = out + bit * (1 - b if k & bit else b)
+        bit *= 2
+    return out
+
+
+class Ring:
+    def __init__(self, NT):
+        self.NT, self.tall = NT, NT // 2
+
+    def place(self, t):
+        b = t % 2
+        return (1 - b) * (self.tall - 1 - t // 2) + b * (self.tall + t // 2)
+
+    def tok(self, q):
+        q = (q + 2 * self.NT) % self.NT
+        b = q // self.tall
+        return (1 - b) * 2 * (self.tall - 1 - q) + b * (2 * (q - self.tall) + 1)
+
+
+def copy_to(src, dst, send, recv, device):
+    return pltpu.make_async_remote_copy(
+        src_ref=src, dst_ref=dst, send_sem=send, recv_sem=recv, device_id=device, device_id_type=MESH
+    )
+
+
+def greet(t, p, NT, NP):
+    barrier = pltpu.get_barrier_semaphore()
+    for r in range(1, NP):
+        pl.semaphore_signal(barrier, inc=1, device_id=(t, xor(p, r)), device_id_type=MESH)
+    for k in range(1, NT):
+        pl.semaphore_signal(barrier, inc=1, device_id=((t + k) % NT, p), device_id_type=MESH)
+    pl.semaphore_wait(barrier, NP - 1 + NT - 1)
+
+
+def start_kernel(
+    NT, NP, x_ref, w_ref, msg_ref, ada_ref, gates_ref, bias_ref, mask_ref,
+    rows_ref, full_ref, mods_ref, sig_ref, cond_ref,
+    part_ref, got_ref, x_send, x_recv, c_send, c_recv, r_send, r_recv, s_send, s_recv, local_sem,
+):
+    NX, SUB = NP // 2, NT // NP
+    I, _, length = x_ref.shape
+    T = length // NX
+    WN = w_ref.shape[1]
+    half = WN // 256 * 128
+    t, p = lax.axis_index("tok"), lax.axis_index("tp")
+    xi = p // 2
+    core = (t, xor(p, 1))
+    ring = Ring(NT)
+    q = ring.place(t)
+    right, left = (ring.tok(q + 1), p), (ring.tok(q - 1), p)
+
+    def where(tt):
+        out = 0
+        for r in range(NP):
+            out = out + jnp.where(p == r, xor(tt // SUB, r), 0)
+        return out * SUB + tt % SUB
+
+    greet(t, p, NT, NP)
+
+    small = []
+    for k in range(1, NT):
+        peer = (t + k) % NT
+        small.append(copy_to(msg_ref.at[peer], cond_ref.at[k], s_send.at[0, k], s_recv.at[0, k], (peer, p)))
+        small[-1].start()
+
+    def hop(d, to_right):
+        side = 0 if to_right else 1
+        block = where(ring.tok(q - (d - 1) if to_right else q + (d - 1)))
+        src = w_ref if d == 1 else full_ref.at[block]
+        dst = full_ref.at[block]
+        if d == NT // 2:
+            cols = pl.ds(0, half) if to_right else pl.ds(half, WN - half)
+            src, dst = src.at[:, cols], dst.at[:, cols]
+        return copy_to(src, dst, r_send.at[side, d], r_recv.at[side, d], right if to_right else left)
+
+    hops = {}
+
+    def start_hop(d):
+        for to_right in (True, False):
+            hops[d, to_right] = hop(d, to_right)
+            hops[d, to_right].start()
+
+    def land_hop(d):
+        for to_right in (True, False):
+            hops[d, to_right].wait_recv()
+
+    sent = {}
+
+    def start_image(i):
+        for k in range(1, NX):
+            peer = xor(xi, k)
+            for j in range(NX):
+                at = pl.ds(pl.multiple_of(xor(peer, j) * T, T), T)
+                cp = copy_to(
+                    x_ref.at[i, :, pl.ds(j * T, T)], rows_ref.at[i, 2 * k, :, at],
+                    x_send.at[i, k, j], x_recv.at[i, k, j], (t, xor(p, 2 * k)),
+                )
+                sent[i, k, j] = cp
+                cp.start()
+
+    locals_, own = [], []
+    start_image(0)
+    start_hop(1)
+    for i in range(1, I):
+        start_image(i)
+    for i in range(I):
+        for j in range(NX):
+            at = pl.ds(pl.multiple_of(xor(xi, j) * T, T), T)
+            src = x_ref.at[i, :, pl.ds(j * T, T)]
+            cp = pltpu.make_async_copy(src, rows_ref.at[i, 0, :, at], local_sem.at[i, j])
+            cp.start()
+            locals_.append(cp)
+            cp = copy_to(src, rows_ref.at[i, 1, :, at], c_send.at[i, 0, j], c_recv.at[i, 0, j], core)
+            cp.start()
+            own.append(cp)
+    cp = pltpu.make_async_copy(w_ref, full_ref.at[where(t)], local_sem.at[I, 0])
+    cp.start()
+    locals_.append(cp)
+
+    cond_ref[0] = msg_ref[t]
+    for cp in small:
+        cp.wait_recv()
+    rb, fr = ada_ref.shape[1], gates_ref.shape[0]
+    feats = cond_ref[...].reshape(NT * 8, -1).astype(bf16)
+    for k in range(6):
+        part = jnp.dot(feats[:, :rb], ada_ref[k], preferred_element_type=f32)
+        part_ref[:, :, k * ML : (k + 1) * ML] = part.reshape(NT, 8, ML)
+    part = jnp.dot(feats[:, 256 : 256 + fr], gates_ref[...], preferred_element_type=f32)
+    part_ref[:, :, 6 * ML :] = part.reshape(NT, 8, 128)
+    for k in range(1, NT):
+        peer = (t + NT - k) % NT
+        cp = copy_to(part_ref.at[k], got_ref.at[k], s_send.at[1, k], s_recv.at[1, k], (peer, p))
+        cp.start()
+        small.append(cp)
+    land_hop(1)
+    start_hop(2)
+    for cp in small[NT - 1 :]:
+        cp.wait_recv()
+    total = part_ref[0]
+    for k in range(1, NT):
+        total = total + got_ref[k]
+    total = total + bias_ref[...]
+    sig = 1.0 / (1.0 + jnp.exp(-total[:, 6 * ML :]))
+    sig_ref[...] = sig
+    mods_ref[0, :, : 6 * ML] = total[:, : 6 * ML]
+    mods_ref[0, :, 6 * ML :] = sig * mask_ref[...]
+    mods = []
+    for r in range(1, NP):
+        cp = copy_to(mods_ref.at[0], mods_ref.at[r], s_send.at[2, r], s_recv.at[2, r], (t, xor(p, r)))
+        cp.start()
+        mods.append(cp)
+
+    passed = []
+
+    def land_image(i):
+        for k in range(1, NX):
+            for j in range(NX):
+                sent[i, k, j].wait_recv()
+            cp = copy_to(
+                rows_ref.at[i, 2 * k], rows_ref.at[i, 2 * k + 1],
+                c_send.at[i, k, 0], c_recv.at[i, k, 0], core,
+            )
+            cp.start()
+            passed.append(cp)
+
+    ring_left = list(range(2, NT // 2 + 1))
+    images_left = list(range(I))
+    while ring_left or images_left:
+        if images_left:
+            land_image(images_left.pop(0))
+        if ring_left:
+            d = ring_left.pop(0)
+            land_hop(d)
+            if d < NT // 2:
+                start_hop(d + 1)
+    for cp in own + passed + mods:
+        cp.wait_recv()
+    for cp in locals_:
+        cp.wait()
+    for cp in small + mods + own + passed + list(sent.values()) + list(hops.values()):
+        cp.wait_send()
+
+
+def start_call(NT, NP, x, w, msg, ada, gates, bias, mask):
+    I, CB, length = x.shape
+    NX = NP // 2
+    RB, WN = w.shape
+    wide = 6 * ML + 128
+    hbm, vmem = pl.BlockSpec(memory_space=pl.ANY), pl.BlockSpec(memory_space=pltpu.VMEM)
+    dma = pltpu.SemaphoreType.DMA
+    return pl.pallas_call(
+        functools.partial(start_kernel, NT, NP),
+        in_specs=[hbm, hbm] + [vmem] * 5,
+        out_specs=[hbm, hbm, vmem, vmem, vmem],
+        out_shape=[
+            jax.ShapeDtypeStruct((I, NP, CB, length), bf16),
+            jax.ShapeDtypeStruct((NT, RB, WN), bf16),
+            jax.ShapeDtypeStruct((NP, 8, wide), f32),
+            jax.ShapeDtypeStruct((8, 128), f32),
+            jax.ShapeDtypeStruct((NT, 8, ML), f32),
+        ],
+        scratch_shapes=[
+            pltpu.VMEM((NT, 8, wide), f32),
+            pltpu.VMEM((NT, 8, wide), f32),
+            dma((I, NX, NX)),
+            dma((I, NX, NX)),
+            dma((I, NX, NX)),
+            dma((I, NX, NX)),
+            dma((2, NT // 2 + 1)),
+            dma((2, NT // 2 + 1)),
+            dma((3, max(NT, NP))),
+            dma((3, max(NT, NP))),
+            dma((I + 1, NX)),
+        ],
+        compiler_params=pltpu.CompilerParams(
+            collective_id=0, has_side_effects=True, vmem_limit_bytes=32 * 2**20
+        ),
+        name="start",
+    )(x, w, msg, ada, gates, bias, mask)
+
+
+def tail_kernel(
+    NT, NP, g_ref, last_ref, ada_ref,
+    out_ref, lasts_ref, cond_ref,
+    part_ref, sum_ref, send_ref, recv_ref, r_send, r_recv, s_send, s_recv,
+):
+    SUB = NT // NP
+    t, p = lax.axis_index("tok"), lax.axis_index("tp")
+    ring = Ring(NT)
+    q = ring.place(t)
+    right, left = (ring.tok(q + 1), p), (ring.tok(q - 1), p)
+    WN = g_ref.shape[2]
+    half = (WN // 2 + 127) // 128 * 128
+    cols = (slice(0, half), slice(half, WN))
+
+    def where(tt):
+        out = 0
+        for r in range(NP):
+            out = out + jnp.where(p == r, xor(tt // SUB, r), 0)
+        return out * SUB + tt % SUB
+
+    greet(t, p, NT, NP)
+    lasts = []
+    for k in range(1, NT):
+        peer = (t + k) % NT
+        cp = copy_to(last_ref, lasts_ref.at[k], s_send.at[0, k], s_recv.at[0, k], (peer, p))
+        cp.start()
+        lasts.append(cp)
+    lasts_ref[0] = last_ref[...]
+
+    chains = []
+    for side in range(2):
+        for s in range(2):
+            chains.append((side, s, NT // 2 if side == s else NT // 2 - 1))
+    flying = {}
+
+    def step(h):
+        for n, (side, s, count) in enumerate(chains):
+            if h >= count:
+                continue
+            d = count - h
+            block = where(ring.tok(q + d if side == 0 else q - d))
+            width = cols[s].stop - cols[s].start
+            v = g_ref[block, :, cols[s]]
+            if h:
+                flying[n, h - 1].wait_recv()
+                v = v + recv_ref[n, h - 1, :, :width].astype(f32)
+            send_ref[n, h, :, :width] = v.astype(bf16)
+            cp = copy_to(
+                send_ref.at[n, h], recv_ref.at[n, h], r_send.at[n, h], r_recv.at[n, h],
+                right if side == 0 else left,
+            )
+            cp.start()
+            flying[n, h] = cp
+
+    step(0)
+    for cp in lasts:
+        cp.wait_recv()
+    grads = lasts_ref[...].reshape(NT * 8, -1)
+    total = 0.0
+    for k in range(6):
+        g = grads[:, k * ML : (k + 1) * ML]
+        high = g.astype(bf16)
+        low = (g - high.astype(f32)).astype(bf16)
+        w = ada_ref[k]
+        total = total + dot(high, w, 1, 1) + dot(low, w, 1, 1)
+    part_ref[:, :, : total.shape[1]] = total.reshape(NT, 8, -1)
+    parts = []
+    for k in range(1, NT):
+        peer = (t + NT - k) % NT
+        cp = copy_to(part_ref.at[k], sum_ref.at[0, t], s_send.at[1, k], s_recv.at[1, k], (peer, p))
+        cp.start()
+        parts.append(cp)
+    sum_ref[0, t] = part_ref[0]
+    step(1)
+    for cp in parts:
+        cp.wait_recv()
+    sums = []
+    for r in range(1, NP):
+        cp = copy_to(sum_ref.at[0], sum_ref.at[r], s_send.at[2, r], s_recv.at[2, r], (t, xor(p, r)))
+        cp.start()
+        sums.append(cp)
+    for h in range(2, NT // 2):
+        step(h)
+    for cp in sums:
+        cp.wait_recv()
+    total = sum_ref[0]
+    for r in range(1, NP):
+        total = total + sum_ref[r]
+    cond_ref[...] = total
+    mine = where(t)
+    for s in range(2):
+        v = g_ref[mine, :, cols[s]]
+        for n, (side, ss, count) in enumerate(chains):
+            if ss == s:
+                flying[n, count - 1].wait_recv()
+                v = v + recv_ref[n, count - 1, :, : cols[s].stop - cols[s].start].astype(f32)
+        out_ref[:, cols[s]] = v
+    for cp in lasts + parts + sums + list(flying.values()):
+        cp.wait_send()
+
+
+def tail_call(NT, NP, g, last, ada):
+    _, RB, WN = g.shape
+    half = (WN // 2 + 127) // 128 * 128
+    vmem = pl.BlockSpec(memory_space=pltpu.VMEM)
+    dma = pltpu.SemaphoreType.DMA
+    hops = NT // 2
+    return pl.pallas_call(
+        functools.partial(tail_kernel, NT, NP),
+        in_specs=[vmem] * 3,
+        out_specs=[vmem] * 3,
+        out_shape=[
+            jax.ShapeDtypeStruct((RB, WN), f32),
+            jax.ShapeDtypeStruct((NT,) + last.shape, f32),
+            jax.ShapeDtypeStruct((NT, 8, 256), f32),
+        ],
+        scratch_shapes=[
+            pltpu.VMEM((NT, 8, 256), f32),
+            pltpu.VMEM((NP, NT, 8, 256), f32),
+            pltpu.VMEM((4, hops, RB, half), bf16),
+            pltpu.VMEM((4, hops, RB, half), bf16),
+            dma((4, hops)),
+            dma((4, hops)),
+            dma((3, max(NT, NP))),
+            dma((3, max(NT, NP))),
+        ],
+        compiler_params=pltpu.CompilerParams(
+            collective_id=1, has_side_effects=True, vmem_limit_bytes=40 * 2**20
+        ),
+        name="tail",
+    )(g, last, ada)
+
+
 def make_body(NT, NP):
     NX = NP // 2
     SUB = NT // NP
     RB = D // NT
     CB = D // NP
     T = LEN // NX
-    wide = 4 if NT >= 16 else 2
-    tall = NT // wide
-    cycle = [r * wide for r in reversed(range(tall))]
-    for r in range(tall):
-        cols = list(range(1, wide))
-        cycle += [r * wide + c for c in (cols if r % 2 == 0 else cols[::-1])]
-    place = [cycle.index(t) for t in range(NT)]
+    table = Ring(NT)
+    cycle = [table.tok(q) for q in range(NT)]
     right_pairs = [(cycle[i], cycle[(i + 1) % NT]) for i in range(NT)]
     left_pairs = [(b, a) for a, b in right_pairs]
     n_right = NT // 2
@@ -152,9 +509,6 @@
 
     def tp_xor(v, r):
         return lax.ppermute(v, "tp", [(p, p ^ r) for p in range(NP)])
-
-    def tok_shift(v, k):
-        return lax.ppermute(v, "tok", [(t, (t + k) % NT) for t in range(NT)])
 
     def swap_tokens(v, k, axis):
         if k == 0:
@@ -192,11 +546,10 @@
         t = lax.axis_index("tok")
         p = lax.axis_index("tp")
         xi = p // 2
-        my_place = jnp.array(place, jnp.int32)[t]
-        ring = jnp.array(cycle, jnp.int32)
+        my_place = table.place(t)
 
         def block_of(d):
-            tt = ring[(my_place + d + NT) % NT]
+            tt = table.tok(my_place + d)
             return jnp.bitwise_xor(tt // SUB, p) * SUB + tt % SUB
 
         def gather_rows(shard):
@@ -209,10 +562,10 @@
             for d in range(1, n_left + 1):
                 v = hop(v, False)
                 pieces.append((d, v))
-            full = jnp.zeros((NT,) + shard.shape, shard.dtype)
+            full = jnp.zeros((2, NT) + shard.shape[1:], shard.dtype)
             for d, v in pieces:
-                full = lax.dynamic_update_slice(full, v[None], (block_of(d), 0, 0))
-            return full.reshape(D, -1)
+                full = lax.dynamic_update_slice(full, v[:, None], (0, block_of(d), 0, 0))
+            return full.reshape(2, D, -1)
 
         def scatter_rows(full):
             blocks = full.reshape(NT, RB, -1)
@@ -236,90 +589,85 @@
             ]
             return jnp.concatenate(parts, axis=axis)
 
-        xin = own_order(block_input, 2)
-        cot_in = own_order(cotangent, 2)
-
-        def gather_features(own):
-            blocks = [None] * NP
-            for k in range(NX):
-                v = own if k == 0 else swap_tokens(tp_xor(own, 2 * k), k, 1)
-                blocks[2 * k] = v
-                blocks[2 * k + 1] = tp_xor(v, 1)
-            return blocks
-
-        rows_blocks = [gather_features(xin[i]) for i in range(I)]
-        rows_full = [jnp.concatenate(b, axis=0) for b in rows_blocks]
-
-        time_feat = embed_time(timesteps).astype(bf16)
-        cond_wide = condition.astype(f32)
-        cond_act = jax.nn.silu(cond_wide).astype(bf16)
-        message = jnp.concatenate(
-            [cond_act.reshape(I, NT, RB), time_feat.reshape(I, NT, FR)], axis=2
-        ).transpose(1, 0, 2)
-        rolled = lax.dynamic_slice_in_dim(
-            jnp.concatenate([message, message], axis=0), t, NT, axis=0
-        )
-        feats = jnp.stack([rolled[0]] + [tok_shift(rolled[k], k) for k in range(1, NT)])
-        feats = feats.reshape(NT * I, RB + FR)
-        cond_rows, time_rows = feats[:, :RB], feats[:, RB:]
-        w_gates = jnp.concatenate([w_head, w_group], axis=1)
-        part = jnp.concatenate(
-            [dot(cond_rows, w_ada.reshape(RB, 6 * CB), 1, 0), dot(time_rows, w_gates, 1, 0)],
-            axis=1,
-        ).reshape(NT, I, -1)
-        summed = part[0]
-        for k in range(1, NT):
-            summed = summed + tok_shift(part[k], NT - k)
-        modulation = summed[:, : 6 * CB].reshape(I, 6, CB) + b_ada.astype(f32)
-        head_sig = jax.nn.sigmoid(summed[:, 6 * CB : 6 * CB + HL] + b_head.astype(f32))
-        group_sig = jax.nn.sigmoid(summed[:, 6 * CB + HL :] + b_group.astype(f32))
-        head_gate = head_mask.astype(f32) * head_sig
-        group_gate = group_mask.astype(f32) * group_sig
-        tp_message = jnp.concatenate(
-            [
-                modulation.reshape(-1),
-                b_out.astype(f32),
-                b_down.astype(f32),
-                group_gate.reshape(-1),
-                b_up.astype(f32),
-            ]
-        )
-        others = [tp_message] + [tp_xor(tp_message, r) for r in range(1, NP)]
-        n_mod = I * 6 * CB
-        vectors = jnp.stack(
-            [m[: n_mod + 2 * CB].reshape(I * 6 + 2, CB) for m in others], axis=1
-        ).reshape(I * 6 + 2, D)
-        columns = vectors.T
-
-        def mod(i, k):
-            return lax.slice_in_dim(columns, i * 6 + k, i * 6 + k + 1, axis=1)
-
-        out_bias = columns[:, I * 6 : I * 6 + 1]
-        down_bias = columns[:, I * 6 + 1 : I * 6 + 2]
-        base = n_mod + 2 * CB
-        gates_x = jnp.concatenate(
-            [others[2 * k][base : base + I * GL].reshape(I, GL) for k in range(NX)], axis=1
-        )
-        gate_cols = jnp.repeat(gates_x, GW, axis=1).T
-        up_bias = jnp.concatenate([others[2 * k][base + I * GL :] for k in range(NX)])[:, None]
-
         qkv_shard = jnp.pad(
             w_qkv.reshape(RB, 3, HL, HD), ((0, 0), (0, 0), (0, 0), (0, HP - HD))
         ).reshape(RB, 3 * HL * HP)
         out_shard = jnp.pad(w_out.T.reshape(RB, HL, HD), ((0, 0), (0, 0), (0, HP - HD))).reshape(
             RB, HL * HP
         )
-        up_shard = jnp.concatenate(
-            [w_up] + [tp_xor(w_up, 2 * k) for k in range(1, NX)], axis=1
-        )
-        down_shard = w_down.T
-        down_shard = jnp.concatenate(
-            [down_shard] + [tp_xor(down_shard, 2 * k) for k in range(1, NX)], axis=1
-        )
-        qkv_full = gather_rows(qkv_shard)
-        out_full = gather_rows(out_shard)
-        up_full = gather_rows(up_shard)
-        down_full = gather_rows(down_shard)
+        time_feat = embed_time(timesteps).astype(bf16)
+        cond_wide = condition.astype(f32)
+        cond_act = jax.nn.silu(cond_wide).astype(bf16)
+        pad8 = lambda v, width: jnp.pad(v, ((0, 8 - v.shape[0]), (0, width - v.shape[1])))
+        message = jnp.concatenate(
+            [
+                jnp.pad(cond_act.reshape(I, NT, RB), ((0, 0), (0, 0), (0, 256 - RB))),
+                jnp.pad(time_feat.reshape(I, NT, FR), ((0, 0), (0, 0), (0, ML - 256 - FR))),
+            ],
+            axis=2,
+        )
+        message = jnp.pad(message.transpose(1, 0, 2).astype(f32), ((0, 0), (0, 8 - I), (0, 0)))
+        ada = jnp.pad(w_ada.transpose(1, 0, 2), ((0, 0), (0, 0), (0, ML - CB)))
+        gates = jnp.concatenate([w_head, w_group], axis=1)
+        gates = jnp.pad(gates, ((0, 0), (0, 128 - HL - GL)))
+        wide = 6 * ML + 128
+        mod_bias = jnp.concatenate(
+            [jnp.pad(b_ada, ((0, 0), (0, ML - CB))).reshape(6 * ML), b_head, b_group]
+        ).astype(f32)
+        bias = jnp.concatenate(
+            [
+                jnp.broadcast_to(pad8(mod_bias[None], wide)[:1], (I, wide)),
+                pad8(jnp.concatenate([jnp.pad(b_out, (0, ML - CB)), b_down]).astype(f32)[None], wide)[:1],
+                pad8(b_up.astype(f32)[None], wide)[: 8 - I - 1],
+            ],
+            axis=0,
+        )
+        mask = pad8(jnp.concatenate([head_mask, group_mask], axis=1).astype(f32), 128)
+        rows_all, early_full, mods, sig, cond_all = start_call(
+            NT,
+            NP,
+            block_input,
+            jnp.concatenate([qkv_shard, out_shard], axis=1),
+            message,
+            ada,
+            gates,
+            bias,
+            mask,
+        )
+        rows_full = [rows_all[i].reshape(D, LEN) for i in range(I)]
+        early_full = early_full.reshape(D, -1)
+        qkv_full, out_full = early_full[:, : 3 * HL * HP], early_full[:, 3 * HL * HP :]
+        head_sig, group_sig = sig[:I, :HL], sig[:I, HL : HL + GL]
+        head_gate = mods[0, :I, 6 * ML : 6 * ML + HL]
+        vectors = mods[:, :I, : 6 * ML].reshape(NP, I * 6, ML)[:, :, :CB]
+        biases_two = mods[:, I, : 2 * ML].reshape(NP, 2, ML)[:, :, :CB]
+        columns = jnp.concatenate([vectors, biases_two], axis=1).transpose(0, 2, 1).reshape(D, -1)
+
+        def mod(i, k):
+            return lax.slice_in_dim(columns, i * 6 + k, i * 6 + k + 1, axis=1)
+
+        out_bias = columns[:, I * 6 : I * 6 + 1]
+        down_bias = columns[:, I * 6 + 1 : I * 6 + 2]
+        gates_x = jnp.concatenate(
+            [mods[2 * k, :I, 6 * ML + HL : 6 * ML + HL + GL] for k in range(NX)], axis=1
+        )
+        gate_cols = jnp.repeat(gates_x, GW, axis=1).T
+        up_bias = jnp.concatenate([mods[2 * k, I + 1, :FL] for k in range(NX)])[:, None]
+
+        cot_in = own_order(cotangent, 2)
+        cot_blocks = []
+        for k in range(NX):
+            v = cot_in[:, :, k * T : (k + 1) * T]
+            v = v if k == 0 else tp_xor(v, 2 * k)
+            cot_blocks.append(v)
+        cot_half = jnp.stack(cot_blocks, axis=1)
+        cot_full = jnp.stack([cot_half, tp_xor(cot_half, 1)], axis=2).reshape(I, D, T)
+
+        late_shard = jnp.stack([w_up, w_down.T])
+        late_parts = [late_shard] + [tp_xor(late_shard, 2 * k) for k in range(1, NX)]
+        late_parts = [gather_rows(v) for v in late_parts]
+        up_full = jnp.concatenate([v[0] for v in late_parts], axis=1)
+        down_full = jnp.concatenate([v[1] for v in late_parts], axis=1)
         qv = b_qv.astype(f32).reshape(2, HL, HD)
         qv_bias = jnp.stack(
             [
@@ -358,15 +706,7 @@
         mids = []
         for i in range(I):
             branch_one = fwd[i][-1]
-            cot_blocks = []
-            for k in range(NX):
-                v = (
-                    cot_in[i, :, :T]
-                    if k == 0
-                    else tp_xor(cot_in[i, :, k * T : (k + 1) * T], 2 * k)
-                )
-                cot_blocks += [v, tp_xor(v, 1)]
-            cot = jnp.concatenate(cot_blocks, axis=0).astype(f32)
+            cot = cot_full[i].astype(f32)
             mid_rows = rows_full[i][:, :T].astype(f32) + mod(i, 2) * branch_one
             centre, inverse = stats(mid_rows)
             normed = (mid_rows - centre) * inverse
@@ -444,18 +784,12 @@
 
         grad_down = sum(dot(m["grad_two"], m["hidden"], 1, 1) for m in mids)
         grad_up = sum(dot(m["mlp_in"], m["grad_pre"], 1, 1) for m in mids)
-        grad_down = scatter_rows(grad_down)
-        grad_up = scatter_rows(grad_up)
-
-        def x_sum(v):
-            total = v[:, :FL]
-            for k in range(1, NX):
-                got = tp_xor(v[:, k * FL : (k + 1) * FL].astype(bf16), 2 * k)
-                total = total + got.astype(f32)
-            return total
-
-        grad_down = x_sum(grad_down)
-        grad_up = x_sum(grad_up)
+        late = scatter_rows(jnp.concatenate([grad_up, grad_down], axis=1))
+        late = late.reshape(RB, 2, NX, FL)
+        total = late[:, :, 0]
+        for k in range(1, NX):
+            total = total + tp_xor(late[:, :, k].astype(bf16), 2 * k).astype(f32)
+        grad_up, grad_down = total[:, 0], total[:, 1]
 
         def x_message(k):
             parts = []
@@ -492,7 +826,7 @@
             for k in range(1, NX):
                 got = tp_xor(both[k].astype(bf16), 2 * k).astype(f32)
                 gnorm = gnorm + swap_tokens(got, k, 1)
-            normed = (xin[i].astype(f32) - centre) * inverse
+            normed = (rows_full[i][:CB].astype(f32) - centre) * inverse
             own_cols = columns[:CB]
             g = gnorm * (1.0 + own_cols[:, i * 6 + 1 : i * 6 + 2])
             sums = jnp.stack([jnp.sum(g, axis=0), jnp.sum(g * normed, axis=0)])
@@ -520,7 +854,6 @@
         )
         grad_out = scatter_rows(grad_out)
         grad_qkv = sum(dot(f[2], b["dqkv"], 1, 1) for f, b in zip(fwd, backs))
-        grad_qkv = scatter_rows(grad_qkv)
 
         grad_mod = jnp.stack(
             [
@@ -536,50 +869,46 @@
         grad_head_gate = jnp.stack([b["heads"] for b in backs])
         head_logit = grad_head_gate * head_mask.astype(f32) * head_sig * (1.0 - head_sig)
         group_logit = grad_group_gate * group_mask.astype(f32) * group_sig * (1.0 - group_sig)
+        image_rows = jnp.concatenate(
+            [
+                jnp.pad(grad_mod, ((0, 0), (0, 0), (0, ML - CB))).reshape(I, 6 * ML),
+                head_logit,
+                group_logit,
+                jnp.zeros((I, 128 - HL - GL), f32),
+            ],
+            axis=1,
+        )
+        widen = lambda v: jnp.pad(v, (0, wide - v.shape[0]))[None]
         last = jnp.concatenate(
             [
-                jnp.concatenate([grad_mod.reshape(I, -1), head_logit, group_logit], axis=1).reshape(
-                    -1
-                ),
-                sum(b["q_sums"] for b in backs),
-                sum(b["v_sums"] for b in backs),
-                bias_sums,
-            ]
-        )
-        lasts = jnp.stack([last] + [tok_shift(last, k) for k in range(1, NT)])
-        n_head = I * (6 * CB + HL + GL)
-        per_all = lasts[:, :n_head].reshape(NT * I, -1)
-        mods_all = per_all[:, : 6 * CB]
-        logits_all = per_all[:, 6 * CB :]
-        biases = jnp.sum(lasts[:, n_head:], axis=0)
-        cond_f = cond_rows.astype(f32)
+                image_rows,
+                widen(sum(b["q_sums"] for b in backs)),
+                widen(sum(b["v_sums"] for b in backs)),
+                widen(bias_sums[: 2 * CB]),
+                widen(bias_sums[2 * CB :]),
+                jnp.zeros((8 - I - 4, wide), f32),
+            ],
+            axis=0,
+        )
+        grad_qkv, lasts, cond_sum = tail_call(NT, NP, grad_qkv.reshape(NT, RB, -1), last, ada)
+        mods_all = (
+            lasts[:, :I, : 6 * ML].reshape(NT * I, 6, ML)[:, :, :CB].reshape(NT * I, 6 * CB)
+        )
+        logits_all = lasts[:, :I, 6 * ML : 6 * ML + HL + GL].reshape(NT * I, HL + GL)
+        bias_rows = jnp.sum(lasts[:, I : I + 4], axis=0)
+        cond_f = cond_all[:, :I, :RB].reshape(NT * I, RB)
+        time_f = cond_all[:, :I, 256 : 256 + FR].reshape(NT * I, FR)
         grad_w_ada = lax.dot_general(
             cond_f, mods_all, (((0,), (0,)), ((), ())), precision=exact_mode
         ).reshape(RB, 6, CB)
         grad_b_ada = jnp.sum(mods_all, axis=0).reshape(6, CB)
         grad_w_gates = lax.dot_general(
-            time_rows.astype(f32), logits_all, (((0,), (0,)), ((), ())), precision=exact_mode
+            time_f, logits_all, (((0,), (0,)), ((), ())), precision=exact_mode
         )
         grad_b_gates = jnp.sum(logits_all, axis=0)
-        cond_part = lax.dot_general(
-            mods_all,
-            w_ada.reshape(RB, 6 * CB).astype(f32),
-            (((1,), (1,)), ((), ())),
-            precision=exact_mode,
-        ).reshape(NT, I, RB)
-        cond_parts = jnp.stack(
-            [cond_part[0]] + [tok_shift(cond_part[k], NT - k) for k in range(1, NT)]
-        )
-        cond_parts = lax.dynamic_slice_in_dim(
-            jnp.concatenate([cond_parts, cond_parts], axis=0), (NT - t) % NT, NT, axis=0
-        )
-        cond_sum = cond_parts.transpose(1, 0, 2).reshape(I, D)
-        cond_total = cond_sum
-        for r in range(1, NP):
-            cond_total = cond_total + tp_xor(cond_sum, r)
+        cond_total = cond_sum[:, :I, :RB].transpose(1, 0, 2).reshape(I, D)
         grad_condition = jax.vjp(jax.nn.silu, cond_wide)[1](cond_total)[0]
 
-        n_qv = 2 * HL * HD
         return (
             block_output,
             grad_input,
@@ -587,13 +916,13 @@
             grad_w_ada,
             grad_b_ada,
             grad_qkv.reshape(RB, 3, HL, HP)[..., :HD].reshape(RB, 3, HL * HD),
-            biases[:n_qv].reshape(2, HL * HD),
+            bias_rows[:2, : HL * HD],
             grad_out.reshape(RB, HL, HP)[..., :HD].reshape(RB, HL * HD).T,
-            biases[n_qv : n_qv + CB],
+            bias_rows[2, :CB],
             grad_up,
-            biases[n_qv + 2 * CB :],
+            bias_rows[3, :FL],
             grad_down.T,
-            biases[n_qv + CB : n_qv + 2 * CB],
+            bias_rows[2, CB : 2 * CB],
             grad_w_gates[:, :HL],
             grad_b_gates[:HL],
             grad_w_gates[:, HL:],

time: 988 us -> 882 us (0.89)
  Pallas kernels: 60 us -> 169 us
  starting transfers between devices: 145 us -> 57 us
  waiting for transfers between devices: 282 us -> 211 us
  matrix products: 180 us -> 146 us
  between operations: 34.6 us -> 5.06 us
  other arithmetic: 105 us -> 123 us
    pallas_call x0 -> x2, Pallas kernels: none -> 109 us  [the longest x1 57 us: start_call(): pl.pallas_call(functools.partial(start_kernel, NT, NP), in_specs=[hbm, hb...]
    ppermute x71 -> x47, waiting for transfers between devices: 169 us -> 105 us  [tp_xor(): return lax.ppermute(v, 'tp', [(p, p ^ r) for p in range(NP)])]
    ppermute x28 -> x0, starting transfers between devices: 44.6 us -> none  [tok_shift(): return lax.ppermute(v, 'tok', [(t, (t + k) % NT) for t in range(NT)])]
    dot_general x38 -> x36, matrix products: 179 us -> 144 us  [dot(): lax.dot_general(a, b, (((ca,), (cb,)), ((), ())), preferred_element_type=...]
    ppermute x56 -> x28, starting transfers between devices: 59.5 us -> 30 us  [hop(): return lax.ppermute(v, 'tok', right_pairs if right else left_pairs)]
    slice x15 -> x21, local copies, waits for them, and re-layouts: 2.24 us -> 23.4 us  [the longest x2 8.36 us: body(): down_full = jnp.concatenate([v[1] for v in late_parts], axis=1)]
    ppermute x71 -> x47, starting transfers between devices: 41.2 us -> 27 us  [tp_xor(): return lax.ppermute(v, 'tp', [(p, p ^ r) for p in range(NP)])]
    convert_element_type x16 -> x8, other arithmetic: 27.4 us -> 15.9 us  [scatter_rows(): v = hop((term if v is None else term + v.astype(f32)).astype(bf16), right)]
  transfers between devices with their start and end apart: 155 -> 75, of which waited for: 49 -> 24; matrix products, arithmetic and copies ran while one was open for 31% -> 38% of each run, Pallas kernels for 6% -> 19%
where the time goes in v2:
time: 882 us; the launch traced here: 871 us
  waiting for transfers between devices  211 us (24%)
  Pallas kernels  169 us (19%)
  local copies, waits for them, and re-layouts  161 us (18%)
  matrix products  146 us (17%)
  other arithmetic  123 us (14%)
  starting transfers between devices  57 us (6%)
    dot_general x36, matrix products, dot(): lax.dot_general(a, b, (((ca,), (cb,)), ((), ())), preferred_element_type=...  144 us
    ppermute x28, waiting for transfers between devices, hop(): return lax.ppermute(v, 'tok', right_pairs if right else left_pairs)  106 us
    ppermute x47, waiting for transfers between devices, tp_xor(): return lax.ppermute(v, 'tp', [(p, p ^ r) for p in range(NP)])  105 us
    pallas_call x1, Pallas kernels, start_call(): pl.pallas_call(functools.partial(start_kernel, NT, NP), in_specs=[hbm, hb...  57 us
    pallas_call x1, Pallas kernels, tail_call(): pl.pallas_call(functools.partial(tail_kernel, NT, NP), in_specs=[vmem] *...  51.8 us
    unnamed x403, local copies, waits for them, and re-layouts  44 us
    pallas_call x3, Pallas kernels, attn_bwd(): pl.pallas_call(functools.partial(attn_bwd_kernel, 256), grid=(heads,), in...  37.6 us
    ppermute x28, starting transfers between devices, hop(): return lax.ppermute(v, 'tok', right_pairs if right else left_pairs)  30 us
  transfers between devices with their start and end apart: 75, of which 24 were waited for; matrix products, arithmetic and copies ran while one was open for 38% of the time, Pallas kernels for 19%

profile of v2, /device:TPU:0, one launch (start us, length us, event | category | flops | bytes accessed | tf_op | source)
XLA Modules:
  0.0 871.5 jit_solution(14496399785609449652)
XLA Ops:
  12.9 57.0 %start.1 = (bf16[3,4,288,1024]{3,2,1,0:T(8,128)(2,1)S(1)}, bf16[8,144,1280]{2,1,0:T(8,128)(2,1)S(1)}, f32[4,8,2432]{2,1,0:T(8,128)S(1)}, f32[8,128]{1,0:T(8,128)S(1)}, f32[8,8,384]{2,1,0:T(8,128)S(1)}) custom-call(bf16[3,288,1024]{2,1,0:T(8,128)(2,1)S(1)} %copy-done.6, bf16[144,1280]{1,0:T(8,128)(2,1)S(1)} %pad_maximum_fusion.31.w_ref, ...), custom_call_target="tpu_custom_call" | custom-call | tf_op jit(solution)/shard_map/start/pallas_call | solution.py:330
  70.7 3.6 fusion.240
  86.3 4.7 add_convert_fusion.5
  91.0 7.5 attn_fwd.3
  106.5 7.3 attn_fwd.4
  123.2 4.7 add_convert_fusion.3
  127.9 7.8 attn_fwd.5
  144.8 8.4 fusion.18
  169.6 14.2 %collective-permute-done.30 = bf16[3,288,512]{2,1,0:T(8,128)(2,1)S(1)} collective-permute-done((bf16[3,288,512]{2,1,0:T(8,128)(2,1)}, bf16[3,288,512]{2,1,0:T(8,128)(2,1)S(1)}, u32[]{:S(2)}, u32[]{:S(2)}) %collective-permute-start.30) | collective-permute-done | bytes 884768 | tf_op jit(solution)/shard_map/ppermute | solution.py:511
  193.5 8.4 collective-permute-done.11
  203.3 11.0 %collective-permute-done.4 = bf16[2,144,1152]{2,1,0:T(8,128)(2,1)S(1)} collective-permute-done((bf16[2,144,1152]{2,1,0:T(8,128)(2,1)}, bf16[2,144,1152]{2,1,0:T(8,128)(2,1)S(1)}, u32[]{:S(2)}, u32[]{:S(2)}) %collective-permute-start.4) | collective-permute-done | bytes 663584 | tf_op jit(solution)/shard_map/ppermute | solution.py:508
  219.9 10.7 %collective-permute-done.21 = bf16[2,288,512]{2,1,0:T(8,128)(2,1)S(1)} collective-permute-done((bf16[2,288,512]{2,1,0:T(8,128)(2,1)S(1)}, bf16[2,288,512]{2,1,0:T(8,128)(2,1)S(1)}, u32[]{:S(2)}, u32[]{:S(2)}) %collective-permute-start.21) | collective-permute-done | bytes 589856 | tf_op jit(solution)/shard_map/ppermute | solution.py:511
  236.5 4.0 collective-permute-done.26
  243.2 5.2 collective-permute-done.12
  250.5 12.1 %collective-permute-done.5 = bf16[2,144,1152]{2,1,0:T(8,128)(2,1)S(1)} collective-permute-done((bf16[2,144,1152]{2,1,0:T(8,128)(2,1)S(1)}, bf16[2,144,1152]{2,1,0:T(8,128)(2,1)S(1)}, u32[]{:S(2)}, u32[]{:S(2)}) %collective-permute-start.5) | collective-permute-done | bytes 663584 | tf_op jit(solution)/shard_map/ppermute | solution.py:508
  264.7 12.2 %collective-permute-done.13 = bf16[2,144,1152]{2,1,0:T(8,128)(2,1)} collective-permute-done((bf16[2,144,1152]{2,1,0:T(8,128)(2,1)S(1)}, bf16[2,144,1152]{2,1,0:T(8,128)(2,1)}, u32[]{:S(2)}, u32[]{:S(2)}) %collective-permute-start.13) | collective-permute-done | bytes 663584 | tf_op jit(solution)/shard_map/ppermute | solution.py:508
  278.9 5.7 collective-permute-done.6
  290.0 5.3 fusion.241
  326.6 3.1 fusion.242
  329.9 3.6 convolution_add_fusion.6
  336.7 7.5 convert_reduce_fusion.5
  344.2 6.2 fusion.222
  350.4 4.8 fusion.280
  355.2 6.3 fusion.221
  361.5 3.6 convolution_add_fusion.4
  365.2 3.1 fusion.225
  370.6 3.7 convolution_add_fusion.5
  374.3 3.3 fusion.224
  379.2 7.3 convert_reduce_fusion.3
  386.5 4.7 fusion.279
  391.7 7.7 convert_reduce_fusion.4
  399.4 4.9 fusion.281
  405.0 9.0 %convolution_add_fusion.1 = f32[1152,2304]{1,0:T(8,128)S(1)} fusion(f32[1152,2304]{1,0:T(8,128)} %fusion.222, bf16[1152,512]{1,0:T(8,128)(2,1)} %fusion.55, f32[2304]{0:T(1024)S(1)} %get-tuple-element.143, f32[2304,512]{0,1:T(8,128)} %copy-done.70), kind=kOutput, calls=%fused_computation.2 | convolution fusion | flops 2732359680 | bytes 27141120 | tf_op jit(solution)/shard_map/dot_general | solution.py:29
  414.1 9.5 %convolution_add_fusion = f32[1152,2304]{1,0:T(8,128)} fusion(f32[1152,2304]{1,0:T(8,128)S(1)} %convolution_add_fusion.1, bf16[1152,512]{1,0:T(8,128)(2,1)S(1)} %copy-done.72, f32[2304]{0:T(1024)S(1)} %get-tuple-element.142, f32[2304,512]{0,1:T(8,128)} %copy-done.69), kind=kOutput, calls=%fused_computation.1 | convolution fusion | flops 2732359680 | bytes 27141120 | tf_op jit(solution)/shard_map/dot_general | solution.py:29
  423.6 4.9 convolution_add_fusion.3
  428.6 5.0 convolution_add_fusion.2
  433.7 6.2 pad_maximum_fusion
  445.8 7.6 fusion.143
  456.2 7.2 collective-permute-done.29
  463.4 6.2 collective-permute-done.24
  471.2 4.4 collective-permute-done.19
  511.2 12.5 %collective-permute-done.59 = f32[5196]{0:T(1024)S(1)} collective-permute-done((f32[5196]{0:T(1024)S(1)}, f32[5196]{0:T(1024)S(1)}, u32[]{:S(2)}, u32[]{:S(2)}) %collective-permute-start.59) | collective-permute-done | bytes 20816 | tf_op jit(solution)/shard_map/ppermute | solution.py:511
  527.3 3.4 fusion.41
  532.2 14.1 %collective-permute-done.42 = bf16[288,512]{1,0:T(8,128)(2,1)S(1)} collective-permute-done((bf16[288,512]{1,0:T(8,128)(2,1)}, bf16[288,512]{1,0:T(8,128)(2,1)S(1)}, u32[]{:S(2)}, u32[]{:S(2)}) %collective-permute-start.42) | collective-permute-done | bytes 294944 | tf_op jit(solution)/shard_map/ppermute | solution.py:511
  547.7 4.9 collective-permute-done.33
  555.5 7.6 collective-permute-done.43
  570.3 12.6 %attn_bwd.5 = (bf16[4,80,1024]{2,1,0:T(8,128)(2,1)S(1)}, bf16[4,80,1024]{2,1,0:T(8,128)(2,1)S(1)}, bf16[4,80,1024]{2,1,0:T(8,128)(2,1)S(1)}, f32[4,1,1024]{2,1,0:T(1,128)S(1)}) custom-call(f32[4]{0:T(128)S(1)} %get-tuple-element.266.gate_ref, bf16[12,80,1024]{2,1,0:T(8,128)(2,1)} %bitcast.692, bf16[12,80,1024]{2,1,0:T(8,128)(2,1)} %bitcast.693, ...), custom_call_target="tpu_custom_call" | custom-call | flops 10737418240 | bytes 6553600 | tf_op jit(solution)/shard_map/attn_bwd/pallas_call | solution.py:114
  582.9 12.3 %attn_bwd.4 = (bf16[4,80,1024]{2,1,0:T(8,128)(2,1)S(1)}, bf16[4,80,1024]{2,1,0:T(8,128)(2,1)S(1)}, bf16[4,80,1024]{2,1,0:T(8,128)(2,1)S(1)}, f32[4,1,1024]{2,1,0:T(1,128)S(1)}) custom-call(f32[4]{0:T(128)S(1)} %get-tuple-element.265.gate_ref, bf16[12,80,1024]{2,1,0:T(8,128)(2,1)} %bitcast.686, bf16[12,80,1024]{2,1,0:T(8,128)(2,1)} %bitcast.687, ...), custom_call_target="tpu_custom_call" | custom-call | flops 10737418240 | bytes 6553600 | tf_op jit(solution)/shard_map/attn_bwd/pallas_call | solution.py:114
  599.2 12.8 %attn_bwd.3 = (bf16[4,80,1024]{2,1,0:T(8,128)(2,1)S(1)}, bf16[4,80,1024]{2,1,0:T(8,128)(2,1)S(1)}, bf16[4,80,1024]{2,1,0:T(8,128)(2,1)S(1)}, f32[4,1,1024]{2,1,0:T(1,128)S(1)}) custom-call(f32[4]{0:T(128)S(1)} %get-tuple-element.264.gate_ref, bf16[12,80,1024]{2,1,0:T(8,128)(2,1)} %bitcast.680, bf16[12,80,1024]{2,1,0:T(8,128)(2,1)} %bitcast.681, ...), custom_call_target="tpu_custom_call" | custom-call | flops 10737418240 | bytes 6553600 | tf_op jit(solution)/shard_map/attn_bwd/pallas_call | solution.py:114
  642.4 5.1 fusion.285
  650.4 4.4 add_add_fusion
  656.8 3.3 collective-permute-done.61
  665.6 6.0 copy.302
  674.9 3.4 fusion.42
  685.4 3.4 fusion.50
  692.8 17.4 %collective-permute-done.69 = bf16[144,4608]{1,0:T(8,128)(2,1)} collective-permute-done((bf16[144,4608]{1,0:T(8,128)(2,1)}, bf16[144,4608]{1,0:T(8,128)(2,1)}, u32[]{:S(2)}, u32[]{:S(2)}) %collective-permute-start.69) | collective-permute-done | bytes 1327136 | tf_op jit(solution)/shard_map/ppermute | solution.py:508
  710.2 5.5 fusion.43
  718.3 6.8 collective-permute-done.46
  725.4 3.7 fusion.86
  734.1 51.8 %tail.1 = (f32[144,960]{1,0:T(8,128)S(1)}, f32[8,8,2432]{2,1,0:T(8,128)S(1)}, f32[8,8,256]{2,1,0:T(8,128)S(1)}) custom-call(f32[8,144,960]{2,1,0:T(8,128)S(1)} %bitcast.662, f32[8,2432]{1,0:T(8,128)S(1)} %concatenate.257.last_ref, bf16[6,144,384]{2,1,0:T(8,128)(2,1)S(1)} %copy-done.3), custom_call_target="tpu_custom_call" | custom-call | tf_op jit(solution)/shard_map/tail/pallas_call | solution.py:468
  815.3 27.0 %collective-permute-done.73 = bf16[144,4608]{1,0:T(8,128)(2,1)S(1)} collective-permute-done((bf16[144,4608]{1,0:T(8,128)(2,1)S(1)}, bf16[144,4608]{1,0:T(8,128)(2,1)S(1)}, u32[]{:S(2)}, u32[]{:S(2)}) %collective-permute-start.73) | collective-permute-done | bytes 1327136 | tf_op jit(solution)/shard_map/ppermute | solution.py:508
  842.2 4.1 fusion.44
  846.3 3.2 reshape.1062
  857.7 10.2 %collective-permute-done.74 = bf16[144,2,1152]{2,1,0:T(2,128)(2,1)S(1)} collective-permute-done((bf16[144,2,1152]{2,1,0:T(2,128)(2,1)S(1)}, bf16[144,2,1152]{2,1,0:T(2,128)(2,1)S(1)}, u32[]{:S(2)}, u32[]{:S(2)}) %collective-permute-start.74) | collective-permute-done | bytes 663584 | tf_op jit(solution)/shard_map/ppermute | solution.py:511
  (902 shorter events, 311.2 us)
Async XLA Ops:
  2.8 159.2 %collective-permute-start.10 = (bf16[2,144,1152]{2,1,0:T(8,128)(2,1)}, bf16[2,144,1152]{2,1,0:T(8,128)(2,1)}, u32[]{:S(2)}, u32[]{:S(2)}) collective-permute-start(bf16[2,144,1152]{2,1,0:T(8,128)(2,1)} %pad_maximum_fusion.27), channel_id=1, source_target_pairs={{0,2},{1,3},{2,0},{3,1},{4,6},{5,7},{6,4},{7,5},{8,10},{9,11},{10,... | collective-permute-start | bytes 1990664 | tf_op jit(solution)/shard_map/ppermute | solution.py:511
  5.8 161.6 %collective-permute-start.3 = (bf16[2,144,1152]{2,1,0:T(8,128)(2,1)}, bf16[2,144,1152]{2,1,0:T(8,128)(2,1)}, u32[]{:S(2)}, u32[]{:S(2)}) collective-permute-start(bf16[2,144,1152]{2,1,0:T(8,128)(2,1)} %pad_maximum_fusion.27), channel_id=1, source_target_pairs={{24,16},{16,8},{8,0},{0,4},{4,12},{12,20},{20,28},{28,24},{25,17},... | collective-permute-start | bytes 1990664 | tf_op jit(solution)/shard_map/ppermute | solution.py:508
  7.3 181.6 %collective-permute-start.7 = (bf16[2,144,1152]{2,1,0:T(8,128)(2,1)}, bf16[2,144,1152]{2,1,0:T(8,128)(2,1)}, u32[]{:S(2)}, u32[]{:S(2)}) collective-permute-start(bf16[2,144,1152]{2,1,0:T(8,128)(2,1)} %pad_maximum_fusion.27), channel_id=1, source_target_pairs={{16,24},{8,16},{0,8},{4,0},{12,4},{20,12},{28,20},{24,28},{17,25},... | collective-permute-start | bytes 1990664 | tf_op jit(solution)/shard_map/ppermute | solution.py:508
  101.3 84.0 %collective-permute-start = (bf16[2,288,1024]{2,1,0:T(8,128)(2,1)}, bf16[2,288,1024]{2,1,0:T(8,128)(2,1)}, u32[]{:S(2)}, u32[]{:S(2)}) collective-permute-start(bf16[2,288,1024]{2,1,0:T(8,128)(2,1)} %fusion.117), channel_id=1, source_target_pairs={{0,1},{1,0},{2,3},{3,2},{4,5},{5,4},{6,7},{7,6},{8,9},{9,8},{10,11... | collective-permute-start | bytes 3538952 | tf_op jit(solution)/shard_map/ppermute | solution.py:511
  116.7 73.2 %collective-permute-start.20 = (bf16[2,288,1024]{2,1,0:T(8,128)(2,1)}, bf16[2,288,1024]{2,1,0:T(8,128)(2,1)}, u32[]{:S(2)}, u32[]{:S(2)}) collective-permute-start(bf16[2,288,1024]{2,1,0:T(8,128)(2,1)} %fusion.118), channel_id=1, source_target_pairs={{0,1},{1,0},{2,3},{3,2},{4,5},{5,4},{6,7},{7,6},{8,9},{9,8},{10,11... | collective-permute-start | bytes 3538952 | tf_op jit(solution)/shard_map/ppermute | solution.py:511
  162.0 21.8 %collective-permute-start.30 = (bf16[3,288,512]{2,1,0:T(8,128)(2,1)}, bf16[3,288,512]{2,1,0:T(8,128)(2,1)S(1)}, u32[]{:S(2)}, u32[]{:S(2)}) collective-permute-start(bf16[3,288,512]{2,1,0:T(8,128)(2,1)} %get-tuple-element.215), channel_id=1, source_target_pairs={{0,2},{1,3},{2,0},{3,1},{4,6},{5,7},{6,4},{7,5},{8,10},{9,11},{10,... | collective-permute-start | bytes 2654216 | tf_op jit(solution)/shard_map/ppermute | solution.py:511
  167.4 25.4 %collective-permute-start.25 = (bf16[2,288,1024]{2,1,0:T(8,128)(2,1)S(1)}, bf16[2,288,1024]{2,1,0:T(8,128)(2,1)S(1)}, u32[]{:S(2)}, u32[]{:S(2)}) collective-permute-start(bf16[2,288,1024]{2,1,0:T(8,128)(2,1)S(1)} %copy-done.109), channel_id=1, source_target_pairs={{0,1},{1,0},{2,3},{3,2},{4,5},{5,4},{6,7},{7,6},{8,9},{9,8},{10,11... | collective-permute-start | bytes 3538952 | tf_op jit(solution)/shard_map/ppermute | solution.py:511
  183.8 18.1 %collective-permute-start.11 = (bf16[2,144,1152]{2,1,0:T(8,128)(2,1)}, bf16[2,144,1152]{2,1,0:T(8,128)(2,1)S(1)}, u32[]{:S(2)}, u32[]{:S(2)}) collective-permute-start(bf16[2,144,1152]{2,1,0:T(8,128)(2,1)} %collective-permute-done.10), channel_id=1, source_target_pairs={{24,16},{16,8},{8,0},{0,4},{4,12},{12,20},{20,28},{28,24},{25,17},... | collective-permute-start | bytes 1990664 | tf_op jit(solution)/shard_map/ppermute | solution.py:508
  185.2 49.3 %collective-permute-start.15 = (bf16[2,144,1152]{2,1,0:T(8,128)(2,1)}, bf16[2,144,1152]{2,1,0:T(8,128)(2,1)S(1)}, u32[]{:S(2)}, u32[]{:S(2)}) collective-permute-start(bf16[2,144,1152]{2,1,0:T(8,128)(2,1)} %collective-permute-done.10), channel_id=1, source_target_pairs={{16,24},{8,16},{0,8},{4,0},{12,4},{20,12},{28,20},{24,28},{17,25},... | collective-permute-start | bytes 1990664 | tf_op jit(solution)/shard_map/ppermute | solution.py:508
  188.9 25.4 %collective-permute-start.4 = (bf16[2,144,1152]{2,1,0:T(8,128)(2,1)}, bf16[2,144,1152]{2,1,0:T(8,128)(2,1)S(1)}, u32[]{:S(2)}, u32[]{:S(2)}) collective-permute-start(bf16[2,144,1152]{2,1,0:T(8,128)(2,1)} %collective-permute-done.3), channel_id=1, source_target_pairs={{24,16},{16,8},{8,0},{0,4},{4,12},{12,20},{20,28},{28,24},{25,17},... | collective-permute-start | bytes 1990664 | tf_op jit(solution)/shard_map/ppermute | solution.py:508
  189.8 45.4 %collective-permute-start.8 = (bf16[2,144,1152]{2,1,0:T(8,128)(2,1)}, bf16[2,144,1152]{2,1,0:T(8,128)(2,1)S(1)}, u32[]{:S(2)}, u32[]{:S(2)}) collective-permute-start(bf16[2,144,1152]{2,1,0:T(8,128)(2,1)} %collective-permute-done.7), channel_id=1, source_target_pairs={{16,24},{8,16},{0,8},{4,0},{12,4},{20,12},{28,20},{24,28},{17,25},... | collective-permute-start | bytes 1990664 | tf_op jit(solution)/shard_map/ppermute | solution.py:508
  192.8 102.4 %collective-permute-start.31 = (bf16[3,2,288,512]{3,2,1,0:T(8,128)(2,1)S(1)}, bf16[3,2,288,512]{3,2,1,0:T(8,128)(2,1)S(1)}, u32[]{:S(2)}, u32[]{:S(2)}) collective-permute-start(bf16[3,2,288,512]{3,2,1,0:T(8,128)(2,1)S(1)} %get-tuple-element.213), channel_id=1, source_target_pairs={{0,1},{1,0},{2,3},{3,2},{4,5},{5,4},{6,7},{7,6},{8,9},{9,8},{10,11... | collective-permute-start | bytes 5308424 | tf_op jit(solution)/shard_map/ppermute | solution.py:511
  201.9 13.9 %collective-permute-start.1 = (bf16[2,288,512]{2,1,0:T(8,128)(2,1)S(1)}, bf16[2,288,512]{2,1,0:T(8,128)(2,1)S(1)}, u32[]{:S(2)}, u32[]{:S(2)}) collective-permute-start(bf16[2,288,512]{2,1,0:T(8,128)(2,1)S(1)} %slice.1428), channel_id=1, source_target_pairs={{0,2},{1,3},{2,0},{3,1},{4,6},{5,7},{6,4},{7,5},{8,10},{9,11},{10,... | collective-permute-start | bytes 1769480 | tf_op jit(solution)/shard_map/ppermute | solution.py:511
  214.3 16.3 %collective-permute-start.21 = (bf16[2,288,512]{2,1,0:T(8,128)(2,1)S(1)}, bf16[2,288,512]{2,1,0:T(8,128)(2,1)S(1)}, u32[]{:S(2)}, u32[]{:S(2)}) collective-permute-start(bf16[2,288,512]{2,1,0:T(8,128)(2,1)S(1)} %slice.1427), channel_id=1, source_target_pairs={{0,2},{1,3},{2,0},{3,1},{4,6},{5,7},{6,4},{7,5},{8,10},{9,11},{10,... | collective-permute-start | bytes 1769480 | tf_op jit(solution)/shard_map/ppermute | solution.py:511
  215.7 24.7 %collective-permute-start.26 = (bf16[2,288,512]{2,1,0:T(8,128)(2,1)S(1)}, bf16[2,288,512]{2,1,0:T(8,128)(2,1)S(1)}, u32[]{:S(2)}, u32[]{:S(2)}) collective-permute-start(bf16[2,288,512]{2,1,0:T(8,128)(2,1)S(1)} %slice.1426), channel_id=1, source_target_pairs={{0,2},{1,3},{2,0},{3,1},{4,6},{5,7},{6,4},{7,5},{8,10},{9,11},{10,... | collective-permute-start | bytes 1769480 | tf_op jit(solution)/shard_map/ppermute | solution.py:511
  230.6 17.8 %collective-permute-start.12 = (bf16[2,144,1152]{2,1,0:T(8,128)(2,1)S(1)}, bf16[2,144,1152]{2,1,0:T(8,128)(2,1)S(1)}, u32[]{:S(2)}, u32[]{:S(2)}) collective-permute-start(bf16[2,144,1152]{2,1,0:T(8,128)(2,1)S(1)} %collective-permute-done.11), channel_id=1, source_target_pairs={{24,16},{16,8},{8,0},{0,4},{4,12},{12,20},{20,28},{28,24},{25,17},... | collective-permute-start | bytes 1990664 | tf_op jit(solution)/shard_map/ppermute | solution.py:508
  234.5 28.1 %collective-permute-start.5 = (bf16[2,144,1152]{2,1,0:T(8,128)(2,1)S(1)}, bf16[2,144,1152]{2,1,0:T(8,128)(2,1)S(1)}, u32[]{:S(2)}, u32[]{:S(2)}) collective-permute-start(bf16[2,144,1152]{2,1,0:T(8,128)(2,1)S(1)} %collective-permute-done.4), channel_id=1, source_target_pairs={{24,16},{16,8},{8,0},{0,4},{4,12},{12,20},{20,28},{28,24},{25,17},... | collective-permute-start | bytes 1990664 | tf_op jit(solution)/shard_map/ppermute | solution.py:508
  235.2 53.4 %collective-permute-start.16 = (bf16[2,144,1152]{2,1,0:T(8,128)(2,1)S(1)}, bf16[2,144,1152]{2,1,0:T(8,128)(2,1)}, u32[]{:S(2)}, u32[]{:S(2)}) collective-permute-start(bf16[2,144,1152]{2,1,0:T(8,128)(2,1)S(1)} %collective-permute-done.15), channel_id=1, source_target_pairs={{16,24},{8,16},{0,8},{4,0},{12,4},{20,12},{28,20},{24,28},{17,25},... | collective-permute-start | bytes 1990664 | tf_op jit(solution)/shard_map/ppermute | solution.py:508
  240.5 48.6 %collective-permute-start.9 = (bf16[2,144,1152]{2,1,0:T(8,128)(2,1)S(1)}, bf16[2,144,1152]{2,1,0:T(8,128)(2,1)S(1)}, u32[]{:S(2)}, u32[]{:S(2)}) collective-permute-start(bf16[2,144,1152]{2,1,0:T(8,128)(2,1)S(1)} %collective-permute-done.8), channel_id=1, source_target_pairs={{16,24},{8,16},{0,8},{4,0},{12,4},{20,12},{28,20},{24,28},{17,25},... | collective-permute-start | bytes 1990664 | tf_op jit(solution)/shard_map/ppermute | solution.py:508
  248.4 28.5 %collective-permute-start.13 = (bf16[2,144,1152]{2,1,0:T(8,128)(2,1)S(1)}, bf16[2,144,1152]{2,1,0:T(8,128)(2,1)}, u32[]{:S(2)}, u32[]{:S(2)}) collective-permute-start(bf16[2,144,1152]{2,1,0:T(8,128)(2,1)S(1)} %collective-permute-done.12), channel_id=1, source_target_pairs={{24,16},{16,8},{8,0},{0,4},{4,12},{12,20},{20,28},{28,24},{25,17},... | collective-permute-start | bytes 1990664 | tf_op jit(solution)/shard_map/ppermute | solution.py:508
  262.6 22.1 %collective-permute-start.6 = (bf16[2,144,1152]{2,1,0:T(8,128)(2,1)S(1)}, bf16[2,144,1152]{2,1,0:T(8,128)(2,1)S(1)}, u32[]{:S(2)}, u32[]{:S(2)}) collective-permute-start(bf16[2,144,1152]{2,1,0:T(8,128)(2,1)S(1)} %collective-permute-done.5), channel_id=1, source_target_pairs={{24,16},{16,8},{8,0},{0,4},{4,12},{12,20},{20,28},{28,24},{25,17},... | collective-permute-start | bytes 1990664 | tf_op jit(solution)/shard_map/ppermute | solution.py:508
  276.9 27.7 %collective-permute-start.2 = (f32[2,288,512]{2,1,0:T(8,128)}, f32[2,288,512]{2,1,0:T(8,128)}, u32[]{:S(2)}, u32[]{:S(2)}) collective-permute-start(f32[2,288,512]{2,1,0:T(8,128)} %slice_add_fusion.2), channel_id=1, source_target_pairs={{0,1},{1,0},{2,3},{3,2},{4,5},{5,4},{6,7},{7,6},{8,9},{9,8},{10,11... | collective-permute-start | bytes 3538952 | tf_op jit(solution)/shard_map/ppermute | solution.py:511
  284.7 22.9 %collective-permute-start.22 = (f32[2,288,512]{2,1,0:T(8,128)}, f32[2,288,512]{2,1,0:T(8,128)}, u32[]{:S(2)}, u32[]{:S(2)}) collective-permute-start(f32[2,288,512]{2,1,0:T(8,128)} %slice_add_fusion.1), channel_id=1, source_target_pairs={{0,1},{1,0},{2,3},{3,2},{4,5},{5,4},{6,7},{7,6},{8,9},{9,8},{10,11... | collective-permute-start | bytes 3538952 | tf_op jit(solution)/shard_map/ppermute | solution.py:511
  288.6 22.1 %collective-permute-start.27 = (f32[2,288,512]{2,1,0:T(8,128)}, f32[2,288,512]{2,1,0:T(8,128)}, u32[]{:S(2)}, u32[]{:S(2)}) collective-permute-start(f32[2,288,512]{2,1,0:T(8,128)} %slice_add_fusion), channel_id=1, source_target_pairs={{0,1},{1,0},{2,3},{3,2},{4,5},{5,4},{6,7},{7,6},{8,9},{9,8},{10,11... | collective-permute-start | bytes 3538952 | tf_op jit(solution)/shard_map/ppermute | solution.py:511
  289.1 35.6 %collective-permute-start.17 = (bf16[2,144,1152]{2,1,0:T(8,128)(2,1)}, bf16[2,144,1152]{2,1,0:T(8,128)(2,1)}, u32[]{:S(2)}, u32[]{:S(2)}) collective-permute-start(bf16[2,144,1152]{2,1,0:T(8,128)(2,1)} %collective-permute-done.16), channel_id=1, source_target_pairs={{16,24},{8,16},{0,8},{4,0},{12,4},{20,12},{28,20},{24,28},{17,25},... | collective-permute-start | bytes 1990664 | tf_op jit(solution)/shard_map/ppermute | solution.py:508
  295.2 24.0 %collective-permute-start.14 = (bf16[2,144,1152]{2,1,0:T(8,128)(2,1)}, bf16[2,144,1152]{2,1,0:T(8,128)(2,1)}, u32[]{:S(2)}, u32[]{:S(2)}) collective-permute-start(bf16[2,144,1152]{2,1,0:T(8,128)(2,1)} %collective-permute-done.13), channel_id=1, source_target_pairs={{24,16},{16,8},{8,0},{0,4},{4,12},{12,20},{20,28},{28,24},{25,17},... | collective-permute-start | bytes 1990664 | tf_op jit(solution)/shard_map/ppermute | solution.py:508
  369.2 72.5 %collective-permute-start.28 = (bf16[2,288,512]{2,1,0:T(8,128)(2,1)}, bf16[2,288,512]{2,1,0:T(8,128)(2,1)S(1)}, u32[]{:S(2)}, u32[]{:S(2)}) collective-permute-start(bf16[2,288,512]{2,1,0:T(8,128)(2,1)} %fusion.151), channel_id=1, source_target_pairs={{0,1},{1,0},{2,3},{3,2},{4,5},{5,4},{6,7},{7,6},{8,9},{9,8},{10,11... | collective-permute-start | bytes 1769480 | tf_op jit(solution)/shard_map/ppermute | solution.py:511
  370.1 71.7 %collective-permute-start.18 = (bf16[2,288,512]{2,1,0:T(8,128)(2,1)}, bf16[2,288,512]{2,1,0:T(8,128)(2,1)}, u32[]{:S(2)}, u32[]{:S(2)}) collective-permute-start(bf16[2,288,512]{2,1,0:T(8,128)(2,1)} %fusion.149), channel_id=1, source_target_pairs={{0,1},{1,0},{2,3},{3,2},{4,5},{5,4},{6,7},{7,6},{8,9},{9,8},{10,11... | collective-permute-start | bytes 1769480 | tf_op jit(solution)/shard_map/ppermute | solution.py:511
  379.2 62.6 %collective-permute-start.23 = (bf16[2,288,512]{2,1,0:T(8,128)(2,1)}, bf16[2,288,512]{2,1,0:T(8,128)(2,1)}, u32[]{:S(2)}, u32[]{:S(2)}) collective-permute-start(bf16[2,288,512]{2,1,0:T(8,128)(2,1)} %fusion.150), channel_id=1, source_target_pairs={{0,1},{1,0},{2,3},{3,2},{4,5},{5,4},{6,7},{7,6},{8,9},{9,8},{10,11... | collective-permute-start | bytes 1769480 | tf_op jit(solution)/shard_map/ppermute | solution.py:511
  391.2 86.3 %collective-permute-start.50 = (bf16[1152,512]{1,0:T(8,128)(2,1)}, bf16[1152,512]{1,0:T(8,128)(2,1)}, u32[]{:S(2)}, u32[]{:S(2)}) collective-permute-start(bf16[1152,512]{1,0:T(8,128)(2,1)} %get-tuple-element.345), channel_id=1, source_target_pairs={{0,1},{1,0},{2,3},{3,2},{4,5},{5,4},{6,7},{7,6},{8,9},{9,8},{10,11... | collective-permute-start | bytes 3538952 | tf_op jit(solution)/shard_map/ppermute | solution.py:511
  404.3 74.5 %collective-permute-start.41 = (bf16[1152,512]{1,0:T(8,128)(2,1)}, bf16[1152,512]{1,0:T(8,128)(2,1)}, u32[]{:S(2)}, u32[]{:S(2)}) collective-permute-start(bf16[1152,512]{1,0:T(8,128)(2,1)} %get-tuple-element.349), channel_id=1, source_target_pairs={{0,1},{1,0},{2,3},{3,2},{4,5},{5,4},{6,7},{7,6},{8,9},{9,8},{10,11... | collective-permute-start | bytes 3538952 | tf_op jit(solution)/shard_map/ppermute | solution.py:511
  453.5 9.9 %collective-permute-start.29 = (bf16[288,512]{1,0:T(8,128)(2,1)S(1)}, bf16[288,512]{1,0:T(8,128)(2,1)S(1)}, u32[]{:S(2)}, u32[]{:S(2)}) collective-permute-start(bf16[288,512]{1,0:T(8,128)(2,1)S(1)} %get-tuple-element.261), channel_id=1, source_target_pairs={{0,2},{1,3},{2,0},{3,1},{4,6},{5,7},{6,4},{7,5},{8,10},{9,11},{10,... | collective-permute-start | bytes 884744 | tf_op jit(solution)/shard_map/ppermute | solution.py:511
  453.9 15.8 %collective-permute-start.24 = (bf16[288,512]{1,0:T(8,128)(2,1)S(1)}, bf16[288,512]{1,0:T(8,128)(2,1)S(1)}, u32[]{:S(2)}, u32[]{:S(2)}) collective-permute-start(bf16[288,512]{1,0:T(8,128)(2,1)S(1)} %get-tuple-element.257), channel_id=1, source_target_pairs={{0,2},{1,3},{2,0},{3,1},{4,6},{5,7},{6,4},{7,5},{8,10},{9,11},{10,... | collective-permute-start | bytes 884744 | tf_op jit(solution)/shard_map/ppermute | solution.py:511
  455.7 19.8 %collective-permute-start.19 = (bf16[288,512]{1,0:T(8,128)(2,1)S(1)}, bf16[288,512]{1,0:T(8,128)(2,1)S(1)}, u32[]{:S(2)}, u32[]{:S(2)}) collective-permute-start(bf16[288,512]{1,0:T(8,128)(2,1)S(1)} %get-tuple-element.253), channel_id=1, source_target_pairs={{0,2},{1,3},{2,0},{3,1},{4,6},{5,7},{6,4},{7,5},{8,10},{9,11},{10,... | collective-permute-start | bytes 884744 | tf_op jit(solution)/shard_map/ppermute | solution.py:511
  463.4 25.1 %collective-permute-start.32 = (bf16[1152,512]{1,0:T(8,128)(2,1)}, bf16[1152,512]{1,0:T(8,128)(2,1)S(1)}, u32[]{:S(2)}, u32[]{:S(2)}) collective-permute-start(bf16[1152,512]{1,0:T(8,128)(2,1)} %get-tuple-element.347), channel_id=1, source_target_pairs={{0,1},{1,0},{2,3},{3,2},{4,5},{5,4},{6,7},{7,6},{8,9},{9,8},{10,11... | collective-permute-start | bytes 3538952 | tf_op jit(solution)/shard_map/ppermute | solution.py:511
  469.7 56.1 %collective-permute-start.67 = (bf16[144,4608]{1,0:T(8,128)(2,1)}, bf16[144,4608]{1,0:T(8,128)(2,1)}, u32[]{:S(2)}, u32[]{:S(2)}) collective-permute-start(bf16[144,4608]{1,0:T(8,128)(2,1)} %get-tuple-element.184), channel_id=1, source_target_pairs={{24,16},{16,8},{8,0},{0,4},{4,12},{12,20},{20,28},{28,24},{25,17},... | collective-permute-start | bytes 3981320 | tf_op jit(solution)/shard_map/ppermute | solution.py:508
  475.6 217.3 %collective-permute-start.71 = (bf16[144,4608]{1,0:T(8,128)(2,1)}, bf16[144,4608]{1,0:T(8,128)(2,1)}, u32[]{:S(2)}, u32[]{:S(2)}) collective-permute-start(bf16[144,4608]{1,0:T(8,128)(2,1)} %get-tuple-element.185), channel_id=1, source_target_pairs={{16,24},{8,16},{0,8},{4,0},{12,4},{20,12},{28,20},{24,28},{17,25},... | collective-permute-start | bytes 3981320 | tf_op jit(solution)/shard_map/ppermute | solution.py:508
  501.6 29.2 %collective-permute-start.51 = (bf16[288,512]{1,0:T(8,128)(2,1)}, bf16[288,512]{1,0:T(8,128)(2,1)S(1)}, u32[]{:S(2)}, u32[]{:S(2)}) collective-permute-start(bf16[288,512]{1,0:T(8,128)(2,1)} %slice.1429), channel_id=1, source_target_pairs={{0,2},{1,3},{2,0},{3,1},{4,6},{5,7},{6,4},{7,5},{8,10},{9,11},{10,... | collective-permute-start | bytes 884744 | tf_op jit(solution)/shard_map/ppermute | solution.py:511
  503.3 52.0 %collective-permute-start.52 = (bf16[2,288,512]{2,1,0:T(8,128)(2,1)}, bf16[2,288,512]{2,1,0:T(8,128)(2,1)S(1)}, u32[]{:S(2)}, u32[]{:S(2)}) collective-permute-start(bf16[2,288,512]{2,1,0:T(8,128)(2,1)} %slice_bitcast_fusion.12), channel_id=1, source_target_pairs={{0,2},{1,3},{2,0},{3,1},{4,6},{5,7},{6,4},{7,5},{8,10},{9,11},{10,... | collective-permute-start | bytes 1769480 | tf_op jit(solution)/shard_map/ppermute | solution.py:511
  505.3 18.4 %collective-permute-start.59 = (f32[5196]{0:T(1024)S(1)}, f32[5196]{0:T(1024)S(1)}, u32[]{:S(2)}, u32[]{:S(2)}) collective-permute-start(f32[5196]{0:T(1024)S(1)} %concatenate.255), channel_id=1, source_target_pairs={{0,2},{1,3},{2,0},{3,1},{4,6},{5,7},{6,4},{7,5},{8,10},{9,11},{10,... | collective-permute-start | bytes 62360 | tf_op jit(solution)/shard_map/ppermute | solution.py:511
  523.7 39.6 %collective-permute-start.34 = (bf16[2,288,512]{2,1,0:T(8,128)(2,1)S(1)}, bf16[2,288,512]{2,1,0:T(8,128)(2,1)S(1)}, u32[]{:S(2)}, u32[]{:S(2)}) collective-permute-start(bf16[2,288,512]{2,1,0:T(8,128)(2,1)S(1)} %slice_bitcast_fusion.16), channel_id=1, source_target_pairs={{0,2},{1,3},{2,0},{3,1},{4,6},{5,7},{6,4},{7,5},{8,10},{9,11},{10,... | collective-permute-start | bytes 1769480 | tf_op jit(solution)/shard_map/ppermute | solution.py:511
  525.8 20.5 %collective-permute-start.42 = (bf16[288,512]{1,0:T(8,128)(2,1)}, bf16[288,512]{1,0:T(8,128)(2,1)S(1)}, u32[]{:S(2)}, u32[]{:S(2)}) collective-permute-start(bf16[288,512]{1,0:T(8,128)(2,1)} %slice.1430), channel_id=1, source_target_pairs={{0,2},{1,3},{2,0},{3,1},{4,6},{5,7},{6,4},{7,5},{8,10},{9,11},{10,... | collective-permute-start | bytes 884744 | tf_op jit(solution)/shard_map/ppermute | solution.py:511
  530.8 21.9 %collective-permute-start.33 = (bf16[288,512]{1,0:T(8,128)(2,1)S(1)}, bf16[288,512]{1,0:T(8,128)(2,1)S(1)}, u32[]{:S(2)}, u32[]{:S(2)}) collective-permute-start(bf16[288,512]{1,0:T(8,128)(2,1)S(1)} %copy-done.120), channel_id=1, source_target_pairs={{0,2},{1,3},{2,0},{3,1},{4,6},{5,7},{6,4},{7,5},{8,10},{9,11},{10,... | collective-permute-start | bytes 884744 | tf_op jit(solution)/shard_map/ppermute | solution.py:511
  546.3 16.8 %collective-permute-start.43 = (bf16[2,288,512]{2,1,0:T(8,128)(2,1)S(1)}, bf16[2,288,512]{2,1,0:T(8,128)(2,1)S(1)}, u32[]{:S(2)}, u32[]{:S(2)}) collective-permute-start(bf16[2,288,512]{2,1,0:T(8,128)(2,1)S(1)} %slice_bitcast_fusion.14), channel_id=1, source_target_pairs={{0,2},{1,3},{2,0},{3,1},{4,6},{5,7},{6,4},{7,5},{8,10},{9,11},{10,... | collective-permute-start | bytes 1769480 | tf_op jit(solution)/shard_map/ppermute | solution.py:511
  552.6 121.6 %collective-permute-start.68 = (bf16[144,4608]{1,0:T(8,128)(2,1)}, bf16[144,4608]{1,0:T(8,128)(2,1)}, u32[]{:S(2)}, u32[]{:S(2)}) collective-permute-start(bf16[144,4608]{1,0:T(8,128)(2,1)} %fusion.41), channel_id=1, source_target_pairs={{24,16},{16,8},{8,0},{0,4},{4,12},{12,20},{20,28},{28,24},{25,17},... | collective-permute-start | bytes 3981320 | tf_op jit(solution)/shard_map/ppermute | solution.py:508
  555.4 8.7 collective-permute-start.53
  563.5 33.8 %collective-permute-start.35 = (bf16[2,288,512]{2,1,0:T(8,128)(2,1)S(1)}, bf16[2,288,512]{2,1,0:T(8,128)(2,1)S(1)}, u32[]{:S(2)}, u32[]{:S(2)}) collective-permute-start(bf16[2,288,512]{2,1,0:T(8,128)(2,1)S(1)} %get-tuple-element.245), channel_id=1, source_target_pairs={{0,1},{1,0},{2,3},{3,2},{4,5},{5,4},{6,7},{7,6},{8,9},{9,8},{10,11... | collective-permute-start | bytes 1769480 | tf_op jit(solution)/shard_map/ppermute | solution.py:511
  618.4 64.2 %collective-permute-start.54 = (bf16[2,288,1024]{2,1,0:T(8,128)(2,1)}, bf16[2,288,1024]{2,1,0:T(8,128)(2,1)}, u32[]{:S(2)}, u32[]{:S(2)}) collective-permute-start(bf16[2,288,1024]{2,1,0:T(8,128)(2,1)} %fusion.122), channel_id=1, source_target_pairs={{0,1},{1,0},{2,3},{3,2},{4,5},{5,4},{6,7},{7,6},{8,9},{9,8},{10,11... | collective-permute-start | bytes 3538952 | tf_op jit(solution)/shard_map/ppermute | solution.py:511
  640.1 14.9 %collective-permute-start.60 = (bf16[144,320]{1,0:T(8,128)(2,1)S(1)}, bf16[144,320]{1,0:T(8,128)(2,1)S(1)}, u32[]{:S(2)}, u32[]{:S(2)}) collective-permute-start(bf16[144,320]{1,0:T(8,128)(2,1)S(1)} %get-tuple-element.210), channel_id=1, source_target_pairs={{24,16},{16,8},{8,0},{0,4},{4,12},{12,20},{20,28},{28,24},{25,17},... | collective-permute-start | bytes 276488 | tf_op jit(solution)/shard_map/ppermute | solution.py:508
  641.6 20.1 %collective-permute-start.64 = (bf16[144,320]{1,0:T(8,128)(2,1)S(1)}, bf16[144,320]{1,0:T(8,128)(2,1)S(1)}, u32[]{:S(2)}, u32[]{:S(2)}) collective-permute-start(bf16[144,320]{1,0:T(8,128)(2,1)S(1)} %get-tuple-element.211), channel_id=1, source_target_pairs={{16,24},{8,16},{0,8},{4,0},{12,4},{20,12},{28,20},{24,28},{17,25},... | collective-permute-start | bytes 276488 | tf_op jit(solution)/shard_map/ppermute | solution.py:508
  661.7 23.7 %collective-permute-start.36 = (bf16[2,288,1024]{2,1,0:T(8,128)(2,1)S(1)}, bf16[2,288,1024]{2,1,0:T(8,128)(2,1)}, u32[]{:S(2)}, u32[]{:S(2)}) collective-permute-start(bf16[2,288,1024]{2,1,0:T(8,128)(2,1)S(1)} %copy-done.110), channel_id=1, source_target_pairs={{0,1},{1,0},{2,3},{3,2},{4,5},{5,4},{6,7},{7,6},{8,9},{9,8},{10,11... | collective-permute-start | bytes 3538952 | tf_op jit(solution)/shard_map/ppermute | solution.py:511
  664.9 6.9 collective-permute-start.65
  678.3 11.5 %collective-permute-start.45 = (bf16[2,288,1024]{2,1,0:T(8,128)(2,1)}, bf16[2,288,1024]{2,1,0:T(8,128)(2,1)}, u32[]{:S(2)}, u32[]{:S(2)}) collective-permute-start(bf16[2,288,1024]{2,1,0:T(8,128)(2,1)} %fusion.121), channel_id=1, source_target_pairs={{0,1},{1,0},{2,3},{3,2},{4,5},{5,4},{6,7},{7,6},{8,9},{9,8},{10,11... | collective-permute-start | bytes 3538952 | tf_op jit(solution)/shard_map/ppermute | solution.py:511
  679.0 31.2 %collective-permute-start.69 = (bf16[144,4608]{1,0:T(8,128)(2,1)}, bf16[144,4608]{1,0:T(8,128)(2,1)}, u32[]{:S(2)}, u32[]{:S(2)}) collective-permute-start(bf16[144,4608]{1,0:T(8,128)(2,1)} %fusion.42), channel_id=1, source_target_pairs={{24,16},{16,8},{8,0},{0,4},{4,12},{12,20},{20,28},{28,24},{25,17},... | collective-permute-start | bytes 3981320 | tf_op jit(solution)/shard_map/ppermute | solution.py:508
  685.0 33.1 %collective-permute-start.55 = (bf16[288,1024]{1,0:T(8,128)(2,1)S(1)}, bf16[288,1024]{1,0:T(8,128)(2,1)S(1)}, u32[]{:S(2)}, u32[]{:S(2)}) collective-permute-start(bf16[288,1024]{1,0:T(8,128)(2,1)S(1)} %fusion.148), channel_id=1, source_target_pairs={{0,2},{1,3},{2,0},{3,1},{4,6},{5,7},{6,4},{7,5},{8,10},{9,11},{10,... | collective-permute-start | bytes 1769480 | tf_op jit(solution)/shard_map/ppermute | solution.py:511
  688.9 29.0 %collective-permute-start.37 = (bf16[288,1024]{1,0:T(8,128)(2,1)S(1)}, bf16[288,1024]{1,0:T(8,128)(2,1)S(1)}, u32[]{:S(2)}, u32[]{:S(2)}) collective-permute-start(bf16[288,1024]{1,0:T(8,128)(2,1)S(1)} %fusion.146), channel_id=1, source_target_pairs={{0,2},{1,3},{2,0},{3,1},{4,6},{5,7},{6,4},{7,5},{8,10},{9,11},{10,... | collective-permute-start | bytes 1769480 | tf_op jit(solution)/shard_map/ppermute | solution.py:511
  691.6 33.5 %collective-permute-start.46 = (bf16[288,1024]{1,0:T(8,128)(2,1)S(1)}, bf16[288,1024]{1,0:T(8,128)(2,1)S(1)}, u32[]{:S(2)}, u32[]{:S(2)}) collective-permute-start(bf16[288,1024]{1,0:T(8,128)(2,1)S(1)} %fusion.147), channel_id=1, source_target_pairs={{0,2},{1,3},{2,0},{3,1},{4,6},{5,7},{6,4},{7,5},{8,10},{9,11},{10,... | collective-permute-start | bytes 1769480 | tf_op jit(solution)/shard_map/ppermute | solution.py:511
  715.7 90.3 %collective-permute-start.72 = (bf16[144,4608]{1,0:T(8,128)(2,1)}, bf16[144,4608]{1,0:T(8,128)(2,1)}, u32[]{:S(2)}, u32[]{:S(2)}) collective-permute-start(bf16[144,4608]{1,0:T(8,128)(2,1)} %get-tuple-element.183), channel_id=1, source_target_pairs={{16,24},{8,16},{0,8},{4,0},{12,4},{20,12},{28,20},{24,28},{17,25},... | collective-permute-start | bytes 3981320 | tf_op jit(solution)/shard_map/ppermute | solution.py:508
  717.4 97.9 %collective-permute-start.70 = (bf16[144,4608]{1,0:T(8,128)(2,1)}, bf16[144,4608]{1,0:T(8,128)(2,1)}, u32[]{:S(2)}, u32[]{:S(2)}) collective-permute-start(bf16[144,4608]{1,0:T(8,128)(2,1)} %get-tuple-element.182), channel_id=1, source_target_pairs={{24,16},{16,8},{8,0},{0,4},{4,12},{12,20},{20,28},{28,24},{25,17},... | collective-permute-start | bytes 3981320 | tf_op jit(solution)/shard_map/ppermute | solution.py:508
  729.1 70.9 %collective-permute-start.57 = (f32[2,1024]{1,0:T(2,128)S(1)}, f32[2,1024]{1,0:T(2,128)S(1)}, u32[]{:S(2)}, u32[]{:S(2)}) collective-permute-start(f32[2,1024]{1,0:T(2,128)S(1)} %pad_maximum_fusion.36), channel_id=1, source_target_pairs={{0,2},{1,3},{2,0},{3,1},{4,6},{5,7},{6,4},{7,5},{8,10},{9,11},{10,... | collective-permute-start | bytes 24584 | tf_op jit(solution)/shard_map/ppermute | solution.py:511
  729.5 70.8 %collective-permute-start.58 = (f32[2,1024]{1,0:T(2,128)S(1)}, f32[2,1024]{1,0:T(2,128)S(1)}, u32[]{:S(2)}, u32[]{:S(2)}) collective-permute-start(f32[2,1024]{1,0:T(2,128)S(1)} %pad_maximum_fusion.36), channel_id=1, source_target_pairs={{0,3},{1,2},{2,1},{3,0},{4,7},{5,6},{6,5},{7,4},{8,11},{9,10},{10,... | collective-permute-start | bytes 24584 | tf_op jit(solution)/shard_map/ppermute | solution.py:511
  729.5 70.8 %collective-permute-start.56 = (f32[2,1024]{1,0:T(2,128)S(1)}, f32[2,1024]{1,0:T(2,128)S(1)}, u32[]{:S(2)}, u32[]{:S(2)}) collective-permute-start(f32[2,1024]{1,0:T(2,128)S(1)} %pad_maximum_fusion.36), channel_id=1, source_target_pairs={{0,1},{1,0},{2,3},{3,2},{4,5},{5,4},{6,7},{7,6},{8,9},{9,8},{10,11... | collective-permute-start | bytes 24584 | tf_op jit(solution)/shard_map/ppermute | solution.py:511
  808.5 33.7 %collective-permute-start.73 = (bf16[144,4608]{1,0:T(8,128)(2,1)S(1)}, bf16[144,4608]{1,0:T(8,128)(2,1)S(1)}, u32[]{:S(2)}, u32[]{:S(2)}) collective-permute-start(bf16[144,4608]{1,0:T(8,128)(2,1)S(1)} %fusion.40), channel_id=1, source_target_pairs={{16,24},{8,16},{0,8},{4,0},{12,4},{20,12},{28,20},{24,28},{17,25},... | collective-permute-start | bytes 3981320 | tf_op jit(solution)/shard_map/ppermute | solution.py:508
  851.6 16.4 %collective-permute-start.74 = (bf16[144,2,1152]{2,1,0:T(2,128)(2,1)S(1)}, bf16[144,2,1152]{2,1,0:T(2,128)(2,1)S(1)}, u32[]{:S(2)}, u32[]{:S(2)}) collective-permute-start(bf16[144,2,1152]{2,1,0:T(2,128)(2,1)S(1)} %copy.312), channel_id=1, source_target_pairs={{0,2},{1,3},{2,0},{3,1},{4,6},{5,7},{6,4},{7,5},{8,10},{9,11},{10,... | collective-permute-start | bytes 1990664 | tf_op jit(solution)/shard_map/ppermute | solution.py:511
  (206 other events, 2445.2 us)

commit v3 on v2

--- a/solution.py
+++ b/solution.py
@@ -35,98 +35,6 @@
     freq_rates = jnp.exp(-math.log(10000.0) * indices / half_width)
     angles = timesteps.astype(f32)[:, None] * freq_rates[None, :]
     return jnp.concatenate([jnp.cos(angles), jnp.sin(angles)], axis=1)
-
-
-def attn_fwd_kernel(gate_ref, q_ref, k_ref, v_ref, mixed_ref, concat_ref, lse_ref):
-    gate = gate_ref[pl.program_id(0)]
-    keys = k_ref[0].T
-    s = jnp.dot(keys, q_ref[0], preferred_element_type=f32)
-    top = jnp.max(s, axis=0, keepdims=True)
-    p = jnp.exp2((s - top) * SCALE2).astype(bf16)
-    out = jnp.dot(v_ref[0], p, preferred_element_type=f32)
-    total = out[HD : HD + 1]
-    mixed = out * (1.0 / total)
-    mixed_ref[0] = mixed
-    concat_ref[0] = (mixed * gate).astype(bf16)
-    lse_ref[0] = top * SCALE2 + jnp.log2(total)
-
-
-def attn_fwd(gate, qkv):
-    heads = gate.shape[0]
-    spec = pl.BlockSpec((1, HP, LEN), lambda i: (i, 0, 0))
-    row = pl.BlockSpec((1, 1, LEN), lambda i: (i, 0, 0))
-    return pl.pallas_call(
-        attn_fwd_kernel,
-        grid=(heads,),
-        in_specs=[pl.BlockSpec(memory_space=pltpu.SMEM)]
-        + [pl.BlockSpec((1, HP, LEN), lambda i, k=k: (i + k * heads, 0, 0)) for k in range(3)],
-        out_specs=[spec, spec, row],
-        out_shape=[
-            jax.ShapeDtypeStruct((heads, HP, LEN), f32),
-            jax.ShapeDtypeStruct((heads, HP, LEN), bf16),
-            jax.ShapeDtypeStruct((heads, 1, LEN), f32),
-        ],
-        compiler_params=pltpu.CompilerParams(vmem_limit_bytes=48 * 2**20),
-        cost_estimate=pl.CostEstimate(
-            flops=heads * 4 * LEN * LEN * 256,
-            bytes_accessed=heads * HP * LEN * 14,
-            transcendentals=heads * LEN * LEN,
-        ),
-        name="attn_fwd",
-    )(gate, qkv, qkv, qkv)
-
-
-def attn_bwd_kernel(
-    chunk, gate_ref, q_ref, k_ref, v_ref, gc_ref, mixed_ref, lse_ref, dq_ref, dk_ref, dv_ref, hg_ref
-):
-    gate = gate_ref[pl.program_id(0)]
-    keys_t = k_ref[0]
-    keys = keys_t.T
-    values = v_ref[0].T
-    gc = gc_ref[0]
-    inner = jnp.sum(mixed_ref[0] * gc, axis=0, keepdims=True)
-    hg_ref[0] = inner
-    delta = gate * inner
-    grad = (gate * gc).astype(bf16)
-    dv = jnp.zeros((LEN, HP), f32)
-    dk = jnp.zeros((LEN, HP), f32)
-    for j in range(LEN // chunk):
-        part = slice(j * chunk, (j + 1) * chunk)
-        q = q_ref[0, :, part]
-        do = grad[:, part]
-        s = jnp.dot(keys, q, preferred_element_type=f32)
-        p = jnp.exp2(s * SCALE2 - lse_ref[0, :, part])
-        dp = jnp.dot(values, do, preferred_element_type=f32)
-        ds = (p * (dp - delta[:, part])).astype(bf16)
-        dv = dv + jnp.dot(p.astype(bf16), do.T, preferred_element_type=f32)
-        dk = dk + jnp.dot(ds, q.T, preferred_element_type=f32)
-        dq = jnp.dot(keys_t, ds, preferred_element_type=f32)
-        dq_ref[0, :, part] = (dq * SCALE).astype(bf16)
-    dk_ref[0] = (dk * SCALE).T.astype(bf16)
-    dv_ref[0] = dv.T.astype(bf16)
-
-
-def attn_bwd(gate, qkv, gc, mixed, lse):
-    heads = gate.shape[0]
-    spec = pl.BlockSpec((1, HP, LEN), lambda i: (i, 0, 0))
-    row = pl.BlockSpec((1, 1, LEN), lambda i: (i, 0, 0))
-    grads = jax.ShapeDtypeStruct((heads, HP, LEN), bf16)
-    return pl.pallas_call(
-        functools.partial(attn_bwd_kernel, 256),
-        grid=(heads,),
-        in_specs=[pl.BlockSpec(memory_space=pltpu.SMEM)]
-        + [pl.BlockSpec((1, HP, LEN), lambda i, k=k: (i + k * heads, 0, 0)) for k in range(3)]
-        + [spec, spec, row],
-        out_specs=[spec, spec, spec, row],
-        out_shape=[grads, grads, grads, jax.ShapeDtypeStruct((heads, 1, LEN), f32)],
-        compiler_params=pltpu.CompilerParams(vmem_limit_bytes=48 * 2**20),
-        cost_estimate=pl.CostEstimate(
-            flops=heads * 10 * LEN * LEN * 256,
-            bytes_accessed=heads * HP * LEN * 20,
-            transcendentals=heads * LEN * LEN,
-        ),
-        name="attn_bwd",
-    )(gate, qkv, qkv, qkv, gc, mixed, lse)
 
 
 MESH = pl.DeviceIdType.MESH
@@ -358,19 +266,27 @@
     )(x, w, msg, ada, gates, bias, mask)
 
 
-def tail_kernel(
-    NT, NP, g_ref, last_ref, ada_ref,
-    out_ref, lasts_ref, cond_ref,
-    part_ref, sum_ref, send_ref, recv_ref, r_send, r_recv, s_send, s_recv,
+def fwd_kernel(
+    NT, NP, gate_ref, rows_ref, w_ref, mod_ref, bias_ref, late_ref,
+    attn_ref, qkv_ref, mixed_ref, concat_ref, lse_ref, stats_ref, branch_ref, full_ref,
+    wt_ref, own_ref, core_out, core_in, x_out, x_in, total_ref,
+    l_send, l_recv, c_send, c_recv, x_send, x_recv, b_send, b_recv, local_sem,
 ):
-    SUB = NT // NP
+    NX, SUB = NP // 2, NT // NP
+    I, CB, T = total_ref.shape[0], total_ref.shape[2], total_ref.shape[3]
+    HL = gate_ref.shape[0] // I
+    QKV = 3 * HL * HP
+    steps = HL + 2
+    i, s = pl.program_id(0), pl.program_id(1)
+    flat = i * steps + s
     t, p = lax.axis_index("tok"), lax.axis_index("tp")
     ring = Ring(NT)
     q = ring.place(t)
     right, left = (ring.tok(q + 1), p), (ring.tok(q - 1), p)
-    WN = g_ref.shape[2]
-    half = (WN // 2 + 127) // 128 * 128
-    cols = (slice(0, half), slice(half, WN))
+    core = (t, xor(p, 1))
+
+    def at(n):
+        return pl.when(flat == n)
 
     def where(tt):
         out = 0
@@ -378,117 +294,807 @@
             out = out + jnp.where(p == r, xor(tt // SUB, r), 0)
         return out * SUB + tt % SUB
 
-    greet(t, p, NT, NP)
-    lasts = []
-    for k in range(1, NT):
-        peer = (t + k) % NT
-        cp = copy_to(last_ref, lasts_ref.at[k], s_send.at[0, k], s_recv.at[0, k], (peer, p))
-        cp.start()
-        lasts.append(cp)
-    lasts_ref[0] = last_ref[...]
-
-    chains = []
-    for side in range(2):
-        for s in range(2):
-            chains.append((side, s, NT // 2 if side == s else NT // 2 - 1))
-    flying = {}
-
-    def step(h):
-        for n, (side, s, count) in enumerate(chains):
-            if h >= count:
-                continue
-            d = count - h
-            block = where(ring.tok(q + d if side == 0 else q - d))
-            width = cols[s].stop - cols[s].start
-            v = g_ref[block, :, cols[s]]
-            if h:
-                flying[n, h - 1].wait_recv()
-                v = v + recv_ref[n, h - 1, :, :width].astype(f32)
-            send_ref[n, h, :, :width] = v.astype(bf16)
-            cp = copy_to(
-                send_ref.at[n, h], recv_ref.at[n, h], r_send.at[n, h], r_recv.at[n, h],
-                right if side == 0 else left,
+    def hop(k, d, side):
+        block = where(ring.tok(q - (d - 1) if side == 0 else q + (d - 1)))
+        dst = full_ref.at[k, :, block]
+        src = late_ref.at[k] if d == 1 else dst
+        if d == NT // 2:
+            src, dst = src.at[side], dst.at[side]
+        return copy_to(src, dst, l_send.at[k, side, d], l_recv.at[k, side, d], left if side else right)
+
+    def keep(k):
+        return pltpu.make_async_copy(late_ref.at[k], full_ref.at[k, :, where(t)], local_sem.at[k])
+
+    def start_hop(k, d):
+        for side in range(2):
+            hop(k, d, side).start()
+
+    def land_hop(k, d):
+        for side in range(2):
+            hop(k, d, side).wait_recv()
+        if d < NT // 2:
+            start_hop(k, d + 1)
+
+    def core_copy(i):
+        return copy_to(core_out.at[i], core_in.at[i], c_send.at[i], c_recv.at[i], core)
+
+    def x_copy(i, k):
+        return copy_to(
+            x_out.at[i, k], x_in.at[i, k], x_send.at[i, k], x_recv.at[i, k], (t, xor(p, 2 * k))
+        )
+
+    def back_copy(i):
+        return copy_to(total_ref.at[i], branch_ref.at[i, 1], b_send.at[i], b_recv.at[i], core)
+
+    def back_keep(i):
+        return pltpu.make_async_copy(total_ref.at[i], branch_ref.at[i, 0], local_sem.at[NX + i])
+
+    def add_core(i):
+        core_copy(i).wait_recv()
+        for f in range(NX):
+            for k in range(NX):
+                cols = slice(k * T, (k + 1) * T)
+                v = own_ref[f, :, cols] + core_in[i, f, :, cols].astype(f32)
+                if k == 0:
+                    total_ref[i, f] = v
+                else:
+                    x_out[i, k, f] = v.astype(bf16)
+        for k in range(1, NX):
+            x_copy(i, k).start()
+
+    def add_x(i):
+        for k in range(1, NX):
+            x_copy(i, k).wait_recv()
+        for f in range(NX):
+            v = total_ref[i, f]
+            for k in range(1, NX):
+                v = v + x_in[i, k, f ^ k].astype(f32)
+            total_ref[i, f] = v
+        back_copy(i).start()
+        back_keep(i).start()
+
+    @at(0)
+    def _():
+        barrier = pltpu.get_barrier_semaphore()
+        peers = [right, left, core] + [(t, xor(p, 2 * k)) for k in range(1, NX)]
+        for peer in peers:
+            pl.semaphore_signal(barrier, inc=1, device_id=peer, device_id_type=MESH)
+        pl.semaphore_wait(barrier, len(peers))
+        for k in range(NX):
+            start_hop(k, 1)
+        for k in range(NX):
+            keep(k).start()
+        wt_ref[...] = w_ref[:, :QKV].T
+
+    @pl.when(s == 0)
+    def _():
+        width = 256
+        for j in range(LEN // width):
+            cols = slice(j * width, (j + 1) * width)
+            v = rows_ref[0, :, cols].astype(f32)
+            centre = jnp.sum(v, axis=0, keepdims=True) * (1.0 / D)
+            square = jnp.sum(v * v, axis=0, keepdims=True) * (1.0 / D)
+            inverse = lax.rsqrt(square - centre * centre + EPS)
+            stats_ref[0, 0:1, cols] = centre
+            stats_ref[0, 1:2, cols] = inverse
+            n = (v - centre) * inverse
+            a = (n * (1.0 + mod_ref[0, :, 1:2]) + mod_ref[0, :, 0:1]).astype(bf16)
+            attn_ref[0, :, cols] = a
+            out = jnp.dot(wt_ref[...], a, preferred_element_type=f32) + bias_ref[...]
+            qkv_ref[0, :, cols] = out.astype(bf16)
+
+    @pl.when((s > 0) & (s <= HL))
+    def _():
+        h = s - 1
+        gate = gate_ref[i * HL + h]
+
+        def head(k):
+            return pl.ds(pl.multiple_of((k * HL + h) * HP, HP), HP)
+
+        keys = qkv_ref[0, head(1)].T
+        sc = jnp.dot(keys, qkv_ref[0, head(0)], preferred_element_type=f32)
+        top = jnp.max(sc, axis=0, keepdims=True)
+        pr = jnp.exp2((sc - top) * SCALE2).astype(bf16)
+        out = jnp.dot(qkv_ref[0, head(2)], pr, preferred_element_type=f32)
+        total = out[HD : HD + 1]
+        mixed = out * (1.0 / total)
+        mixed_ref[0, head(0)] = mixed
+        concat_ref[0, head(0)] = (mixed * gate).astype(bf16)
+        lse_ref[0, pl.ds(h, 1)] = top * SCALE2 + jnp.log2(total)
+
+    @pl.when(s == HL + 1)
+    def _():
+        for r in range(NP):
+            w = w_ref[r * CB : (r + 1) * CB, w_ref.shape[1] - HL * HP :]
+            part = jnp.dot(w, concat_ref[0], preferred_element_type=f32)
+            if r % 2 == 0:
+                own_ref[r // 2] = part
+            else:
+                core_out[i, r // 2] = part.astype(bf16)
+        core_copy(i).start()
+
+    for n in range(I - 1):
+        at((n + 1) * steps + 1)(functools.partial(add_core, n))
+        at((n + 1) * steps + HL)(functools.partial(add_x, n))
+
+    events = [(k, d) for d in range(1, NT // 2 + 1) for k in range(NX)]
+    early = [steps + HL, 2 * steps - 1][: len(events)] if I > 1 else []
+    for n, (k, d) in zip(early, events):
+        at(n)(functools.partial(land_hop, k, d))
+
+    @at(I * steps - 1)
+    def _():
+        add_core(I - 1)
+        rest = events[len(early) :]
+        for n, (k, d) in enumerate(rest):
+            land_hop(k, d)
+            if n == 0:
+                add_x(I - 1)
+        for n in range(I):
+            back_copy(n).wait_recv()
+        for n in range(I):
+            core_copy(n).wait_send()
+            back_copy(n).wait_send()
+            back_keep(n).wait()
+            for k in range(1, NX):
+                x_copy(n, k).wait_send()
+        for k in range(NX):
+            keep(k).wait()
+            for d in range(1, NT // 2 + 1):
+                for side in range(2):
+                    hop(k, d, side).wait_send()
+
+
+def fwd_call(NT, NP, gate, rows, w, mods, bias, late):
+    I, _, length = rows.shape
+    NX = NP // 2
+    CB, T = D // NP, length // NX
+    HL = gate.shape[0] // I
+    QKV = 3 * HL * HP
+    RB, FL = late.shape[2:]
+    hbm = pl.BlockSpec(memory_space=pl.ANY)
+    dma = pltpu.SemaphoreType.DMA
+
+    def image(*shape):
+        return pl.BlockSpec((1,) + shape, lambda i, s: (i,) + (0,) * len(shape))
+
+    def whole(*shape):
+        return pl.BlockSpec(shape, lambda i, s: (0,) * len(shape))
+
+    return pl.pallas_call(
+        functools.partial(fwd_kernel, NT, NP),
+        grid=(I, HL + 2),
+        in_specs=[
+            pl.BlockSpec(memory_space=pltpu.SMEM),
+            image(D, length),
+            whole(*w.shape),
+            image(D, mods.shape[2]),
+            whole(*bias.shape),
+            hbm,
+        ],
+        out_specs=[
+            image(D, length),
+            image(QKV, length),
+            image(HL * HP, length),
+            image(HL * HP, length),
+            image(HL, length),
+            image(8, length),
+            hbm,
+            hbm,
+        ],
+        out_shape=[
+            jax.ShapeDtypeStruct((I, D, length), bf16),
+            jax.ShapeDtypeStruct((I, QKV, length), bf16),
+            jax.ShapeDtypeStruct((I, HL * HP, length), f32),
+            jax.ShapeDtypeStruct((I, HL * HP, length), bf16),
+            jax.ShapeDtypeStruct((I, HL, length), f32),
+            jax.ShapeDtypeStruct((I, 8, length), f32),
+            jax.ShapeDtypeStruct((I, 2, NX, CB, T), f32),
+            jax.ShapeDtypeStruct((NX, 2, NT, RB, FL), bf16),
+        ],
+        scratch_shapes=[
+            pltpu.VMEM((QKV, D), bf16),
+            pltpu.VMEM((NX, CB, length), f32),
+            pltpu.VMEM((I, NX, CB, length), bf16),
+            pltpu.VMEM((I, NX, CB, length), bf16),
+            pltpu.VMEM((I, NX, NX, CB, T), bf16),
+            pltpu.VMEM((I, NX, NX, CB, T), bf16),
+            pltpu.VMEM((I, NX, CB, T), f32),
+            dma((NX, 2, NT // 2 + 1)),
+            dma((NX, 2, NT // 2 + 1)),
+            dma((I,)),
+            dma((I,)),
+            dma((I, NX)),
+            dma((I, NX)),
+            dma((I,)),
+            dma((I,)),
+            dma((NX + I,)),
+        ],
+        compiler_params=pltpu.CompilerParams(
+            collective_id=2, has_side_effects=True, vmem_limit_bytes=60 * 2**20
+        ),
+        name="forward",
+    )(gate, rows, w, mods, bias, late)
+
+
+def bwd_kernel(
+    NT, NP, gate_ref, go_ref, gms_ref, gm_ref, qkv_ref, mixed_ref, lse_ref, concat_ref, attn_ref,
+    rows_ref, stats_ref, scale_ref, w_ref, late_ref, base_ref, factor_ref, ada_ref,
+    gin_ref, late_out, gqkv_ref, gout_ref, lasts_ref, cond_ref, gox_ref,
+    go_buf, gmx_ref, own_ref, core_out, core_in, x_out, x_in, gn_ref, accq_ref, acco_ref, wt_ref,
+    gc_ref, dqkv_ref, rows_buf, gin_buf, st_out, st_in, msg_ref, heads_ref, qv_ref,
+    l_own, l_out, l_in, lx_out, lx_in, q_out, q_in, part_ref, sum_ref, lasts_buf,
+    g_send, g_recv, c_send, c_recv, x_send, x_recv, t_send, t_recv, l_send, l_recv, lx_send, lx_recv,
+    q_send, q_recv, s_send, s_recv, m_send, m_recv, local_sem, own_sem,
+):
+    NX, SUB = NP // 2, NT // NP
+    I, CB, T = gm_ref.shape
+    HL = gate_ref.shape[0] // I
+    QKV, HO = 3 * HL * HP, HL * HP
+    RB = D // NT
+    HOPS = NT // 2
+    steps = HL + 2
+    i, s = pl.program_id(0), pl.program_id(1)
+    flat = i * steps + s
+    t, p = lax.axis_index("tok"), lax.axis_index("tp")
+    xi = p // 2
+    ring = Ring(NT)
+    q = ring.place(t)
+    right, left = (ring.tok(q + 1), p), (ring.tok(q - 1), p)
+    core = (t, xor(p, 1))
+
+    def at(n):
+        return pl.when(flat == n)
+
+    def partner(k):
+        return (t, xor(p, 2 * k))
+
+    def where(tt):
+        out = 0
+        for r in range(NP):
+            out = out + jnp.where(p == r, xor(tt // SUB, r), 0)
+        return out * SUB + tt % SUB
+
+    def go_x(n, k, f):
+        return copy_to(
+            go_ref.at[n, f, 0], gox_ref.at[n, k, f ^ k, 0], g_send.at[0, n, k, f],
+            g_recv.at[0, n, k, f], partner(k),
+        )
+
+    def go_core(n, k, f):
+        return copy_to(
+            gox_ref.at[n, k, f, 0], gox_ref.at[n, k, f, 1], g_send.at[1, n, k, f],
+            g_recv.at[1, n, k, f], core,
+        )
+
+    def gm_x(n, k):
+        return copy_to(gms_ref.at[n, k], gmx_ref.at[n, k - 1], m_send.at[n, k], m_recv.at[n, k], partner(k))
+
+    def send_go(n):
+        for k in range(1, NX):
+            for f in range(NX):
+                go_x(n, k, f).start()
+
+    def pass_go(n):
+        for k in range(1, NX):
+            for f in range(NX):
+                go_x(n, k, f ^ k).wait_recv()
+                go_core(n, k, f).start()
+        if n + 1 < I:
+            send_go(n + 1)
+        for m in [n - 1] if n + 1 < I else [n - 1, n]:
+            if m >= 0:
+                for k in range(1, NX):
+                    gm_x(m, k).start()
+
+    def load_go(n):
+        def load(k):
+            src = go_ref.at[n] if k == 0 else gox_ref.at[n, k]
+            return pltpu.make_async_copy(src, go_buf.at[k], local_sem.at[k])
+
+        load(0).start()
+        for k in range(1, NX):
+            for f in range(NX):
+                go_core(n, k, f).wait_recv()
+            load(k).start()
+        for k in range(NX):
+            load(k).wait()
+
+    def rows_copy(n):
+        return pltpu.make_async_copy(rows_ref.at[n, 0], rows_buf.at[n], local_sem.at[NX + n])
+
+    def core_copy(n):
+        return copy_to(core_out, core_in.at[n % 2], c_send.at[n], c_recv.at[n], core)
+
+    def x_copy(n, k):
+        return copy_to(
+            x_out.at[n % 2, k - 1], x_in.at[n % 2, k - 1], x_send.at[n, k], x_recv.at[n, k], partner(k)
+        )
+
+    def st_copy(n, r):
+        return copy_to(
+            st_out.at[n], st_in.at[n, r], t_send.at[n, r], t_recv.at[n, r], (t, xor(p, r))
+        )
+
+    def gin_copy(n, j):
+        to = pl.ds(pl.multiple_of(xor(xi, j) * T, T), T)
+        return pltpu.make_async_copy(
+            gin_buf.at[n % 2, :, pl.ds(j * T, T)], gin_ref.at[n, :, to], local_sem.at[NX + I + n * NX + j]
+        )
+
+    def add_core(n):
+        core_copy(n).wait_recv()
+        if n >= 2:
+            for k in range(1, NX):
+                x_copy(n - 2, k).wait_send()
+        for f in range(NX):
+            v = own_ref[f] + core_in[n % 2, f].astype(f32)
+            if f == 0:
+                gn_ref[...] = v
+            else:
+                x_out[n % 2, f - 1] = v.astype(bf16)
+        for k in range(1, NX):
+            x_copy(n, k).start()
+
+    def tokens(v):
+        total = v[:, :128]
+        for j in range(1, LEN // 128):
+            total = total + v[:, j * 128 : (j + 1) * 128]
+        return jnp.sum(total.T, axis=0, keepdims=True)
+
+    def normed(n):
+        return (rows_buf[n].astype(f32) - stats_ref[n, 0:1]) * stats_ref[n, 1:2]
+
+    def add_x(n):
+        for k in range(1, NX):
+            x_copy(n, k).wait_recv()
+        for j in range(NX):
+            v = gn_ref[:, j * T : (j + 1) * T]
+            for k in range(1, NX):
+                v = v + x_in[n % 2, k - 1, :, (j ^ k) * T : ((j ^ k) + 1) * T].astype(f32)
+            gn_ref[:, j * T : (j + 1) * T] = v
+        v = gn_ref[...]
+        vn = v * normed(n)
+        scale = 1.0 + scale_ref[n]
+        st_out[n, 0:1] = jnp.sum(v * scale, axis=0, keepdims=True)
+        st_out[n, 1:2] = jnp.sum(vn * scale, axis=0, keepdims=True)
+        for r in range(1, NP):
+            st_copy(n, r).start()
+        msg_ref[n : n + 1, :CB] = tokens(v)
+        msg_ref[n : n + 1, ML : ML + CB] = tokens(vn)
+
+    def add_stats(n):
+        for r in range(1, NP):
+            st_copy(n, r).wait_recv()
+        if n >= 2:
+            for j in range(NX):
+                gin_copy(n - 2, j).wait()
+        for k in range(1, NX):
+            gm_x(n, k).wait_recv()
+        for j in range(NX):
+            cols = slice(j * T, (j + 1) * T)
+            a, b = st_out[n, 0:1, cols], st_out[n, 1:2, cols]
+            for r in range(1, NP):
+                m = j ^ (r // 2)
+                a = a + st_in[n, r, 0:1, m * T : (m + 1) * T]
+                b = b + st_in[n, r, 1:2, m * T : (m + 1) * T]
+            centre, inverse = stats_ref[n, 0:1, cols], stats_ref[n, 1:2, cols]
+            nrm = (rows_buf[n, :, cols].astype(f32) - centre) * inverse
+            g = gn_ref[:, cols] * (1.0 + scale_ref[n])
+            mid = gm_ref[n] if j == 0 else gmx_ref[n, j - 1].astype(f32)
+            gin_buf[n % 2, :, cols] = mid + inverse * (g - a * (1.0 / D) - nrm * (b * (1.0 / D)))
+        for j in range(NX):
+            gin_copy(n, j).start()
+
+    def l_block(side, h):
+        d = HOPS - h
+        return where(ring.tok(q + d if side == 0 else q - d))
+
+    def l_load(k, side, h):
+        return pltpu.make_async_copy(
+            late_ref.at[k, :, l_block(side, h)], l_own.at[k, side], own_sem.at[k, side]
+        )
+
+    def l_hop(k, side, h):
+        to = left if side else right
+        if h == 0:
+            return copy_to(
+                late_ref.at[k, side, l_block(side, 0)], l_in.at[k, side, 0, side],
+                l_send.at[k, side, h], l_recv.at[k, side, h], to,
             )
-            cp.start()
-            flying[n, h] = cp
-
-    step(0)
-    for cp in lasts:
-        cp.wait_recv()
-    grads = lasts_ref[...].reshape(NT * 8, -1)
-    total = 0.0
-    for k in range(6):
-        g = grads[:, k * ML : (k + 1) * ML]
-        high = g.astype(bf16)
-        low = (g - high.astype(f32)).astype(bf16)
-        w = ada_ref[k]
-        total = total + dot(high, w, 1, 1) + dot(low, w, 1, 1)
-    part_ref[:, :, : total.shape[1]] = total.reshape(NT, 8, -1)
-    parts = []
-    for k in range(1, NT):
-        peer = (t + NT - k) % NT
-        cp = copy_to(part_ref.at[k], sum_ref.at[0, t], s_send.at[1, k], s_recv.at[1, k], (peer, p))
-        cp.start()
-        parts.append(cp)
-    sum_ref[0, t] = part_ref[0]
-    step(1)
-    for cp in parts:
-        cp.wait_recv()
-    sums = []
-    for r in range(1, NP):
-        cp = copy_to(sum_ref.at[0], sum_ref.at[r], s_send.at[2, r], s_recv.at[2, r], (t, xor(p, r)))
-        cp.start()
-        sums.append(cp)
-    for h in range(2, NT // 2):
-        step(h)
-    for cp in sums:
-        cp.wait_recv()
-    total = sum_ref[0]
-    for r in range(1, NP):
-        total = total + sum_ref[r]
-    cond_ref[...] = total
-    mine = where(t)
-    for s in range(2):
-        v = g_ref[mine, :, cols[s]]
-        for n, (side, ss, count) in enumerate(chains):
-            if ss == s:
-                flying[n, count - 1].wait_recv()
-                v = v + recv_ref[n, count - 1, :, : cols[s].stop - cols[s].start].astype(f32)
-        out_ref[:, cols[s]] = v
-    for cp in lasts + parts + sums + list(flying.values()):
-        cp.wait_send()
-
-
-def tail_call(NT, NP, g, last, ada):
-    _, RB, WN = g.shape
-    half = (WN // 2 + 127) // 128 * 128
+        return copy_to(
+            l_out.at[k, side], l_in.at[k, side, h % 2], l_send.at[k, side, h], l_recv.at[k, side, h], to
+        )
+
+    def l_event(k, h):
+        for side in range(2):
+            l_hop(k, side, h - 1).wait_recv()
+        for side in range(2):
+            if h < HOPS or side == 0:
+                l_load(k, side, h).wait()
+            if 1 < h < HOPS:
+                l_hop(k, side, h - 1).wait_send()
+        if h < HOPS:
+            for side in range(2):
+                for u in range(2):
+                    v = l_own[k, side, u]
+                    if h > 1 or u == side:
+                        v = (v.astype(f32) + l_in[k, side, (h - 1) % 2, u].astype(f32)).astype(bf16)
+                    l_out[k, side, u] = v
+            for side in range(2):
+                l_hop(k, side, h).start()
+                if h + 1 < HOPS or side == 0:
+                    l_load(k, side, h + 1).start()
+        else:
+            for u in range(2):
+                v = l_own[k, 0, u].astype(f32)
+                for side in range(2):
+                    if HOPS > 1 or u == side:
+                        v = v + l_in[k, side, (h - 1) % 2, u].astype(f32)
+                if k == 0:
+                    late_out[u] = v
+                else:
+                    lx_out[k - 1, u] = v.astype(bf16)
+            if k:
+                lx_copy(k).start()
+
+    def lx_copy(k):
+        return copy_to(lx_out.at[k - 1], lx_in.at[k - 1], lx_send.at[k], lx_recv.at[k], partner(k))
+
+    half = (QKV // 2 + 127) // 128 * 128
+
+    def q_block(side, h):
+        return l_block(side, h)
+
+    def q_hop(side, h):
+        to = left if side else right
+        return copy_to(
+            q_out.at[side], q_in.at[side, h % 2], q_send.at[side, h], q_recv.at[side, h], to
+        )
+
+    def q_event(h):
+        if h:
+            for side in range(2):
+                q_hop(side, h - 1).wait_recv()
+        if h < HOPS:
+            for side in range(2):
+                if h:
+                    q_hop(side, h - 1).wait_send()
+                block = q_block(side, h)
+                a, b = accq_ref[block], acco_ref[block]
+                if h:
+                    a = a + q_in[side, (h - 1) % 2, :, :QKV].astype(f32)
+                    b = b + q_in[side, (h - 1) % 2, :, QWIDE:].astype(f32)
+                else:
+                    lane = lax.broadcasted_iota(jnp.int32, a.shape, 1)
+                    a = jnp.where((lane < half) if side == 0 else (lane >= half), a, 0.0)
+                    b = b if side == 0 else jnp.zeros_like(b)
+                q_out[side, :, :QKV] = a.astype(bf16)
+                q_out[side, :, QWIDE:] = b.astype(bf16)
+            for side in range(2):
+                q_hop(side, h).start()
+        else:
+            a, b = accq_ref[q_block(0, h)], acco_ref[q_block(0, h)]
+            for side in range(2):
+                a = a + q_in[side, (h - 1) % 2, :, :QKV].astype(f32)
+                b = b + q_in[side, (h - 1) % 2, :, QWIDE:].astype(f32)
+            gqkv_ref[...] = a
+            gout_ref[...] = b
+
+    QWIDE = (QKV + 127) // 128 * 128
+
+    def last_copy(k):
+        return copy_to(msg_ref, lasts_buf.at[k], s_send.at[0, k], s_recv.at[0, k], ((t + k) % NT, p))
+
+    def part_copy(k):
+        return copy_to(
+            part_ref.at[k], sum_ref.at[0, t], s_send.at[1, k], s_recv.at[1, k], ((t + NT - k) % NT, p)
+        )
+
+    def sum_copy(r):
+        return copy_to(sum_ref.at[0], sum_ref.at[r], s_send.at[2, r], s_recv.at[2, r], (t, xor(p, r)))
+
+    def cond_first():
+        msg_ref[I : I + 1, :QKV] = qv_ref[0:1, :QKV]
+        msg_ref[:, 6 * ML :] = msg_ref[:, 6 * ML :] + heads_ref[...] * factor_ref[...]
+        for k in range(1, NT):
+            last_copy(k).start()
+        lasts_buf[0] = msg_ref[...]
+
+    def cond_second():
+        for k in range(1, NT):
+            last_copy(k).wait_recv()
+        lasts_ref[...] = lasts_buf[...]
+        grads = lasts_buf[...].reshape(NT * 8, -1)
+        total = 0.0
+        for k in range(6):
+            g = grads[:, k * ML : (k + 1) * ML]
+            high = g.astype(bf16)
+            low = (g - high.astype(f32)).astype(bf16)
+            total = total + dot(high, ada_ref[k], 1, 1) + dot(low, ada_ref[k], 1, 1)
+        part_ref[...] = jnp.zeros_like(part_ref)
+        part_ref[:, :, :RB] = total.reshape(NT, 8, RB)
+        for k in range(1, NT):
+            part_copy(k).start()
+        sum_ref[0, t] = part_ref[0]
+
+    def cond_third():
+        for k in range(1, NT):
+            part_copy(k).wait_recv()
+        for r in range(1, NP):
+            sum_copy(r).start()
+
+    def cond_last():
+        total = sum_ref[0]
+        for r in range(1, NP):
+            sum_copy(r).wait_recv()
+            total = total + sum_ref[r]
+        cond_ref[...] = total
+
+    @at(0)
+    def _():
+        greet(t, p, NT, NP)
+        send_go(0)
+        for k in range(NX):
+            for side in range(2):
+                l_hop(k, side, 0).start()
+                l_load(k, side, 1).start()
+        for n in range(I):
+            rows_copy(n).start()
+        msg_ref[...] = base_ref[...]
+        heads_ref[...] = jnp.zeros_like(heads_ref)
+        qv_ref[...] = jnp.zeros_like(qv_ref)
+        wt_ref[...] = w_ref[:, w_ref.shape[1] - HO :].T
+        accq_ref[...] = jnp.zeros_like(accq_ref)
+        acco_ref[...] = jnp.zeros_like(acco_ref)
+        for n in range(I):
+            rows_copy(n).wait()
+
+    for n in range(I):
+        at(max(n - 1, 0) * steps + (HL if n else 0))(functools.partial(pass_go, n))
+        at(n * steps)(functools.partial(load_go, n))
+
+    @pl.when(s == 0)
+    def _():
+        for k in range(NX):
+            v = go_buf[k].reshape(D, T)
+            gc_ref[:, k * T : (k + 1) * T] = jnp.dot(wt_ref[...], v, preferred_element_type=f32)
+
+    @pl.when((s > 0) & (s <= HL))
+    def _():
+        h = s - 1
+        gate = gate_ref[i * HL + h]
+
+        def head(k):
+            return pl.ds(pl.multiple_of((k * HL + h) * HP, HP), HP)
+
+        keys_t = qkv_ref[0, head(1)]
+        keys = keys_t.T
+        values = qkv_ref[0, head(2)].T
+        gc = gc_ref[head(0)]
+        inner = jnp.sum(mixed_ref[0, head(0)] * gc, axis=0, keepdims=True)
+        lane = lax.broadcasted_iota(jnp.int32, (1, 128), 1)
+        row = heads_ref[pl.ds(i, 1)]
+        heads_ref[pl.ds(i, 1)] = row + jnp.where(lane == h, jnp.sum(inner), 0.0)
+        delta = gate * inner
+        grad = (gate * gc).astype(bf16)
+        lse = lse_ref[0, pl.ds(h, 1)]
+        queries = qkv_ref[0, head(0)]
+        dv = jnp.zeros((LEN, HP), f32)
+        dk = jnp.zeros((LEN, HP), f32)
+        chunk = 256
+        for j in range(LEN // chunk):
+            part = slice(j * chunk, (j + 1) * chunk)
+            qj = queries[:, part]
+            do = grad[:, part]
+            sc = jnp.dot(keys, qj, preferred_element_type=f32)
+            pr = jnp.exp2(sc * SCALE2 - lse[:, part])
+            dp = jnp.dot(values, do, preferred_element_type=f32)
+            ds = (pr * (dp - delta[:, part])).astype(bf16)
+            dv = dv + jnp.dot(pr.astype(bf16), do.T, preferred_element_type=f32)
+            dk = dk + jnp.dot(ds, qj.T, preferred_element_type=f32)
+            dq = jnp.dot(keys_t, ds, preferred_element_type=f32)
+            dqkv_ref[head(0), part] = (dq * SCALE).astype(bf16)
+        dqkv_ref[head(1)] = (dk * SCALE).T.astype(bf16)
+        dqkv_ref[head(2)] = dv.T.astype(bf16)
+
+    @pl.when(s == HL + 1)
+    def _():
+        for r in range(NP):
+            w = w_ref[r * CB : (r + 1) * CB, :QKV]
+            part = jnp.dot(w, dqkv_ref[...], preferred_element_type=f32)
+            if r % 2 == 0:
+                own_ref[r // 2] = part
+            else:
+                core_out[r // 2] = part.astype(bf16)
+        for b in range(0, NT, 2):
+            rows = slice(b * RB, (b + 2) * RB)
+            v = dot(attn_ref[0, rows], dqkv_ref[...], 1, 1)
+            accq_ref[b : b + 2] = accq_ref[b : b + 2] + v.reshape(2, RB, QKV)
+            v = 0.0
+            for k in range(NX):
+                g = go_buf[k].reshape(D, T)[rows]
+                v = v + dot(g, concat_ref[0, :, k * T : (k + 1) * T], 1, 1)
+            acco_ref[b : b + 2] = acco_ref[b : b + 2] + v.reshape(2, RB, HO)
+        qv_ref[0:1, :QKV] = qv_ref[0:1, :QKV] + tokens(dqkv_ref[...].astype(f32))
+
+    for n in range(I):
+        at(n * steps + HL + 1)(lambda n=n: core_copy(n).start())
+    for n in range(I - 1):
+        at((n + 1) * steps + 1)(functools.partial(add_core, n))
+        at((n + 1) * steps + HL - 1)(functools.partial(add_x, n))
+
+        @at((n + 1) * steps + HL)
+        def _(n=n):
+            add_stats(n)
+            core_copy(n).wait_send()
+
+    events = [functools.partial(l_event, k, h) for h in range(1, HOPS + 1) for k in range(NX)]
+    early = [steps - 1, steps, 2 * steps - 2, 2 * steps - 1, 3 * steps - 2, 3 * steps - 1] if I > 2 else []
+    early = early[: len(events)]
+    for n, event in zip(early, events):
+        at(n)(event)
+
+    @at(I * steps - 1)
+    def _():
+        rest = events[len(early) :]
+        q_event(0)
+        add_core(I - 1)
+        todo = [functools.partial(add_x, I - 1), cond_first, functools.partial(q_event, 1),
+                functools.partial(add_stats, I - 1), cond_second]
+        todo += [functools.partial(q_event, h) for h in range(2, 3)] + [cond_third]
+        todo += [functools.partial(q_event, h) for h in range(3, HOPS + 1)] + [cond_last]
+        ratio = max(1, len(todo) // max(1, len(rest)))
+        while todo or rest:
+            if rest:
+                rest.pop(0)()
+            for _ in range(ratio if rest else len(todo)):
+                if todo:
+                    todo.pop(0)()
+        for k in range(1, NX):
+            lx_copy(k).wait_recv()
+            for u in range(2):
+                late_out[u] = late_out[u] + lx_in[k - 1, u].astype(f32)
+        core_copy(I - 1).wait_send()
+        for n in range(I):
+            for k in range(1, NX):
+                gm_x(n, k).wait_send()
+                for f in range(NX):
+                    go_x(n, k, f).wait_send()
+                    go_core(n, k, f).wait_send()
+                if n >= I - 2:
+                    x_copy(n, k).wait_send()
+            for r in range(1, NP):
+                st_copy(n, r).wait_send()
+            if n >= I - 2:
+                for j in range(NX):
+                    gin_copy(n, j).wait()
+        for k in range(NX):
+            for side in range(2):
+                l_hop(k, side, 0).wait_send()
+                if HOPS > 1:
+                    l_hop(k, side, HOPS - 1).wait_send()
+        for side in range(2):
+            q_hop(side, HOPS - 1).wait_send()
+        for k in range(1, NX):
+            lx_copy(k).wait_send()
+        for k in range(1, NT):
+            last_copy(k).wait_send()
+            part_copy(k).wait_send()
+        for r in range(1, NP):
+            sum_copy(r).wait_send()
+
+
+def bwd_call(
+    NT, NP, gate, go, gms, gm, qkv, mixed, lse, concat, attn, rows, stats, scale, w, late, base, factor, ada
+):
+    I, CB, T = gm.shape
+    NX = NP // 2
+    length = attn.shape[2]
+    HL = gate.shape[0] // I
+    QKV, HO = 3 * HL * HP, HL * HP
+    QWIDE = (QKV + 127) // 128 * 128
+    RB, FL = late.shape[3:]
+    HOPS = NT // 2
+    hbm = pl.BlockSpec(memory_space=pl.ANY)
     vmem = pl.BlockSpec(memory_space=pltpu.VMEM)
     dma = pltpu.SemaphoreType.DMA
-    hops = NT // 2
+    once = pl.Buffered(buffer_count=1)
+
+    def image(*shape):
+        return pl.BlockSpec(
+            (1,) + shape, lambda i, s: (i,) + (0,) * len(shape), pipeline_mode=once
+        )
+
     return pl.pallas_call(
-        functools.partial(tail_kernel, NT, NP),
-        in_specs=[vmem] * 3,
-        out_specs=[vmem] * 3,
+        functools.partial(bwd_kernel, NT, NP),
+        grid=(I, HL + 2),
+        in_specs=[
+            pl.BlockSpec(memory_space=pltpu.SMEM),
+            hbm,
+            hbm,
+            vmem,
+            image(QKV, length),
+            image(HO, length),
+            image(HL, length),
+            image(HO, length),
+            image(D, length),
+            hbm,
+            vmem,
+            vmem,
+            vmem,
+            hbm,
+            vmem,
+            vmem,
+            vmem,
+        ],
+        out_specs=[hbm, vmem, vmem, vmem, vmem, vmem, hbm],
         out_shape=[
-            jax.ShapeDtypeStruct((RB, WN), f32),
-            jax.ShapeDtypeStruct((NT,) + last.shape, f32),
+            jax.ShapeDtypeStruct((I, CB, length), f32),
+            jax.ShapeDtypeStruct((2, RB, FL), f32),
+            jax.ShapeDtypeStruct((RB, QKV), f32),
+            jax.ShapeDtypeStruct((RB, HO), f32),
+            jax.ShapeDtypeStruct((NT,) + base.shape, f32),
             jax.ShapeDtypeStruct((NT, 8, 256), f32),
+            jax.ShapeDtypeStruct((I, NX, NX, 2, CB, T), bf16),
         ],
         scratch_shapes=[
+            pltpu.VMEM((NX, NX, 2, CB, T), bf16),
+            pltpu.VMEM((I, NX - 1, CB, T), bf16),
+            pltpu.VMEM((NX, CB, length), f32),
+            pltpu.VMEM((NX, CB, length), bf16),
+            pltpu.VMEM((2, NX, CB, length), bf16),
+            pltpu.VMEM((2, NX - 1, CB, length), bf16),
+            pltpu.VMEM((2, NX - 1, CB, length), bf16),
+            pltpu.VMEM((CB, length), f32),
+            pltpu.VMEM((NT, RB, QKV), f32),
+            pltpu.VMEM((NT, RB, HO), f32),
+            pltpu.VMEM((HO, D), bf16),
+            pltpu.VMEM((HO, length), f32),
+            pltpu.VMEM((QKV, length), bf16),
+            pltpu.VMEM((I, CB, length), bf16),
+            pltpu.VMEM((2, CB, length), f32),
+            pltpu.VMEM((I, 8, length), f32),
+            pltpu.VMEM((I, NP, 8, length), f32),
+            pltpu.VMEM(base.shape, f32),
+            pltpu.VMEM((8, 128), f32),
+            pltpu.VMEM((8, QWIDE), f32),
+            pltpu.VMEM((NX, 2, 2, RB, FL), bf16),
+            pltpu.VMEM((NX, 2, 2, RB, FL), bf16),
+            pltpu.VMEM((NX, 2, 2, 2, RB, FL), bf16),
+            pltpu.VMEM((NX - 1, 2, RB, FL), bf16),
+            pltpu.VMEM((NX - 1, 2, RB, FL), bf16),
+            pltpu.VMEM((2, RB, QWIDE + HO), bf16),
+            pltpu.VMEM((2, 2, RB, QWIDE + HO), bf16),
             pltpu.VMEM((NT, 8, 256), f32),
             pltpu.VMEM((NP, NT, 8, 256), f32),
-            pltpu.VMEM((4, hops, RB, half), bf16),
-            pltpu.VMEM((4, hops, RB, half), bf16),
-            dma((4, hops)),
-            dma((4, hops)),
+            pltpu.VMEM((NT,) + base.shape, f32),
+            dma((2, I, NX, NX)),
+            dma((2, I, NX, NX)),
+            dma((I,)),
+            dma((I,)),
+            dma((I, NX)),
+            dma((I, NX)),
+            dma((I, NP)),
+            dma((I, NP)),
+            dma((NX, 2, HOPS)),
+            dma((NX, 2, HOPS)),
+            dma((NX,)),
+            dma((NX,)),
+            dma((2, HOPS)),
+            dma((2, HOPS)),
             dma((3, max(NT, NP))),
             dma((3, max(NT, NP))),
+            dma((I, NX)),
+            dma((I, NX)),
+            dma((NX + I + I * NX,)),
+            dma((NX, 2)),
         ],
         compiler_params=pltpu.CompilerParams(
-            collective_id=1, has_side_effects=True, vmem_limit_bytes=40 * 2**20
+            collective_id=1, has_side_effects=True, vmem_limit_bytes=63 * 2**20
         ),
-        name="tail",
-    )(g, last, ada)
+        name="backward",
+    )(gate, go, gms, gm, qkv, mixed, lse, concat, attn, rows, stats, scale, w, late, base, factor, ada)
 
 
 def make_body(NT, NP):
@@ -497,24 +1103,9 @@
     RB = D // NT
     CB = D // NP
     T = LEN // NX
-    table = Ring(NT)
-    cycle = [table.tok(q) for q in range(NT)]
-    right_pairs = [(cycle[i], cycle[(i + 1) % NT]) for i in range(NT)]
-    left_pairs = [(b, a) for a, b in right_pairs]
-    n_right = NT // 2
-    n_left = NT - 1 - n_right
-
-    def hop(v, right):
-        return lax.ppermute(v, "tok", right_pairs if right else left_pairs)
 
     def tp_xor(v, r):
         return lax.ppermute(v, "tp", [(p, p ^ r) for p in range(NP)])
-
-    def swap_tokens(v, k, axis):
-        if k == 0:
-            return v
-        parts = [lax.slice_in_dim(v, (j ^ k) * T, (j ^ k) * T + T, axis=axis) for j in range(NX)]
-        return jnp.concatenate(parts, axis=axis)
 
     def body(
         block_input,
@@ -546,41 +1137,6 @@
         t = lax.axis_index("tok")
         p = lax.axis_index("tp")
         xi = p // 2
-        my_place = table.place(t)
-
-        def block_of(d):
-            tt = table.tok(my_place + d)
-            return jnp.bitwise_xor(tt // SUB, p) * SUB + tt % SUB
-
-        def gather_rows(shard):
-            pieces = [(0, shard)]
-            v = shard
-            for d in range(1, n_right + 1):
-                v = hop(v, True)
-                pieces.append((-d, v))
-            v = shard
-            for d in range(1, n_left + 1):
-                v = hop(v, False)
-                pieces.append((d, v))
-            full = jnp.zeros((2, NT) + shard.shape[1:], shard.dtype)
-            for d, v in pieces:
-                full = lax.dynamic_update_slice(full, v[:, None], (0, block_of(d), 0, 0))
-            return full.reshape(2, D, -1)
-
-        def scatter_rows(full):
-            blocks = full.reshape(NT, RB, -1)
-
-            def own(d):
-                return lax.dynamic_index_in_dim(blocks, block_of(d), 0, keepdims=False)
-
-            total = own(0)
-            for count, right in ((n_right, True), (n_left, False)):
-                v = None
-                for d in range(count, 0, -1):
-                    term = own(d if right else -d)
-                    v = hop((term if v is None else term + v.astype(f32)).astype(bf16), right)
-                total = total + v.astype(f32)
-            return total
 
         def own_order(v, axis):
             parts = [
@@ -594,6 +1150,15 @@
         ).reshape(RB, 3 * HL * HP)
         out_shard = jnp.pad(w_out.T.reshape(RB, HL, HD), ((0, 0), (0, 0), (0, HP - HD))).reshape(
             RB, HL * HP
+        )
+        QKV = 3 * HL * HP
+        gap = -QKV % 128
+        early_shard = jnp.concatenate(
+            [qkv_shard, jnp.zeros((RB, gap), bf16), out_shard], axis=1
+        )
+        late_shard = jnp.stack([w_up, w_down.T])
+        late_shards = jnp.stack(
+            [late_shard] + [tp_xor(late_shard, 2 * k) for k in range(1, NX)]
         )
         time_feat = embed_time(timesteps).astype(bf16)
         cond_wide = condition.astype(f32)
@@ -627,7 +1192,7 @@
             NT,
             NP,
             block_input,
-            jnp.concatenate([qkv_shard, out_shard], axis=1),
+            early_shard,
             message,
             ada,
             gates,
@@ -636,7 +1201,7 @@
         )
         rows_full = [rows_all[i].reshape(D, LEN) for i in range(I)]
         early_full = early_full.reshape(D, -1)
-        qkv_full, out_full = early_full[:, : 3 * HL * HP], early_full[:, 3 * HL * HP :]
+        qkv_full, out_full = early_full[:, :QKV], early_full[:, QKV + gap :]
         head_sig, group_sig = sig[:I, :HL], sig[:I, HL : HL + GL]
         head_gate = mods[0, :I, 6 * ML : 6 * ML + HL]
         vectors = mods[:, :I, : 6 * ML].reshape(NP, I * 6, ML)[:, :, :CB]
@@ -663,11 +1228,6 @@
         cot_half = jnp.stack(cot_blocks, axis=1)
         cot_full = jnp.stack([cot_half, tp_xor(cot_half, 1)], axis=2).reshape(I, D, T)
 
-        late_shard = jnp.stack([w_up, w_down.T])
-        late_parts = [late_shard] + [tp_xor(late_shard, 2 * k) for k in range(1, NX)]
-        late_parts = [gather_rows(v) for v in late_parts]
-        up_full = jnp.concatenate([v[0] for v in late_parts], axis=1)
-        down_full = jnp.concatenate([v[1] for v in late_parts], axis=1)
         qv = b_qv.astype(f32).reshape(2, HL, HD)
         qv_bias = jnp.stack(
             [
@@ -684,28 +1244,24 @@
             square = jnp.sum(v * v, axis=0, keepdims=True) * (1.0 / D)
             return centre, lax.rsqrt(square - centre * centre + EPS)
 
-        fwd = []
-        for i in range(I):
-            wide_rows = rows_full[i].astype(f32)
-            centre, inverse = stats(wide_rows)
-            attn_in = ((wide_rows - centre) * inverse * (1.0 + mod(i, 1)) + mod(i, 0)).astype(bf16)
-            qkv = (dot(qkv_full, attn_in, 0, 0) + qv_bias).astype(bf16).reshape(3 * HL, HP, LEN)
-            mixed, concat, lse = attn_fwd(head_gate[i], qkv)
-            concat = concat.reshape(HL * HP, LEN)
-            part = dot(out_full, concat, 1, 0).reshape(NX, 2, CB, LEN)
-            got = tp_xor(part[:, 1].astype(bf16), 1)
-            both = part[:, 0] + got.astype(f32)
-            total = both[:, :, :T]
-            for k in range(1, NX):
-                got = tp_xor(both[:, :, k * T : (k + 1) * T].astype(bf16), 2 * k).astype(f32)
-                total = total + jnp.stack([got[j ^ k] for j in range(NX)])
-            total_other = tp_xor(total, 1)
-            branch_one = jnp.stack([total, total_other], axis=1).reshape(D, T) + out_bias
-            fwd.append((centre, inverse, attn_in, qkv, mixed, concat, lse, branch_one))
-
+        image_mods = columns[:, : I * 6].reshape(D, I, 6).transpose(1, 0, 2)
+        attn_all, qkv_all, mixed_all, concat_all, lse_all, stats_all, branch, late_full = fwd_call(
+            NT,
+            NP,
+            head_gate.reshape(-1),
+            rows_all.reshape(I, D, LEN),
+            early_full,
+            image_mods,
+            qv_bias,
+            late_shards,
+        )
+        late_full = late_full.reshape(NX, 2, D, FL)
+        up_full = jnp.concatenate([late_full[k, 0] for k in range(NX)], axis=1)
+        down_full = jnp.concatenate([late_full[k, 1] for k in range(NX)], axis=1)
+        branch = branch.transpose(0, 2, 1, 3, 4).reshape(I, D, T)
         mids = []
         for i in range(I):
-            branch_one = fwd[i][-1]
+            branch_one = branch[i] + out_bias
             cot = cot_full[i].astype(f32)
             mid_rows = rows_full[i][:, :T].astype(f32) + mod(i, 2) * branch_one
             centre, inverse = stats(mid_rows)
@@ -737,19 +1293,6 @@
             gate_one_sums = jnp.sum(grad_mid * branch_one, axis=1)
             grad_one = (mod(i, 2) * grad_mid).astype(bf16)
             out_sums = jnp.sum(grad_one.astype(f32), axis=1)
-            own_half = grad_one.reshape(NX, 2, CB, T)[:, 0]
-            tok_blocks = [grad_one]
-            for k in range(1, NX):
-                got = tp_xor(own_half, 2 * k)
-                got = jnp.stack([got[j ^ k] for j in range(NX)])
-                tok_blocks.append(jnp.stack([got, tp_xor(got, 1)], axis=1).reshape(D, T))
-            grad_one_full = jnp.concatenate(tok_blocks, axis=1)
-            mid_blocks = [grad_mid[:CB]]
-            for k in range(1, NX):
-                mid_blocks.append(
-                    tp_xor(grad_mid[2 * k * CB : (2 * k + 1) * CB].astype(bf16), 2 * k).astype(f32)
-                )
-            grad_mid_own = jnp.concatenate(mid_blocks, axis=1)
             bpart = dot(down_full, hidden, 1, 0).reshape(NX, 2, CB, T)
             branch_two = (
                 bpart[:, 0]
@@ -768,8 +1311,8 @@
                     hidden=hidden,
                     grad_pre=grad_pre,
                     mlp_in=mlp_in,
-                    grad_one_full=grad_one_full,
-                    grad_mid_own=grad_mid_own,
+                    grad_one=grad_one,
+                    grad_mid=grad_mid,
                     out_own=out_own,
                     sums=(gate_one_sums, shift_sums, scale_sums),
                     gate_two_sums=gate_two_sums,
@@ -784,12 +1327,12 @@
 
         grad_down = sum(dot(m["grad_two"], m["hidden"], 1, 1) for m in mids)
         grad_up = sum(dot(m["mlp_in"], m["grad_pre"], 1, 1) for m in mids)
-        late = scatter_rows(jnp.concatenate([grad_up, grad_down], axis=1))
-        late = late.reshape(RB, 2, NX, FL)
-        total = late[:, :, 0]
-        for k in range(1, NX):
-            total = total + tp_xor(late[:, :, k].astype(bf16), 2 * k).astype(f32)
-        grad_up, grad_down = total[:, 0], total[:, 1]
+        late_grads = jnp.stack(
+            [
+                jnp.stack([g[:, k * FL : (k + 1) * FL] for g in (grad_up, grad_down)])
+                for k in range(NX)
+            ]
+        ).astype(bf16).reshape(NX, 2, NT, RB, FL)
 
         def x_message(k):
             parts = []
@@ -812,90 +1355,58 @@
         grad_group_gate = per_image[:, 4 * CB :]
         bias_sums = x_total[I * per :]
 
-        backs = []
-        for i in range(I):
-            centre, inverse, attn_in, qkv, mixed, concat, lse, _ = fwd[i]
-            m = mids[i]
-            gc = dot(out_full, m["grad_one_full"], 0, 0).reshape(HL, HP, LEN)
-            dq, dk, dv, inner = attn_bwd(head_gate[i], qkv, gc, mixed, lse)
-            dqkv = jnp.concatenate([dq, dk, dv], axis=0).reshape(3 * HL * HP, LEN)
-            part = dot(qkv_full, dqkv, 1, 0).reshape(NX, 2, CB, LEN)
-            got = tp_xor(part[:, 1].astype(bf16), 1)
-            both = part[:, 0] + got.astype(f32)
-            gnorm = both[0]
-            for k in range(1, NX):
-                got = tp_xor(both[k].astype(bf16), 2 * k).astype(f32)
-                gnorm = gnorm + swap_tokens(got, k, 1)
-            normed = (rows_full[i][:CB].astype(f32) - centre) * inverse
-            own_cols = columns[:CB]
-            g = gnorm * (1.0 + own_cols[:, i * 6 + 1 : i * 6 + 2])
-            sums = jnp.stack([jnp.sum(g, axis=0), jnp.sum(g * normed, axis=0)])
-            total = sums
-            for r in range(1, NP):
-                total = total + swap_tokens(tp_xor(sums, r), r // 2, 1)
-            grad_in = m["grad_mid_own"] + inverse * (
-                g - total[0:1] * (1.0 / D) - normed * (total[1:2] * (1.0 / D))
-            )
-            backs.append(
-                dict(
-                    dqkv=dqkv,
-                    grad_in=grad_in,
-                    shift=jnp.sum(gnorm, axis=1),
-                    scale=jnp.sum(gnorm * normed, axis=1),
-                    heads=jnp.sum(inner, axis=(1, 2)),
-                    q_sums=jnp.sum(dq.astype(f32), axis=2)[:, :HD].reshape(-1),
-                    v_sums=jnp.sum(dv.astype(f32), axis=2)[:, :HD].reshape(-1),
-                )
-            )
-        grad_input = own_order(jnp.stack([b["grad_in"] for b in backs]), 2)
-
-        grad_out = sum(
-            dot(m["grad_one_full"], f[5], 1, 1) for m, f in zip(mids, fwd)
-        )
-        grad_out = scatter_rows(grad_out)
-        grad_qkv = sum(dot(f[2], b["dqkv"], 1, 1) for f, b in zip(fwd, backs))
-
-        grad_mod = jnp.stack(
-            [
-                jnp.stack([b["shift"] for b in backs]),
-                jnp.stack([b["scale"] for b in backs]),
-                late_mods[:, 0],
-                late_mods[:, 1],
-                late_mods[:, 2],
-                late_mods[:, 3],
-            ],
-            axis=1,
-        )
-        grad_head_gate = jnp.stack([b["heads"] for b in backs])
-        head_logit = grad_head_gate * head_mask.astype(f32) * head_sig * (1.0 - head_sig)
+        head_factor = head_mask.astype(f32) * head_sig * (1.0 - head_sig)
         group_logit = grad_group_gate * group_mask.astype(f32) * group_sig * (1.0 - group_sig)
         image_rows = jnp.concatenate(
             [
-                jnp.pad(grad_mod, ((0, 0), (0, 0), (0, ML - CB))).reshape(I, 6 * ML),
-                head_logit,
+                jnp.pad(late_mods, ((0, 0), (2, 0), (0, ML - CB))).reshape(I, 6 * ML),
+                jnp.zeros((I, HL), f32),
                 group_logit,
                 jnp.zeros((I, 128 - HL - GL), f32),
             ],
             axis=1,
         )
         widen = lambda v: jnp.pad(v, (0, wide - v.shape[0]))[None]
-        last = jnp.concatenate(
+        base = jnp.concatenate(
             [
                 image_rows,
-                widen(sum(b["q_sums"] for b in backs)),
-                widen(sum(b["v_sums"] for b in backs)),
+                jnp.zeros((1, wide), f32),
                 widen(bias_sums[: 2 * CB]),
                 widen(bias_sums[2 * CB :]),
-                jnp.zeros((8 - I - 4, wide), f32),
+                jnp.zeros((8 - I - 3, wide), f32),
             ],
             axis=0,
         )
-        grad_qkv, lasts, cond_sum = tail_call(NT, NP, grad_qkv.reshape(NT, RB, -1), last, ada)
+        grad_one = jnp.stack([m["grad_one"] for m in mids]).reshape(I, NX, 2, CB, T)
+        grad_mid = jnp.stack([m["grad_mid"] for m in mids]).reshape(I, NX, 2, CB, T)
+        grad_input, late, grad_qkv, grad_out, lasts, cond_sum, _ = bwd_call(
+            NT,
+            NP,
+            head_gate.reshape(-1),
+            grad_one,
+            grad_mid[:, :, 0].astype(bf16),
+            grad_mid[:, 0, 0],
+            qkv_all,
+            mixed_all,
+            lse_all,
+            concat_all,
+            attn_all,
+            rows_all,
+            stats_all,
+            columns[:CB, : I * 6].reshape(CB, I, 6)[:, :, 1].T[:, :, None],
+            early_full,
+            late_grads,
+            base,
+            pad8(head_factor, 128),
+            ada,
+        )
+        grad_up, grad_down = late[0], late[1]
         mods_all = (
             lasts[:, :I, : 6 * ML].reshape(NT * I, 6, ML)[:, :, :CB].reshape(NT * I, 6 * CB)
         )
         logits_all = lasts[:, :I, 6 * ML : 6 * ML + HL + GL].reshape(NT * I, HL + GL)
-        bias_rows = jnp.sum(lasts[:, I : I + 4], axis=0)
+        bias_rows = jnp.sum(lasts[:, I : I + 3], axis=0)
+        qv_rows = bias_rows[0, :QKV].reshape(3, HL, HP)[:, :, :HD].reshape(3, HL * HD)
         cond_f = cond_all[:, :I, :RB].reshape(NT * I, RB)
         time_f = cond_all[:, :I, 256 : 256 + FR].reshape(NT * I, FR)
         grad_w_ada = lax.dot_general(
@@ -916,13 +1427,13 @@
             grad_w_ada,
             grad_b_ada,
             grad_qkv.reshape(RB, 3, HL, HP)[..., :HD].reshape(RB, 3, HL * HD),
-            bias_rows[:2, : HL * HD],
+            jnp.stack([qv_rows[0], qv_rows[2]]),
             grad_out.reshape(RB, HL, HP)[..., :HD].reshape(RB, HL * HD).T,
-            bias_rows[2, :CB],
+            bias_rows[1, :CB],
             grad_up,
-            bias_rows[3, :FL],
+            bias_rows[2, :FL],
             grad_down.T,
-            bias_rows[2, CB : 2 * CB],
+            bias_rows[1, CB : 2 * CB],
             grad_w_gates[:, :HL],
             grad_b_gates[:HL],
             grad_w_gates[:, HL:],

time: 882 us -> 663 us (0.75)
  Pallas kernels: 169 us -> 384 us
  waiting for transfers between devices: 211 us -> 0.03 us
  local copies, waits for them, and re-layouts: 161 us -> 90 us
  other arithmetic: 123 us -> 53.1 us
  starting transfers between devices: 57 us -> 8.56 us
  matrix products: 146 us -> 120 us
    pallas_call x7 -> x2, Pallas kernels: 112 us -> 314 us  [the longest x1 196 us: bwd_call(): pl.pallas_call(functools.partial(bwd_kernel, NT, NP), grid=(I, HL + 2), i...]
    ppermute x28 -> x0, waiting for transfers between devices: 106 us -> none  [hop(): return lax.ppermute(v, 'tok', right_pairs if right else left_pairs)]
    ppermute x47 -> x13, waiting for transfers between devices: 105 us -> 0.03 us  [tp_xor(): return lax.ppermute(v, 'tp', [(p, p ^ r) for p in range(NP)])]
    ppermute x28 -> x0, starting transfers between devices: 30 us -> none  [hop(): return lax.ppermute(v, 'tok', right_pairs if right else left_pairs)]
    add x21 -> x0, other arithmetic: 29.7 us -> none  [the longest x6 12.2 us: body(): both = part[:, 0] + got.astype(f32)]
    dot_general x36 -> x18, matrix products: 144 us -> 116 us  [dot(): lax.dot_general(a, b, (((ca,), (cb,)), ((), ())), preferred_element_type=...]
    convert_element_type x12 -> x0, other arithmetic: 24.7 us -> none  [the longest x8 15.9 us: scatter_rows(): v = hop((term if v is None else term + v.astype(f32)).astype(bf16), right)]
    dynamic_update_slice x15 -> x0, local copies, waits for them, and re-layouts: 22.1 us -> none  [gather_rows(): full = lax.dynamic_update_slice(full, v[:, None], (0, block_of(d), 0, 0))]
  transfers between devices with their start and end apart: 75 -> 13, of which waited for: 24 -> 0; matrix products, arithmetic and copies ran while one was open for 38% -> 29% of each run, Pallas kernels for 19% -> 29%
where the time goes in v3:
time: 663 us; the launch traced here: 659 us
  Pallas kernels  384 us (58%)
  matrix products  120 us (18%)
  local copies, waits for them, and re-layouts  90 us (14%)
  other arithmetic  53.1 us (8%)
  starting transfers between devices  8.56 us (1%)
    pallas_call x1, Pallas kernels, bwd_call(): pl.pallas_call(functools.partial(bwd_kernel, NT, NP), grid=(I, HL + 2), i...  196 us
    pallas_call x1, Pallas kernels, fwd_call(): pl.pallas_call(functools.partial(fwd_kernel, NT, NP), grid=(I, HL + 2), i...  118 us
    dot_general x18, matrix products, dot(): lax.dot_general(a, b, (((ca,), (cb,)), ((), ())), preferred_element_type=...  116 us
    pallas_call x1, Pallas kernels, start_call(): pl.pallas_call(functools.partial(start_kernel, NT, NP), in_specs=[hbm, hb...  70.4 us
    unnamed x208, local copies, waits for them, and re-layouts  24.9 us
  transfers between devices with their start and end apart: 13, of which 0 were waited for; matrix products, arithmetic and copies ran while one was open for 29% of the time, Pallas kernels for 29%

profile of v3, /device:TPU:0, one launch (start us, length us, event | category | flops | bytes accessed | tf_op | source)
XLA Modules:
  0.0 659.1 jit_solution(15013291215407160985)
XLA Ops:
  0.7 2.4 fusion.80
  3.1 2.9 collective-permute-start
  6.0 1.4 dynamic-slice_bitcast_fusion
  11.3 70.4 %start.1 = (bf16[3,4,288,1024]{3,2,1,0:T(8,128)(2,1)S(1)}, bf16[8,144,1344]{2,1,0:T(8,128)(2,1)S(1)}, f32[4,8,2432]{2,1,0:T(8,128)S(1)}, f32[8,128]{1,0:T(8,128)S(1)}, f32[8,8,384]{2,1,0:T(8,128)S(1)}) custom-call(bf16[3,288,1024]{2,1,0:T(8,128)(2,1)S(1)} %copy-done.3, bf16[144,1344]{1,0:T(8,128)(2,1)S(1)} %concatenate.100.w_ref, ...), custom_call_target="tpu_custom_call" | custom-call | tf_op jit(solution)/shard_map/start/pallas_call | solution.py:238
  81.7 2.9 copy-done
  84.7 1.7 copy-done.1
  89.1 1.8 copy.159
  94.4 6.2 fusion.104
  100.6 2.3 pad_maximum_fusion.7.late_ref
  102.9 117.6 %forward.1 = (bf16[3,1152,1024]{2,1,0:T(8,128)(2,1)}, bf16[3,960,1024]{2,1,0:T(8,128)(2,1)}, f32[3,320,1024]{2,1,0:T(8,128)}, bf16[3,320,1024]{2,1,0:T(8,128)(2,...) custom-call(f32[12]{0:T(128)} %reshape_squeeze.21.gate_ref, ...), custom_call_target="tpu_custom_call" | custom-call | tf_op jit(solution)/shard_map/forward/pallas_call | solution.py:464
  220.6 4.2 fusion.105
  226.4 2.4 slice-done.2
  228.7 5.0 slice_bitcast_fusion.3
  234.2 3.5 fusion.96
  237.8 3.7 convolution_add_fusion.4
  242.0 3.1 fusion.89
  245.3 3.8 convolution_add_fusion.6
  249.1 3.3 fusion.87
  254.0 1.4 fusion.84
  255.9 3.7 convolution_add_fusion.5
  259.7 3.1 fusion.88
  263.0 1.6 convert_reduce_fusion.5
  265.2 10.5 %convert_reduce_fusion.2 = (f32[2304]{0:T(1024)S(1)}, bf16[2304,512]{0,1:T(8,128)(2,1)}, f32[2304]{0:T(1024)S(1)}) fusion(f32[2304]{0:T(1024)S(1)} %get-tuple-element.91, f32[2304,512]{0,1:T(8,128)} %copy-done.89, bf16[1152,512]{1,0:T(8,128)(2,1)S(1)} %fusion.28, bf16[1152,1152]{1,0:T(8,128)(2,1)S(1)} %copy-done.40, bf16[1152,1152]{1,0:T(8,128)(2,1)S(1)} %copy-done.38), kind=kOutput, calls=%fused_computation.45 | convolution fusion | flops 2758012416 | bytes 13593600 | tf_op jit(solution)/shard_map/dot_general | solution.py:29
  275.8 6.4 fusion.86
  282.8 3.0 copy-done.91
  285.9 3.1 fusion.85
  289.0 8.0 %fusion.131 = (bf16[1152,512]{1,0:T(8,128)(2,1)}, f32[1152,512]{1,0:T(8,128)}) fusion(bf16[2304,512]{0,1:T(8,128)(2,1)} %get-tuple-element.111, bf16[1152,1152]{1,0:T(8,128)(2,1)} %get-tuple-element.133, bf16[1152,1152]{1,0:T(8,128)(2,1)} %get-tuple-element.134), kind=kOutput, calls=%fused_computation.341 | convolution fusion | flops 2729115648 | bytes 11206656 | tf_op jit(solution)/shard_map/dot_general | solution.py:29
  297.8 3.0 fusion.44
  303.0 1.5 collective-permute-start.4
  306.4 10.6 %convert_reduce_fusion = (f32[2304]{0:T(1024)S(1)}, bf16[2304,512]{0,1:T(8,128)(2,1)}, f32[2304]{0:T(1024)S(1)}) fusion(f32[2304]{0:T(1024)S(1)} %get-tuple-element.92, f32[2304,512]{0,1:T(8,128)} %copy-done.90, bf16[1152,512]{1,0:T(8,128)(2,1)S(1)} %fusion.26, bf16[1152,1152]{1,0:T(8,128)(2,1)} %get-tuple-element.135, bf16[1152,1152]{1,0:T(8,128)(2,1)S(1)} %copy-done.39), kind=kOutput, calls=%fused_computation.43 | convolution fusion | flops 2758012416 | bytes 13593600 | tf_op jit(solution)/shard_map/dot_general | solution.py:29
  317.1 7.4 %fusion.129 = (bf16[1152,512]{1,0:T(8,128)(2,1)}, f32[1152,512]{1,0:T(8,128)}) fusion(bf16[2304,512]{0,1:T(8,128)(2,1)} %get-tuple-element.113, bf16[1152,1152]{1,0:T(8,128)(2,1)S(1)} %copy-done.35, bf16[1152,1152]{1,0:T(8,128)(2,1)} %get-tuple-element.134), kind=kOutput, calls=%fused_computation.339 | convolution fusion | flops 2729115648 | bytes 11206656 | tf_op jit(solution)/shard_map/dot_general | solution.py:29
  324.8 10.2 %convert_reduce_fusion.1 = (f32[2304]{0:T(1024)S(1)}, bf16[2304,512]{0,1:T(8,128)(2,1)}, f32[2304]{0:T(1024)S(1)}) fusion(f32[2304]{0:T(1024)S(1)} %get-tuple-element.93, f32[2304,512]{0,1:T(8,128)S(1)} %bitcast.347, bf16[1152,512]{1,0:T(8,128)(2,1)S(1)} %fusion.27, bf16[1152,1152]{1,0:T(8,128)(2,1)} %get-tuple-element.135, ...), kind=kOutput, calls=%fused_computation.44 | convolution fusion | flops 2758012416 | bytes 13593600 | tf_op jit(solution)/shard_map/dot_general | solution.py:29
  335.0 6.6 %fusion.130 = (bf16[1152,512]{1,0:T(8,128)(2,1)}, f32[1152,512]{1,0:T(8,128)}) fusion(bf16[2304,512]{0,1:T(8,128)(2,1)} %get-tuple-element.109, bf16[1152,1152]{1,0:T(8,128)(2,1)S(1)} %copy-done.35, bf16[1152,1152]{1,0:T(8,128)(2,1)S(1)} %copy-done.37), kind=kOutput, calls=%fused_computation.340 | convolution fusion | flops 2729115648 | bytes 11206656 | tf_op jit(solution)/shard_map/dot_general | solution.py:29
  342.2 8.8 %convolution_add_fusion.1 = f32[1152,2304]{1,0:T(8,128)} fusion(f32[1152,2304]{1,0:T(8,128)} %fusion.86, bf16[1152,512]{1,0:T(8,128)(2,1)S(1)} %fusion.27, f32[2304]{0:T(1024)S(1)} %get-tuple-element.93, f32[2304,512]{0,1:T(8,128)S(1)} %bitcast.347), kind=kOutput, calls=%fused_computation.1 | convolution fusion | flops 2732359680 | bytes 27141120 | tf_op jit(solution)/shard_map/dot_general | solution.py:29
  351.0 10.9 %fusion.1 = bf16[1152,2304]{1,0:T(8,128)(2,1)} fusion(f32[1152,2304]{1,0:T(8,128)} %convolution_add_fusion.1, bf16[1152,512]{1,0:T(8,128)(2,1)S(1)} %fusion.26, f32[2304]{0:T(1024)S(1)} %get-tuple-element.92, f32[2304,512]{0,1:T(8,128)} %copy-done.90), kind=kOutput, calls=%fused_computation.5 | convolution fusion | flops 2735013888 | bytes 21832704 | tf_op jit(solution)/shard_map/dot_general | solution.py:29
  361.9 5.5 fusion.107
  367.5 5.9 convolution_add_fusion.3
  373.4 6.8 %fusion = bf16[1152,2304]{1,0:T(8,128)(2,1)S(1)} fusion(f32[1152,2304]{1,0:T(8,128)} %convolution_add_fusion.3, bf16[2304,512]{0,1:T(8,128)(2,1)} %get-tuple-element.113, f32[1152,512]{1,0:T(8,128)S(1)} %get-tuple-element.214, f32[1152]{0:T(1024)S(1)} %copy-done.71, f32[1152]{0:T(1024)S(1)} %copy-done.62, f32[512]{0:T(512)S(1)} %copy-done.68, ...), kind=kOutput, calls=%fused_computation.4 | convolution fusion | flops 2726166528 | bytes 20657152 | tf_op jit(solution)/shard_map/dot_general | solution.py:29
  380.2 2.7 fusion.106
  383.8 9.5 %maximum_maximum_fusion.late_ref = bf16[2,2,8,144,1152]{4,3,2,1,0:T(8,128)(2,1)} fusion(bf16[1,1,8,144,1152]{4,3,2,1,0:T(8,128)(2,1)} %bitcast.332, bf16[1,1,8,144,1152]{4,3,2,1,0:T(8,128)(2,1)} %bitcast.334, bf16[1,1,8,144,1152]{4,3,2,1,0:T(8,128)(2,1)} %bitcast.331, bf16[1,1,8,144,1152]{4,3,2,1,0:T(8,128)(2,1)} %bitcast.333), kind=kLoop, calls=%fused_computation.6 | loop fusion | flops 15925248 | bytes 21233664 | tf_op jit(solution)/shard_map/stack | solution.py:1330
  397.0 1.5 pad_maximum_fusion.5
  398.5 1.3 fusion.110
  399.9 1.5 fusion.109
  401.9 1.3 copy-done.11
  403.8 2.8 multiply_reduce_fusion.3
  406.8 1.5 copy-done.23
  408.3 2.3 convert_reduce_fusion.6
  410.6 2.3 convert_reduce_fusion.7
  413.6 2.0 copy-done.9
  415.6 1.3 multiply_reduce_fusion.7
  417.3 2.3 convert_reduce_fusion.8
  422.5 1.4 fusion.29
  424.6 1.3 collective-permute-start.12
  425.9 3.6 pad_maximum_fusion.3.go_ref
  430.6 1.3 maximum_bitcast_fusion.gm_ref
  432.7 1.4 copy.181.gms_ref
  436.2 196.3 %backward.1 = (f32[3,288,1024]{2,1,0:T(8,128)}, f32[2,144,1152]{2,1,0:T(8,128)}, f32[144,960]{1,0:T(8,128)}, f32[144,320]{1,0:T(8,128)}, f32[8,8,2432]{2,1,0:T(8...) custom-call(f32[12]{0:T(128)} %reshape_squeeze.21.gate_ref, ...), custom_call_target="tpu_custom_call" | custom-call | tf_op jit(solution)/shard_map/backward/pallas_call | solution.py:1009
  633.7 1.2 slice_reduce_fusion
  636.1 1.9 slice_reduce_fusion.30
  646.1 2.0 reshape.498
  648.0 2.4 slice_bitcast_fusion.7
  652.0 1.3 fusion.125
  653.3 3.3 fusion.50
  657.2 1.8 copy.258
  (414 shorter events, 48.1 us)
Async XLA Ops:
  0.7 5.3 copy-start.42
  0.7 6.8 %copy-start.50 = (bf16[144,3,288]{2,0,1:T(8,128)(2,1)S(1)}, bf16[144,3,288]{2,0,1:T(8,128)(2,1)}, u32[]{:S(2)}) copy-start(bf16[144,3,288]{2,0,1:T(8,128)(2,1)} %param.27) | copy-start | bytes 746500
  3.1 97.5 %collective-permute-start = (bf16[2,144,1152]{2,1,0:T(8,128)(2,1)}, bf16[2,144,1152]{2,1,0:T(8,128)(2,1)}, u32[]{:S(2)}, u32[]{:S(2)}) collective-permute-start(bf16[2,144,1152]{2,1,0:T(8,128)(2,1)} %get-tuple-element.171), channel_id=1, source_target_pairs={{0,2},{1,3},{2,0},{3,1},{4,6},{5,7},{6,4},{7,5},{8,10},{9,11},{10,... | collective-permute-start | bytes 1990664 | tf_op jit(solution)/shard_map/ppermute | solution.py:1108
  7.4 246.5 %collective-permute-start.7 = (bf16[3,288,512]{2,1,0:T(8,128)(2,1)}, bf16[3,288,512]{2,1,0:T(8,128)(2,1)}, u32[]{:S(2)}, u32[]{:S(2)}) collective-permute-start(bf16[3,288,512]{2,1,0:T(8,128)(2,1)} %get-tuple-element.159), channel_id=1, source_target_pairs={{0,2},{1,3},{2,0},{3,1},{4,6},{5,7},{6,4},{7,5},{8,10},{9,11},{10,... | collective-permute-start | bytes 2654216 | tf_op jit(solution)/shard_map/ppermute | solution.py:1108
  10.6 76.1 %copy-start.2 = (bf16[6,144,384]{2,1,0:T(8,128)(2,1)}, bf16[6,144,384]{2,1,0:T(8,128)(2,1)S(1)}, u32[]{:S(2)}) copy-start(bf16[6,144,384]{2,1,0:T(8,128)(2,1)S(1)} %pad.83.ada_ref) | copy-start | bytes 1990660
  86.4 4.5 copy-start.80
  87.1 146.7 %copy-start.53 = (f32[1152]{0:T(1024)}, f32[1152]{0:T(1024)S(1)}, u32[]{:S(2)}) copy-start(f32[1152]{0:T(1024)S(1)} %get-tuple-element.87) | copy-start | bytes 13828
  87.1 146.7 %copy-start.55 = (f32[1152]{0:T(1024)}, f32[1152]{0:T(1024)S(1)}, u32[]{:S(2)}) copy-start(f32[1152]{0:T(1024)S(1)} %get-tuple-element.88) | copy-start | bytes 13828
  87.1 146.7 %copy-start.57 = (f32[1152]{0:T(1024)}, f32[1152]{0:T(1024)S(1)}, u32[]{:S(2)}) copy-start(f32[1152]{0:T(1024)S(1)} %get-tuple-element.83) | copy-start | bytes 13828
  87.1 146.7 %copy-start.59 = (f32[1152]{0:T(1024)}, f32[1152]{0:T(1024)S(1)}, u32[]{:S(2)}) copy-start(f32[1152]{0:T(1024)S(1)} %get-tuple-element.79) | copy-start | bytes 13828
  87.1 150.7 %copy-start.61 = (f32[1152]{0:T(1024)}, f32[1152]{0:T(1024)S(1)}, u32[]{:S(2)}) copy-start(f32[1152]{0:T(1024)S(1)} %get-tuple-element.77) | copy-start | bytes 13828
  87.1 150.7 %copy-start.70 = (f32[1152]{0:T(1024)}, f32[1152]{0:T(1024)S(1)}, u32[]{:S(2)}) copy-start(f32[1152]{0:T(1024)S(1)} %get-tuple-element.76) | copy-start | bytes 13828
  94.4 6.2 copy-start.33
  220.5 4.9 slice-start
  220.5 5.8 slice-start.1
  225.0 8.9 %copy-start.12 = (f32[1,2,2,288,512]{4,3,2,1,0:T(8,128)}, f32[1,2,2,288,512]{4,3,2,1,0:T(8,128)S(1)}, u32[]{:S(2)}) copy-start(f32[1,2,2,288,512]{4,3,2,1,0:T(8,128)S(1)} %copy.161) | copy-start | bytes 7077892
  225.2 8.6 %copy-start.14 = (f32[1,2,2,288,512]{4,3,2,1,0:T(8,128)}, f32[1,2,2,288,512]{4,3,2,1,0:T(8,128)S(1)}, u32[]{:S(2)}) copy-start(f32[1,2,2,288,512]{4,3,2,1,0:T(8,128)S(1)} %copy.165) | copy-start | bytes 7077892
  225.4 8.4 %copy-start.16 = (f32[1,2,2,288,512]{4,3,2,1,0:T(8,128)}, f32[1,2,2,288,512]{4,3,2,1,0:T(8,128)S(1)}, u32[]{:S(2)}) copy-start(f32[1,2,2,288,512]{4,3,2,1,0:T(8,128)S(1)} %copy.169) | copy-start | bytes 7077892
  228.7 5.1 copy-start.28
  228.7 5.5 copy-start.29
  237.7 60.1 %copy-start.8 = (f32[1152,512]{1,0:T(8,128)}, f32[1152,512]{1,0:T(8,128)S(1)}, u32[]{:S(2)}) copy-start(f32[1152,512]{1,0:T(8,128)S(1)} %get-tuple-element.129) | copy-start | bytes 7077892
  237.7 135.7 %copy-start.10 = (f32[1152,512]{1,0:T(8,128)}, f32[1152,512]{1,0:T(8,128)S(1)}, u32[]{:S(2)}) copy-start(f32[1152,512]{1,0:T(8,128)S(1)} %get-tuple-element.214) | copy-start | bytes 7077892
  237.7 3.8 copy-start.65
  237.7 3.8 copy-start.67
  237.8 3.8 copy-start.38
  237.8 4.2 copy-start.40
  245.1 3.9 copy-start.43
  245.2 51.8 %collective-permute-start.5 = (bf16[2,288,512]{2,1,0:T(8,128)(2,1)S(1)}, bf16[2,288,512]{2,1,0:T(8,128)(2,1)S(1)}, u32[]{:S(2)}, u32[]{:S(2)}) collective-permute-start(bf16[2,288,512]{2,1,0:T(8,128)(2,1)S(1)} %fusion.49), channel_id=1, source_target_pairs={{0,1},{1,0},{2,3},{3,2},{4,5},{5,4},{6,7},{7,6},{8,9},{9,8},{10,11... | collective-permute-start | bytes 1769480 | tf_op jit(solution)/shard_map/ppermute | solution.py:1108
  249.1 4.9 copy-start.32
  253.4 43.6 %collective-permute-start.1 = (bf16[2,288,512]{2,1,0:T(8,128)(2,1)}, bf16[2,288,512]{2,1,0:T(8,128)(2,1)S(1)}, u32[]{:S(2)}, u32[]{:S(2)}) collective-permute-start(bf16[2,288,512]{2,1,0:T(8,128)(2,1)} %fusion.47), channel_id=1, source_target_pairs={{0,1},{1,0},{2,3},{3,2},{4,5},{5,4},{6,7},{7,6},{8,9},{9,8},{10,11... | collective-permute-start | bytes 1769480 | tf_op jit(solution)/shard_map/ppermute | solution.py:1108
  255.4 7.6 %collective-permute-start.8 = (bf16[3,2,288,512]{3,2,1,0:T(8,128)(2,1)S(1)}, bf16[3,2,288,512]{3,2,1,0:T(8,128)(2,1)S(1)}, u32[]{:S(2)}, u32[]{:S(2)}) collective-permute-start(bf16[3,2,288,512]{3,2,1,0:T(8,128)(2,1)S(1)} %get-tuple-element.157), channel_id=1, source_target_pairs={{0,1},{1,0},{2,3},{3,2},{4,5},{5,4},{6,7},{7,6},{8,9},{9,8},{10,11... | collective-permute-start | bytes 5308424 | tf_op jit(solution)/shard_map/ppermute | solution.py:1108
  262.9 34.1 %collective-permute-start.3 = (bf16[2,288,512]{2,1,0:T(8,128)(2,1)S(1)}, bf16[2,288,512]{2,1,0:T(8,128)(2,1)S(1)}, u32[]{:S(2)}, u32[]{:S(2)}) collective-permute-start(bf16[2,288,512]{2,1,0:T(8,128)(2,1)S(1)} %fusion.48), channel_id=1, source_target_pairs={{0,1},{1,0},{2,3},{3,2},{4,5},{5,4},{6,7},{7,6},{8,9},{9,8},{10,11... | collective-permute-start | bytes 1769480 | tf_op jit(solution)/shard_map/ppermute | solution.py:1108
  265.0 10.8 %copy-start.18 = (f32[1,2,2,288,512]{4,3,2,1,0:T(8,128)}, f32[1,2,2,288,512]{4,3,2,1,0:T(8,128)S(1)}, u32[]{:S(2)}) copy-start(f32[1,2,2,288,512]{4,3,2,1,0:T(8,128)S(1)} %copy.174) | copy-start | bytes 7077892
  265.0 10.8 %slice-start.5 = ((s8[4718592]{0:T(1024)(128)(4,1)}), s8[4194304]{0:T(1024)(128)(4,1)S(1)}, s32[]{:S(2)}) async-start(s8[4718592]{0:T(1024)(128)(4,1)} %bitcast.377), calls=%async_computation.5 | async-start | bytes 8388608
  265.2 10.5 %slice-start.6 = ((s8[4718592]{0:T(1024)(128)(4,1)}), s8[524288]{0:T(1024)(128)(4,1)S(1)}, s32[]{:S(2)}) async-start(s8[4718592]{0:T(1024)(128)(4,1)} %bitcast.377), calls=%async_computation.6 | async-start | bytes 1048576
  282.5 23.4 %copy-start.22 = (f32[1,2,2,288,512]{4,3,2,1,0:T(8,128)}, f32[1,2,2,288,512]{4,3,2,1,0:T(8,128)S(1)}, u32[]{:S(2)}) copy-start(f32[1,2,2,288,512]{4,3,2,1,0:T(8,128)S(1)} %copy.176) | copy-start | bytes 7077892
  282.8 41.7 %copy-start.20 = (f32[1,2,2,288,512]{4,3,2,1,0:T(8,128)}, f32[1,2,2,288,512]{4,3,2,1,0:T(8,128)S(1)}, u32[]{:S(2)}) copy-start(f32[1,2,2,288,512]{4,3,2,1,0:T(8,128)S(1)} %copy.175) | copy-start | bytes 7077892
  301.6 91.8 %collective-permute-start.6 = (bf16[288,512]{1,0:T(8,128)(2,1)}, bf16[288,512]{1,0:T(8,128)(2,1)}, u32[]{:S(2)}, u32[]{:S(2)}) collective-permute-start(bf16[288,512]{1,0:T(8,128)(2,1)} %get-tuple-element.179), channel_id=1, source_target_pairs={{0,2},{1,3},{2,0},{3,1},{4,6},{5,7},{6,4},{7,5},{8,10},{9,11},{10,... | collective-permute-start | bytes 884744 | tf_op jit(solution)/shard_map/ppermute | solution.py:1108
  303.0 91.5 %collective-permute-start.4 = (bf16[288,512]{1,0:T(8,128)(2,1)}, bf16[288,512]{1,0:T(8,128)(2,1)}, u32[]{:S(2)}, u32[]{:S(2)}) collective-permute-start(bf16[288,512]{1,0:T(8,128)(2,1)} %get-tuple-element.177), channel_id=1, source_target_pairs={{0,2},{1,3},{2,0},{3,1},{4,6},{5,7},{6,4},{7,5},{8,10},{9,11},{10,... | collective-permute-start | bytes 884744 | tf_op jit(solution)/shard_map/ppermute | solution.py:1108
  305.4 90.2 %collective-permute-start.2 = (bf16[288,512]{1,0:T(8,128)(2,1)}, bf16[288,512]{1,0:T(8,128)(2,1)}, u32[]{:S(2)}, u32[]{:S(2)}) collective-permute-start(bf16[288,512]{1,0:T(8,128)(2,1)} %get-tuple-element.175), channel_id=1, source_target_pairs={{0,2},{1,3},{2,0},{3,1},{4,6},{5,7},{6,4},{7,5},{8,10},{9,11},{10,... | collective-permute-start | bytes 884744 | tf_op jit(solution)/shard_map/ppermute | solution.py:1108
  306.4 10.7 %copy-start.35 = (bf16[1152,1152]{1,0:T(8,128)(2,1)S(1)}, bf16[1152,1152]{1,0:T(8,128)(2,1)}, u32[]{:S(2)}) copy-start(bf16[1152,1152]{1,0:T(8,128)(2,1)} %get-tuple-element.133) | copy-start | bytes 7962628
  317.1 7.6 %slice-start.3 = ((s8[4718592]{0:T(1024)(128)(4,1)}), s8[4194304]{0:T(1024)(128)(4,1)S(1)}, s32[]{:S(2)}) async-start(s8[4718592]{0:T(1024)(128)(4,1)} %bitcast.346), calls=%async_computation.3 | async-start | bytes 8388608
  317.1 7.6 %slice-start.4 = ((s8[4718592]{0:T(1024)(128)(4,1)}), s8[524288]{0:T(1024)(128)(4,1)S(1)}, s32[]{:S(2)}) async-start(s8[4718592]{0:T(1024)(128)(4,1)} %bitcast.346), calls=%async_computation.4 | async-start | bytes 1048576
  324.5 74.0 %collective-permute-start.11 = (bf16[1152,512]{1,0:T(8,128)(2,1)}, bf16[1152,512]{1,0:T(8,128)(2,1)}, u32[]{:S(2)}, u32[]{:S(2)}) collective-permute-start(bf16[1152,512]{1,0:T(8,128)(2,1)} %get-tuple-element.237), channel_id=1, source_target_pairs={{0,1},{1,0},{2,3},{3,2},{4,5},{5,4},{6,7},{7,6},{8,9},{9,8},{10,11... | collective-permute-start | bytes 3538952 | tf_op jit(solution)/shard_map/ppermute | solution.py:1108
  324.8 10.2 %copy-start.37 = (bf16[1152,1152]{1,0:T(8,128)(2,1)S(1)}, bf16[1152,1152]{1,0:T(8,128)(2,1)}, u32[]{:S(2)}) copy-start(bf16[1152,1152]{1,0:T(8,128)(2,1)} %get-tuple-element.134) | copy-start | bytes 7962628
  341.7 58.2 %collective-permute-start.10 = (bf16[1152,512]{1,0:T(8,128)(2,1)}, bf16[1152,512]{1,0:T(8,128)(2,1)}, u32[]{:S(2)}, u32[]{:S(2)}) collective-permute-start(bf16[1152,512]{1,0:T(8,128)(2,1)} %get-tuple-element.239), channel_id=1, source_target_pairs={{0,1},{1,0},{2,3},{3,2},{4,5},{5,4},{6,7},{7,6},{8,9},{9,8},{10,11... | collective-permute-start | bytes 3538952 | tf_op jit(solution)/shard_map/ppermute | solution.py:1108
  361.9 5.5 copy-start.41
  367.4 5.9 copy-start.62
  367.4 5.9 copy-start.66
  367.4 5.9 copy-start.68
  367.5 5.9 copy-start.71
  383.8 9.7 %copy-start.87 = (bf16[1152,512]{1,0:T(8,128)(2,1)S(1)}, bf16[1152,512]{1,0:T(8,128)(2,1)}, u32[]{:S(2)}) copy-start(bf16[1152,512]{1,0:T(8,128)(2,1)} %get-tuple-element.241) | copy-start | bytes 3538948
  383.8 10.8 %copy-start.46 = (bf16[288,512]{1,0:T(8,128)(2,1)S(1)}, bf16[288,512]{1,0:T(8,128)(2,1)}, u32[]{:S(2)}) copy-start(bf16[288,512]{1,0:T(8,128)(2,1)} %get-tuple-element.176) | copy-start | bytes 884740
  393.4 13.3 %collective-permute-start.9 = (bf16[1152,512]{1,0:T(8,128)(2,1)S(1)}, bf16[1152,512]{1,0:T(8,128)(2,1)S(1)}, u32[]{:S(2)}, u32[]{:S(2)}) collective-permute-start(bf16[1152,512]{1,0:T(8,128)(2,1)S(1)} %copy-done.87), channel_id=1, source_target_pairs={{0,1},{1,0},{2,3},{3,2},{4,5},{5,4},{6,7},{7,6},{8,9},{9,8},{10,11... | collective-permute-start | bytes 3538952 | tf_op jit(solution)/shard_map/ppermute | solution.py:1108
  410.6 11.2 %copy-start.4 = (f32[1152,512]{1,0:T(8,128)}, f32[1152,512]{1,0:T(8,128)S(1)}, u32[]{:S(2)}) copy-start(f32[1152,512]{1,0:T(8,128)S(1)} %get-tuple-element.128) | copy-start | bytes 7077892
  412.9 8.9 %copy-start.6 = (f32[1152,512]{1,0:T(8,128)}, f32[1152,512]{1,0:T(8,128)S(1)}, u32[]{:S(2)}) copy-start(f32[1152,512]{1,0:T(8,128)S(1)} %get-tuple-element.122) | copy-start | bytes 7077892
  424.6 9.6 %collective-permute-start.12 = (f32[5196]{0:T(1024)S(1)}, f32[5196]{0:T(1024)S(1)}, u32[]{:S(2)}, u32[]{:S(2)}) collective-permute-start(f32[5196]{0:T(1024)S(1)} %concatenate.124), channel_id=1, source_target_pairs={{0,2},{1,3},{2,0},{3,1},{4,6},{5,7},{6,4},{7,5},{8,10},{9,11},{10,... | collective-permute-start | bytes 62360 | tf_op jit(solution)/shard_map/ppermute | solution.py:1108
  425.9 4.7 copy-start.7
  436.2 202.8 %copy-start.64 = (bf16[3,1152]{1,0:T(4,128)(2,1)S(1)}, bf16[3,1152]{1,0:T(4,128)(2,1)}, u32[]{:S(2)}) copy-start(bf16[3,1152]{1,0:T(4,128)(2,1)} %param.21) | copy-start | bytes 20740
  632.5 8.9 %copy-start.49 = (f32[144,960]{1,0:T(8,128)S(1)}, f32[144,960]{1,0:T(8,128)}, u32[]{:S(2)}) copy-start(f32[144,960]{1,0:T(8,128)} %get-tuple-element.52) | copy-start | bytes 1658884
  642.8 7.6 %copy-start.69 = (f32[8,3,32]{2,1,0:T(4,128)S(1)}, f32[8,3,32]{2,1,0:T(4,128)}, u32[]{:S(2)}) copy-start(f32[8,3,32]{2,1,0:T(4,128)} %slice.639) | copy-start | bytes 9220
  646.1 11.1 %copy-start.31 = (f32[3,288,1024]{2,1,0:T(8,128)S(1)}, f32[3,288,1024]{2,1,0:T(8,128)}, u32[]{:S(2)}) copy-start(f32[3,288,1024]{2,1,0:T(8,128)} %get-tuple-element.273) | copy-start | bytes 10616836
  648.0 8.5 %copy-start.77 = (f32[1,288]{1,0:T(1,128)S(1)}, f32[1,288]{1,0:T(1,128)}, u32[]{:S(2)}) copy-start(f32[1,288]{1,0:T(1,128)} %slice.632) | copy-start | bytes 3460
  648.0 8.5 %copy-start.78 = (f32[1,288]{1,0:T(1,128)S(1)}, f32[1,288]{1,0:T(1,128)}, u32[]{:S(2)}) copy-start(f32[1,288]{1,0:T(1,128)} %slice.630) | copy-start | bytes 3460
  (48 other events, 123.0 us)

commit v4 on v3

--- a/solution.py
+++ b/solution.py
@@ -79,19 +79,83 @@
     pl.semaphore_wait(barrier, NP - 1 + NT - 1)
 
 
+class ImageMoves:
+    def __init__(self, NP, x_ref, rows_ref, x_send, x_recv, c_send, c_recv, local_sem):
+        self.NX = NP // 2
+        self.T = x_ref.shape[2] // self.NX
+        self.refs = (x_ref, rows_ref)
+        self.sems = (x_send, x_recv, c_send, c_recv, local_sem)
+        self.t, self.p = lax.axis_index("tok"), lax.axis_index("tp")
+        self.core = (self.t, xor(self.p, 1))
+
+    def tokens(self, who, j):
+        return pl.ds(pl.multiple_of(xor(who, j) * self.T, self.T), self.T)
+
+    def src(self, i, j):
+        return self.refs[0].at[i, :, pl.ds(j * self.T, self.T)]
+
+    def x(self, i, k, j):
+        x_send, x_recv = self.sems[:2]
+        at = self.tokens(xor(self.p // 2, k), j)
+        dst = self.refs[1].at[i, 2 * k, :, at]
+        device = (self.t, xor(self.p, 2 * k))
+        return copy_to(self.src(i, j), dst, x_send.at[i, k, j], x_recv.at[i, k, j], device)
+
+    def own(self, i, j):
+        dst = self.refs[1].at[i, 0, :, self.tokens(self.p // 2, j)]
+        return pltpu.make_async_copy(self.src(i, j), dst, self.sems[4].at[i, j])
+
+    def own_core(self, i, j):
+        dst = self.refs[1].at[i, 1, :, self.tokens(self.p // 2, j)]
+        c_send, c_recv = self.sems[2:4]
+        return copy_to(self.src(i, j), dst, c_send.at[i, 0, j], c_recv.at[i, 0, j], self.core)
+
+    def passed(self, i, k):
+        rows = self.refs[1]
+        c_send, c_recv = self.sems[2:4]
+        return copy_to(
+            rows.at[i, 2 * k], rows.at[i, 2 * k + 1], c_send.at[i, k, 0], c_recv.at[i, k, 0], self.core
+        )
+
+    def start(self, i):
+        for k in range(1, self.NX):
+            for j in range(self.NX):
+                self.x(i, k, j).start()
+        for j in range(self.NX):
+            self.own(i, j).start()
+            self.own_core(i, j).start()
+
+    def land(self, i):
+        for k in range(1, self.NX):
+            for j in range(self.NX):
+                self.x(i, k, j).wait_recv()
+            self.passed(i, k).start()
+
+    def finish(self, i):
+        for j in range(self.NX):
+            self.own(i, j).wait()
+            self.own_core(i, j).wait_recv()
+        for k in range(1, self.NX):
+            self.passed(i, k).wait_recv()
+
+    def left(self, i):
+        for j in range(self.NX):
+            self.own_core(i, j).wait_send()
+        for k in range(1, self.NX):
+            self.passed(i, k).wait_send()
+            for j in range(self.NX):
+                self.x(i, k, j).wait_send()
+
+
 def start_kernel(
     NT, NP, x_ref, w_ref, msg_ref, ada_ref, gates_ref, bias_ref, mask_ref,
     rows_ref, full_ref, mods_ref, sig_ref, cond_ref,
     part_ref, got_ref, x_send, x_recv, c_send, c_recv, r_send, r_recv, s_send, s_recv, local_sem,
 ):
     NX, SUB = NP // 2, NT // NP
-    I, _, length = x_ref.shape
-    T = length // NX
     WN = w_ref.shape[1]
     half = WN // 256 * 128
     t, p = lax.axis_index("tok"), lax.axis_index("tp")
-    xi = p // 2
-    core = (t, xor(p, 1))
     ring = Ring(NT)
     q = ring.place(t)
     right, left = (ring.tok(q + 1), p), (ring.tok(q - 1), p)
@@ -131,38 +195,11 @@
         for to_right in (True, False):
             hops[d, to_right].wait_recv()
 
-    sent = {}
-
-    def start_image(i):
-        for k in range(1, NX):
-            peer = xor(xi, k)
-            for j in range(NX):
-                at = pl.ds(pl.multiple_of(xor(peer, j) * T, T), T)
-                cp = copy_to(
-                    x_ref.at[i, :, pl.ds(j * T, T)], rows_ref.at[i, 2 * k, :, at],
-                    x_send.at[i, k, j], x_recv.at[i, k, j], (t, xor(p, 2 * k)),
-                )
-                sent[i, k, j] = cp
-                cp.start()
-
-    locals_, own = [], []
-    start_image(0)
+    images = ImageMoves(NP, x_ref, rows_ref, x_send, x_recv, c_send, c_recv, local_sem)
+    images.start(0)
     start_hop(1)
-    for i in range(1, I):
-        start_image(i)
-    for i in range(I):
-        for j in range(NX):
-            at = pl.ds(pl.multiple_of(xor(xi, j) * T, T), T)
-            src = x_ref.at[i, :, pl.ds(j * T, T)]
-            cp = pltpu.make_async_copy(src, rows_ref.at[i, 0, :, at], local_sem.at[i, j])
-            cp.start()
-            locals_.append(cp)
-            cp = copy_to(src, rows_ref.at[i, 1, :, at], c_send.at[i, 0, j], c_recv.at[i, 0, j], core)
-            cp.start()
-            own.append(cp)
-    cp = pltpu.make_async_copy(w_ref, full_ref.at[where(t)], local_sem.at[I, 0])
-    cp.start()
-    locals_.append(cp)
+    keep = pltpu.make_async_copy(w_ref, full_ref.at[where(t)], local_sem.at[1, 0])
+    keep.start()
 
     cond_ref[0] = msg_ref[t]
     for cp in small:
@@ -197,39 +234,22 @@
         cp.start()
         mods.append(cp)
 
-    passed = []
-
-    def land_image(i):
-        for k in range(1, NX):
-            for j in range(NX):
-                sent[i, k, j].wait_recv()
-            cp = copy_to(
-                rows_ref.at[i, 2 * k], rows_ref.at[i, 2 * k + 1],
-                c_send.at[i, k, 0], c_recv.at[i, k, 0], core,
-            )
-            cp.start()
-            passed.append(cp)
-
-    ring_left = list(range(2, NT // 2 + 1))
-    images_left = list(range(I))
-    while ring_left or images_left:
-        if images_left:
-            land_image(images_left.pop(0))
-        if ring_left:
-            d = ring_left.pop(0)
-            land_hop(d)
-            if d < NT // 2:
-                start_hop(d + 1)
-    for cp in own + passed + mods:
+    images.land(0)
+    for d in range(2, NT // 2 + 1):
+        land_hop(d)
+        if d < NT // 2:
+            start_hop(d + 1)
+    images.finish(0)
+    for cp in mods:
         cp.wait_recv()
-    for cp in locals_:
-        cp.wait()
-    for cp in small + mods + own + passed + list(sent.values()) + list(hops.values()):
+    keep.wait()
+    images.left(0)
+    for cp in small + mods + list(hops.values()):
         cp.wait_send()
 
 
 def start_call(NT, NP, x, w, msg, ada, gates, bias, mask):
-    I, CB, length = x.shape
+    _, CB, length = x.shape
     NX = NP // 2
     RB, WN = w.shape
     wide = 6 * ML + 128
@@ -237,10 +257,11 @@
     dma = pltpu.SemaphoreType.DMA
     return pl.pallas_call(
         functools.partial(start_kernel, NT, NP),
-        in_specs=[hbm, hbm] + [vmem] * 5,
+        in_specs=[pl.BlockSpec((1, CB, length), lambda i: (0, 0, 0))] + [vmem] * 6,
+        grid=(1,),
         out_specs=[hbm, hbm, vmem, vmem, vmem],
         out_shape=[
-            jax.ShapeDtypeStruct((I, NP, CB, length), bf16),
+            jax.ShapeDtypeStruct((1, NP, CB, length), bf16),
             jax.ShapeDtypeStruct((NT, RB, WN), bf16),
             jax.ShapeDtypeStruct((NP, 8, wide), f32),
             jax.ShapeDtypeStruct((8, 128), f32),
@@ -249,15 +270,15 @@
         scratch_shapes=[
             pltpu.VMEM((NT, 8, wide), f32),
             pltpu.VMEM((NT, 8, wide), f32),
-            dma((I, NX, NX)),
-            dma((I, NX, NX)),
-            dma((I, NX, NX)),
-            dma((I, NX, NX)),
+            dma((1, NX, NX)),
+            dma((1, NX, NX)),
+            dma((1, NX, NX)),
+            dma((1, NX, NX)),
             dma((2, NT // 2 + 1)),
             dma((2, NT // 2 + 1)),
             dma((3, max(NT, NP))),
             dma((3, max(NT, NP))),
-            dma((I + 1, NX)),
+            dma((2, NX)),
         ],
         compiler_params=pltpu.CompilerParams(
             collective_id=0, has_side_effects=True, vmem_limit_bytes=32 * 2**20
@@ -266,11 +287,18 @@
     )(x, w, msg, ada, gates, bias, mask)
 
 
+def spread(mods_ref, r, rows, CB):
+    parts = [mods_ref[r, row, at : at + ML] for row, at in rows]
+    parts += [jnp.zeros((8 - len(parts), ML), f32)] if len(parts) < 8 else []
+    return jnp.concatenate(parts, axis=0).T[:CB]
+
+
 def fwd_kernel(
-    NT, NP, gate_ref, rows_ref, w_ref, mod_ref, bias_ref, late_ref,
-    attn_ref, qkv_ref, mixed_ref, concat_ref, lse_ref, stats_ref, branch_ref, full_ref,
+    NT, NP, gate_ref, x_ref, cot_ref, first_ref, w_ref, mod_ref, bias_ref, late_ref,
+    attn_ref, qkv_ref, mixed_ref, concat_ref, lse_ref, stats_ref, branch_ref, full_ref, rows_ref, cots_ref,
     wt_ref, own_ref, core_out, core_in, x_out, x_in, total_ref,
-    l_send, l_recv, c_send, c_recv, x_send, x_recv, b_send, b_recv, local_sem,
+    mcol_ref, l_send, l_recv, c_send, c_recv, x_send, x_recv, b_send, b_recv, local_sem,
+    rows_buf, rx_send, rx_recv, rc_send, rc_recv, r_sem, t_send, t_recv, t_sem,
 ):
     NX, SUB = NP // 2, NT // NP
     I, CB, T = total_ref.shape[0], total_ref.shape[2], total_ref.shape[3]
@@ -288,6 +316,48 @@
     def at(n):
         return pl.when(flat == n)
 
+    images = ImageMoves(NP, x_ref, rows_ref, rx_send, rx_recv, rc_send, rc_recv, r_sem)
+
+    def first_keep():
+        return pltpu.make_async_copy(rows_buf, rows_ref.at[0], r_sem.at[0, 0])
+
+    def load_rows(n):
+        if n:
+            images.finish(n)
+        if n == 1:
+            first_keep().wait()
+        src = rows_ref.at[n] if n else first_ref.at[0]
+        cp = pltpu.make_async_copy(src, rows_buf, r_sem.at[I, 0])
+        cp.start()
+        cp.wait()
+        if n == 0:
+            first_keep().start()
+
+    def cot_x(n, k):
+        src = cot_ref.at[n, :, images.tokens(xor(p // 2, k), 0)]
+        return copy_to(
+            src, cots_ref.at[n, k, 0], t_send.at[0, n, k], t_recv.at[0, n, k], (t, xor(p, 2 * k))
+        )
+
+    def cot_keep(n):
+        src = cot_ref.at[n, :, images.tokens(p // 2, 0)]
+        return pltpu.make_async_copy(src, cots_ref.at[n, 0, 0], t_sem.at[n])
+
+    def cot_core(n, k):
+        src = cots_ref.at[n, k, 0] if k else cot_ref.at[n, :, images.tokens(p // 2, 0)]
+        return copy_to(src, cots_ref.at[n, k, 1], t_send.at[1, n, k], t_recv.at[1, n, k], core)
+
+    def start_cot():
+        for n in range(I):
+            for k in range(1, NX):
+                cot_x(n, k).start()
+
+    def land_cot():
+        for n in range(I):
+            for k in range(1, NX):
+                cot_x(n, k).wait_recv()
+                cot_core(n, k).start()
+
     def where(tt):
         out = 0
         for r in range(NP):
@@ -360,25 +430,46 @@
         for peer in peers:
             pl.semaphore_signal(barrier, inc=1, device_id=peer, device_id_type=MESH)
         pl.semaphore_wait(barrier, len(peers))
+        if I > 1:
+            images.start(1)
         for k in range(NX):
             start_hop(k, 1)
+        for n in range(I):
+            cot_keep(n).start()
+            cot_core(n, 0).start()
         for k in range(NX):
             keep(k).start()
         wt_ref[...] = w_ref[:, :QKV].T
 
+    for n in range(I):
+        if n:
+
+            @at((n - 1) * steps + HL)
+            def _(n=n):
+                images.land(n)
+                if n + 1 < I:
+                    images.start(n + 1)
+                else:
+                    start_cot()
+
+        at(n * steps)(functools.partial(load_rows, n))
+
     @pl.when(s == 0)
     def _():
+        for r in range(NP):
+            rows = [(pl.ds(i, 1), 0), (pl.ds(i, 1), ML)]
+            mcol_ref[r * CB : (r + 1) * CB] = spread(mod_ref, r, rows, CB)
         width = 256
         for j in range(LEN // width):
             cols = slice(j * width, (j + 1) * width)
-            v = rows_ref[0, :, cols].astype(f32)
+            v = rows_buf[:, :, cols].reshape(D, width).astype(f32)
             centre = jnp.sum(v, axis=0, keepdims=True) * (1.0 / D)
             square = jnp.sum(v * v, axis=0, keepdims=True) * (1.0 / D)
             inverse = lax.rsqrt(square - centre * centre + EPS)
             stats_ref[0, 0:1, cols] = centre
             stats_ref[0, 1:2, cols] = inverse
             n = (v - centre) * inverse
-            a = (n * (1.0 + mod_ref[0, :, 1:2]) + mod_ref[0, :, 0:1]).astype(bf16)
+            a = (n * (1.0 + mcol_ref[:, 1:2]) + mcol_ref[:, 0:1]).astype(bf16)
             attn_ref[0, :, cols] = a
             out = jnp.dot(wt_ref[...], a, preferred_element_type=f32) + bias_ref[...]
             qkv_ref[0, :, cols] = out.astype(bf16)
@@ -424,7 +515,10 @@
 
     @at(I * steps - 1)
     def _():
+        if I == 1:
+            start_cot()
         add_core(I - 1)
+        land_cot()
         rest = events[len(early) :]
         for n, (k, d) in enumerate(rest):
             land_hop(k, d)
@@ -432,6 +526,17 @@
                 add_x(I - 1)
         for n in range(I):
             back_copy(n).wait_recv()
+        if I == 1:
+            first_keep().wait()
+        for n in range(I):
+            if n:
+                images.left(n)
+            cot_keep(n).wait()
+            for k in range(NX):
+                cot_core(n, k).wait_recv()
+                cot_core(n, k).wait_send()
+                if k:
+                    cot_x(n, k).wait_send()
         for n in range(I):
             core_copy(n).wait_send()
             back_copy(n).wait_send()
@@ -445,32 +550,32 @@
                     hop(k, d, side).wait_send()
 
 
-def fwd_call(NT, NP, gate, rows, w, mods, bias, late):
-    I, _, length = rows.shape
+def fwd_call(NT, NP, gate, x, cot, first, w, mods, bias, late):
+    I, _, length = x.shape
     NX = NP // 2
     CB, T = D // NP, length // NX
     HL = gate.shape[0] // I
     QKV = 3 * HL * HP
     RB, FL = late.shape[2:]
     hbm = pl.BlockSpec(memory_space=pl.ANY)
+    vmem = pl.BlockSpec(memory_space=pltpu.VMEM)
     dma = pltpu.SemaphoreType.DMA
 
     def image(*shape):
         return pl.BlockSpec((1,) + shape, lambda i, s: (i,) + (0,) * len(shape))
-
-    def whole(*shape):
-        return pl.BlockSpec(shape, lambda i, s: (0,) * len(shape))
 
     return pl.pallas_call(
         functools.partial(fwd_kernel, NT, NP),
         grid=(I, HL + 2),
         in_specs=[
             pl.BlockSpec(memory_space=pltpu.SMEM),
-            image(D, length),
-            whole(*w.shape),
-            image(D, mods.shape[2]),
-            whole(*bias.shape),
+            vmem,
+            vmem,
             hbm,
+            vmem,
+            vmem,
+            vmem,
+            vmem,
         ],
         out_specs=[
             image(D, length),
@@ -479,6 +584,8 @@
             image(HL * HP, length),
             image(HL, length),
             image(8, length),
+            hbm,
+            hbm,
             hbm,
             hbm,
         ],
@@ -491,6 +598,8 @@
             jax.ShapeDtypeStruct((I, 8, length), f32),
             jax.ShapeDtypeStruct((I, 2, NX, CB, T), f32),
             jax.ShapeDtypeStruct((NX, 2, NT, RB, FL), bf16),
+            jax.ShapeDtypeStruct((I, NP, CB, length), bf16),
+            jax.ShapeDtypeStruct((I, NX, 2, CB, T), bf16),
         ],
         scratch_shapes=[
             pltpu.VMEM((QKV, D), bf16),
@@ -500,6 +609,7 @@
             pltpu.VMEM((I, NX, NX, CB, T), bf16),
             pltpu.VMEM((I, NX, NX, CB, T), bf16),
             pltpu.VMEM((I, NX, CB, T), f32),
+            pltpu.VMEM((D, 8), f32),
             dma((NX, 2, NT // 2 + 1)),
             dma((NX, 2, NT // 2 + 1)),
             dma((I,)),
@@ -509,16 +619,343 @@
             dma((I,)),
             dma((I,)),
             dma((NX + I,)),
+            pltpu.VMEM((NP, CB, length), bf16),
+            dma((I, NX, NX)),
+            dma((I, NX, NX)),
+            dma((I, NX, NX)),
+            dma((I, NX, NX)),
+            dma((I + 1, NX)),
+            dma((2, I, NX)),
+            dma((2, I, NX)),
+            dma((I,)),
         ],
         compiler_params=pltpu.CompilerParams(
             collective_id=2, has_side_effects=True, vmem_limit_bytes=60 * 2**20
         ),
         name="forward",
-    )(gate, rows, w, mods, bias, late)
+    )(gate, x, cot, first, w, mods, bias, late)
+
+
+def lane_sum(v):
+    total = v[:, :128]
+    for j in range(1, v.shape[1] // 128):
+        total = total + v[:, j * 128 : (j + 1) * 128]
+    return jnp.sum(total.T, axis=0, keepdims=True)
+
+
+def mlp_kernel(
+    NT, NP, branch_ref, rows_ref, cot_ref, mods_ref, gate_ref, w_ref,
+    lhs_ref, rhs_ref, go_ref, gms_ref, gm_ref, sums_ref, fsums_ref, out_ref, go0_ref,
+    mid_ref, gn_ref, b2_ref, st_ref, gn_out, gn_in, b2_out, b2_in, o_buf,
+    mcol_ref, g_send, g_recv, b_send, b_recv, x_send, x_recv, local_sem, go_buf, f_send, f_recv,
+):
+    NX = NP // 2
+    _, _, D_, T = lhs_ref.shape
+    CB = D // NP
+    I = pl.num_programs(0)
+    FL = w_ref.shape[3]
+    i = pl.program_id(0)
+    slot = i % 2
+    t, p = lax.axis_index("tok"), lax.axis_index("tp")
+    xi = p // 2
+    core = (t, xor(p, 1))
+
+    def gn_copy(n):
+        return copy_to(gn_out, gn_in.at[n % 2], g_send.at[n], g_recv.at[n], core)
+
+    def b2_copy(n):
+        return copy_to(b2_out, b2_in.at[n % 2], b_send.at[n], b_recv.at[n], core)
+
+    def place(n):
+        return out_ref.at[n, :, pl.ds(pl.multiple_of(xi * T, T), T)]
+
+    def out_copy(n, k):
+        return copy_to(
+            o_buf.at[n % 2, k], place(n), x_send.at[n, k], x_recv.at[n, k], (t, xor(p, 2 * k))
+        )
+
+    def out_keep(n):
+        return pltpu.make_async_copy(o_buf.at[n % 2, 0], place(n), local_sem.at[n])
+
+    def out_left(n):
+        out_keep(n).wait()
+        for k in range(1, NX):
+            out_copy(n, k).wait_send()
+
+    def go_x(k, f):
+        return copy_to(
+            go_buf.at[f], go0_ref.at[k, f ^ k, 0], f_send.at[0, k, f], f_recv.at[0, k, f],
+            (t, xor(p, 2 * k)),
+        )
+
+    def go_core(k, f):
+        return copy_to(
+            go0_ref.at[k, f, 0], go0_ref.at[k, f, 1], f_send.at[1, k, f], f_recv.at[1, k, f], core
+        )
+
+    @pl.when(i == 0)
+    def _():
+        barrier = pltpu.get_barrier_semaphore()
+        peers = [core] + [(t, xor(p, 2 * k)) for k in range(1, NX)]
+        for peer in peers:
+            pl.semaphore_signal(barrier, inc=1, device_id=peer, device_id_type=MESH)
+        pl.semaphore_wait(barrier, len(peers))
+
+    count = out_ref.shape[0]
+    for r in range(NP):
+        rows = [(pl.ds(i, 1), k * ML) for k in range(6)]
+        rows += [(slice(count, count + 1), 0), (slice(count, count + 1), ML)]
+        mcol_ref[r * CB : (r + 1) * CB] = spread(mods_ref, r, rows, CB)
+
+    def col(k):
+        return mcol_ref[:, k : k + 1]
+
+    width = min(256, T)
+    chunks = [slice(j * width, (j + 1) * width) for j in range(T // width)]
+
+    def branch_one(cols):
+        parts = [branch_ref[0, r % 2, r // 2, :, cols] for r in range(NP)]
+        return jnp.concatenate(parts, axis=0) + col(6)
+
+    for cols in chunks:
+        x = jnp.concatenate([rows_ref[0, r, :, cols] for r in range(NP)], axis=0).astype(f32)
+        mid = x + col(2) * branch_one(cols)
+        mid_ref[:, cols] = mid
+        centre = jnp.sum(mid, axis=0, keepdims=True) * (1.0 / D)
+        square = jnp.sum(mid * mid, axis=0, keepdims=True) * (1.0 / D)
+        inverse = lax.rsqrt(square - centre * centre + EPS)
+        st_ref[0:1, cols] = centre
+        st_ref[1:2, cols] = inverse
+        n = (mid - centre) * inverse
+        lhs_ref[0, 0, :, cols] = (n * (1.0 + col(4)) + col(3)).astype(bf16)
+        lhs_ref[0, 1, :, cols] = (col(5) * cot_ref[0, :, cols].astype(f32)).astype(bf16)
+
+    root = math.sqrt(2.0 / math.pi)
+    tile = 384
+    for k in range(NX):
+        for at in range(0, FL, tile):
+            rows = slice(at, min(at + tile, FL))
+            size = rows.stop - rows.start
+            vec = [gate_ref[k, pl.ds(i, 1), rows], mods_ref[2 * k, count + 1 : count + 2, rows]]
+            vec = jnp.concatenate(vec + [jnp.zeros((6, size), f32)], axis=0).T
+            pre = dot(w_ref[k, 0, :, rows], lhs_ref[0, 0], 0, 0) + vec[:, 1:2]
+            grad_hid = dot(w_ref[k, 1, :, rows], lhs_ref[0, 1], 0, 0)
+            gate = vec[:, 0:1]
+            square = pre * pre
+            inner = jnp.tanh(pre * (root + (root * 0.044715) * square))
+            half = 0.5 * (1.0 + inner)
+            act = pre * half
+            slope = half + (0.5 * pre) * (1.0 - inner * inner) * (root + (3.0 * root * 0.044715) * square)
+            rhs_ref[0, 1, k, rows] = (act * gate).astype(bf16)
+            grad_pre = (slope * gate * grad_hid).astype(bf16)
+            rhs_ref[0, 0, k, rows] = grad_pre
+            to = slice(k * FL + rows.start, k * FL + rows.stop)
+            fsums_ref[0, 0:1, to] = lane_sum(grad_pre.astype(f32))
+            fsums_ref[0, 1:2, to] = lane_sum(grad_hid * act)
+
+    def product(u, r):
+        total = 0.0
+        for k in range(NX):
+            w = w_ref[k, u, r * CB : (r + 1) * CB]
+            total = total + jnp.dot(w, rhs_ref[0, u, k], preferred_element_type=f32)
+        return total
+
+    for r in range(NP):
+        v = product(0, r)
+        gn_ref[r * CB : (r + 1) * CB] = v
+        gn_out[r * CB : (r + 1) * CB] = v.astype(bf16)
+    gn_copy(i).start()
+    for r in range(NP):
+        v = product(1, r)
+        if r % 2:
+            b2_out[r // 2] = v.astype(bf16)
+        else:
+            b2_ref[r // 2] = v
+    b2_copy(i).start()
+
+    gn_copy(i).wait_recv()
+    gn_copy(i).wait_send()
+    for r in range(NP):
+        mine, theirs = slice(r * CB, (r + 1) * CB), slice((r ^ 1) * CB, ((r ^ 1) + 1) * CB)
+        gn_ref[mine] = gn_ref[mine] + gn_in[slot, theirs].astype(f32)
+    totals = [0.0] * 5
+
+    def fold(v):
+        total = v[:, :128]
+        for j in range(1, v.shape[1] // 128):
+            total = total + v[:, j * 128 : (j + 1) * 128]
+        return total
+
+    for cols in chunks:
+        gnorm = gn_ref[:, cols]
+        inverse = st_ref[1:2, cols]
+        n = (mid_ref[:, cols] - st_ref[0:1, cols]) * inverse
+        g = gnorm * (1.0 + col(4))
+        mean_g = jnp.sum(g, axis=0, keepdims=True) * (1.0 / D)
+        mean_gn = jnp.sum(g * n, axis=0, keepdims=True) * (1.0 / D)
+        grad_mid = cot_ref[0, :, cols].astype(f32) + inverse * (g - mean_g - n * mean_gn)
+        grad_one = (col(2) * grad_mid).astype(bf16)
+        go_ref[0, :, cols] = grad_one
+        gm_ref[0, :, cols] = grad_mid[:CB]
+        for k in range(NX):
+            gms_ref[0, k, :, cols] = grad_mid[2 * k * CB : (2 * k + 1) * CB].astype(bf16)
+        terms = (
+            grad_mid * branch_one(cols),
+            gnorm,
+            gnorm * n,
+            grad_one.astype(f32),
+            lhs_ref[0, 1, :, cols].astype(f32),
+        )
+        totals = [a + fold(b) for a, b in zip(totals, terms)]
+    @pl.when(i == 0)
+    def _():
+        for f in range(NX):
+            go_buf[f] = go_ref[0, 2 * f * CB : (2 * f + 1) * CB]
+        for k in range(1, NX):
+            for f in range(NX):
+                go_x(k, f).start()
+
+    for row, v in enumerate(totals):
+        sums_ref[0, row : row + 1, :] = jnp.sum(v.T, axis=0, keepdims=True)
+
+    @pl.when(i >= 2)
+    def _():
+        out_left(i - 2)
+
+    b2_copy(i).wait_recv()
+    b2_copy(i).wait_send()
+    for f in range(NX):
+        rows = slice(2 * f * CB, (2 * f + 1) * CB)
+        v = b2_ref[f] + b2_in[slot, f].astype(f32) + mcol_ref[rows, 7:8]
+        sums_ref[0, 5 : 6, f * CB : (f + 1) * CB] = lane_sum(cot_ref[0, rows].astype(f32) * v)
+        o_buf[slot, f] = (mid_ref[rows] + mcol_ref[rows, 5:6] * v).astype(bf16)
+    out_keep(i).start()
+    for k in range(1, NX):
+        out_copy(i, k).start()
+
+    @pl.when(i == I - 1)
+    def _():
+        for k in range(1, NX):
+            for f in range(NX):
+                go_x(k, f ^ k).wait_recv()
+                go_core(k, f).start()
+        for n in range(x_send.shape[0]):
+            for k in range(1, NX):
+                out_copy(n, k).wait_recv()
+            if n >= x_send.shape[0] - 2:
+                out_left(n)
+        for k in range(1, NX):
+            for f in range(NX):
+                go_core(k, f).wait_recv()
+                go_core(k, f).wait_send()
+                go_x(k, f).wait_send()
+
+
+def mlp_call(NT, NP, branch, rows, cot, mods, gates, w):
+    I, NX = branch.shape[0], NP // 2
+    CB, T = branch.shape[3:]
+    FL = w.shape[3]
+    hbm = pl.BlockSpec(memory_space=pl.ANY)
+    vmem = pl.BlockSpec(memory_space=pltpu.VMEM)
+    dma = pltpu.SemaphoreType.DMA
+
+    def image(*shape):
+        return pl.BlockSpec((1,) + shape, lambda i: (i,) + (0,) * len(shape))
+
+    return pl.pallas_call(
+        functools.partial(mlp_kernel, NT, NP),
+        grid=(I,),
+        in_specs=[
+            pl.BlockSpec(
+                (1, 2, NX, CB, T), lambda i: (i, 0, 0, 0, 0), pipeline_mode=pl.Buffered(buffer_count=1)
+            ),
+            image(NP, CB, T),
+            image(D, T),
+            vmem,
+            vmem,
+            vmem,
+        ],
+        out_specs=[
+            image(2, D, T),
+            image(2, NX, FL, T),
+            image(D, T),
+            image(NX, CB, T),
+            image(CB, T),
+            image(8, D),
+            image(8, NX * FL),
+            hbm,
+            hbm,
+        ],
+        out_shape=[
+            jax.ShapeDtypeStruct((I, 2, D, T), bf16),
+            jax.ShapeDtypeStruct((I, 2, NX, FL, T), bf16),
+            jax.ShapeDtypeStruct((I, D, T), bf16),
+            jax.ShapeDtypeStruct((I, NX, CB, T), bf16),
+            jax.ShapeDtypeStruct((I, CB, T), f32),
+            jax.ShapeDtypeStruct((I, 8, D), f32),
+            jax.ShapeDtypeStruct((I, 8, NX * FL), f32),
+            jax.ShapeDtypeStruct((I, CB, NX * T), bf16),
+            jax.ShapeDtypeStruct((NX, NX, 2, CB, T), bf16),
+        ],
+        scratch_shapes=[
+            pltpu.VMEM((D, T), f32),
+            pltpu.VMEM((D, T), f32),
+            pltpu.VMEM((NX, CB, T), f32),
+            pltpu.VMEM((8, T), f32),
+            pltpu.VMEM((D, T), bf16),
+            pltpu.VMEM((2, D, T), bf16),
+            pltpu.VMEM((NX, CB, T), bf16),
+            pltpu.VMEM((2, NX, CB, T), bf16),
+            pltpu.VMEM((2, NX, CB, T), bf16),
+            pltpu.VMEM((D, 8), f32),
+            dma((I,)),
+            dma((I,)),
+            dma((I,)),
+            dma((I,)),
+            dma((I, NX)),
+            dma((I, NX)),
+            dma((I,)),
+            pltpu.VMEM((NX, CB, T), bf16),
+            dma((2, NX, NX)),
+            dma((2, NX, NX)),
+        ],
+        compiler_params=pltpu.CompilerParams(
+            collective_id=3, has_side_effects=True, vmem_limit_bytes=60 * 2**20
+        ),
+        name="feed_forward",
+    )(branch, rows, cot, mods, gates, w)
+
+
+def grads_kernel(lhs_ref, rhs_ref, out_ref):
+    I, _, rows, _ = lhs_ref.shape
+    NT, RB = out_ref.shape[2:4]
+    for b in range(0, NT, 2):
+        total = 0.0
+        for i in range(I):
+            a = lhs_ref[i, 0, b * RB : (b + 2) * RB]
+            total = total + dot(a, rhs_ref[i, 0, 0], 1, 1)
+        out_ref[0, 0, b : b + 2] = total.astype(bf16).reshape(2, RB, -1)
+
+
+def grads_call(NT, lhs, rhs):
+    I, _, NX, FL, T = rhs.shape
+    RB = D // NT
+    return pl.pallas_call(
+        grads_kernel,
+        grid=(2, NX),
+        in_specs=[
+            pl.BlockSpec((I, 1, D, T), lambda u, k: (0, u, 0, 0)),
+            pl.BlockSpec((I, 1, 1, FL, T), lambda u, k: (0, u, k, 0, 0)),
+        ],
+        out_specs=pl.BlockSpec((1, 1, NT, RB, FL), lambda u, k: (k, u, 0, 0, 0)),
+        out_shape=jax.ShapeDtypeStruct((NX, 2, NT, RB, FL), bf16),
+        compiler_params=pltpu.CompilerParams(vmem_limit_bytes=48 * 2**20),
+        name="late_grads",
+    )(lhs, rhs)
 
 
 def bwd_kernel(
-    NT, NP, gate_ref, go_ref, gms_ref, gm_ref, qkv_ref, mixed_ref, lse_ref, concat_ref, attn_ref,
+    NT, NP, gate_ref, go_ref, go0_ref, gms_ref, gm_ref, qkv_ref, mixed_ref, lse_ref, concat_ref, attn_ref,
     rows_ref, stats_ref, scale_ref, w_ref, late_ref, base_ref, factor_ref, ada_ref,
     gin_ref, late_out, gqkv_ref, gout_ref, lasts_ref, cond_ref, gox_ref,
     go_buf, gmx_ref, own_ref, core_out, core_in, x_out, x_in, gn_ref, accq_ref, acco_ref, wt_ref,
@@ -589,12 +1026,12 @@
 
     def load_go(n):
         def load(k):
-            src = go_ref.at[n] if k == 0 else gox_ref.at[n, k]
+            src = go_ref.at[n] if k == 0 else gox_ref.at[n, k] if n else go0_ref.at[k]
             return pltpu.make_async_copy(src, go_buf.at[k], local_sem.at[k])
 
         load(0).start()
         for k in range(1, NX):
-            for f in range(NX):
+            for f in range(NX if n else 0):
                 go_core(n, k, f).wait_recv()
             load(k).start()
         for k in range(NX):
@@ -642,6 +1079,9 @@
             total = total + v[:, j * 128 : (j + 1) * 128]
         return jnp.sum(total.T, axis=0, keepdims=True)
 
+    def own_scale(n):
+        return 1.0 + scale_ref[0, :, ML : 2 * ML].T[:CB, n : n + 1]
+
     def normed(n):
         return (rows_buf[n].astype(f32) - stats_ref[n, 0:1]) * stats_ref[n, 1:2]
 
@@ -655,7 +1095,7 @@
             gn_ref[:, j * T : (j + 1) * T] = v
         v = gn_ref[...]
         vn = v * normed(n)
-        scale = 1.0 + scale_ref[n]
+        scale = own_scale(n)
         st_out[n, 0:1] = jnp.sum(v * scale, axis=0, keepdims=True)
         st_out[n, 1:2] = jnp.sum(vn * scale, axis=0, keepdims=True)
         for r in range(1, NP):
@@ -680,7 +1120,7 @@
                 b = b + st_in[n, r, 1:2, m * T : (m + 1) * T]
             centre, inverse = stats_ref[n, 0:1, cols], stats_ref[n, 1:2, cols]
             nrm = (rows_buf[n, :, cols].astype(f32) - centre) * inverse
-            g = gn_ref[:, cols] * (1.0 + scale_ref[n])
+            g = gn_ref[:, cols] * own_scale(n)
             mid = gm_ref[n] if j == 0 else gmx_ref[n, j - 1].astype(f32)
             gin_buf[n % 2, :, cols] = mid + inverse * (g - a * (1.0 / D) - nrm * (b * (1.0 / D)))
         for j in range(NX):
@@ -834,7 +1274,8 @@
     @at(0)
     def _():
         greet(t, p, NT, NP)
-        send_go(0)
+        if I > 1:
+            send_go(1)
         for k in range(NX):
             for side in range(2):
                 l_hop(k, side, 0).start()
@@ -851,7 +1292,8 @@
             rows_copy(n).wait()
 
     for n in range(I):
-        at(max(n - 1, 0) * steps + (HL if n else 0))(functools.partial(pass_go, n))
+        if n:
+            at((n - 1) * steps + HL)(functools.partial(pass_go, n))
         at(n * steps)(functools.partial(load_go, n))
 
     @pl.when(s == 0)
@@ -930,7 +1372,7 @@
             core_copy(n).wait_send()
 
     events = [functools.partial(l_event, k, h) for h in range(1, HOPS + 1) for k in range(NX)]
-    early = [steps - 1, steps, 2 * steps - 2, 2 * steps - 1, 3 * steps - 2, 3 * steps - 1] if I > 2 else []
+    early = [2, 3, steps + HL - 1, steps + HL, 3 * steps - 2, 3 * steps - 1] if I > 2 else []
     early = early[: len(events)]
     for n, event in zip(early, events):
         at(n)(event)
@@ -959,7 +1401,7 @@
         for n in range(I):
             for k in range(1, NX):
                 gm_x(n, k).wait_send()
-                for f in range(NX):
+                for f in range(NX if n else 0):
                     go_x(n, k, f).wait_send()
                     go_core(n, k, f).wait_send()
                 if n >= I - 2:
@@ -986,7 +1428,7 @@
 
 
 def bwd_call(
-    NT, NP, gate, go, gms, gm, qkv, mixed, lse, concat, attn, rows, stats, scale, w, late, base, factor, ada
+    NT, NP, gate, go, go0, gms, gm, qkv, mixed, lse, concat, attn, rows, stats, scale, w, late, base, factor, ada
 ):
     I, CB, T = gm.shape
     NX = NP // 2
@@ -1011,6 +1453,7 @@
         grid=(I, HL + 2),
         in_specs=[
             pl.BlockSpec(memory_space=pltpu.SMEM),
+            hbm,
             hbm,
             hbm,
             vmem,
@@ -1094,7 +1537,7 @@
             collective_id=1, has_side_effects=True, vmem_limit_bytes=63 * 2**20
         ),
         name="backward",
-    )(gate, go, gms, gm, qkv, mixed, lse, concat, attn, rows, stats, scale, w, late, base, factor, ada)
+    )(gate, go, go0, gms, gm, qkv, mixed, lse, concat, attn, rows, stats, scale, w, late, base, factor, ada)
 
 
 def make_body(NT, NP):
@@ -1138,13 +1581,6 @@
         p = lax.axis_index("tp")
         xi = p // 2
 
-        def own_order(v, axis):
-            parts = [
-                lax.dynamic_slice_in_dim(v, jnp.bitwise_xor(j, xi) * T, T, axis=axis)
-                for j in range(NX)
-            ]
-            return jnp.concatenate(parts, axis=axis)
-
         qkv_shard = jnp.pad(
             w_qkv.reshape(RB, 3, HL, HD), ((0, 0), (0, 0), (0, 0), (0, HP - HD))
         ).reshape(RB, 3 * HL * HP)
@@ -1188,7 +1624,7 @@
             axis=0,
         )
         mask = pad8(jnp.concatenate([head_mask, group_mask], axis=1).astype(f32), 128)
-        rows_all, early_full, mods, sig, cond_all = start_call(
+        first, early_full, mods, sig, cond_all = start_call(
             NT,
             NP,
             block_input,
@@ -1199,34 +1635,15 @@
             bias,
             mask,
         )
-        rows_full = [rows_all[i].reshape(D, LEN) for i in range(I)]
         early_full = early_full.reshape(D, -1)
-        qkv_full, out_full = early_full[:, :QKV], early_full[:, QKV + gap :]
         head_sig, group_sig = sig[:I, :HL], sig[:I, HL : HL + GL]
         head_gate = mods[0, :I, 6 * ML : 6 * ML + HL]
-        vectors = mods[:, :I, : 6 * ML].reshape(NP, I * 6, ML)[:, :, :CB]
-        biases_two = mods[:, I, : 2 * ML].reshape(NP, 2, ML)[:, :, :CB]
-        columns = jnp.concatenate([vectors, biases_two], axis=1).transpose(0, 2, 1).reshape(D, -1)
-
-        def mod(i, k):
-            return lax.slice_in_dim(columns, i * 6 + k, i * 6 + k + 1, axis=1)
-
-        out_bias = columns[:, I * 6 : I * 6 + 1]
-        down_bias = columns[:, I * 6 + 1 : I * 6 + 2]
-        gates_x = jnp.concatenate(
-            [mods[2 * k, :I, 6 * ML + HL : 6 * ML + HL + GL] for k in range(NX)], axis=1
-        )
-        gate_cols = jnp.repeat(gates_x, GW, axis=1).T
-        up_bias = jnp.concatenate([mods[2 * k, I + 1, :FL] for k in range(NX)])[:, None]
-
-        cot_in = own_order(cotangent, 2)
-        cot_blocks = []
-        for k in range(NX):
-            v = cot_in[:, :, k * T : (k + 1) * T]
-            v = v if k == 0 else tp_xor(v, 2 * k)
-            cot_blocks.append(v)
-        cot_half = jnp.stack(cot_blocks, axis=1)
-        cot_full = jnp.stack([cot_half, tp_xor(cot_half, 1)], axis=2).reshape(I, D, T)
+        group_rows = jnp.stack(
+            [
+                jnp.repeat(mods[2 * k, :, 6 * ML + HL : 6 * ML + HL + GL], GW, axis=1)
+                for k in range(NX)
+            ]
+        )
 
         qv = b_qv.astype(f32).reshape(2, HL, HD)
         qv_bias = jnp.stack(
@@ -1239,111 +1656,52 @@
             ]
         ).reshape(3 * HL * HP, 1)
 
-        def stats(v):
-            centre = jnp.sum(v, axis=0, keepdims=True) * (1.0 / D)
-            square = jnp.sum(v * v, axis=0, keepdims=True) * (1.0 / D)
-            return centre, lax.rsqrt(square - centre * centre + EPS)
-
-        image_mods = columns[:, : I * 6].reshape(D, I, 6).transpose(1, 0, 2)
-        attn_all, qkv_all, mixed_all, concat_all, lse_all, stats_all, branch, late_full = fwd_call(
+        attn_all, qkv_all, mixed_all, concat_all, lse_all, stats_all, branch, late_full, rows_all, cots = (
+            fwd_call(
+                NT,
+                NP,
+                head_gate.reshape(-1),
+                block_input,
+                cotangent,
+                first,
+                early_full,
+                mods,
+                qv_bias,
+                late_shards,
+            )
+        )
+        late_full = late_full.reshape(NX, 2, D, FL)
+
+        lhs, rhs, grad_one, grad_mid_out, grad_mid_own, sums, fsums, block_output, go_first = mlp_call(
             NT,
             NP,
-            head_gate.reshape(-1),
-            rows_all.reshape(I, D, LEN),
-            early_full,
-            image_mods,
-            qv_bias,
-            late_shards,
-        )
-        late_full = late_full.reshape(NX, 2, D, FL)
-        up_full = jnp.concatenate([late_full[k, 0] for k in range(NX)], axis=1)
-        down_full = jnp.concatenate([late_full[k, 1] for k in range(NX)], axis=1)
-        branch = branch.transpose(0, 2, 1, 3, 4).reshape(I, D, T)
-        mids = []
-        for i in range(I):
-            branch_one = branch[i] + out_bias
-            cot = cot_full[i].astype(f32)
-            mid_rows = rows_full[i][:, :T].astype(f32) + mod(i, 2) * branch_one
-            centre, inverse = stats(mid_rows)
-            normed = (mid_rows - centre) * inverse
-            mlp_in = (normed * (1.0 + mod(i, 4)) + mod(i, 3)).astype(bf16)
-            grad_two = (mod(i, 5) * cot).astype(bf16)
-            pre = dot(up_full, mlp_in, 0, 0) + up_bias
-            grad_hid = dot(down_full, grad_two, 0, 0)
-            gate = gate_cols[:, i : i + 1]
-            inner = jnp.tanh(math.sqrt(2.0 / math.pi) * (pre + 0.044715 * pre * pre * pre))
-            act = 0.5 * pre * (1.0 + inner)
-            slope = 0.5 * (1.0 + inner) + 0.5 * pre * (1.0 - inner * inner) * math.sqrt(
-                2.0 / math.pi
-            ) * (1.0 + 3.0 * 0.044715 * pre * pre)
-            hidden = (act * gate).astype(bf16)
-            grad_pre = (slope * gate * grad_hid).astype(bf16)
-            gate_sums = jnp.sum(jnp.sum(grad_hid * act, axis=1).reshape(NX * GL, GW), axis=1)
-            up_sums = jnp.sum(grad_pre.astype(f32), axis=1)
-            gpart = dot(up_full, grad_pre, 1, 0)
-            got = tp_xor(gpart.astype(bf16), 1).reshape(NX, 2, CB, T)
-            got = jnp.stack([got[:, 1], got[:, 0]], axis=1).reshape(D, T)
-            gnorm = gpart + got.astype(f32)
-            shift_sums = jnp.sum(gnorm, axis=1)
-            scale_sums = jnp.sum(gnorm * normed, axis=1)
-            g = gnorm * (1.0 + mod(i, 4))
-            mean_g = jnp.sum(g, axis=0, keepdims=True) * (1.0 / D)
-            mean_gn = jnp.sum(g * normed, axis=0, keepdims=True) * (1.0 / D)
-            grad_mid = cot + inverse * (g - mean_g - normed * mean_gn)
-            gate_one_sums = jnp.sum(grad_mid * branch_one, axis=1)
-            grad_one = (mod(i, 2) * grad_mid).astype(bf16)
-            out_sums = jnp.sum(grad_one.astype(f32), axis=1)
-            bpart = dot(down_full, hidden, 1, 0).reshape(NX, 2, CB, T)
-            branch_two = (
-                bpart[:, 0]
-                + tp_xor(bpart[:, 1].astype(bf16), 1).astype(f32)
-                + down_bias.reshape(NX, 2, CB, 1)[:, 0]
-            )
-            half = lambda v: v.reshape(NX, 2, CB, -1)[:, 0]
-            gate_two_sums = jnp.sum(half(cot) * branch_two, axis=2)
-            out_half = (half(mid_rows) + half(mod(i, 5)) * branch_two).astype(bf16)
-            out_blocks = [out_half[0]] + [tp_xor(out_half[k], 2 * k) for k in range(1, NX)]
-            out_own = jnp.concatenate(out_blocks, axis=1)
-            down_sums = jnp.sum(grad_two.astype(f32), axis=1)
-            mids.append(
-                dict(
-                    grad_two=grad_two,
-                    hidden=hidden,
-                    grad_pre=grad_pre,
-                    mlp_in=mlp_in,
-                    grad_one=grad_one,
-                    grad_mid=grad_mid,
-                    out_own=out_own,
-                    sums=(gate_one_sums, shift_sums, scale_sums),
-                    gate_two_sums=gate_two_sums,
-                    gate_sums=gate_sums,
-                    up_sums=up_sums,
-                    out_sums=out_sums,
-                    down_sums=down_sums,
-                )
-            )
-
-        block_output = own_order(jnp.stack([m["out_own"] for m in mids]), 2)
-
-        grad_down = sum(dot(m["grad_two"], m["hidden"], 1, 1) for m in mids)
-        grad_up = sum(dot(m["mlp_in"], m["grad_pre"], 1, 1) for m in mids)
-        late_grads = jnp.stack(
-            [
-                jnp.stack([g[:, k * FL : (k + 1) * FL] for g in (grad_up, grad_down)])
-                for k in range(NX)
+            branch,
+            rows_all,
+            cots.reshape(I, D, T),
+            mods,
+            group_rows,
+            late_full,
+        )
+        late_grads = grads_call(NT, lhs, rhs)
+
+        gate_sums = jnp.sum(fsums[:, 1].reshape(I, NX * GL, GW), axis=2)
+        up_sums = jnp.sum(fsums[:, 0], axis=0)
+        all_sums = jnp.sum(sums[:, 3:5], axis=0)
+
+        def x_message(k):
+            mine = slice(2 * k * CB, (2 * k + 1) * CB)
+            parts = [
+                jnp.concatenate(
+                    [
+                        sums[:, :3, mine].reshape(I, 3 * CB),
+                        sums[:, 5, k * CB : (k + 1) * CB],
+                        gate_sums[:, k * GL : (k + 1) * GL],
+                    ],
+                    axis=1,
+                ).reshape(-1),
+                all_sums[:, mine].reshape(-1),
+                up_sums[k * FL : (k + 1) * FL],
             ]
-        ).astype(bf16).reshape(NX, 2, NT, RB, FL)
-
-        def x_message(k):
-            parts = []
-            for m in mids:
-                for v in m["sums"]:
-                    parts.append(v[2 * k * CB : (2 * k + 1) * CB])
-                parts.append(m["gate_two_sums"][k])
-                parts.append(m["gate_sums"][k * GL : (k + 1) * GL])
-            for name, size in (("out_sums", 2 * k * CB), ("down_sums", 2 * k * CB)):
-                parts.append(sum(m[name] for m in mids)[size : size + CB])
-            parts.append(sum(m["up_sums"] for m in mids)[k * FL : (k + 1) * FL])
             return jnp.concatenate(parts)
 
         x_total = x_message(0)
@@ -1377,15 +1735,14 @@
             ],
             axis=0,
         )
-        grad_one = jnp.stack([m["grad_one"] for m in mids]).reshape(I, NX, 2, CB, T)
-        grad_mid = jnp.stack([m["grad_mid"] for m in mids]).reshape(I, NX, 2, CB, T)
         grad_input, late, grad_qkv, grad_out, lasts, cond_sum, _ = bwd_call(
             NT,
             NP,
             head_gate.reshape(-1),
-            grad_one,
-            grad_mid[:, :, 0].astype(bf16),
-            grad_mid[:, 0, 0],
+            grad_one.reshape(I, NX, 2, CB, T),
+            go_first,
+            grad_mid_out,
+            grad_mid_own,
             qkv_all,
             mixed_all,
             lse_all,
@@ -1393,7 +1750,7 @@
             attn_all,
             rows_all,
             stats_all,
-            columns[:CB, : I * 6].reshape(CB, I, 6)[:, :, 1].T[:, :, None],
+            mods,
             early_full,
             late_grads,
             base,

time: 663 us -> 537 us (0.81)
  matrix products: 120 us -> 2.49 us
  Pallas kernels: 384 us -> 479 us
  local copies, waits for them, and re-layouts: 90 us -> 31.2 us
  other arithmetic: 53.1 us -> 15.5 us
    dot_general x18 -> x0, matrix products: 116 us -> none  [dot(): lax.dot_general(a, b, (((ca,), (cb,)), ((), ())), preferred_element_type=...]
    pallas_call x1 -> x3, Pallas kernels: 70.4 us -> 164 us  [the longest x1 87 us: mlp_call(): pl.pallas_call(functools.partial(mlp_kernel, NT, NP), grid=(I,), in_specs...]
    slice x35 -> x6, local copies, waits for them, and re-layouts: 23.2 us -> 1.95 us  [the longest x1 0.92 us: x_message(): sums[:, 5, k * CB:(k + 1) * CB]]
    reduce_sum x12 -> x3, other arithmetic: 20.5 us -> 2.17 us  [the longest x1 1.16 us: body(): up_sums = jnp.sum(fsums[:, 0], axis=0)]
    another operation x12 -> x2, other arithmetic: 18.8 us -> 0.79 us  [the longest x1 0.65 us: body(): jnp.stack([jnp.repeat(mods[2 * k, :, 6 * ML + HL:6 * ML + HL + GL], GW, a...]
    unnamed x208 -> x38, local copies, waits for them, and re-layouts: 24.9 us -> 7 us
    pallas_call x1, Pallas kernels: 118 us -> 130 us  [fwd_call(): pl.pallas_call(functools.partial(fwd_kernel, NT, NP), grid=(I, HL + 2), i...]
    pallas_call x1, Pallas kernels: 196 us -> 185 us  [bwd_call(): pl.pallas_call(functools.partial(bwd_kernel, NT, NP), grid=(I, HL + 2), i...]
  transfers between devices with their start and end apart: 13 -> 2, of which waited for: 0 -> 0; matrix products, arithmetic and copies ran while one was open for 29% -> 3% of each run, Pallas kernels for 29% -> 15%
where the time goes in v4:
time: 537 us; the launch traced here: 533 us
  Pallas kernels  479 us (89%)
  local copies, waits for them, and re-layouts  31.2 us (6%)
  other arithmetic  15.5 us (3%)
    pallas_call x1, Pallas kernels, bwd_call(): pl.pallas_call(functools.partial(bwd_kernel, NT, NP), grid=(I, HL + 2), i...  185 us
    pallas_call x1, Pallas kernels, fwd_call(): pl.pallas_call(functools.partial(fwd_kernel, NT, NP), grid=(I, HL + 2), i...  130 us
    pallas_call x1, Pallas kernels, mlp_call(): pl.pallas_call(functools.partial(mlp_kernel, NT, NP), grid=(I,), in_specs...  87 us
    pallas_call x1, Pallas kernels, start_call(): pl.pallas_call(functools.partial(start_kernel, NT, NP), in_specs=[pl.Bloc...  53.5 us
    pallas_call x1, Pallas kernels, grads_call(): pl.pallas_call(grads_kernel, grid=(2, NX), in_specs=[pl.BlockSpec((I, 1,...  23.9 us
  transfers between devices with their start and end apart: 2, of which 0 were waited for; matrix products, arithmetic and copies ran while one was open for 3% of the time, Pallas kernels for 15%

profile of v4, /device:TPU:0, one launch (start us, length us, event | category | flops | bytes accessed | tf_op | source)
XLA Modules:
  0.0 533.3 jit_solution(10924246110862032976)
XLA Ops:
  0.7 2.3 fusion.27
  3.0 2.9 collective-permute-start
  5.9 0.7 convert_element_type.82
  6.8 0.7 pad.87
  7.5 0.7 concatenate.80
  8.2 0.8 add_convert_fusion
  9.0 0.7 convert_element_type.85
  9.8 0.7 broadcast_in_dim.46
  10.5 0.7 pad_maximum_fusion.6
  11.3 0.7 pad_bitcast_fusion.1
  12.0 0.8 concatenate.78
  12.8 0.7 fusion.9
  13.7 0.1 reshape.231
  13.9 0.1 reshape.232
  14.1 0.3 reshape.229
  14.4 0.2 copy.61
  14.6 0.2 pad.77
  14.8 1.0 reshape.230
  15.9 1.0 reshape.259.bias_ref
  16.9 1.2 pad.83.ada_ref
  18.1 0.1 fusion.22
  18.4 1.1 concatenate.71.w_ref
  19.5 53.5 %start.1 = (bf16[1,4,288,1024]{3,2,1,0:T(8,128)(2,1)S(1)}, bf16[8,144,1344]{2,1,0:T(8,128)(2,1)S(1)}, f32[4,8,2432]{2,1,0:T(8,128)S(1)}, f32[8,128]{1,0:T(8,128)S(1)}, f32[8,8,384]{2,1,0:T(8,128)S(1)}) custom-call(bf16[3,288,1024]{2,1,0:T(8,128)(2,1)S(1)} %copy-done.1, bf16[144,1344]{1,0:T(8,128)(2,1)S(1)} %concatenate.71.w_ref, ...), custom_call_target="tpu_custom_call" | custom-call | tf_op jit(solution)/shard_map/start/pallas_call | solution.py:258
  73.0 1.7 copy-done
  74.7 1.5 copy-done.4
  76.2 0.6 reshape_squeeze.10.gate_ref
  77.2 0.6 pad_maximum_fusion.3.gate_ref
  77.9 2.5 pad_maximum_fusion.late_ref
  80.4 130.2 %forward.1 = (bf16[3,1152,1024]{2,1,0:T(8,128)(2,1)}, bf16[3,960,1024]{2,1,0:T(8,128)(2,1)}, f32[3,320,1024]{2,1,0:T(8,128)}, bf16[3,320,1024]{2,1,0:T(8,128)(2,...) custom-call(f32[12]{0:T(128)} %reshape_squeeze.10.gate_ref, ...), custom_call_target="tpu_custom_call" | custom-call | tf_op jit(solution)/shard_map/forward/pallas_call | solution.py:567
  210.6 87.0 %feed_forward.1 = (bf16[3,2,1152,512]{3,2,1,0:T(8,128)(2,1)}, bf16[3,2,2,1152,512]{4,3,2,1,0:T(8,128)(2,1)}, bf16[3,1152,512]{2,1,0:T(8,128)(2,1)}, bf16[3,2,288...) custom-call(f32[3,2,2,288,512]{4,3,2,1,0:T(8,128)} %get-tuple-elemen, ...), custom_call_target="tpu_custom_call" | custom-call | tf_op jit(solution)/shard_map/feed_forward/pallas_call | solution.py:865
  297.6 0.9 slice_reduce_fusion.2
  298.5 0.9 fusion.28
  299.4 0.9 fusion.29
  300.5 1.2 slice_reduce_fusion.1
  302.2 0.7 collective-permute-start.1
  303.4 23.9 %late_grads.1.late_ref = bf16[2,2,8,144,1152]{4,3,2,1,0:T(8,128)(2,1)} custom-call(bf16[3,2,1152,512]{3,2,1,0:T(8,128)(2,1)} %get-tuple-element.65.lhs_ref, bf16[3,2,2,1152,512]{4,3,2,1,0:T(8,128)(2,1)} %get-tuple-element.66.rhs_ref), custom_call_target="tpu_custom_call" | custom-call | tf_op jit(solution)/shard_map/late_grads/pallas_call | solution.py:943
  327.8 0.6 pad.95.factor_ref
  328.5 0.1 concatenate.89
  328.6 0.7 concatenate.90.base_ref
  329.3 184.6 %backward.1 = (f32[3,288,1024]{2,1,0:T(8,128)}, f32[2,144,1152]{2,1,0:T(8,128)}, f32[144,960]{1,0:T(8,128)}, f32[144,320]{1,0:T(8,128)}, f32[8,8,2432]{2,1,0:T(8...) custom-call(f32[12]{0:T(128)} %reshape_squeeze.10.gate_ref, bf16[3,2,2,288,512]{4,3,2,1,0:T(8,128)(2,1)} %bitcast.62, ...), custom_call_target="tpu_custom_call" | custom-call | tf_op jit(solution)/shard_map/backward/pallas_call | solution.py:1451
  513.9 0.9 slice_reduce_fusion.10
  514.8 1.2 slice_reduce_fusion
  515.9 1.1 slice.200
  517.1 0.7 slice_reduce_fusion.6
  517.7 0.6 slice_reduce_fusion.4
  518.3 0.2 convolution_bitcast_fusion
  518.5 0.6 fusion.33
  519.1 0.6 fusion.35
  519.7 0.8 slice_bitcast_fusion.2
  520.7 0.6 fusion.11
  521.3 0.1 reshape.250
  521.7 0.6 slice_reduce_fusion.11
  522.3 0.1 reshape.251
  522.4 0.1 dot_general.11
  522.6 0.2 reshape.254
  522.8 0.9 reshape.255
  523.7 0.6 reshape.252
  524.3 0.9 reshape.261
  525.2 0.9 copy.76
  526.1 1.1 slice_bitcast_fusion
  527.2 0.6 pad_maximum_fusion.5
  527.8 2.3 fusion
  530.1 1.2 copy.93
  531.3 1.8 copy.94
  (108 shorter events, 3.5 us)
Async XLA Ops:
  0.7 13.0 %copy-start.11 = (bf16[288,144]{0,1:T(8,128)(2,1)S(1)}, bf16[288,144]{0,1:T(8,128)(2,1)}, u32[]{:S(2)}) copy-start(bf16[288,144]{0,1:T(8,128)(2,1)} %param.29) | copy-start | bytes 248836
  0.7 13.4 %copy-start.9 = (bf16[144,3,288]{2,0,1:T(8,128)(2,1)S(1)}, bf16[144,3,288]{2,0,1:T(8,128)(2,1)}, u32[]{:S(2)}) copy-start(bf16[144,3,288]{2,0,1:T(8,128)(2,1)} %param.27) | copy-start | bytes 746500
  3.0 74.9 %collective-permute-start = (bf16[2,144,1152]{2,1,0:T(8,128)(2,1)}, bf16[2,144,1152]{2,1,0:T(8,128)(2,1)}, u32[]{:S(2)}, u32[]{:S(2)}) collective-permute-start(bf16[2,144,1152]{2,1,0:T(8,128)(2,1)} %get-tuple-element.86), channel_id=1, source_target_pairs={{0,2},{1,3},{2,0},{3,1},{4,6},{5,7},{6,4},{7,5},{8,10},{9,11},{10,... | collective-permute-start | bytes 1990664 | tf_op jit(solution)/shard_map/ppermute | solution.py:1551
  14.5 4.9 copy-start.1
  18.1 59.8 %copy-start.2 = (bf16[6,144,384]{2,1,0:T(8,128)(2,1)}, bf16[6,144,384]{2,1,0:T(8,128)(2,1)S(1)}, u32[]{:S(2)}) copy-start(bf16[6,144,384]{2,1,0:T(8,128)(2,1)S(1)} %pad.83.ada_ref) | copy-start | bytes 1990660
  73.0 1.7 copy-start
  74.7 1.5 copy-start.4
  76.2 4.2 copy-start.3
  302.2 25.1 %collective-permute-start.1 = (f32[5196]{0:T(1024)S(1)}, f32[5196]{0:T(1024)S(1)}, u32[]{:S(2)}, u32[]{:S(2)}) collective-permute-start(f32[5196]{0:T(1024)S(1)} %concatenate.88), channel_id=1, source_target_pairs={{0,2},{1,3},{2,0},{3,1},{4,6},{5,7},{6,4},{7,5},{8,10},{9,11},{10,... | collective-permute-start | bytes 62360 | tf_op jit(solution)/shard_map/ppermute | solution.py:1551
  303.3 24.3 %copy-start.13 = (s32[3,4]{1,0:T(4,128)S(1)}, s32[3,4]{1,0:T(4,128)}, u32[]{:S(2)}) copy-start(s32[3,4]{1,0:T(4,128)} %param.24) | copy-start | bytes 148
  303.3 24.3 %copy-start.14 = (s32[3,4]{1,0:T(4,128)S(1)}, s32[3,4]{1,0:T(4,128)}, u32[]{:S(2)}) copy-start(s32[3,4]{1,0:T(4,128)} %param.23) | copy-start | bytes 148
  329.3 191.4 %copy-start.12 = (bf16[3,1152]{1,0:T(4,128)(2,1)S(1)}, bf16[3,1152]{1,0:T(4,128)(2,1)}, u32[]{:S(2)}) copy-start(bf16[3,1152]{1,0:T(4,128)(2,1)} %param.21) | copy-start | bytes 20740
  513.9 8.7 %copy-start.10 = (f32[144,320]{1,0:T(8,128)S(1)}, f32[144,320]{1,0:T(8,128)}, u32[]{:S(2)}) copy-start(f32[144,320]{1,0:T(8,128)} %get-tuple-element.75) | copy-start | bytes 552964
  513.9 9.8 %copy-start.8 = (f32[144,960]{1,0:T(8,128)S(1)}, f32[144,960]{1,0:T(8,128)}, u32[]{:S(2)}) copy-start(f32[144,960]{1,0:T(8,128)} %get-tuple-element.74) | copy-start | bytes 1658884
  523.7 2.4 copy-start.7
  526.0 4.0 copy-start.6
  527.8 3.5 copy-start.5

commit v5 on v4

--- a/solution.py
+++ b/solution.py
@@ -509,7 +509,7 @@
         at((n + 1) * steps + HL)(functools.partial(add_x, n))
 
     events = [(k, d) for d in range(1, NT // 2 + 1) for k in range(NX)]
-    early = [steps + HL, 2 * steps - 1][: len(events)] if I > 1 else []
+    early = [6, 7, 13, 14] if I > 2 else []
     for n, (k, d) in zip(early, events):
         at(n)(functools.partial(land_hop, k, d))
 
@@ -962,7 +962,7 @@
     gc_ref, dqkv_ref, rows_buf, gin_buf, st_out, st_in, msg_ref, heads_ref, qv_ref,
     l_own, l_out, l_in, lx_out, lx_in, q_out, q_in, part_ref, sum_ref, lasts_buf,
     g_send, g_recv, c_send, c_recv, x_send, x_recv, t_send, t_recv, l_send, l_recv, lx_send, lx_recv,
-    q_send, q_recv, s_send, s_recv, m_send, m_recv, local_sem, own_sem,
+    q_send, q_recv, s_send, s_recv, m_send, m_recv, m2_send, m2_recv, local_sem, own_sem,
 ):
     NX, SUB = NP // 2, NT // NP
     I, CB, T = gm_ref.shape
@@ -1223,8 +1223,14 @@
 
     QWIDE = (QKV + 127) // 128 * 128
 
-    def last_copy(k):
-        return copy_to(msg_ref, lasts_buf.at[k], s_send.at[0, k], s_recv.at[0, k], ((t + k) % NT, p))
+    pieces = ((1024, 6 * ML - 1024), (0, 1024), (6 * ML, 128))
+
+    def last_copy(k, n):
+        lanes = pl.ds(*pieces[n])
+        return copy_to(
+            msg_ref.at[:, lanes], lasts_buf.at[k, :, lanes], m2_send.at[n, k], m2_recv.at[n, k],
+            ((t + k) % NT, p),
+        )
 
     def part_copy(k):
         return copy_to(
@@ -1238,12 +1244,14 @@
         msg_ref[I : I + 1, :QKV] = qv_ref[0:1, :QKV]
         msg_ref[:, 6 * ML :] = msg_ref[:, 6 * ML :] + heads_ref[...] * factor_ref[...]
         for k in range(1, NT):
-            last_copy(k).start()
+            last_copy(k, 1).start()
+            last_copy(k, 2).start()
         lasts_buf[0] = msg_ref[...]
 
     def cond_second():
         for k in range(1, NT):
-            last_copy(k).wait_recv()
+            for n in range(3):
+                last_copy(k, n).wait_recv()
         lasts_ref[...] = lasts_buf[...]
         grads = lasts_buf[...].reshape(NT * 8, -1)
         total = 0.0
@@ -1271,6 +1279,12 @@
             total = total + sum_ref[r]
         cond_ref[...] = total
 
+    def finish_core():
+        if I > 1:
+            add_x(I - 2)
+            add_stats(I - 2)
+        add_core(I - 1)
+
     @at(0)
     def _():
         greet(t, p, NT, NP)
@@ -1283,6 +1297,8 @@
         for n in range(I):
             rows_copy(n).start()
         msg_ref[...] = base_ref[...]
+        for k in range(1, NT):
+            last_copy(k, 0).start()
         heads_ref[...] = jnp.zeros_like(heads_ref)
         qv_ref[...] = jnp.zeros_like(qv_ref)
         wt_ref[...] = w_ref[:, w_ref.shape[1] - HO :].T
@@ -1342,6 +1358,8 @@
 
     @pl.when(s == HL + 1)
     def _():
+        for n in range(1, I):
+            at(n * steps + HL + 1)(lambda n=n: core_copy(n - 1).wait_send())
         for r in range(NP):
             w = w_ref[r * CB : (r + 1) * CB, :QKV]
             part = jnp.dot(w, dqkv_ref[...], preferred_element_type=f32)
@@ -1349,10 +1367,15 @@
                 own_ref[r // 2] = part
             else:
                 core_out[r // 2] = part.astype(bf16)
+        for n in range(I):
+            at(n * steps + HL + 1)(lambda n=n: core_copy(n).start())
         for b in range(0, NT, 2):
             rows = slice(b * RB, (b + 2) * RB)
             v = dot(attn_ref[0, rows], dqkv_ref[...], 1, 1)
             accq_ref[b : b + 2] = accq_ref[b : b + 2] + v.reshape(2, RB, QKV)
+        at(I * steps - 1)(functools.partial(finish_core))
+        for b in range(0, NT, 2):
+            rows = slice(b * RB, (b + 2) * RB)
             v = 0.0
             for k in range(NX):
                 g = go_buf[k].reshape(D, T)[rows]
@@ -1360,19 +1383,17 @@
             acco_ref[b : b + 2] = acco_ref[b : b + 2] + v.reshape(2, RB, HO)
         qv_ref[0:1, :QKV] = qv_ref[0:1, :QKV] + tokens(dqkv_ref[...].astype(f32))
 
-    for n in range(I):
-        at(n * steps + HL + 1)(lambda n=n: core_copy(n).start())
     for n in range(I - 1):
         at((n + 1) * steps + 1)(functools.partial(add_core, n))
-        at((n + 1) * steps + HL - 1)(functools.partial(add_x, n))
-
-        @at((n + 1) * steps + HL)
-        def _(n=n):
-            add_stats(n)
-            core_copy(n).wait_send()
-
-    events = [functools.partial(l_event, k, h) for h in range(1, HOPS + 1) for k in range(NX)]
-    early = [2, 3, steps + HL - 1, steps + HL, 3 * steps - 2, 3 * steps - 1] if I > 2 else []
+        if n + 2 < I:
+            at((n + 1) * steps + HL + 1)(functools.partial(add_x, n))
+        if n + 2 < I:
+            at((n + 2) * steps)(functools.partial(add_stats, n))
+
+    events = [
+        functools.partial(l_event, k, h) for h in range(1, HOPS + 1) for k in reversed(range(NX))
+    ]
+    early = [2, 3, 8, 9, 13, 14] if I > 2 else []
     early = early[: len(events)]
     for n, event in zip(early, events):
         at(n)(event)
@@ -1381,18 +1402,13 @@
     def _():
         rest = events[len(early) :]
         q_event(0)
-        add_core(I - 1)
-        todo = [functools.partial(add_x, I - 1), cond_first, functools.partial(q_event, 1),
-                functools.partial(add_stats, I - 1), cond_second]
-        todo += [functools.partial(q_event, h) for h in range(2, 3)] + [cond_third]
-        todo += [functools.partial(q_event, h) for h in range(3, HOPS + 1)] + [cond_last]
-        ratio = max(1, len(todo) // max(1, len(rest)))
-        while todo or rest:
-            if rest:
-                rest.pop(0)()
-            for _ in range(ratio if rest else len(todo)):
-                if todo:
-                    todo.pop(0)()
+        todo = [functools.partial(add_x, I - 1), cond_first, functools.partial(q_event, 1)]
+        todo += [functools.partial(add_stats, I - 1), cond_second]
+        todo += rest[:-1] + [functools.partial(q_event, 2), cond_third] + rest[-1:]
+        todo += [functools.partial(q_event, h) for h in range(3, HOPS)] + [cond_last]
+        todo += [functools.partial(q_event, HOPS)]
+        for step in todo:
+            step()
         for k in range(1, NX):
             lx_copy(k).wait_recv()
             for u in range(2):
@@ -1421,7 +1437,8 @@
         for k in range(1, NX):
             lx_copy(k).wait_send()
         for k in range(1, NT):
-            last_copy(k).wait_send()
+            for n in range(3):
+                last_copy(k, n).wait_send()
             part_copy(k).wait_send()
         for r in range(1, NP):
             sum_copy(r).wait_send()
@@ -1530,6 +1547,8 @@
             dma((3, max(NT, NP))),
             dma((I, NX)),
             dma((I, NX)),
+            dma((3, NT)),
+            dma((3, NT)),
             dma((NX + I + I * NX,)),
             dma((NX, 2)),
         ],

time: 537 us -> 496 us (0.924)
  Pallas kernels: 479 us -> 438 us
    pallas_call x1, Pallas kernels: 185 us -> 164 us  [bwd_call(): pl.pallas_call(functools.partial(bwd_kernel, NT, NP), grid=(I, HL + 2), i...]
    pallas_call x1, Pallas kernels: 130 us -> 110 us  [fwd_call(): pl.pallas_call(functools.partial(fwd_kernel, NT, NP), grid=(I, HL + 2), i...]
  transfers between devices with their start and end apart: 2 -> 2, of which waited for: 0 -> 0; matrix products, arithmetic and copies ran while one was open for 3% -> 3% of each run, Pallas kernels for 15% -> 16%
where the time goes in v5:
time: 496 us; the launch traced here: 493 us
  Pallas kernels  438 us (88%)
  local copies, waits for them, and re-layouts  31.2 us (6%)
  other arithmetic  15.5 us (3%)
    pallas_call x1, Pallas kernels, bwd_call(): pl.pallas_call(functools.partial(bwd_kernel, NT, NP), grid=(I, HL + 2), i...  164 us
    pallas_call x1, Pallas kernels, fwd_call(): pl.pallas_call(functools.partial(fwd_kernel, NT, NP), grid=(I, HL + 2), i...  110 us
    pallas_call x1, Pallas kernels, mlp_call(): pl.pallas_call(functools.partial(mlp_kernel, NT, NP), grid=(I,), in_specs...  86.6 us
    pallas_call x1, Pallas kernels, start_call(): pl.pallas_call(functools.partial(start_kernel, NT, NP), in_specs=[pl.Bloc...  53.5 us
    pallas_call x1, Pallas kernels, grads_call(): pl.pallas_call(grads_kernel, grid=(2, NX), in_specs=[pl.BlockSpec((I, 1,...  23.9 us
  transfers between devices with their start and end apart: 2, of which 0 were waited for; matrix products, arithmetic and copies ran while one was open for 3% of the time, Pallas kernels for 16%

profile of v5, /device:TPU:0, one launch (start us, length us, event | category | flops | bytes accessed | tf_op | source)
XLA Modules:
  0.0 492.5 jit_solution(10729301425638694714)
XLA Ops:
  0.7 2.3 fusion.27
  3.0 2.9 collective-permute-start
  5.9 0.7 convert_element_type.82
  6.8 0.7 pad.87
  7.5 0.7 concatenate.80
  8.2 0.8 add_convert_fusion
  9.0 0.7 convert_element_type.85
  9.8 0.7 broadcast_in_dim.46
  10.5 0.7 pad_maximum_fusion.6
  11.3 0.7 pad_bitcast_fusion.1
  12.0 0.8 concatenate.78
  12.8 0.7 fusion.9
  13.7 0.1 reshape.231
  13.9 0.1 reshape.232
  14.1 0.3 reshape.229
  14.4 0.2 copy.61
  14.6 0.2 pad.77
  14.8 1.0 reshape.230
  15.9 1.0 reshape.259.bias_ref
  16.9 1.2 pad.83.ada_ref
  18.1 0.1 fusion.22
  18.4 1.1 concatenate.71.w_ref
  19.5 53.5 %start.1 = (bf16[1,4,288,1024]{3,2,1,0:T(8,128)(2,1)S(1)}, bf16[8,144,1344]{2,1,0:T(8,128)(2,1)S(1)}, f32[4,8,2432]{2,1,0:T(8,128)S(1)}, f32[8,128]{1,0:T(8,128)S(1)}, f32[8,8,384]{2,1,0:T(8,128)S(1)}) custom-call(bf16[3,288,1024]{2,1,0:T(8,128)(2,1)S(1)} %copy-done.1, bf16[144,1344]{1,0:T(8,128)(2,1)S(1)} %concatenate.71.w_ref, ...), custom_call_target="tpu_custom_call" | custom-call | tf_op jit(solution)/shard_map/start/pallas_call | solution.py:258
  73.0 1.7 copy-done
  74.7 1.5 copy-done.4
  76.2 0.6 reshape_squeeze.10.gate_ref
  77.2 0.6 pad_maximum_fusion.3.gate_ref
  77.9 2.5 pad_maximum_fusion.late_ref
  80.4 109.9 %forward.1 = (bf16[3,1152,1024]{2,1,0:T(8,128)(2,1)}, bf16[3,960,1024]{2,1,0:T(8,128)(2,1)}, f32[3,320,1024]{2,1,0:T(8,128)}, bf16[3,320,1024]{2,1,0:T(8,128)(2,...) custom-call(f32[12]{0:T(128)} %reshape_squeeze.10.gate_ref, ...), custom_call_target="tpu_custom_call" | custom-call | tf_op jit(solution)/shard_map/forward/pallas_call | solution.py:567
  190.3 86.6 %feed_forward.1 = (bf16[3,2,1152,512]{3,2,1,0:T(8,128)(2,1)}, bf16[3,2,2,1152,512]{4,3,2,1,0:T(8,128)(2,1)}, bf16[3,1152,512]{2,1,0:T(8,128)(2,1)}, bf16[3,2,288...) custom-call(f32[3,2,2,288,512]{4,3,2,1,0:T(8,128)} %get-tuple-elemen, ...), custom_call_target="tpu_custom_call" | custom-call | tf_op jit(solution)/shard_map/feed_forward/pallas_call | solution.py:865
  276.9 0.9 slice_reduce_fusion.2
  277.9 0.9 fusion.28
  278.8 0.9 fusion.29
  279.9 1.2 slice_reduce_fusion.1
  281.6 1.0 collective-permute-start.1
  283.0 23.9 %late_grads.1.late_ref = bf16[2,2,8,144,1152]{4,3,2,1,0:T(8,128)(2,1)} custom-call(bf16[3,2,1152,512]{3,2,1,0:T(8,128)(2,1)} %get-tuple-element.65.lhs_ref, bf16[3,2,2,1152,512]{4,3,2,1,0:T(8,128)(2,1)} %get-tuple-element.66.rhs_ref), custom_call_target="tpu_custom_call" | custom-call | tf_op jit(solution)/shard_map/late_grads/pallas_call | solution.py:943
  307.4 0.6 pad.95.factor_ref
  308.1 0.1 concatenate.89
  308.2 0.7 concatenate.90.base_ref
  308.9 164.2 %backward.1 = (f32[3,288,1024]{2,1,0:T(8,128)}, f32[2,144,1152]{2,1,0:T(8,128)}, f32[144,960]{1,0:T(8,128)}, f32[144,320]{1,0:T(8,128)}, f32[8,8,2432]{2,1,0:T(8...) custom-call(f32[12]{0:T(128)} %reshape_squeeze.10.gate_ref, bf16[3,2,2,288,512]{4,3,2,1,0:T(8,128)(2,1)} %bitcast.62, ...), custom_call_target="tpu_custom_call" | custom-call | tf_op jit(solution)/shard_map/backward/pallas_call | solution.py:1468
  473.1 0.9 slice_reduce_fusion.10
  474.0 1.2 slice_reduce_fusion
  475.1 1.1 slice.200
  476.3 0.7 slice_reduce_fusion.6
  476.9 0.6 slice_reduce_fusion.4
  477.6 0.2 convolution_bitcast_fusion
  477.7 0.6 fusion.33
  478.4 0.6 fusion.35
  478.9 0.8 slice_bitcast_fusion.2
  479.9 0.6 fusion.11
  480.5 0.1 reshape.250
  480.9 0.6 slice_reduce_fusion.11
  481.5 0.1 reshape.251
  481.7 0.1 dot_general.11
  481.8 0.2 reshape.254
  482.0 0.9 reshape.255
  482.9 0.6 reshape.252
  483.5 0.9 reshape.261
  484.4 0.9 copy.76
  485.3 1.1 slice_bitcast_fusion
  486.4 0.6 pad_maximum_fusion.5
  487.0 2.3 fusion
  489.3 1.2 copy.93
  490.5 1.8 copy.94
  (108 shorter events, 3.5 us)
Async XLA Ops:
  0.7 13.0 %copy-start.11 = (bf16[288,144]{0,1:T(8,128)(2,1)S(1)}, bf16[288,144]{0,1:T(8,128)(2,1)}, u32[]{:S(2)}) copy-start(bf16[288,144]{0,1:T(8,128)(2,1)} %param.29) | copy-start | bytes 248836
  0.7 13.4 %copy-start.9 = (bf16[144,3,288]{2,0,1:T(8,128)(2,1)S(1)}, bf16[144,3,288]{2,0,1:T(8,128)(2,1)}, u32[]{:S(2)}) copy-start(bf16[144,3,288]{2,0,1:T(8,128)(2,1)} %param.27) | copy-start | bytes 746500
  3.0 74.9 %collective-permute-start = (bf16[2,144,1152]{2,1,0:T(8,128)(2,1)}, bf16[2,144,1152]{2,1,0:T(8,128)(2,1)}, u32[]{:S(2)}, u32[]{:S(2)}) collective-permute-start(bf16[2,144,1152]{2,1,0:T(8,128)(2,1)} %get-tuple-element.86), channel_id=1, source_target_pairs={{0,2},{1,3},{2,0},{3,1},{4,6},{5,7},{6,4},{7,5},{8,10},{9,11},{10,... | collective-permute-start | bytes 1990664 | tf_op jit(solution)/shard_map/ppermute | solution.py:1570
  14.5 4.9 copy-start.1
  18.1 59.8 %copy-start.2 = (bf16[6,144,384]{2,1,0:T(8,128)(2,1)}, bf16[6,144,384]{2,1,0:T(8,128)(2,1)S(1)}, u32[]{:S(2)}) copy-start(bf16[6,144,384]{2,1,0:T(8,128)(2,1)S(1)} %pad.83.ada_ref) | copy-start | bytes 1990660
  73.0 1.7 copy-start
  74.7 1.5 copy-start.4
  76.2 4.2 copy-start.3
  281.6 25.3 %collective-permute-start.1 = (f32[5196]{0:T(1024)S(1)}, f32[5196]{0:T(1024)S(1)}, u32[]{:S(2)}, u32[]{:S(2)}) collective-permute-start(f32[5196]{0:T(1024)S(1)} %concatenate.88), channel_id=1, source_target_pairs={{0,2},{1,3},{2,0},{3,1},{4,6},{5,7},{6,4},{7,5},{8,10},{9,11},{10,... | collective-permute-start | bytes 62360 | tf_op jit(solution)/shard_map/ppermute | solution.py:1570
  282.9 24.3 %copy-start.13 = (s32[3,4]{1,0:T(4,128)S(1)}, s32[3,4]{1,0:T(4,128)}, u32[]{:S(2)}) copy-start(s32[3,4]{1,0:T(4,128)} %param.24) | copy-start | bytes 148
  283.0 24.3 %copy-start.14 = (s32[3,4]{1,0:T(4,128)S(1)}, s32[3,4]{1,0:T(4,128)}, u32[]{:S(2)}) copy-start(s32[3,4]{1,0:T(4,128)} %param.23) | copy-start | bytes 148
  308.9 171.0 %copy-start.12 = (bf16[3,1152]{1,0:T(4,128)(2,1)S(1)}, bf16[3,1152]{1,0:T(4,128)(2,1)}, u32[]{:S(2)}) copy-start(bf16[3,1152]{1,0:T(4,128)(2,1)} %param.21) | copy-start | bytes 20740
  473.1 8.7 %copy-start.10 = (f32[144,320]{1,0:T(8,128)S(1)}, f32[144,320]{1,0:T(8,128)}, u32[]{:S(2)}) copy-start(f32[144,320]{1,0:T(8,128)} %get-tuple-element.75) | copy-start | bytes 552964
  473.1 9.8 %copy-start.8 = (f32[144,960]{1,0:T(8,128)S(1)}, f32[144,960]{1,0:T(8,128)}, u32[]{:S(2)}) copy-start(f32[144,960]{1,0:T(8,128)} %get-tuple-element.74) | copy-start | bytes 1658884
  482.9 2.4 copy-start.7
  485.3 4.0 copy-start.6
  487.0 3.5 copy-start.5

commit v6 on v5

--- a/solution.py
+++ b/solution.py
@@ -506,7 +506,7 @@
 
     for n in range(I - 1):
         at((n + 1) * steps + 1)(functools.partial(add_core, n))
-        at((n + 1) * steps + HL)(functools.partial(add_x, n))
+        at((n + 1) * steps + HL + 1)(functools.partial(add_x, n))
 
     events = [(k, d) for d in range(1, NT // 2 + 1) for k in range(NX)]
     early = [6, 7, 13, 14] if I > 2 else []

time: 496 us -> 494 us (level)
  no operation moved by 1% of the time
where the time goes in v6:
time: 494 us; the launch traced here: 490 us
  Pallas kernels  436 us (88%)
  local copies, waits for them, and re-layouts  31.2 us (6%)
  other arithmetic  15.5 us (3%)
    pallas_call x1, Pallas kernels, bwd_call(): pl.pallas_call(functools.partial(bwd_kernel, NT, NP), grid=(I, HL + 2), i...  162 us
    pallas_call x1, Pallas kernels, fwd_call(): pl.pallas_call(functools.partial(fwd_kernel, NT, NP), grid=(I, HL + 2), i...  110 us
    pallas_call x1, Pallas kernels, mlp_call(): pl.pallas_call(functools.partial(mlp_kernel, NT, NP), grid=(I,), in_specs...  86.6 us
    pallas_call x1, Pallas kernels, start_call(): pl.pallas_call(functools.partial(start_kernel, NT, NP), in_specs=[pl.Bloc...  53.5 us
    pallas_call x1, Pallas kernels, grads_call(): pl.pallas_call(grads_kernel, grid=(2, NX), in_specs=[pl.BlockSpec((I, 1,...  23.9 us
  transfers between devices with their start and end apart: 2, of which 0 were waited for; matrix products, arithmetic and copies ran while one was open for 3% of the time, Pallas kernels for 16%

profile of v6, /device:TPU:0, one launch (start us, length us, event | category | flops | bytes accessed | tf_op | source)
XLA Modules:
  0.0 490.4 jit_solution(4705059952896051950)
XLA Ops:
  0.7 2.3 fusion.27
  3.0 2.9 collective-permute-start
  5.9 0.7 convert_element_type.82
  6.8 0.7 pad.87
  7.5 0.7 concatenate.80
  8.2 0.8 add_convert_fusion
  9.0 0.7 convert_element_type.85
  9.8 0.7 broadcast_in_dim.46
  10.5 0.7 pad_maximum_fusion.6
  11.3 0.7 pad_bitcast_fusion.1
  12.0 0.8 concatenate.78
  12.8 0.7 fusion.9
  13.7 0.1 reshape.231
  13.9 0.1 reshape.232
  14.1 0.3 reshape.229
  14.4 0.2 copy.61
  14.6 0.2 pad.77
  14.8 1.0 reshape.230
  15.9 1.0 reshape.259.bias_ref
  16.9 1.2 pad.83.ada_ref
  18.1 0.1 fusion.22
  18.4 1.1 concatenate.71.w_ref
  19.5 53.5 %start.1 = (bf16[1,4,288,1024]{3,2,1,0:T(8,128)(2,1)S(1)}, bf16[8,144,1344]{2,1,0:T(8,128)(2,1)S(1)}, f32[4,8,2432]{2,1,0:T(8,128)S(1)}, f32[8,128]{1,0:T(8,128)S(1)}, f32[8,8,384]{2,1,0:T(8,128)S(1)}) custom-call(bf16[3,288,1024]{2,1,0:T(8,128)(2,1)S(1)} %copy-done.1, bf16[144,1344]{1,0:T(8,128)(2,1)S(1)} %concatenate.71.w_ref, ...), custom_call_target="tpu_custom_call" | custom-call | tf_op jit(solution)/shard_map/start/pallas_call | solution.py:258
  73.0 1.7 copy-done
  74.7 1.5 copy-done.4
  76.2 0.6 reshape_squeeze.10.gate_ref
  77.2 0.6 pad_maximum_fusion.3.gate_ref
  77.9 2.5 pad_maximum_fusion.late_ref
  80.4 109.9 %forward.1 = (bf16[3,1152,1024]{2,1,0:T(8,128)(2,1)}, bf16[3,960,1024]{2,1,0:T(8,128)(2,1)}, f32[3,320,1024]{2,1,0:T(8,128)}, bf16[3,320,1024]{2,1,0:T(8,128)(2,...) custom-call(f32[12]{0:T(128)} %reshape_squeeze.10.gate_ref, ...), custom_call_target="tpu_custom_call" | custom-call | tf_op jit(solution)/shard_map/forward/pallas_call | solution.py:567
  190.3 86.6 %feed_forward.1 = (bf16[3,2,1152,512]{3,2,1,0:T(8,128)(2,1)}, bf16[3,2,2,1152,512]{4,3,2,1,0:T(8,128)(2,1)}, bf16[3,1152,512]{2,1,0:T(8,128)(2,1)}, bf16[3,2,288...) custom-call(f32[3,2,2,288,512]{4,3,2,1,0:T(8,128)} %get-tuple-elemen, ...), custom_call_target="tpu_custom_call" | custom-call | tf_op jit(solution)/shard_map/feed_forward/pallas_call | solution.py:865
  276.9 0.9 slice_reduce_fusion.2
  277.9 0.9 fusion.28
  278.8 0.9 fusion.29
  279.9 1.2 slice_reduce_fusion.1
  281.6 1.0 collective-permute-start.1
  283.0 23.9 %late_grads.1.late_ref = bf16[2,2,8,144,1152]{4,3,2,1,0:T(8,128)(2,1)} custom-call(bf16[3,2,1152,512]{3,2,1,0:T(8,128)(2,1)} %get-tuple-element.65.lhs_ref, bf16[3,2,2,1152,512]{4,3,2,1,0:T(8,128)(2,1)} %get-tuple-element.66.rhs_ref), custom_call_target="tpu_custom_call" | custom-call | tf_op jit(solution)/shard_map/late_grads/pallas_call | solution.py:943
  307.4 0.6 pad.95.factor_ref
  308.1 0.1 concatenate.89
  308.2 0.7 concatenate.90.base_ref
  308.9 162.1 %backward.1 = (f32[3,288,1024]{2,1,0:T(8,128)}, f32[2,144,1152]{2,1,0:T(8,128)}, f32[144,960]{1,0:T(8,128)}, f32[144,320]{1,0:T(8,128)}, f32[8,8,2432]{2,1,0:T(8...) custom-call(f32[12]{0:T(128)} %reshape_squeeze.10.gate_ref, bf16[3,2,2,288,512]{4,3,2,1,0:T(8,128)(2,1)} %bitcast.62, ...), custom_call_target="tpu_custom_call" | custom-call | tf_op jit(solution)/shard_map/backward/pallas_call | solution.py:1468
  471.0 0.9 slice_reduce_fusion.10
  471.8 1.2 slice_reduce_fusion
  473.0 1.1 slice.200
  474.1 0.7 slice_reduce_fusion.6
  474.8 0.6 slice_reduce_fusion.4
  475.4 0.2 convolution_bitcast_fusion
  475.6 0.6 fusion.33
  476.2 0.6 fusion.35
  476.8 0.8 slice_bitcast_fusion.2
  477.8 0.6 fusion.11
  478.4 0.1 reshape.250
  478.8 0.6 slice_reduce_fusion.11
  479.4 0.1 reshape.251
  479.5 0.1 dot_general.11
  479.7 0.2 reshape.254
  479.9 0.9 reshape.255
  480.8 0.6 reshape.252
  481.4 0.9 reshape.261
  482.3 0.9 copy.76
  483.1 1.1 slice_bitcast_fusion
  484.3 0.6 pad_maximum_fusion.5
  484.9 2.3 fusion
  487.2 1.2 copy.93
  488.4 1.8 copy.94
  (108 shorter events, 3.5 us)
Async XLA Ops:
  0.7 13.0 %copy-start.11 = (bf16[288,144]{0,1:T(8,128)(2,1)S(1)}, bf16[288,144]{0,1:T(8,128)(2,1)}, u32[]{:S(2)}) copy-start(bf16[288,144]{0,1:T(8,128)(2,1)} %param.29) | copy-start | bytes 248836
  0.7 13.4 %copy-start.9 = (bf16[144,3,288]{2,0,1:T(8,128)(2,1)S(1)}, bf16[144,3,288]{2,0,1:T(8,128)(2,1)}, u32[]{:S(2)}) copy-start(bf16[144,3,288]{2,0,1:T(8,128)(2,1)} %param.27) | copy-start | bytes 746500
  3.0 74.9 %collective-permute-start = (bf16[2,144,1152]{2,1,0:T(8,128)(2,1)}, bf16[2,144,1152]{2,1,0:T(8,128)(2,1)}, u32[]{:S(2)}, u32[]{:S(2)}) collective-permute-start(bf16[2,144,1152]{2,1,0:T(8,128)(2,1)} %get-tuple-element.86), channel_id=1, source_target_pairs={{0,2},{1,3},{2,0},{3,1},{4,6},{5,7},{6,4},{7,5},{8,10},{9,11},{10,... | collective-permute-start | bytes 1990664 | tf_op jit(solution)/shard_map/ppermute | solution.py:1570
  14.5 4.9 %copy-start.1 = (bf16[3,288,1024]{2,1,0:T(8,128)(2,1)S(1)}, bf16[3,288,1024]{2,1,0:T(8,128)(2,1)}, u32[]{:S(2)}) copy-start(bf16[3,288,1024]{2,1,0:T(8,128)(2,1)} %x_ref.3) | copy-start | bytes 5308420
  18.1 59.8 %copy-start.2 = (bf16[6,144,384]{2,1,0:T(8,128)(2,1)}, bf16[6,144,384]{2,1,0:T(8,128)(2,1)S(1)}, u32[]{:S(2)}) copy-start(bf16[6,144,384]{2,1,0:T(8,128)(2,1)S(1)} %pad.83.ada_ref) | copy-start | bytes 1990660
  73.0 1.7 copy-start
  74.7 1.5 copy-start.4
  76.2 4.2 copy-start.3
  281.6 25.3 %collective-permute-start.1 = (f32[5196]{0:T(1024)S(1)}, f32[5196]{0:T(1024)S(1)}, u32[]{:S(2)}, u32[]{:S(2)}) collective-permute-start(f32[5196]{0:T(1024)S(1)} %concatenate.88), channel_id=1, source_target_pairs={{0,2},{1,3},{2,0},{3,1},{4,6},{5,7},{6,4},{7,5},{8,10},{9,11},{10,... | collective-permute-start | bytes 62360 | tf_op jit(solution)/shard_map/ppermute | solution.py:1570
  282.9 24.3 %copy-start.13 = (s32[3,4]{1,0:T(4,128)S(1)}, s32[3,4]{1,0:T(4,128)}, u32[]{:S(2)}) copy-start(s32[3,4]{1,0:T(4,128)} %param.24) | copy-start | bytes 148
  283.0 24.3 %copy-start.14 = (s32[3,4]{1,0:T(4,128)S(1)}, s32[3,4]{1,0:T(4,128)}, u32[]{:S(2)}) copy-start(s32[3,4]{1,0:T(4,128)} %param.23) | copy-start | bytes 148
  308.9 168.9 %copy-start.12 = (bf16[3,1152]{1,0:T(4,128)(2,1)S(1)}, bf16[3,1152]{1,0:T(4,128)(2,1)}, u32[]{:S(2)}) copy-start(bf16[3,1152]{1,0:T(4,128)(2,1)} %param.21) | copy-start | bytes 20740
  471.0 8.7 %copy-start.10 = (f32[144,320]{1,0:T(8,128)S(1)}, f32[144,320]{1,0:T(8,128)}, u32[]{:S(2)}) copy-start(f32[144,320]{1,0:T(8,128)} %get-tuple-element.75) | copy-start | bytes 552964
  471.0 9.8 %copy-start.8 = (f32[144,960]{1,0:T(8,128)S(1)}, f32[144,960]{1,0:T(8,128)}, u32[]{:S(2)}) copy-start(f32[144,960]{1,0:T(8,128)} %get-tuple-element.74) | copy-start | bytes 1658884
  480.8 2.4 copy-start.7
  483.1 4.0 copy-start.6
  484.9 3.5 copy-start.5
